TPU v7x, 32 devices: a whole 2x2x4 slice. The times are simulated.
32 devices in a mesh: ctx: 16 (over z, x, core), pipe: 2 (over y).
Axes of the slice: x: 2, y: 2, z: 4, core: 2. Of those that a mesh axis runs over, the one named last changes fastest.
Arguments:
- query_fwd: bfloat16 [2, 2048, 2048], P('pipe', 'ctx'), may hold values from -6 to 6
- key_fwd: bfloat16 [2, 2048, 512], P('pipe', 'ctx'), may hold values from -6 to 6
- value_fwd: bfloat16 [2, 2048, 512], P('pipe', 'ctx'), may hold values from -6 to 6
- gate_fwd: bfloat16 [2, 2048, 2048], P('pipe', 'ctx'), may hold values from -6 to 6
- types_fwd: int32 [2, 2048], P('pipe', 'ctx'), may hold values from 0 to 63
- query_bwd: bfloat16 [2, 2048, 2048], P('pipe', 'ctx'), may hold values from -6 to 6
- key_bwd: bfloat16 [2, 2048, 512], P('pipe', 'ctx'), may hold values from -6 to 6
- value_bwd: bfloat16 [2, 2048, 512], P('pipe', 'ctx'), may hold values from -6 to 6
- grad_out: bfloat16 [2, 2048, 2048], P('pipe', 'ctx'), may hold values from -6 to 6
- types_bwd: int32 [2, 2048], P('pipe', 'ctx'), may hold values from 0 to 63
- type_key: bfloat16 [2, 64, 512], P('pipe'), may hold values from -4.1875 to 4.1875
- norm_gain: float32 [2, 2048], P('pipe'), may hold values from 0.5 to 1.5
- stretch_order: int32 [2, 32], P('pipe'), may hold values from 0 to 31, as said below
Outputs:
- handed: bfloat16 [2, 2048, 2048], P('pipe', 'ctx')
- query_grad: bfloat16 [2, 2048, 2048], P('pipe', 'ctx')
- key_grad: bfloat16 [2, 2048, 512], P('pipe', 'ctx')
- value_grad: bfloat16 [2, 2048, 512], P('pipe', 'ctx')
Inputs may be any that keep to these rules, and one draw needn't show every extreme that they name: `stretch_order`: in each section's row the stored stretch slots 2 c and 2 c + 1 (those of index c of ctx) hold two stretches whose numbers add to 31, in either order; each row names every stretch once.
All inputs are finite; a program needn't handle non-finite values.
Results may differ from a plain program's by a relative error of at most 0.02.
Values may be sent and summed in bfloat16 or wider, within the bound.
No kernel may reach another device: no remote copies, remote signals or barrier semaphores. Data moves between devices by JAX's collectives and lax.ppermute only.
A program may use at most 128 MiB of HBM per device.

v0:
```python
import functools
import math

import jax
import jax.numpy as jnp
from jax import lax
from jax.experimental import pallas as pl
from jax.experimental.pallas import tpu as pltpu
from jax.sharding import PartitionSpec as P

HEAD = 128
QUAD = 4
SCALE = HEAD ** (-0.5)
EXP2_SCALE = -SCALE / math.log(2.0)
GAIN_ROWS = 16
norm_eps = 1e-06

VMEM = pl.BlockSpec(memory_space=pltpu.VMEM)
HBM = pl.BlockSpec(memory_space=pltpu.HBM)
SMEM = pl.BlockSpec(memory_space=pltpu.SMEM)
MIB = 1024 * 1024

NN = (((1,), (0,)), ((), ()))
NT = (((1,), (1,)), ((), ()))
TN = (((0,), (0,)), ((), ()))


def dot(a, b, dims):
    return lax.dot_general(a, b, dims, preferred_element_type=jnp.float32)


def bf16(*shape):
    return jax.ShapeDtypeStruct(shape, jnp.bfloat16)


def place():
    index = lax.axis_index("ctx")
    return index // QUAD, index % QUAD


def columns(index, width):
    return pl.ds(pl.multiple_of(index * width, width), width)


def pack_keys(key_ref, value_ref, types_ref, table_ref, *refs):
    pieces, (keys, types, table, typed, arrived, placed) = refs[:QUAD], refs[QUAD:]
    _, member = place()
    copies = [
        pltpu.make_async_copy(source, target, arrived.at[i])
        for i, (source, target) in enumerate(
            [(types_ref, types), (table_ref.at[0], table), (key_ref.at[0], keys)]
        )
    ]
    copies += [
        pltpu.make_async_copy(
            value_ref.at[0, :, columns(member ^ d, HEAD)], pieces[d].at[:, HEAD:], placed.at[d]
        )
        for d in range(QUAD)
    ]
    for copy in copies:
        copy.start()
    for copy in copies[:3]:
        copy.wait()
    onehot = (
        lax.broadcasted_iota(jnp.int32, (table.shape[0], types.shape[1]), 0) == types[...]
    ).astype(jnp.float32).astype(jnp.bfloat16)
    type_rows = dot(onehot, table[...], TN)
    typed[...] = (keys[...].astype(jnp.float32) + type_rows).astype(jnp.bfloat16)
    for d in range(QUAD):
        pieces[d][:, :HEAD] = typed[:, columns(member ^ d, HEAD)]
    for copy in copies[3:]:
        copy.wait()


def pack_queries(query_ref, grad_ref, forward_ref, gate_ref, gain_ref, *refs):
    pieces, forward_pieces, (gate_out, placed) = refs[:QUAD], refs[QUAD : 2 * QUAD], refs[2 * QUAD :]
    _, member = place()
    width = query_ref.shape[2] // QUAD
    rows = gate_ref.shape[1]
    copies = []
    for d in reversed(range(QUAD)):
        for i, (source, target) in enumerate(
            [
                (query_ref, pieces[d].at[:, :width]),
                (grad_ref, pieces[d].at[:, width:]),
                (forward_ref, forward_pieces[d]),
            ]
        ):
            source = source.at[0, :, columns(member ^ d, width)]
            copies.append(pltpu.make_async_copy(source, target, placed.at[3 * d + i]))
    copies.append(
        pltpu.make_async_copy(gate_ref.at[0], gate_out.at[:rows, :], placed.at[3 * QUAD])
    )
    for copy in copies:
        copy.start()
    rest = gain_ref[...]
    parts = []
    for _ in range(3):
        part = rest.astype(jnp.bfloat16).astype(jnp.float32)
        parts.append(part)
        rest = rest - part
    parts.append(jnp.zeros((GAIN_ROWS - 3, rest.shape[1]), jnp.float32))
    gate_out[rows:, :] = jnp.concatenate(parts, axis=0).astype(jnp.bfloat16)
    for copy in copies:
        copy.wait()


def stretch_of(order_ref, quad_index, member, d, e):
    return order_ref[0, 2 * (quad_index * QUAD + (member ^ d)) + e]


def rows_at(index, count):
    return pl.ds(pl.multiple_of(index * count, count), count)


def in_sequence(order_ref, stacks, stretch_rows, keys, values):
    z, member = place()
    nz = len(stacks)
    for s, stack in enumerate(stacks):
        source = lax.rem(z - s + nz, nz)
        for d in range(QUAD):
            for e in range(2):
                rows = rows_at(stretch_of(order_ref, source, member, d, e), stretch_rows)
                lower = (2 * d + e) * stretch_rows
                keys[rows, :] = stack[lower : lower + stretch_rows, :HEAD]
                values[rows, :] = stack[lower : lower + stretch_rows, HEAD:]


def shrink_of(stretch, stretch_rows):
    pos = stretch * stretch_rows + lax.broadcasted_iota(jnp.int32, (stretch_rows, HEAD), 0)
    return lax.rsqrt((pos + 1).astype(jnp.float32))


def step_place(first, second, step, d, groups):
    blocks = first // groups + 1
    late = step >= blocks
    row = jnp.where(late, 2 * d + 1, 2 * d)
    stretch = jnp.where(late, second, first)
    block = jnp.where(late, step - blocks, step)
    return row, stretch, block


def sigmoid_of(raw, visible):
    part = pl.reciprocal(1.0 + jnp.exp2(raw * EXP2_SCALE), approx=True)
    return jnp.where(visible, part, 0.0)


def forward_kernel(nz, order_ref, *refs):
    queries, refs = refs[:QUAD], refs[QUAD:]
    stacks, refs = refs[:nz], refs[nz:]
    outs, refs = refs[:QUAD], refs[QUAD:]
    keys, values, stacked, total, gap = refs
    z, member = place()
    stretch_rows = queries[0].shape[0] // 2
    groups = outs[0].shape[1] // HEAD
    block_rows = groups * stretch_rows
    steps = keys.shape[0] // block_rows + 1
    in_sequence(order_ref, stacks, stretch_rows, keys, values)
    for d in range(QUAD):
        for e in range(2):
            for g in range(groups):
                stacked[2 * d + e, g * stretch_rows : (g + 1) * stretch_rows, :] = queries[d][
                    e * stretch_rows : (e + 1) * stretch_rows,
                    g * HEAD : (g + 1) * HEAD,
                ]
    total[...] = jnp.zeros_like(total)
    gap[...] = lax.broadcasted_iota(jnp.int32, gap.shape, 1) - lax.rem(
        lax.broadcasted_iota(jnp.int32, gap.shape, 0), stretch_rows
    )

    def advance(step, _):
        for d in range(QUAD):
            row, stretch, block = step_place(
                stretch_of(order_ref, z, member, d, 0),
                stretch_of(order_ref, z, member, d, 1),
                step,
                d,
                groups,
            )
            rows = rows_at(block, block_rows)
            raw = dot(stacked[row], keys[rows, :], NT)
            visible = gap[...] <= stretch * stretch_rows - block * block_rows
            weights = (raw * SCALE * sigmoid_of(raw, visible)).astype(jnp.bfloat16)
            total[row] += dot(weights, values[rows, :], NN)
        return 0

    lax.fori_loop(0, steps, advance, 0)
    for d in range(QUAD):
        for e in range(2):
            shrink = shrink_of(stretch_of(order_ref, z, member, d, e), stretch_rows)
            for g in range(groups):
                outs[d][e * stretch_rows : (e + 1) * stretch_rows, g * HEAD : (g + 1) * HEAD] = (
                    total[2 * d + e, g * stretch_rows : (g + 1) * stretch_rows, :] * shrink
                ).astype(jnp.bfloat16)


def backward_kernel(nz, order_ref, *refs):
    queries, refs = refs[:QUAD], refs[QUAD:]
    stacks, refs = refs[:nz], refs[nz:]
    query_outs, refs = refs[:QUAD], refs[QUAD:]
    key_outs, refs = refs[:nz], refs[nz:]
    keys, values, keys_t, stacked, grads, total_t, key_total, value_total, gap = refs
    z, member = place()
    stretch_rows = queries[0].shape[0] // 2
    groups = queries[0].shape[1] // (2 * HEAD)
    block_rows = groups * stretch_rows
    blocks = keys.shape[0] // block_rows
    steps = blocks + 1
    in_sequence(order_ref, stacks, stretch_rows, keys, values)
    for block in range(blocks):
        lower = block * block_rows
        keys_t[block] = keys[lower : lower + block_rows, :].T
    offset = groups * HEAD
    for d in range(QUAD):
        for e in range(2):
            shrink = shrink_of(stretch_of(order_ref, z, member, d, e), stretch_rows)
            rows = slice(e * stretch_rows, (e + 1) * stretch_rows)
            for g in range(groups):
                into = slice(g * stretch_rows, (g + 1) * stretch_rows)
                stacked[2 * d + e, into, :] = queries[d][rows, g * HEAD : (g + 1) * HEAD]
                grads[2 * d + e, into, :] = (
                    queries[d][rows, offset + g * HEAD : offset + (g + 1) * HEAD].astype(
                        jnp.float32
                    )
                    * shrink
                ).astype(jnp.bfloat16)
    total_t[...] = jnp.zeros_like(total_t)
    key_total[...] = jnp.zeros_like(key_total)
    value_total[...] = jnp.zeros_like(value_total)
    gap[...] = lax.broadcasted_iota(jnp.int32, gap.shape, 0) - lax.rem(
        lax.broadcasted_iota(jnp.int32, gap.shape, 1), stretch_rows
    )

    def advance(step, _):
        for d in range(QUAD):
            row, stretch, block = step_place(
                stretch_of(order_ref, z, member, d, 0),
                stretch_of(order_ref, z, member, d, 1),
                step,
                d,
                groups,
            )
            rows = rows_at(block, block_rows)
            raw = dot(keys[rows, :], stacked[row], NT)
            weight_grad = dot(values[rows, :], grads[row], NT)
            visible = gap[...] <= stretch * stretch_rows - block * block_rows
            part = sigmoid_of(raw, visible)
            weights = raw * SCALE * part
            score_grad = (weight_grad * (part + weights * (1.0 - part))).astype(jnp.bfloat16)
            weights = weights.astype(jnp.bfloat16)
            total_t[row] += dot(keys_t[block], score_grad, NN)
            key_total[rows, :] += dot(score_grad, stacked[row], NN)
            value_total[rows, :] += dot(weights, grads[row], NN)
        return 0

    lax.fori_loop(0, steps, advance, 0)
    for d in range(QUAD):
        for e in range(2):
            query_grad = (total_t[2 * d + e].T * SCALE).astype(jnp.bfloat16)
            for g in range(groups):
                query_outs[d][
                    e * stretch_rows : (e + 1) * stretch_rows, g * HEAD : (g + 1) * HEAD
                ] = query_grad[g * stretch_rows : (g + 1) * stretch_rows, :]
    for s in range(nz):
        target = lax.rem(z + s, nz)
        for d in range(QUAD):
            for e in range(2):
                rows = rows_at(stretch_of(order_ref, target, member, d, e), stretch_rows)
                lower = (2 * d + e) * stretch_rows
                key_outs[s][lower : lower + stretch_rows, :HEAD] = (
                    key_total[rows, :] * SCALE
                ).astype(jnp.bfloat16)
                key_outs[s][lower : lower + stretch_rows, HEAD:] = value_total[rows, :].astype(
                    jnp.bfloat16
                )


def sum_kernel(*refs):
    parts, pieces = refs[:3], refs[3:]
    rows = pieces[0].shape[0]
    for d in range(QUAD):
        lower = d * rows
        pieces[d][...] = sum(
            part[lower : lower + rows, :].astype(jnp.float32) for part in parts
        ).astype(jnp.bfloat16)


def key_grad_kernel(*refs):
    pieces, (key_out, value_out) = refs[:QUAD], refs[QUAD:]
    _, member = place()
    for d in range(QUAD):
        head = columns(member ^ d, HEAD)
        key_out[0, :, head] = pieces[d][:, :HEAD]
        value_out[0, :, head] = pieces[d][:, HEAD:]


def query_grad_kernel(*refs):
    pieces, out = refs[:QUAD], refs[QUAD]
    _, member = place()
    for d in range(QUAD):
        out[0, :, columns(member ^ d, pieces[d].shape[1])] = pieces[d][...]


def gate_kernel(*refs):
    pieces, (gate_ref, out) = refs[:QUAD], refs[QUAD:]
    _, member = place()
    rows = out.shape[1]
    attended = [piece[...].astype(jnp.float32) for piece in pieces]
    square = sum(jnp.sum(part * part, axis=1, keepdims=True) for part in attended)
    factor = lax.rsqrt(square / out.shape[2] + norm_eps)
    for d in range(QUAD):
        head = columns(member ^ d, pieces[d].shape[1])
        gain = sum(gate_ref[rows : rows + GAIN_ROWS, head].astype(jnp.float32)[i : i + 1] for i in range(3))
        out[0, :, head] = (
            attended[d] * factor * gain * gate_ref[:rows, head].astype(jnp.float32)
        ).astype(jnp.bfloat16)


def call(kernel, name, out_shape, specs, *args, scratch=(), flops=0, transcendentals=0, vmem=40):
    size = sum(a.size * a.dtype.itemsize for a in args)
    size += sum(math.prod(o.shape) * o.dtype.itemsize for o in out_shape)
    return pl.pallas_call(
        kernel,
        name=name,
        out_shape=out_shape,
        in_specs=specs,
        out_specs=[VMEM] * len(out_shape),
        scratch_shapes=list(scratch),
        compiler_params=pltpu.CompilerParams(vmem_limit_bytes=vmem * MIB),
        cost_estimate=pl.CostEstimate(
            flops=flops, bytes_accessed=size, transcendentals=transcendentals
        ),
    )(*args)


def body(
    query_fwd,
    key_fwd,
    value_fwd,
    gate_fwd,
    types_fwd,
    query_bwd,
    key_bwd,
    value_bwd,
    grad_out,
    types_bwd,
    type_key,
    norm_gain,
    stretch_order,
):
    devices = lax.axis_size("ctx")
    nz = devices // QUAD
    rows = query_fwd.shape[1]
    total_rows = rows * devices
    width = query_fwd.shape[2] // QUAD
    groups = width // HEAD
    stretch_rows = rows // 2
    block_rows = groups * stretch_rows
    steps = total_rows // block_rows + 1
    pairs = steps * QUAD * block_rows * block_rows

    def swap(pieces):
        return [pieces[0]] + [
            lax.ppermute(pieces[d], "ctx", [(i, i ^ d) for i in range(devices)])
            for d in range(1, QUAD)
        ]

    def turn(block, s):
        return lax.ppermute(
            block, "ctx", [(i, (i + s * QUAD) % devices) for i in range(devices)]
        )

    def hand(block, d):
        sections = lax.axis_size("pipe")
        route = [
            (i * sections + p, (i ^ d) * sections + (p + 1) % sections)
            for i in range(devices)
            for p in range(sections)
        ]
        return lax.ppermute(block, ("ctx", "pipe"), route)

    def pack(key, value, types, name):
        return call(
            pack_keys,
            name,
            [bf16(rows, 2 * HEAD)] * QUAD,
            [HBM] * 4,
            key,
            value,
            types,
            type_key,
            scratch=[
                pltpu.VMEM(key.shape[1:], jnp.bfloat16),
                pltpu.VMEM(types.shape, jnp.int32),
                pltpu.VMEM(type_key.shape[1:], jnp.bfloat16),
                pltpu.VMEM(key.shape[1:], jnp.bfloat16),
                pltpu.SemaphoreType.DMA((3,)),
                pltpu.SemaphoreType.DMA((QUAD,)),
            ],
            vmem=60,
        )

    ahead = nz // 2

    def ring_up(block):
        return turn(block, 1)

    def ring_down(block):
        return turn(block, nz - 1)

    def gather_first(stack):
        return [stack, ring_up(stack)], [ring_down(stack)]

    def gather_rest(up, down):
        while len(up) <= ahead:
            up = up + [ring_up(up[-1])]
        while len(up) + len(down) < nz:
            down = down + [ring_down(down[-1])]
        return up + down[::-1]

    def reduce_first(parts):
        return ring_up(parts[ahead]), ring_down(parts[ahead + 1])

    def add(a, b):
        return (a.astype(jnp.float32) + b.astype(jnp.float32)).astype(jnp.bfloat16)

    def reduce_rest(parts, up, down):
        for s in range(ahead - 1, 0, -1):
            up = ring_up(add(up, parts[s]))
        for s in range(ahead + 2, nz):
            down = ring_down(add(down, parts[s]))
        return parts[0], up, down

    back_pieces = swap(pack(key_bwd, value_bwd, types_bwd, "pack_keys_bwd"))
    packed = call(
        pack_queries,
        "pack_queries",
        [bf16(rows, 2 * width)] * QUAD
        + [bf16(rows, width)] * QUAD
        + [bf16(rows + GAIN_ROWS, QUAD * width)],
        [HBM] * 4 + [VMEM],
        query_bwd,
        grad_out,
        query_fwd,
        gate_fwd,
        norm_gain,
        scratch=[pltpu.SemaphoreType.DMA((3 * QUAD + 1,))],
        vmem=60,
    )
    back_pieces, packed = lax.optimization_barrier((back_pieces, packed))
    back_queries, queries, gate_before = swap(packed[:QUAD]), packed[QUAD:-1], packed[-1]
    back_stacks = gather_rest(*gather_first(jnp.concatenate(back_pieces, axis=0)))
    pieces = pack(key_fwd, value_fwd, types_fwd, "pack_keys_fwd")
    gate_before = hand(gate_before, 0)
    back_queries, pieces, queries = lax.optimization_barrier((back_queries, pieces, queries))
    stack = jnp.concatenate(swap(pieces), axis=0)
    stack, queries, back_stacks, gate_before = lax.optimization_barrier(
        (stack, queries, back_stacks, gate_before)
    )
    stacks = [stack] + [turn(stack, s) for s in range(1, nz)]
    queries = swap(queries)

    sequence = [pltpu.VMEM((total_rows, HEAD), jnp.bfloat16)] * 2
    stacked = pltpu.VMEM((2 * QUAD, block_rows, HEAD), jnp.bfloat16)
    gap = pltpu.VMEM((block_rows, block_rows), jnp.int32)
    outs = call(
        functools.partial(backward_kernel, nz),
        "backward",
        [bf16(rows, width)] * QUAD + [bf16(QUAD * rows, 2 * HEAD)] * nz,
        [SMEM] + [VMEM] * (QUAD + nz),
        stretch_order,
        *back_queries,
        *back_stacks,
        scratch=sequence
        + [
            pltpu.VMEM((total_rows // block_rows, HEAD, block_rows), jnp.bfloat16),
            stacked,
            stacked,
            pltpu.VMEM((2 * QUAD, HEAD, block_rows), jnp.float32),
            pltpu.VMEM((total_rows, HEAD), jnp.float32),
            pltpu.VMEM((total_rows, HEAD), jnp.float32),
            gap,
        ],
        flops=10 * pairs * HEAD,
        transcendentals=2 * pairs,
    )
    query_pieces, key_parts = outs[:QUAD], outs[QUAD:]
    query_pieces, key_parts, stacks, queries = lax.optimization_barrier(
        (query_pieces, key_parts, stacks, queries)
    )
    key_sums = reduce_first(key_parts)
    query_pieces = swap(query_pieces)
    attended = call(
        functools.partial(forward_kernel, nz),
        "forward",
        [bf16(rows, width)] * QUAD,
        [SMEM] + [VMEM] * (QUAD + nz),
        stretch_order,
        *queries,
        *stacks,
        scratch=sequence
        + [stacked, pltpu.VMEM((2 * QUAD, block_rows, HEAD), jnp.float32), gap],
    )
    attended, key_up = lax.optimization_barrier((attended, key_sums[0]))
    (handed,) = call(
        gate_kernel,
        "gate",
        [bf16(*gate_fwd.shape)],
        [VMEM] * (QUAD + 1),
        *[hand(attended[d], d) for d in range(QUAD)],
        gate_before,
    )
    key_sums = reduce_rest(key_parts, key_up, key_sums[1])
    key_pieces = swap(
        call(
            sum_kernel,
            "sum_key_parts",
            [bf16(rows, 2 * HEAD)] * QUAD,
            [VMEM] * 3,
            *key_sums,
        )
    )
    handed, query_pieces = lax.optimization_barrier((handed, query_pieces))
    (query_grad,) = call(
        query_grad_kernel,
        "query_grad",
        [bf16(*query_bwd.shape)],
        [VMEM] * QUAD,
        *query_pieces,
    )
    key_grad, value_grad = call(
        key_grad_kernel,
        "key_grad",
        [bf16(*key_bwd.shape), bf16(*value_bwd.shape)],
        [VMEM] * QUAD,
        *key_pieces,
    )
    return handed, query_grad, key_grad, value_grad


def solution(mesh):
    rows = P("pipe", "ctx", None)
    types = P("pipe", "ctx")
    return jax.shard_map(
        body,
        mesh=mesh,
        in_specs=(
            rows,
            rows,
            rows,
            rows,
            types,
            rows,
            rows,
            rows,
            rows,
            types,
            P("pipe", None, None),
            P("pipe", None),
            P("pipe", None),
        ),
        out_specs=(rows, rows, rows, rows),
        check_vma=False,
    )
```

profile of v0, /device:TPU:0, one launch (start us, length us, event | category | flops | bytes accessed | tf_op | source)
XLA Modules:
  0.0 98.6 jit_solution(104405644833946297)
XLA Ops:
  0.6 2.0 %pack_keys_bwd.1 = (bf16[128,256]{1,0:T(8,128)(2,1)}, bf16[128,256]{1,0:T(8,128)(2,1)}, bf16[128,256]{1,0:T(8,128)(2,1)}, bf16[128,256]{1,0:T(8,128)(2,1)}) custom-call(bf16[1,128,512]{2,1,0:T(8,128)(2,1)} %key_ref.2, bf16[1,128,512]{2,1,0:T(8,128)(2,1)} %value_ref.2, s32[1,128]{1,0:T(1,128)} %types_ref.2, bf16[1,64,512]{2,1,0:T(8,128)(2,1)} %table_ref.3), custom_call_target="tpu_custom_call" | custom-call | bytes 590336 | tf_op jit(solution)/shard_map/pack_keys_bwd/pallas_call | solution.py:322
  2.6 0.5 collective-permute-start
  3.1 2.6 %collective-permute-start.1 = (bf16[128,256]{1,0:T(8,128)(2,1)}, bf16[128,256]{1,0:T(8,128)(2,1)S(1)}, u32[]{:S(2)}, u32[]{:S(2)}) collective-permute-start(bf16[128,256]{1,0:T(8,128)(2,1)} %get-tuple-element.102), channel_id=1, source_target_pairs={{0,4},{2,6},{4,0},{6,2},{8,12},{10,14},{12,8},{14,10},{16,20},{18,... | collective-permute-start | bytes 196616 | tf_op jit(solution)/shard_map/ppermute | solution.py:364
  5.7 0.1 collective-permute-start.2
  5.8 3.8 %pack_queries.1 = (bf16[128,1024]{1,0:T(8,128)(2,1)}, bf16[128,1024]{1,0:T(8,128)(2,1)}, bf16[128,1024]{1,0:T(8,128)(2,1)}, bf16[128,1024]{1,0:T(8,128)(2,1)}, b...) custom-call(bf16[1,128,2048]{2,1,0:T(8,128)(2,1)} %query_ref.1, ...), custom_call_target="tpu_custom_call" | custom-call | bytes 4268032 | tf_op jit(solution)/shard_map/pack_queries/pallas_call | solution.py:322
  9.6 0.5 collective-permute-done.2
  10.1 1.6 %collective-permute-start.12 = (bf16[144,2048]{1,0:T(8,128)(2,1)}, bf16[144,2048]{1,0:T(8,128)(2,1)S(1)}, u32[]{:S(2)}, u32[]{:S(2)}) collective-permute-start(bf16[144,2048]{1,0:T(8,128)(2,1)} %get-tuple-element.141), channel_id=1, source_target_pairs={{0,1},{1,0},{2,3},{3,2},{4,5},{5,4},{6,7},{7,6},{8,9},{9,8},{10,11... | collective-permute-start | bytes 1769480 | tf_op jit(solution)/shard_map/ppermute | solution.py:380
  11.7 1.6 %collective-permute-start.9 = (bf16[512,256]{1,0:T(8,128)(2,1)S(1)}, bf16[512,256]{1,0:T(8,128)(2,1)S(1)}, u32[]{:S(2)}, u32[]{:S(2)}) collective-permute-start(bf16[512,256]{1,0:T(8,128)(2,1)S(1)} %constant_dynamic-update-slice_fusion.refs_4_), channel_id=1, source_target_pairs={{0,8},{2,10},{4,12},{6,14},{8,16},{10,18},{12,20},{14,22},{16,24},... | collective-permute-start | bytes 786440 | tf_op jit(solution)/shard_map/ppermute | solution.py:369
  13.3 0.0 collective-permute-start.3
  13.3 1.3 %collective-permute-start.4 = (bf16[128,1024]{1,0:T(8,128)(2,1)S(1)}, bf16[128,1024]{1,0:T(8,128)(2,1)S(1)}, u32[]{:S(2)}, u32[]{:S(2)}) collective-permute-start(bf16[128,1024]{1,0:T(8,128)(2,1)S(1)} %copy-done.5), channel_id=1, source_target_pairs={{0,4},{2,6},{4,0},{6,2},{8,12},{10,14},{12,8},{14,10},{16,20},{18,... | collective-permute-start | bytes 786440 | tf_op jit(solution)/shard_map/ppermute | solution.py:364
  14.6 0.5 collective-permute-start.5
  15.2 6.5 %collective-permute-done.9.refs_5_ = bf16[512,256]{1,0:T(8,128)(2,1)S(1)} collective-permute-done((bf16[512,256]{1,0:T(8,128)(2,1)S(1)}, bf16[512,256]{1,0:T(8,128)(2,1)S(1)}, u32[]{:S(2)}, u32[]{:S(2)}) %collective-permute-start.9) | collective-permute-done | bytes 262176 | tf_op jit(solution)/shard_map/ppermute | solution.py:369
  21.7 1.7 %collective-permute-start.11 = (bf16[512,256]{1,0:T(8,128)(2,1)S(1)}, bf16[512,256]{1,0:T(8,128)(2,1)S(1)}, u32[]{:S(2)}, u32[]{:S(2)}) collective-permute-start(bf16[512,256]{1,0:T(8,128)(2,1)S(1)} %constant_dynamic-update-slice_fusion.refs_4_), channel_id=1, source_target_pairs={{0,24},{2,26},{4,28},{6,30},{8,0},{10,2},{12,4},{14,6},{16,8},{18,... | collective-permute-start | bytes 786440 | tf_op jit(solution)/shard_map/ppermute | solution.py:369
  23.4 0.0 collective-permute-done.3.refs_1_
  23.4 0.3 collective-permute-start.10
  23.7 2.0 %pack_keys_fwd.1 = (bf16[128,256]{1,0:T(8,128)(2,1)}, bf16[128,256]{1,0:T(8,128)(2,1)}, bf16[128,256]{1,0:T(8,128)(2,1)}, bf16[128,256]{1,0:T(8,128)(2,1)}) custom-call(bf16[1,128,512]{2,1,0:T(8,128)(2,1)} %key_ref.3, bf16[1,128,512]{2,1,0:T(8,128)(2,1)} %value_ref.3, s32[1,128]{1,0:T(1,128)} %types_ref.3, bf16[1,64,512]{2,1,0:T(8,128)(2,1)} %table_ref.3), custom_call_target="tpu_custom_call" | custom-call | bytes 590336 | tf_op jit(solution)/shard_map/pack_keys_fwd/pallas_call | solution.py:322
  25.7 0.0 collective-permute-done.4.refs_2_
  25.7 1.5 %collective-permute-done.5.refs_3_ = bf16[128,1024]{1,0:T(8,128)(2,1)S(1)} collective-permute-done((bf16[128,1024]{1,0:T(8,128)(2,1)S(1)}, bf16[128,1024]{1,0:T(8,128)(2,1)S(1)}, u32[]{:S(2)}, u32[]{:S(2)}) %collective-permute-start.5) | collective-permute-done | bytes 262176 | tf_op jit(solution)/shard_map/ppermute | solution.py:364
  27.3 0.6 collective-permute-start.6
  27.9 1.3 %collective-permute-start.7 = (bf16[128,256]{1,0:T(8,128)(2,1)}, bf16[128,256]{1,0:T(8,128)(2,1)S(1)}, u32[]{:S(2)}, u32[]{:S(2)}) collective-permute-start(bf16[128,256]{1,0:T(8,128)(2,1)} %get-tuple-element.131), channel_id=1, source_target_pairs={{0,4},{2,6},{4,0},{6,2},{8,12},{10,14},{12,8},{14,10},{16,20},{18,... | collective-permute-start | bytes 196616 | tf_op jit(solution)/shard_map/ppermute | solution.py:364
  29.2 1.1 %collective-permute-start.8 = (bf16[128,256]{1,0:T(8,128)(2,1)}, bf16[128,256]{1,0:T(8,128)(2,1)S(1)}, u32[]{:S(2)}, u32[]{:S(2)}) collective-permute-start(bf16[128,256]{1,0:T(8,128)(2,1)} %get-tuple-element.132), channel_id=1, source_target_pairs={{0,6},{2,4},{4,2},{6,0},{8,14},{10,12},{12,10},{14,8},{16,22},{18,... | collective-permute-start | bytes 196616 | tf_op jit(solution)/shard_map/ppermute | solution.py:364
  30.2 2.1 %collective-permute-done.7 = bf16[128,256]{1,0:T(8,128)(2,1)S(1)} collective-permute-done((bf16[128,256]{1,0:T(8,128)(2,1)}, bf16[128,256]{1,0:T(8,128)(2,1)S(1)}, u32[]{:S(2)}, u32[]{:S(2)}) %collective-permute-start.7) | collective-permute-done | bytes 65568 | tf_op jit(solution)/shard_map/ppermute | solution.py:364
  32.3 1.1 %collective-permute-done.8 = bf16[128,256]{1,0:T(8,128)(2,1)S(1)} collective-permute-done((bf16[128,256]{1,0:T(8,128)(2,1)}, bf16[128,256]{1,0:T(8,128)(2,1)S(1)}, u32[]{:S(2)}, u32[]{:S(2)}) %collective-permute-start.8) | collective-permute-done | bytes 65568 | tf_op jit(solution)/shard_map/ppermute | solution.py:364
  33.4 0.9 pad_maximum_fusion.refs_4_
  34.3 0.0 copy-start
  34.3 0.4 collective-permute-done.10.refs_6_
  34.7 0.2 collective-permute-start.16
  34.9 2.2 %collective-permute-start.15 = (bf16[512,256]{1,0:T(8,128)(2,1)S(1)}, bf16[512,256]{1,0:T(8,128)(2,1)S(1)}, u32[]{:S(2)}, u32[]{:S(2)}) collective-permute-start(bf16[512,256]{1,0:T(8,128)(2,1)S(1)} %pad_maximum_fusion.refs_4_), channel_id=1, source_target_pairs={{0,24},{2,26},{4,28},{6,30},{8,0},{10,2},{12,4},{14,6},{16,8},{18,... | collective-permute-start | bytes 786440 | tf_op jit(solution)/shard_map/ppermute | solution.py:369
  37.1 0.8 collective-permute-start.14
  37.9 1.3 %collective-permute-start.13 = (bf16[512,256]{1,0:T(8,128)(2,1)S(1)}, bf16[512,256]{1,0:T(8,128)(2,1)S(1)}, u32[]{:S(2)}, u32[]{:S(2)}) collective-permute-start(bf16[512,256]{1,0:T(8,128)(2,1)S(1)} %pad_maximum_fusion.refs_4_), channel_id=1, source_target_pairs={{0,8},{2,10},{4,12},{6,14},{8,16},{10,18},{12,20},{14,22},{16,24},... | collective-permute-start | bytes 786440 | tf_op jit(solution)/shard_map/ppermute | solution.py:369
  39.2 1.5 %collective-permute-start.17 = (bf16[128,512]{1,0:T(8,128)(2,1)S(1)}, bf16[128,512]{1,0:T(8,128)(2,1)S(1)}, u32[]{:S(2)}, u32[]{:S(2)}) collective-permute-start(bf16[128,512]{1,0:T(8,128)(2,1)S(1)} %copy-done.7), channel_id=1, source_target_pairs={{0,4},{2,6},{4,0},{6,2},{8,12},{10,14},{12,8},{14,10},{16,20},{18,... | collective-permute-start | bytes 393224 | tf_op jit(solution)/shard_map/ppermute | solution.py:364
  40.8 0.0 collective-permute-start.18
  40.8 14.1 %backward.1 = (bf16[128,512]{1,0:T(8,128)(2,1)S(1)}, bf16[128,512]{1,0:T(8,128)(2,1)S(1)}, bf16[128,512]{1,0:T(8,128)(2,1)S(1)}, bf16[128,512]{1,0:T(8,128)(2,1)...) custom-call(s32[1,32]{1,0:T(1,128)S(1)} %copy-done.1, ...), custom_call_target="tpu_custom_call" | custom-call | flops 3019898880 | bytes 3670144 | tf_op jit(solution)/shard_map/backward/pallas_call | solution.py:322
  54.9 0.0 collective-permute-done.18.refs_3_
  54.9 0.0 collective-permute-done.15.refs_7_
  54.9 6.5 %collective-permute-done.14.refs_6_ = bf16[512,256]{1,0:T(8,128)(2,1)S(1)} collective-permute-done((bf16[512,256]{1,0:T(8,128)(2,1)S(1)}, bf16[512,256]{1,0:T(8,128)(2,1)S(1)}, u32[]{:S(2)}, u32[]{:S(2)}) %collective-permute-start.14) | collective-permute-done | bytes 262176 | tf_op jit(solution)/shard_map/ppermute | solution.py:369
  61.4 0.0 collective-permute-done.13.refs_5_
  61.4 0.0 collective-permute-start.19
  61.4 3.8 %collective-permute-start.28 = (bf16[512,256]{1,0:T(8,128)(2,1)S(1)}, bf16[512,256]{1,0:T(8,128)(2,1)S(1)}, u32[]{:S(2)}, u32[]{:S(2)}) collective-permute-start(bf16[512,256]{1,0:T(8,128)(2,1)S(1)} %get-tuple-element.189), channel_id=1, source_target_pairs={{0,24},{2,26},{4,28},{6,30},{8,0},{10,2},{12,4},{14,6},{16,8},{18,... | collective-permute-start | bytes 786440 | tf_op jit(solution)/shard_map/ppermute | solution.py:369
  65.2 7.6 %forward.1 = (bf16[128,512]{1,0:T(8,128)(2,1)S(1)}, bf16[128,512]{1,0:T(8,128)(2,1)S(1)}, bf16[128,512]{1,0:T(8,128)(2,1)S(1)}, bf16[128,512]{1,0:T(8,128)(2,1)S(1)}) custom-call(s32[1,32]{1,0:T(1,128)S(1)} %copy-done.1, bf16[128,512]{1,0:T(8,128)(2,1)S(1)} %copy-done, bf16[128,512]{1,0:T(8,128)(2,1)S(1)} %collective-permute-done.16.refs_1_, ...), custom_call_target="tpu_custom_call" | custom-call | bytes 2097280 | tf_op jit(solution)/shard_map/forward/pallas_call | solution.py:322
  72.8 0.0 collective-permute-done.19
  72.8 0.1 add_convert_fusion
  72.9 3.2 %collective-permute-start.27 = (bf16[512,256]{1,0:T(8,128)(2,1)S(1)}, bf16[512,256]{1,0:T(8,128)(2,1)S(1)}, u32[]{:S(2)}, u32[]{:S(2)}) collective-permute-start(bf16[512,256]{1,0:T(8,128)(2,1)S(1)} %add_convert_fusion), channel_id=1, source_target_pairs={{0,8},{2,10},{4,12},{6,14},{8,16},{10,18},{12,20},{14,22},{16,24},... | collective-permute-start | bytes 786440 | tf_op jit(solution)/shard_map/ppermute | solution.py:369
  76.1 0.0 collective-permute-start.24
  76.1 0.5 collective-permute-start.20
  76.6 1.4 %collective-permute-start.21 = (bf16[128,512]{1,0:T(8,128)(2,1)S(1)}, bf16[128,512]{1,0:T(8,128)(2,1)S(1)}, u32[]{:S(2)}, u32[]{:S(2)}) collective-permute-start(bf16[128,512]{1,0:T(8,128)(2,1)S(1)} %get-tuple-element.173), channel_id=1, source_target_pairs={{0,3},{1,2},{2,1},{3,0},{4,7},{5,6},{6,5},{7,4},{8,11},{9,10},{10,... | collective-permute-start | bytes 393224 | tf_op jit(solution)/shard_map/ppermute | solution.py:380
  78.0 1.2 %collective-permute-start.22 = (bf16[128,512]{1,0:T(8,128)(2,1)S(1)}, bf16[128,512]{1,0:T(8,128)(2,1)S(1)}, u32[]{:S(2)}, u32[]{:S(2)}) collective-permute-start(bf16[128,512]{1,0:T(8,128)(2,1)S(1)} %get-tuple-element.174), channel_id=1, source_target_pairs={{0,5},{1,4},{2,7},{3,6},{4,1},{5,0},{6,3},{7,2},{8,13},{9,12},{10,... | collective-permute-start | bytes 393224 | tf_op jit(solution)/shard_map/ppermute | solution.py:380
  79.2 0.0 collective-permute-done.28.refs_2_
  79.2 1.3 %collective-permute-start.23 = (bf16[128,512]{1,0:T(8,128)(2,1)S(1)}, bf16[128,512]{1,0:T(8,128)(2,1)S(1)}, u32[]{:S(2)}, u32[]{:S(2)}) collective-permute-start(bf16[128,512]{1,0:T(8,128)(2,1)S(1)} %get-tuple-element.175), channel_id=1, source_target_pairs={{0,7},{1,6},{2,5},{3,4},{4,3},{5,2},{6,1},{7,0},{8,15},{9,14},{10,... | collective-permute-start | bytes 393224 | tf_op jit(solution)/shard_map/ppermute | solution.py:380
  80.5 7.5 %collective-permute-done.20.refs_0_ = bf16[128,512]{1,0:T(8,128)(2,1)S(1)} collective-permute-done((bf16[128,512]{1,0:T(8,128)(2,1)S(1)}, bf16[128,512]{1,0:T(8,128)(2,1)S(1)}, u32[]{:S(2)}, u32[]{:S(2)}) %collective-permute-start.20) | collective-permute-done | bytes 131104 | tf_op jit(solution)/shard_map/ppermute | solution.py:380
  88.0 1.3 %collective-permute-start.25 = (bf16[128,512]{1,0:T(8,128)(2,1)S(1)}, bf16[128,512]{1,0:T(8,128)(2,1)S(1)}, u32[]{:S(2)}, u32[]{:S(2)}) collective-permute-start(bf16[128,512]{1,0:T(8,128)(2,1)S(1)} %get-tuple-element.179), channel_id=1, source_target_pairs={{0,4},{2,6},{4,0},{6,2},{8,12},{10,14},{12,8},{14,10},{16,20},{18,... | collective-permute-start | bytes 393224 | tf_op jit(solution)/shard_map/ppermute | solution.py:364
  89.2 0.0 collective-permute-done.27.refs_1_
  89.2 0.0 collective-permute-start.26
  89.2 0.1 sum_key_parts.1
  89.4 0.7 collective-permute-done.21.refs_1_
  90.1 0.2 collective-permute-start.29
  90.3 1.3 %collective-permute-start.30 = (bf16[128,256]{1,0:T(8,128)(2,1)S(1)}, bf16[128,256]{1,0:T(8,128)(2,1)S(1)}, u32[]{:S(2)}, u32[]{:S(2)}) collective-permute-start(bf16[128,256]{1,0:T(8,128)(2,1)S(1)} %get-tuple-element.192), channel_id=1, source_target_pairs={{0,4},{2,6},{4,0},{6,2},{8,12},{10,14},{12,8},{14,10},{16,20},{18,... | collective-permute-start | bytes 196616 | tf_op jit(solution)/shard_map/ppermute | solution.py:364
  91.6 0.4 collective-permute-start.31
  91.9 1.2 %gate.1 = bf16[1,128,2048]{2,1,0:T(8,128)(2,1)} custom-call(bf16[128,512]{1,0:T(8,128)(2,1)S(1)} %collective-permute-done.20.refs_0_, bf16[128,512]{1,0:T(8,128)(2,1)S(1)} %collective-permute-done.21.refs_1_, bf16[128,512]{1,0:T(8,128)(2,1)S(1)} %collective-permute-done.22.refs_2_, bf16[128,512]{1,0:T(8,128)(2,1)S(1)} %collective-permute-done.23.refs_3_, ...), custom_call_target="tpu_custom_call" | custom-call | bytes 1638400 | tf_op jit(solution)/shard_map/gate/pallas_call | solution.py:322
  93.1 0.6 collective-permute-done.25.refs_2_
  93.7 2.0 %collective-permute-done.26.refs_3_ = bf16[128,512]{1,0:T(8,128)(2,1)S(1)} collective-permute-done((bf16[128,512]{1,0:T(8,128)(2,1)S(1)}, bf16[128,512]{1,0:T(8,128)(2,1)S(1)}, u32[]{:S(2)}, u32[]{:S(2)}) %collective-permute-start.26) | collective-permute-done | bytes 131104 | tf_op jit(solution)/shard_map/ppermute | solution.py:364
  95.7 0.8 query_grad.1
  96.6 1.3 %collective-permute-done.30.refs_2_ = bf16[128,256]{1,0:T(8,128)(2,1)S(1)} collective-permute-done((bf16[128,256]{1,0:T(8,128)(2,1)S(1)}, bf16[128,256]{1,0:T(8,128)(2,1)S(1)}, u32[]{:S(2)}, u32[]{:S(2)}) %collective-permute-start.30) | collective-permute-done | bytes 65568 | tf_op jit(solution)/shard_map/ppermute | solution.py:364
  97.9 0.8 key_grad.1
  (33 shorter events, 0.1 us)
Async XLA Ops:
  2.6 7.0 %collective-permute-start = (bf16[128,256]{1,0:T(8,128)(2,1)}, bf16[128,256]{1,0:T(8,128)(2,1)S(1)}, u32[]{:S(2)}, u32[]{:S(2)}) collective-permute-start(bf16[128,256]{1,0:T(8,128)(2,1)} %get-tuple-element.101), channel_id=1, source_target_pairs={{0,2},{2,0},{4,6},{6,4},{8,10},{10,8},{12,14},{14,12},{16,18},{18,... | collective-permute-start | bytes 196616 | tf_op jit(solution)/shard_map/ppermute | solution.py:364
  3.1 6.4 %collective-permute-start.1 = (bf16[128,256]{1,0:T(8,128)(2,1)}, bf16[128,256]{1,0:T(8,128)(2,1)S(1)}, u32[]{:S(2)}, u32[]{:S(2)}) collective-permute-start(bf16[128,256]{1,0:T(8,128)(2,1)} %get-tuple-element.102), channel_id=1, source_target_pairs={{0,4},{2,6},{4,0},{6,2},{8,12},{10,14},{12,8},{14,10},{16,20},{18,... | collective-permute-start | bytes 196616 | tf_op jit(solution)/shard_map/ppermute | solution.py:364
  5.7 4.4 %copy-start.3 = (bf16[128,256]{1,0:T(8,128)(2,1)S(1)}, bf16[128,256]{1,0:T(8,128)(2,1)}, u32[]{:S(2)}) copy-start(bf16[128,256]{1,0:T(8,128)(2,1)} %get-tuple-element.137) | copy-start | bytes 196612
  5.7 4.3 %collective-permute-start.2 = (bf16[128,256]{1,0:T(8,128)(2,1)}, bf16[128,256]{1,0:T(8,128)(2,1)S(1)}, u32[]{:S(2)}, u32[]{:S(2)}) collective-permute-start(bf16[128,256]{1,0:T(8,128)(2,1)} %get-tuple-element.103), channel_id=1, source_target_pairs={{0,6},{2,4},{4,2},{6,0},{8,14},{10,12},{12,10},{14,8},{16,22},{18,... | collective-permute-start | bytes 196616 | tf_op jit(solution)/shard_map/ppermute | solution.py:364
  10.1 3.3 %copy-start.5 = (bf16[128,1024]{1,0:T(8,128)(2,1)S(1)}, bf16[128,1024]{1,0:T(8,128)(2,1)}, u32[]{:S(2)}) copy-start(bf16[128,1024]{1,0:T(8,128)(2,1)} %get-tuple-element.115) | copy-start | bytes 786436
  10.1 4.6 %copy-start.4 = (bf16[128,1024]{1,0:T(8,128)(2,1)S(1)}, bf16[128,1024]{1,0:T(8,128)(2,1)}, u32[]{:S(2)}) copy-start(bf16[128,1024]{1,0:T(8,128)(2,1)} %get-tuple-element.116) | copy-start | bytes 786436
  10.1 24.6 %collective-permute-start.12 = (bf16[144,2048]{1,0:T(8,128)(2,1)}, bf16[144,2048]{1,0:T(8,128)(2,1)S(1)}, u32[]{:S(2)}, u32[]{:S(2)}) collective-permute-start(bf16[144,2048]{1,0:T(8,128)(2,1)} %get-tuple-element.141), channel_id=1, source_target_pairs={{0,1},{1,0},{2,3},{3,2},{4,5},{5,4},{6,7},{7,6},{8,9},{9,8},{10,11... | collective-permute-start | bytes 1769480 | tf_op jit(solution)/shard_map/ppermute | solution.py:380
  11.7 10.0 %collective-permute-start.9 = (bf16[512,256]{1,0:T(8,128)(2,1)S(1)}, bf16[512,256]{1,0:T(8,128)(2,1)S(1)}, u32[]{:S(2)}, u32[]{:S(2)}) collective-permute-start(bf16[512,256]{1,0:T(8,128)(2,1)S(1)} %constant_dynamic-update-slice_fusion.refs_4_), channel_id=1, source_target_pairs={{0,8},{2,10},{4,12},{6,14},{8,16},{10,18},{12,20},{14,22},{16,24},... | collective-permute-start | bytes 786440 | tf_op jit(solution)/shard_map/ppermute | solution.py:369
  13.3 10.1 %collective-permute-start.3 = (bf16[128,1024]{1,0:T(8,128)(2,1)}, bf16[128,1024]{1,0:T(8,128)(2,1)S(1)}, u32[]{:S(2)}, u32[]{:S(2)}) collective-permute-start(bf16[128,1024]{1,0:T(8,128)(2,1)} %get-tuple-element.114), channel_id=1, source_target_pairs={{0,2},{2,0},{4,6},{6,4},{8,10},{10,8},{12,14},{14,12},{16,18},{18,... | collective-permute-start | bytes 786440 | tf_op jit(solution)/shard_map/ppermute | solution.py:364
  13.3 12.4 %collective-permute-start.4 = (bf16[128,1024]{1,0:T(8,128)(2,1)S(1)}, bf16[128,1024]{1,0:T(8,128)(2,1)S(1)}, u32[]{:S(2)}, u32[]{:S(2)}) collective-permute-start(bf16[128,1024]{1,0:T(8,128)(2,1)S(1)} %copy-done.5), channel_id=1, source_target_pairs={{0,4},{2,6},{4,0},{6,2},{8,12},{10,14},{12,8},{14,10},{16,20},{18,... | collective-permute-start | bytes 786440 | tf_op jit(solution)/shard_map/ppermute | solution.py:364
  14.6 12.6 %collective-permute-start.5 = (bf16[128,1024]{1,0:T(8,128)(2,1)S(1)}, bf16[128,1024]{1,0:T(8,128)(2,1)S(1)}, u32[]{:S(2)}, u32[]{:S(2)}) collective-permute-start(bf16[128,1024]{1,0:T(8,128)(2,1)S(1)} %copy-done.4), channel_id=1, source_target_pairs={{0,6},{2,4},{4,2},{6,0},{8,14},{10,12},{12,10},{14,8},{16,22},{18,... | collective-permute-start | bytes 786440 | tf_op jit(solution)/shard_map/ppermute | solution.py:364
  21.7 12.6 %collective-permute-start.11 = (bf16[512,256]{1,0:T(8,128)(2,1)S(1)}, bf16[512,256]{1,0:T(8,128)(2,1)S(1)}, u32[]{:S(2)}, u32[]{:S(2)}) collective-permute-start(bf16[512,256]{1,0:T(8,128)(2,1)S(1)} %constant_dynamic-update-slice_fusion.refs_4_), channel_id=1, source_target_pairs={{0,24},{2,26},{4,28},{6,30},{8,0},{10,2},{12,4},{14,6},{16,8},{18,... | collective-permute-start | bytes 786440 | tf_op jit(solution)/shard_map/ppermute | solution.py:369
  23.4 11.3 %collective-permute-start.10 = (bf16[512,256]{1,0:T(8,128)(2,1)S(1)}, bf16[512,256]{1,0:T(8,128)(2,1)S(1)}, u32[]{:S(2)}, u32[]{:S(2)}) collective-permute-start(bf16[512,256]{1,0:T(8,128)(2,1)S(1)} %collective-permute-done.9.refs_5_), channel_id=1, source_target_pairs={{0,8},{2,10},{4,12},{6,14},{8,16},{10,18},{12,20},{14,22},{16,24},... | collective-permute-start | bytes 786440 | tf_op jit(solution)/shard_map/ppermute | solution.py:369
  23.7 11.0 %copy-start.8 = (bf16[128,512]{1,0:T(8,128)(2,1)S(1)}, bf16[128,512]{1,0:T(8,128)(2,1)}, u32[]{:S(2)}) copy-start(bf16[128,512]{1,0:T(8,128)(2,1)} %get-tuple-element.156) | copy-start | bytes 393220
  27.3 11.9 %copy-start.7 = (bf16[128,512]{1,0:T(8,128)(2,1)S(1)}, bf16[128,512]{1,0:T(8,128)(2,1)}, u32[]{:S(2)}) copy-start(bf16[128,512]{1,0:T(8,128)(2,1)} %get-tuple-element.157) | copy-start | bytes 393220
  27.3 13.5 %copy-start.6 = (bf16[128,512]{1,0:T(8,128)(2,1)S(1)}, bf16[128,512]{1,0:T(8,128)(2,1)}, u32[]{:S(2)}) copy-start(bf16[128,512]{1,0:T(8,128)(2,1)} %get-tuple-element.158) | copy-start | bytes 393220
  27.3 13.5 %copy-start.1 = (s32[1,32]{1,0:T(1,128)S(1)}, s32[1,32]{1,0:T(1,128)}, u32[]{:S(2)}) copy-start(s32[1,32]{1,0:T(1,128)} %order_ref.3) | copy-start | bytes 388
  27.3 13.5 %copy-start.2 = (bf16[128,1024]{1,0:T(8,128)(2,1)S(1)}, bf16[128,1024]{1,0:T(8,128)(2,1)}, u32[]{:S(2)}) copy-start(bf16[128,1024]{1,0:T(8,128)(2,1)} %get-tuple-element.125.refs_0_) | copy-start | bytes 786436
  27.3 1.9 %collective-permute-start.6 = (bf16[128,256]{1,0:T(8,128)(2,1)}, bf16[128,256]{1,0:T(8,128)(2,1)S(1)}, u32[]{:S(2)}, u32[]{:S(2)}) collective-permute-start(bf16[128,256]{1,0:T(8,128)(2,1)} %get-tuple-element.130), channel_id=1, source_target_pairs={{0,2},{2,0},{4,6},{6,4},{8,10},{10,8},{12,14},{14,12},{16,18},{18,... | collective-permute-start | bytes 196616 | tf_op jit(solution)/shard_map/ppermute | solution.py:364
  27.9 4.5 %collective-permute-start.7 = (bf16[128,256]{1,0:T(8,128)(2,1)}, bf16[128,256]{1,0:T(8,128)(2,1)S(1)}, u32[]{:S(2)}, u32[]{:S(2)}) collective-permute-start(bf16[128,256]{1,0:T(8,128)(2,1)} %get-tuple-element.131), channel_id=1, source_target_pairs={{0,4},{2,6},{4,0},{6,2},{8,12},{10,14},{12,8},{14,10},{16,20},{18,... | collective-permute-start | bytes 196616 | tf_op jit(solution)/shard_map/ppermute | solution.py:364
  29.2 4.3 %collective-permute-start.8 = (bf16[128,256]{1,0:T(8,128)(2,1)}, bf16[128,256]{1,0:T(8,128)(2,1)S(1)}, u32[]{:S(2)}, u32[]{:S(2)}) collective-permute-start(bf16[128,256]{1,0:T(8,128)(2,1)} %get-tuple-element.132), channel_id=1, source_target_pairs={{0,6},{2,4},{4,2},{6,0},{8,14},{10,12},{12,10},{14,8},{16,22},{18,... | collective-permute-start | bytes 196616 | tf_op jit(solution)/shard_map/ppermute | solution.py:364
  34.3 30.9 %copy-start = (bf16[128,512]{1,0:T(8,128)(2,1)S(1)}, bf16[128,512]{1,0:T(8,128)(2,1)}, u32[]{:S(2)}) copy-start(bf16[128,512]{1,0:T(8,128)(2,1)} %get-tuple-element.159.refs_0_) | copy-start | bytes 393220
  34.7 6.1 %collective-permute-start.16 = (bf16[128,512]{1,0:T(8,128)(2,1)S(1)}, bf16[128,512]{1,0:T(8,128)(2,1)S(1)}, u32[]{:S(2)}, u32[]{:S(2)}) collective-permute-start(bf16[128,512]{1,0:T(8,128)(2,1)S(1)} %copy-done.8), channel_id=1, source_target_pairs={{0,2},{2,0},{4,6},{6,4},{8,10},{10,8},{12,14},{14,12},{16,18},{18,... | collective-permute-start | bytes 393224 | tf_op jit(solution)/shard_map/ppermute | solution.py:364
  34.9 20.0 %collective-permute-start.15 = (bf16[512,256]{1,0:T(8,128)(2,1)S(1)}, bf16[512,256]{1,0:T(8,128)(2,1)S(1)}, u32[]{:S(2)}, u32[]{:S(2)}) collective-permute-start(bf16[512,256]{1,0:T(8,128)(2,1)S(1)} %pad_maximum_fusion.refs_4_), channel_id=1, source_target_pairs={{0,24},{2,26},{4,28},{6,30},{8,0},{10,2},{12,4},{14,6},{16,8},{18,... | collective-permute-start | bytes 786440 | tf_op jit(solution)/shard_map/ppermute | solution.py:369
  37.1 24.3 %collective-permute-start.14 = (bf16[512,256]{1,0:T(8,128)(2,1)S(1)}, bf16[512,256]{1,0:T(8,128)(2,1)S(1)}, u32[]{:S(2)}, u32[]{:S(2)}) collective-permute-start(bf16[512,256]{1,0:T(8,128)(2,1)S(1)} %pad_maximum_fusion.refs_4_), channel_id=1, source_target_pairs={{0,16},{2,18},{4,20},{6,22},{8,24},{10,26},{12,28},{14,30},{16,0},... | collective-permute-start | bytes 786440 | tf_op jit(solution)/shard_map/ppermute | solution.py:369
  37.9 23.5 %collective-permute-start.13 = (bf16[512,256]{1,0:T(8,128)(2,1)S(1)}, bf16[512,256]{1,0:T(8,128)(2,1)S(1)}, u32[]{:S(2)}, u32[]{:S(2)}) collective-permute-start(bf16[512,256]{1,0:T(8,128)(2,1)S(1)} %pad_maximum_fusion.refs_4_), channel_id=1, source_target_pairs={{0,8},{2,10},{4,12},{6,14},{8,16},{10,18},{12,20},{14,22},{16,24},... | collective-permute-start | bytes 786440 | tf_op jit(solution)/shard_map/ppermute | solution.py:369
  39.2 15.7 %collective-permute-start.17 = (bf16[128,512]{1,0:T(8,128)(2,1)S(1)}, bf16[128,512]{1,0:T(8,128)(2,1)S(1)}, u32[]{:S(2)}, u32[]{:S(2)}) collective-permute-start(bf16[128,512]{1,0:T(8,128)(2,1)S(1)} %copy-done.7), channel_id=1, source_target_pairs={{0,4},{2,6},{4,0},{6,2},{8,12},{10,14},{12,8},{14,10},{16,20},{18,... | collective-permute-start | bytes 393224 | tf_op jit(solution)/shard_map/ppermute | solution.py:364
  40.8 14.1 %collective-permute-start.18 = (bf16[128,512]{1,0:T(8,128)(2,1)S(1)}, bf16[128,512]{1,0:T(8,128)(2,1)S(1)}, u32[]{:S(2)}, u32[]{:S(2)}) collective-permute-start(bf16[128,512]{1,0:T(8,128)(2,1)S(1)} %copy-done.6), channel_id=1, source_target_pairs={{0,6},{2,4},{4,2},{6,0},{8,14},{10,12},{12,10},{14,8},{16,22},{18,... | collective-permute-start | bytes 393224 | tf_op jit(solution)/shard_map/ppermute | solution.py:364
  61.4 11.4 %collective-permute-start.19 = (bf16[512,256]{1,0:T(8,128)(2,1)S(1)}, bf16[512,256]{1,0:T(8,128)(2,1)S(1)}, u32[]{:S(2)}, u32[]{:S(2)}) collective-permute-start(bf16[512,256]{1,0:T(8,128)(2,1)S(1)} %get-tuple-element.171), channel_id=1, source_target_pairs={{0,8},{2,10},{4,12},{6,14},{8,16},{10,18},{12,20},{14,22},{16,24},... | collective-permute-start | bytes 786440 | tf_op jit(solution)/shard_map/ppermute | solution.py:369
  61.4 17.8 %collective-permute-start.28 = (bf16[512,256]{1,0:T(8,128)(2,1)S(1)}, bf16[512,256]{1,0:T(8,128)(2,1)S(1)}, u32[]{:S(2)}, u32[]{:S(2)}) collective-permute-start(bf16[512,256]{1,0:T(8,128)(2,1)S(1)} %get-tuple-element.189), channel_id=1, source_target_pairs={{0,24},{2,26},{4,28},{6,30},{8,0},{10,2},{12,4},{14,6},{16,8},{18,... | collective-permute-start | bytes 786440 | tf_op jit(solution)/shard_map/ppermute | solution.py:369
  72.9 16.4 %collective-permute-start.27 = (bf16[512,256]{1,0:T(8,128)(2,1)S(1)}, bf16[512,256]{1,0:T(8,128)(2,1)S(1)}, u32[]{:S(2)}, u32[]{:S(2)}) collective-permute-start(bf16[512,256]{1,0:T(8,128)(2,1)S(1)} %add_convert_fusion), channel_id=1, source_target_pairs={{0,8},{2,10},{4,12},{6,14},{8,16},{10,18},{12,20},{14,22},{16,24},... | collective-permute-start | bytes 786440 | tf_op jit(solution)/shard_map/ppermute | solution.py:369
  76.1 1.9 %collective-permute-start.24 = (bf16[128,512]{1,0:T(8,128)(2,1)S(1)}, bf16[128,512]{1,0:T(8,128)(2,1)S(1)}, u32[]{:S(2)}, u32[]{:S(2)}) collective-permute-start(bf16[128,512]{1,0:T(8,128)(2,1)S(1)} %get-tuple-element.178), channel_id=1, source_target_pairs={{0,2},{2,0},{4,6},{6,4},{8,10},{10,8},{12,14},{14,12},{16,18},{18,... | collective-permute-start | bytes 393224 | tf_op jit(solution)/shard_map/ppermute | solution.py:364
  76.1 11.9 %collective-permute-start.20 = (bf16[128,512]{1,0:T(8,128)(2,1)S(1)}, bf16[128,512]{1,0:T(8,128)(2,1)S(1)}, u32[]{:S(2)}, u32[]{:S(2)}) collective-permute-start(bf16[128,512]{1,0:T(8,128)(2,1)S(1)} %get-tuple-element.172), channel_id=1, source_target_pairs={{0,1},{1,0},{2,3},{3,2},{4,5},{5,4},{6,7},{7,6},{8,9},{9,8},{10,11... | collective-permute-start | bytes 393224 | tf_op jit(solution)/shard_map/ppermute | solution.py:380
  76.6 13.4 %collective-permute-start.21 = (bf16[128,512]{1,0:T(8,128)(2,1)S(1)}, bf16[128,512]{1,0:T(8,128)(2,1)S(1)}, u32[]{:S(2)}, u32[]{:S(2)}) collective-permute-start(bf16[128,512]{1,0:T(8,128)(2,1)S(1)} %get-tuple-element.173), channel_id=1, source_target_pairs={{0,3},{1,2},{2,1},{3,0},{4,7},{5,6},{6,5},{7,4},{8,11},{9,10},{10,... | collective-permute-start | bytes 393224 | tf_op jit(solution)/shard_map/ppermute | solution.py:380
  78.0 12.3 %collective-permute-start.22 = (bf16[128,512]{1,0:T(8,128)(2,1)S(1)}, bf16[128,512]{1,0:T(8,128)(2,1)S(1)}, u32[]{:S(2)}, u32[]{:S(2)}) collective-permute-start(bf16[128,512]{1,0:T(8,128)(2,1)S(1)} %get-tuple-element.174), channel_id=1, source_target_pairs={{0,5},{1,4},{2,7},{3,6},{4,1},{5,0},{6,3},{7,2},{8,13},{9,12},{10,... | collective-permute-start | bytes 393224 | tf_op jit(solution)/shard_map/ppermute | solution.py:380
  79.2 12.4 %collective-permute-start.23 = (bf16[128,512]{1,0:T(8,128)(2,1)S(1)}, bf16[128,512]{1,0:T(8,128)(2,1)S(1)}, u32[]{:S(2)}, u32[]{:S(2)}) collective-permute-start(bf16[128,512]{1,0:T(8,128)(2,1)S(1)} %get-tuple-element.175), channel_id=1, source_target_pairs={{0,7},{1,6},{2,5},{3,4},{4,3},{5,2},{6,1},{7,0},{8,15},{9,14},{10,... | collective-permute-start | bytes 393224 | tf_op jit(solution)/shard_map/ppermute | solution.py:380
  88.0 5.7 %collective-permute-start.25 = (bf16[128,512]{1,0:T(8,128)(2,1)S(1)}, bf16[128,512]{1,0:T(8,128)(2,1)S(1)}, u32[]{:S(2)}, u32[]{:S(2)}) collective-permute-start(bf16[128,512]{1,0:T(8,128)(2,1)S(1)} %get-tuple-element.179), channel_id=1, source_target_pairs={{0,4},{2,6},{4,0},{6,2},{8,12},{10,14},{12,8},{14,10},{16,20},{18,... | collective-permute-start | bytes 393224 | tf_op jit(solution)/shard_map/ppermute | solution.py:364
  89.2 6.5 %collective-permute-start.26 = (bf16[128,512]{1,0:T(8,128)(2,1)S(1)}, bf16[128,512]{1,0:T(8,128)(2,1)S(1)}, u32[]{:S(2)}, u32[]{:S(2)}) collective-permute-start(bf16[128,512]{1,0:T(8,128)(2,1)S(1)} %get-tuple-element.180), channel_id=1, source_target_pairs={{0,6},{2,4},{4,2},{6,0},{8,14},{10,12},{12,10},{14,8},{16,22},{18,... | collective-permute-start | bytes 393224 | tf_op jit(solution)/shard_map/ppermute | solution.py:364
  90.1 6.5 %collective-permute-start.29 = (bf16[128,256]{1,0:T(8,128)(2,1)S(1)}, bf16[128,256]{1,0:T(8,128)(2,1)S(1)}, u32[]{:S(2)}, u32[]{:S(2)}) collective-permute-start(bf16[128,256]{1,0:T(8,128)(2,1)S(1)} %get-tuple-element.191), channel_id=1, source_target_pairs={{0,2},{2,0},{4,6},{6,4},{8,10},{10,8},{12,14},{14,12},{16,18},{18,... | collective-permute-start | bytes 196616 | tf_op jit(solution)/shard_map/ppermute | solution.py:364
  90.3 7.6 %collective-permute-start.30 = (bf16[128,256]{1,0:T(8,128)(2,1)S(1)}, bf16[128,256]{1,0:T(8,128)(2,1)S(1)}, u32[]{:S(2)}, u32[]{:S(2)}) collective-permute-start(bf16[128,256]{1,0:T(8,128)(2,1)S(1)} %get-tuple-element.192), channel_id=1, source_target_pairs={{0,4},{2,6},{4,0},{6,2},{8,12},{10,14},{12,8},{14,10},{16,20},{18,... | collective-permute-start | bytes 196616 | tf_op jit(solution)/shard_map/ppermute | solution.py:364
  91.6 6.3 %collective-permute-start.31 = (bf16[128,256]{1,0:T(8,128)(2,1)S(1)}, bf16[128,256]{1,0:T(8,128)(2,1)S(1)}, u32[]{:S(2)}, u32[]{:S(2)}) collective-permute-start(bf16[128,256]{1,0:T(8,128)(2,1)S(1)} %get-tuple-element.193), channel_id=1, source_target_pairs={{0,6},{2,4},{4,2},{6,0},{8,14},{10,12},{12,10},{14,8},{16,22},{18,... | collective-permute-start | bytes 196616 | tf_op jit(solution)/shard_map/ppermute | solution.py:364
where the time goes:
time: 99 us; the launch traced here: 98.6 us
  starting transfers between devices  33.8 us (34%)
  Pallas kernels  32.2 us (33%)
  waiting for transfers between devices  30.7 us (31%)
    pallas_call x9, Pallas kernels, call(): pl.pallas_call(kernel, name=name, out_shape=out_shape, in_specs=specs, ou...  32.2 us
    ppermute x9, starting transfers between devices, turn(): lax.ppermute(block, 'ctx', [(i, (i + s * QUAD) % devices) for i in range(...  15.1 us
    ppermute x9, waiting for transfers between devices, turn(): lax.ppermute(block, 'ctx', [(i, (i + s * QUAD) % devices) for i in range(...  13.4 us
    ppermute x18, starting transfers between devices, swap(): lax.ppermute(pieces[d], 'ctx', [(i, i ^ d) for i in range(devices)])  12.8 us
    ppermute x18, waiting for transfers between devices, swap(): lax.ppermute(pieces[d], 'ctx', [(i, i ^ d) for i in range(devices)])  9.18 us
    ppermute x5, waiting for transfers between devices, hand(): return lax.ppermute(block, ('ctx', 'pipe'), route)  8.19 us
    ppermute x5, starting transfers between devices, hand(): return lax.ppermute(block, ('ctx', 'pipe'), route)  5.98 us
  transfers between devices with their start and end apart: 32, of which 12 were waited for; matrix products, arithmetic and copies ran while one was open for 1% of the time, Pallas kernels for 30%

commit v1 on v0

--- a/solution.py
+++ b/solution.py
@@ -42,9 +42,9 @@
     return pl.ds(pl.multiple_of(index * width, width), width)
 
 
-def pack_keys(key_ref, value_ref, types_ref, table_ref, *refs):
-    pieces, (keys, types, table, typed, arrived, placed) = refs[:QUAD], refs[QUAD:]
-    _, member = place()
+def pack_keys(
+    key_ref, value_ref, types_ref, table_ref, pieces, keys, types, table, typed, arrived, placed
+):
     copies = [
         pltpu.make_async_copy(source, target, arrived.at[i])
         for i, (source, target) in enumerate(
@@ -53,7 +53,9 @@
     ]
     copies += [
         pltpu.make_async_copy(
-            value_ref.at[0, :, columns(member ^ d, HEAD)], pieces[d].at[:, HEAD:], placed.at[d]
+            value_ref.at[0, :, d * HEAD : (d + 1) * HEAD],
+            pieces.at[d, :, HEAD:],
+            placed.at[d],
         )
         for d in range(QUAD)
     ]
@@ -67,26 +69,26 @@
     type_rows = dot(onehot, table[...], TN)
     typed[...] = (keys[...].astype(jnp.float32) + type_rows).astype(jnp.bfloat16)
     for d in range(QUAD):
-        pieces[d][:, :HEAD] = typed[:, columns(member ^ d, HEAD)]
+        pieces[d, :, :HEAD] = typed[:, d * HEAD : (d + 1) * HEAD]
     for copy in copies[3:]:
         copy.wait()
 
 
-def pack_queries(query_ref, grad_ref, forward_ref, gate_ref, gain_ref, *refs):
-    pieces, forward_pieces, (gate_out, placed) = refs[:QUAD], refs[QUAD : 2 * QUAD], refs[2 * QUAD :]
-    _, member = place()
+def pack_queries(
+    query_ref, grad_ref, forward_ref, gate_ref, gain_ref, pieces, forward_pieces, gate_out, placed
+):
     width = query_ref.shape[2] // QUAD
     rows = gate_ref.shape[1]
     copies = []
-    for d in reversed(range(QUAD)):
+    for d in range(QUAD):
         for i, (source, target) in enumerate(
             [
-                (query_ref, pieces[d].at[:, :width]),
-                (grad_ref, pieces[d].at[:, width:]),
-                (forward_ref, forward_pieces[d]),
+                (query_ref, pieces.at[d, :, :width]),
+                (grad_ref, pieces.at[d, :, width:]),
+                (forward_ref, forward_pieces.at[d]),
             ]
         ):
-            source = source.at[0, :, columns(member ^ d, width)]
+            source = source.at[0, :, d * width : (d + 1) * width]
             copies.append(pltpu.make_async_copy(source, target, placed.at[3 * d + i]))
     copies.append(
         pltpu.make_async_copy(gate_ref.at[0], gate_out.at[:rows, :], placed.at[3 * QUAD])
@@ -105,8 +107,8 @@
         copy.wait()
 
 
-def stretch_of(order_ref, quad_index, member, d, e):
-    return order_ref[0, 2 * (quad_index * QUAD + (member ^ d)) + e]
+def stretch_of(order_ref, quad_index, d, e):
+    return order_ref[0, 2 * (quad_index * QUAD + d) + e]
 
 
 def rows_at(index, count):
@@ -114,16 +116,15 @@
 
 
 def in_sequence(order_ref, stacks, stretch_rows, keys, values):
-    z, member = place()
+    z, _ = place()
     nz = len(stacks)
     for s, stack in enumerate(stacks):
         source = lax.rem(z - s + nz, nz)
         for d in range(QUAD):
             for e in range(2):
-                rows = rows_at(stretch_of(order_ref, source, member, d, e), stretch_rows)
-                lower = (2 * d + e) * stretch_rows
-                keys[rows, :] = stack[lower : lower + stretch_rows, :HEAD]
-                values[rows, :] = stack[lower : lower + stretch_rows, HEAD:]
+                rows = rows_at(stretch_of(order_ref, source, d, e), stretch_rows)
+                keys[rows, :] = stack[d, e * stretch_rows : (e + 1) * stretch_rows, :HEAD]
+                values[rows, :] = stack[d, e * stretch_rows : (e + 1) * stretch_rows, HEAD:]
 
 
 def shrink_of(stretch, stretch_rows):
@@ -146,12 +147,12 @@
 
 
 def forward_kernel(nz, order_ref, *refs):
-    queries, refs = refs[:QUAD], refs[QUAD:]
+    queries, refs = refs[0], refs[1:]
     stacks, refs = refs[:nz], refs[nz:]
     outs, refs = refs[:QUAD], refs[QUAD:]
     keys, values, stacked, total, gap = refs
     z, member = place()
-    stretch_rows = queries[0].shape[0] // 2
+    stretch_rows = queries.shape[1] // 2
     groups = outs[0].shape[1] // HEAD
     block_rows = groups * stretch_rows
     steps = keys.shape[0] // block_rows + 1
@@ -159,7 +160,8 @@
     for d in range(QUAD):
         for e in range(2):
             for g in range(groups):
-                stacked[2 * d + e, g * stretch_rows : (g + 1) * stretch_rows, :] = queries[d][
+                stacked[2 * d + e, g * stretch_rows : (g + 1) * stretch_rows, :] = queries[
+                    member ^ d,
                     e * stretch_rows : (e + 1) * stretch_rows,
                     g * HEAD : (g + 1) * HEAD,
                 ]
@@ -171,8 +173,8 @@
     def advance(step, _):
         for d in range(QUAD):
             row, stretch, block = step_place(
-                stretch_of(order_ref, z, member, d, 0),
-                stretch_of(order_ref, z, member, d, 1),
+                stretch_of(order_ref, z, member ^ d, 0),
+                stretch_of(order_ref, z, member ^ d, 1),
                 step,
                 d,
                 groups,
@@ -187,7 +189,7 @@
     lax.fori_loop(0, steps, advance, 0)
     for d in range(QUAD):
         for e in range(2):
-            shrink = shrink_of(stretch_of(order_ref, z, member, d, e), stretch_rows)
+            shrink = shrink_of(stretch_of(order_ref, z, member ^ d, e), stretch_rows)
             for g in range(groups):
                 outs[d][e * stretch_rows : (e + 1) * stretch_rows, g * HEAD : (g + 1) * HEAD] = (
                     total[2 * d + e, g * stretch_rows : (g + 1) * stretch_rows, :] * shrink
@@ -195,14 +197,14 @@
 
 
 def backward_kernel(nz, order_ref, *refs):
-    queries, refs = refs[:QUAD], refs[QUAD:]
+    queries, refs = refs[0], refs[1:]
     stacks, refs = refs[:nz], refs[nz:]
-    query_outs, refs = refs[:QUAD], refs[QUAD:]
+    query_out, refs = refs[0], refs[1:]
     key_outs, refs = refs[:nz], refs[nz:]
     keys, values, keys_t, stacked, grads, total_t, key_total, value_total, gap = refs
-    z, member = place()
-    stretch_rows = queries[0].shape[0] // 2
-    groups = queries[0].shape[1] // (2 * HEAD)
+    z, _ = place()
+    stretch_rows = queries.shape[1] // 2
+    groups = queries.shape[2] // (2 * HEAD)
     block_rows = groups * stretch_rows
     blocks = keys.shape[0] // block_rows
     steps = blocks + 1
@@ -213,13 +215,13 @@
     offset = groups * HEAD
     for d in range(QUAD):
         for e in range(2):
-            shrink = shrink_of(stretch_of(order_ref, z, member, d, e), stretch_rows)
+            shrink = shrink_of(stretch_of(order_ref, z, d, e), stretch_rows)
             rows = slice(e * stretch_rows, (e + 1) * stretch_rows)
             for g in range(groups):
                 into = slice(g * stretch_rows, (g + 1) * stretch_rows)
-                stacked[2 * d + e, into, :] = queries[d][rows, g * HEAD : (g + 1) * HEAD]
+                stacked[2 * d + e, into, :] = queries[d, rows, g * HEAD : (g + 1) * HEAD]
                 grads[2 * d + e, into, :] = (
-                    queries[d][rows, offset + g * HEAD : offset + (g + 1) * HEAD].astype(
+                    queries[d, rows, offset + g * HEAD : offset + (g + 1) * HEAD].astype(
                         jnp.float32
                     )
                     * shrink
@@ -234,8 +236,8 @@
     def advance(step, _):
         for d in range(QUAD):
             row, stretch, block = step_place(
-                stretch_of(order_ref, z, member, d, 0),
-                stretch_of(order_ref, z, member, d, 1),
+                stretch_of(order_ref, z, d, 0),
+                stretch_of(order_ref, z, d, 1),
                 step,
                 d,
                 groups,
@@ -258,47 +260,39 @@
         for e in range(2):
             query_grad = (total_t[2 * d + e].T * SCALE).astype(jnp.bfloat16)
             for g in range(groups):
-                query_outs[d][
-                    e * stretch_rows : (e + 1) * stretch_rows, g * HEAD : (g + 1) * HEAD
+                query_out[
+                    d, e * stretch_rows : (e + 1) * stretch_rows, g * HEAD : (g + 1) * HEAD
                 ] = query_grad[g * stretch_rows : (g + 1) * stretch_rows, :]
     for s in range(nz):
         target = lax.rem(z + s, nz)
         for d in range(QUAD):
             for e in range(2):
-                rows = rows_at(stretch_of(order_ref, target, member, d, e), stretch_rows)
-                lower = (2 * d + e) * stretch_rows
-                key_outs[s][lower : lower + stretch_rows, :HEAD] = (
+                rows = rows_at(stretch_of(order_ref, target, d, e), stretch_rows)
+                into = slice(e * stretch_rows, (e + 1) * stretch_rows)
+                key_outs[s][d, into, :HEAD] = (
                     key_total[rows, :] * SCALE
                 ).astype(jnp.bfloat16)
-                key_outs[s][lower : lower + stretch_rows, HEAD:] = value_total[rows, :].astype(
+                key_outs[s][d, into, HEAD:] = value_total[rows, :].astype(
                     jnp.bfloat16
                 )
 
 
-def sum_kernel(*refs):
-    parts, pieces = refs[:3], refs[3:]
-    rows = pieces[0].shape[0]
-    for d in range(QUAD):
-        lower = d * rows
-        pieces[d][...] = sum(
-            part[lower : lower + rows, :].astype(jnp.float32) for part in parts
-        ).astype(jnp.bfloat16)
-
-
-def key_grad_kernel(*refs):
-    pieces, (key_out, value_out) = refs[:QUAD], refs[QUAD:]
-    _, member = place()
-    for d in range(QUAD):
-        head = columns(member ^ d, HEAD)
-        key_out[0, :, head] = pieces[d][:, :HEAD]
-        value_out[0, :, head] = pieces[d][:, HEAD:]
-
-
-def query_grad_kernel(*refs):
-    pieces, out = refs[:QUAD], refs[QUAD]
-    _, member = place()
-    for d in range(QUAD):
-        out[0, :, columns(member ^ d, pieces[d].shape[1])] = pieces[d][...]
+def sum_kernel(a, b, c, out):
+    out[...] = (
+        a[...].astype(jnp.float32) + b[...].astype(jnp.float32) + c[...].astype(jnp.float32)
+    ).astype(jnp.bfloat16)
+
+
+def key_grad_kernel(pieces, key_out, value_out):
+    for d in range(QUAD):
+        key_out[0, :, d * HEAD : (d + 1) * HEAD] = pieces[d, :, :HEAD]
+        value_out[0, :, d * HEAD : (d + 1) * HEAD] = pieces[d, :, HEAD:]
+
+
+def query_grad_kernel(pieces, out):
+    width = pieces.shape[2]
+    for d in range(QUAD):
+        out[0, :, d * width : (d + 1) * width] = pieces[d]
 
 
 def gate_kernel(*refs):
@@ -359,11 +353,10 @@
     steps = total_rows // block_rows + 1
     pairs = steps * QUAD * block_rows * block_rows
 
+    quads = [[z * QUAD + d for d in range(QUAD)] for z in range(nz)]
+
     def swap(pieces):
-        return [pieces[0]] + [
-            lax.ppermute(pieces[d], "ctx", [(i, i ^ d) for i in range(devices)])
-            for d in range(1, QUAD)
-        ]
+        return lax.all_to_all(pieces, "ctx", 0, 0, axis_index_groups=quads)
 
     def turn(block, s):
         return lax.ppermute(
@@ -383,7 +376,7 @@
         return call(
             pack_keys,
             name,
-            [bf16(rows, 2 * HEAD)] * QUAD,
+            [bf16(QUAD, rows, 2 * HEAD)],
             [HBM] * 4,
             key,
             value,
@@ -398,7 +391,7 @@
                 pltpu.SemaphoreType.DMA((QUAD,)),
             ],
             vmem=60,
-        )
+        )[0]
 
     ahead = nz // 2
 
@@ -412,6 +405,7 @@
         return [stack, ring_up(stack)], [ring_down(stack)]
 
     def gather_rest(up, down):
+        up, down = lax.optimization_barrier((up, down))
         while len(up) <= ahead:
             up = up + [ring_up(up[-1])]
         while len(up) + len(down) < nz:
@@ -435,8 +429,7 @@
     packed = call(
         pack_queries,
         "pack_queries",
-        [bf16(rows, 2 * width)] * QUAD
-        + [bf16(rows, width)] * QUAD
+        [bf16(QUAD, rows, 2 * width), bf16(QUAD, rows, width)]
         + [bf16(rows + GAIN_ROWS, QUAD * width)],
         [HBM] * 4 + [VMEM],
         query_bwd,
@@ -448,17 +441,19 @@
         vmem=60,
     )
     back_pieces, packed = lax.optimization_barrier((back_pieces, packed))
-    back_queries, queries, gate_before = swap(packed[:QUAD]), packed[QUAD:-1], packed[-1]
-    back_stacks = gather_rest(*gather_first(jnp.concatenate(back_pieces, axis=0)))
+    back_queries, queries, gate_before = swap(packed[0]), packed[1], packed[2]
+    back_stacks = gather_first(back_pieces)
     pieces = pack(key_fwd, value_fwd, types_fwd, "pack_keys_fwd")
     gate_before = hand(gate_before, 0)
-    back_queries, pieces, queries = lax.optimization_barrier((back_queries, pieces, queries))
-    stack = jnp.concatenate(swap(pieces), axis=0)
+    back_stacks, back_queries, pieces, queries = lax.optimization_barrier(
+        (back_stacks, back_queries, pieces, queries)
+    )
+    back_stacks = gather_rest(*back_stacks)
+    stack, queries = swap(pieces), swap(queries)
     stack, queries, back_stacks, gate_before = lax.optimization_barrier(
         (stack, queries, back_stacks, gate_before)
     )
     stacks = [stack] + [turn(stack, s) for s in range(1, nz)]
-    queries = swap(queries)
 
     sequence = [pltpu.VMEM((total_rows, HEAD), jnp.bfloat16)] * 2
     stacked = pltpu.VMEM((2 * QUAD, block_rows, HEAD), jnp.bfloat16)
@@ -466,10 +461,10 @@
     outs = call(
         functools.partial(backward_kernel, nz),
         "backward",
-        [bf16(rows, width)] * QUAD + [bf16(QUAD * rows, 2 * HEAD)] * nz,
-        [SMEM] + [VMEM] * (QUAD + nz),
+        [bf16(QUAD, rows, width)] + [bf16(QUAD, rows, 2 * HEAD)] * nz,
+        [SMEM] + [VMEM] * (1 + nz),
         stretch_order,
-        *back_queries,
+        back_queries,
         *back_stacks,
         scratch=sequence
         + [
@@ -484,19 +479,17 @@
         flops=10 * pairs * HEAD,
         transcendentals=2 * pairs,
     )
-    query_pieces, key_parts = outs[:QUAD], outs[QUAD:]
-    query_pieces, key_parts, stacks, queries = lax.optimization_barrier(
-        (query_pieces, key_parts, stacks, queries)
-    )
+    query_pieces, key_parts = outs[0], outs[1:]
+    key_parts, stacks = lax.optimization_barrier((key_parts, stacks))
     key_sums = reduce_first(key_parts)
     query_pieces = swap(query_pieces)
     attended = call(
         functools.partial(forward_kernel, nz),
         "forward",
         [bf16(rows, width)] * QUAD,
-        [SMEM] + [VMEM] * (QUAD + nz),
+        [SMEM] + [VMEM] * (1 + nz),
         stretch_order,
-        *queries,
+        queries,
         *stacks,
         scratch=sequence
         + [stacked, pltpu.VMEM((2 * QUAD, block_rows, HEAD), jnp.float32), gap],
@@ -515,25 +508,25 @@
         call(
             sum_kernel,
             "sum_key_parts",
-            [bf16(rows, 2 * HEAD)] * QUAD,
+            [bf16(QUAD, rows, 2 * HEAD)],
             [VMEM] * 3,
             *key_sums,
-        )
+        )[0]
     )
     handed, query_pieces = lax.optimization_barrier((handed, query_pieces))
     (query_grad,) = call(
         query_grad_kernel,
         "query_grad",
         [bf16(*query_bwd.shape)],
-        [VMEM] * QUAD,
-        *query_pieces,
+        [VMEM],
+        query_pieces,
     )
     key_grad, value_grad = call(
         key_grad_kernel,
         "key_grad",
         [bf16(*key_bwd.shape), bf16(*value_bwd.shape)],
-        [VMEM] * QUAD,
-        *key_pieces,
+        [VMEM],
+        key_pieces,
     )
     return handed, query_grad, key_grad, value_grad
 

time: 99 us -> 133 us (1.34)
  waiting for transfers between devices: 30.7 us -> 40.9 us
  blocking collectives: 0 us -> 9.41 us
  local copies, waits for them, and re-layouts: 0.06 us -> 7.11 us
  starting transfers between devices: 33.8 us -> 38.7 us
  Pallas kernels: 32.2 us -> 33.9 us
    all_to_all x0 -> x5, starting transfers between devices: none -> 18.5 us  [swap(): return lax.all_to_all(pieces, 'ctx', 0, 0, axis_index_groups=quads)]
    ppermute x9, waiting for transfers between devices: 13.4 us -> 26.9 us  [turn(): lax.ppermute(block, 'ctx', [(i, (i + s * QUAD) % devices) for i in range(...]
    ppermute x18 -> x0, starting transfers between devices: 12.8 us -> none  [swap(): lax.ppermute(pieces[d], 'ctx', [(i, i ^ d) for i in range(devices)])]
    all_to_all x0 -> x1, blocking collectives: none -> 9.41 us  [swap(): return lax.all_to_all(pieces, 'ctx', 0, 0, axis_index_groups=quads)]
    ppermute x18 -> x0, waiting for transfers between devices: 9.18 us -> none  [swap(): lax.ppermute(pieces[d], 'ctx', [(i, i ^ d) for i in range(devices)])]
    unnamed x21 -> x46, local copies, waits for them, and re-layouts: 0.05 us -> 7.11 us
    ppermute x5, waiting for transfers between devices: 8.19 us -> 11.7 us  [hand(): return lax.ppermute(block, ('ctx', 'pipe'), route)]
    all_to_all x0 -> x5, waiting for transfers between devices: none -> 2.25 us  [swap(): return lax.all_to_all(pieces, 'ctx', 0, 0, axis_index_groups=quads)]
  transfers between devices with their start and end apart: 32 -> 19, of which waited for: 12 -> 9; matrix products, arithmetic and copies ran while one was open for 1% -> 1% of each run, Pallas kernels for 30% -> 24%
where the time goes in v1:
time: 133 us; the launch traced here: 132 us
  waiting for transfers between devices  40.9 us (31%)
  starting transfers between devices  38.7 us (29%)
  Pallas kernels  33.9 us (25%)
  blocking collectives  9.41 us (7%)
  local copies, waits for them, and re-layouts  7.11 us (5%)
    pallas_call x9, Pallas kernels, call(): pl.pallas_call(kernel, name=name, out_shape=out_shape, in_specs=specs, ou...  33.9 us
    ppermute x9, waiting for transfers between devices, turn(): lax.ppermute(block, 'ctx', [(i, (i + s * QUAD) % devices) for i in range(...  26.9 us
    all_to_all x5, starting transfers between devices, swap(): return lax.all_to_all(pieces, 'ctx', 0, 0, axis_index_groups=quads)  18.5 us
    ppermute x9, starting transfers between devices, turn(): lax.ppermute(block, 'ctx', [(i, (i + s * QUAD) % devices) for i in range(...  13.9 us
    ppermute x5, waiting for transfers between devices, hand(): return lax.ppermute(block, ('ctx', 'pipe'), route)  11.7 us
    all_to_all x1, blocking collectives, swap(): return lax.all_to_all(pieces, 'ctx', 0, 0, axis_index_groups=quads)  9.41 us
    unnamed x46, local copies, waits for them, and re-layouts  7.11 us
    ppermute x5, starting transfers between devices, hand(): return lax.ppermute(block, ('ctx', 'pipe'), route)  6.22 us
  transfers between devices with their start and end apart: 19, of which 9 were waited for; matrix products, arithmetic and copies ran while one was open for 1% of the time, Pallas kernels for 24%

profile of v1, /device:TPU:0, one launch (start us, length us, event | category | flops | bytes accessed | tf_op | source)
XLA Modules:
  0.0 131.9 jit_solution(3175652672069985640)
XLA Ops:
  0.6 2.0 %pack_keys_bwd.1 = bf16[4,128,256]{2,1,0:T(8,128)(2,1)} custom-call(bf16[1,128,512]{2,1,0:T(8,128)(2,1)} %key_ref.2, bf16[1,128,512]{2,1,0:T(8,128)(2,1)} %value_ref.2, s32[1,128]{1,0:T(1,128)} %types_ref.2, bf16[1,64,512]{2,1,0:T(8,128)(2,1)} %table_ref.3), custom_call_target="tpu_custom_call" | custom-call | bytes 590336 | tf_op jit(solution)/shard_map/pack_keys_bwd/pallas_call | solution.py:316
  2.7 4.2 %all-to-all-start = ((bf16[4,128,256]{2,1,0:T(8,128)(2,1)}), bf16[4,128,256]{2,1,0:T(8,128)(2,1)S(1)}, u32[]{:S(2)}, u32[]{:S(2)}) async-start(bf16[4,128,256]{2,1,0:T(8,128)(2,1)} %pack_keys_bwd.1), calls=%async_computation | async-start | bytes 524288 | tf_op jit(solution)/shard_map/all_to_all | solution.py:359
  6.9 3.8 %pack_queries.1 = (bf16[4,128,1024]{2,1,0:T(8,128)(2,1)}, bf16[4,128,512]{2,1,0:T(8,128)(2,1)}, bf16[144,2048]{1,0:T(8,128)(2,1)}) custom-call(bf16[1,128,2048]{2,1,0:T(8,128)(2,1)} %query_ref.1, bf16[1,128,2048]{2,1,0:T(8,128)(2,1)} %grad_ref.1, bf16[1,128,2048]{2,1,0:T(8,128)(2,1)} %forward_ref.1, bf16[1,128,2048]{2,1,0:T(8,128)(2,1)} %gate_ref.1, ...), custom_call_target="tpu_custom_call" | custom-call | bytes 4268032 | tf_op jit(solution)/shard_map/pack_queries/pallas_call | solution.py:316
  10.7 2.2 %all-to-all-done.refs_1_ = bf16[4,128,256]{2,1,0:T(8,128)(2,1)S(1)} async-done(((bf16[4,128,256]{2,1,0:T(8,128)(2,1)}), bf16[4,128,256]{2,1,0:T(8,128)(2,1)S(1)}, u32[]{:S(2)}, u32[]{:S(2)}) %all-to-all-start) | async-done | bytes 262176 | tf_op jit(solution)/shard_map/all_to_all | solution.py:359
  12.9 3.5 %all-to-all-start.1 = ((bf16[4,128,1024]{2,1,0:T(8,128)(2,1)}), bf16[4,128,1024]{2,1,0:T(8,128)(2,1)S(1)}, u32[]{:S(2)}, u32[]{:S(2)}) async-start(bf16[4,128,1024]{2,1,0:T(8,128)(2,1)} %get-tuple-element.57), calls=%async_computation.1 | async-start | bytes 2097152 | tf_op jit(solution)/shard_map/all_to_all | solution.py:359
  16.4 2.2 %collective-permute-start = (bf16[4,128,256]{2,1,0:T(8,128)(2,1)S(1)}, bf16[4,128,256]{2,1,0:T(8,128)(2,1)S(1)}, u32[]{:S(2)}, u32[]{:S(2)}) collective-permute-start(bf16[4,128,256]{2,1,0:T(8,128)(2,1)S(1)} %all-to-all-done.refs_1_), channel_id=1, source_target_pairs={{0,8},{2,10},{4,12},{6,14},{8,16},{10,18},{12,20},{14,22},{16,24},... | collective-permute-start | bytes 786440 | tf_op jit(solution)/shard_map/ppermute | solution.py:362
  18.7 2.1 %collective-permute-start.1 = (bf16[4,128,256]{2,1,0:T(8,128)(2,1)S(1)}, bf16[4,128,256]{2,1,0:T(8,128)(2,1)S(1)}, u32[]{:S(2)}, u32[]{:S(2)}) collective-permute-start(bf16[4,128,256]{2,1,0:T(8,128)(2,1)S(1)} %all-to-all-done.refs_1_), channel_id=1, source_target_pairs={{0,24},{2,26},{4,28},{6,30},{8,0},{10,2},{12,4},{14,6},{16,8},{18,... | collective-permute-start | bytes 786440 | tf_op jit(solution)/shard_map/ppermute | solution.py:362
  20.8 2.0 %pack_keys_fwd.1 = bf16[4,128,256]{2,1,0:T(8,128)(2,1)} custom-call(bf16[1,128,512]{2,1,0:T(8,128)(2,1)} %key_ref.3, bf16[1,128,512]{2,1,0:T(8,128)(2,1)} %value_ref.3, s32[1,128]{1,0:T(1,128)} %types_ref.3, bf16[1,64,512]{2,1,0:T(8,128)(2,1)} %table_ref.3), custom_call_target="tpu_custom_call" | custom-call | bytes 590336 | tf_op jit(solution)/shard_map/pack_keys_fwd/pallas_call | solution.py:316
  22.8 1.7 %collective-permute-start.3 = (bf16[144,2048]{1,0:T(8,128)(2,1)}, bf16[144,2048]{1,0:T(8,128)(2,1)S(1)}, u32[]{:S(2)}, u32[]{:S(2)}) collective-permute-start(bf16[144,2048]{1,0:T(8,128)(2,1)} %get-tuple-element.67), channel_id=1, source_target_pairs={{0,1},{1,0},{2,3},{3,2},{4,5},{5,4},{6,7},{7,6},{8,9},{9,8},{10,11... | collective-permute-start | bytes 1769480 | tf_op jit(solution)/shard_map/ppermute | solution.py:373
  24.5 3.4 %collective-permute-done.refs_2_ = bf16[4,128,256]{2,1,0:T(8,128)(2,1)S(1)} collective-permute-done((bf16[4,128,256]{2,1,0:T(8,128)(2,1)S(1)}, bf16[4,128,256]{2,1,0:T(8,128)(2,1)S(1)}, u32[]{:S(2)}, u32[]{:S(2)}) %collective-permute-start) | collective-permute-done | bytes 262176 | tf_op jit(solution)/shard_map/ppermute | solution.py:362
  27.9 4.7 %collective-permute-done.1.refs_4_ = bf16[4,128,256]{2,1,0:T(8,128)(2,1)S(1)} collective-permute-done((bf16[4,128,256]{2,1,0:T(8,128)(2,1)S(1)}, bf16[4,128,256]{2,1,0:T(8,128)(2,1)S(1)}, u32[]{:S(2)}, u32[]{:S(2)}) %collective-permute-start.1) | collective-permute-done | bytes 262176 | tf_op jit(solution)/shard_map/ppermute | solution.py:362
  32.7 0.7 copy-done.9
  33.4 0.0 all-to-all-done.1.refs_0_
  33.4 9.4 %all_to_all.30.refs_1_ = bf16[4,128,256]{2,1,0:T(8,128)(2,1)S(1)} all-to-all(bf16[4,128,256]{2,1,0:T(8,128)(2,1)} %pack_keys_fwd.1), channel_id=1, replica_groups={{0,2,4,6},{8,10,12,14},{16,18,20,22},{24,26,28,30},{1,3,5,7},{9,11,13,1..., dimensions={0} | all-to-all | bytes 524288 | tf_op jit(solution)/shard_map/all_to_all | solution.py:359
  42.8 3.6 %all-to-all-start.3 = ((bf16[4,128,512]{2,1,0:T(8,128)(2,1)}), bf16[4,128,512]{2,1,0:T(8,128)(2,1)S(1)}, u32[]{:S(2)}, u32[]{:S(2)}) async-start(bf16[4,128,512]{2,1,0:T(8,128)(2,1)} %get-tuple-element.60), calls=%async_computation.3 | async-start | bytes 1048576 | tf_op jit(solution)/shard_map/all_to_all | solution.py:359
  46.4 1.2 collective-permute-start.2
  47.6 0.0 collective-permute-done.3.refs_4_
  47.6 9.3 %collective-permute-done.2.refs_3_ = bf16[4,128,256]{2,1,0:T(8,128)(2,1)S(1)} collective-permute-done((bf16[4,128,256]{2,1,0:T(8,128)(2,1)S(1)}, bf16[4,128,256]{2,1,0:T(8,128)(2,1)S(1)}, u32[]{:S(2)}, u32[]{:S(2)}) %collective-permute-start.2) | collective-permute-done | bytes 262176 | tf_op jit(solution)/shard_map/ppermute | solution.py:362
  56.9 0.7 copy-done.13
  57.6 0.0 all-to-all-done.3.refs_0_
  57.6 0.0 collective-permute-start.4
  57.6 1.1 collective-permute-start.5
  58.7 2.7 %collective-permute-start.6 = (bf16[4,128,256]{2,1,0:T(8,128)(2,1)S(1)}, bf16[4,128,256]{2,1,0:T(8,128)(2,1)S(1)}, u32[]{:S(2)}, u32[]{:S(2)}) collective-permute-start(bf16[4,128,256]{2,1,0:T(8,128)(2,1)S(1)} %all_to_all.30.refs_1_), channel_id=1, source_target_pairs={{0,24},{2,26},{4,28},{6,30},{8,0},{10,2},{12,4},{14,6},{16,8},{18,... | collective-permute-start | bytes 786440 | tf_op jit(solution)/shard_map/ppermute | solution.py:362
  61.4 0.0 copy-done.6
  61.4 0.9 copy-done.8
  62.4 0.9 copy-done.10
  63.3 0.9 copy-done.14
  64.3 14.9 %backward.1 = (bf16[4,128,512]{2,1,0:T(8,128)(2,1)}, bf16[4,128,256]{2,1,0:T(8,128)(2,1)S(1)}, bf16[4,128,256]{2,1,0:T(8,128)(2,1)S(1)}, bf16[4,128,256]{2,1,0:T(8,128)(2,1)}, bf16[4,128,256]{2,1,0:T(8,128)(2,1)S(1)}) custom-call(s32[1,32]{1,0:T(1,128)S(1)} %copy-done.6, bf16[4,128,1024]{2,1,0:T(8,128)(2,1)S(1)} %all-to-all-done.1.refs_0_, ...), custom_call_target="tpu_custom_call" | custom-call | flops 3019898880 | bytes 3670144 | tf_op jit(solution)/shard_map/backward/pallas_call | solution.py:316
  79.2 0.7 copy-done.11
  79.9 0.0 collective-permute-done.4.refs_2_
  79.9 0.7 copy-done
  80.6 0.0 collective-permute-done.5.refs_3_
  80.6 0.7 copy-done.2
  81.3 0.0 collective-permute-done.6.refs_4_
  81.3 0.7 copy-done.4
  82.0 2.5 %collective-permute-start.7 = (bf16[4,128,256]{2,1,0:T(8,128)(2,1)}, bf16[4,128,256]{2,1,0:T(8,128)(2,1)}, u32[]{:S(2)}, u32[]{:S(2)}) collective-permute-start(bf16[4,128,256]{2,1,0:T(8,128)(2,1)} %get-tuple-element.87), channel_id=1, source_target_pairs={{0,8},{2,10},{4,12},{6,14},{8,16},{10,18},{12,20},{14,22},{16,24},... | collective-permute-start | bytes 786440 | tf_op jit(solution)/shard_map/ppermute | solution.py:362
  84.5 3.6 %all-to-all-start.4 = ((bf16[4,128,512]{2,1,0:T(8,128)(2,1)}), bf16[4,128,512]{2,1,0:T(8,128)(2,1)S(1)}, u32[]{:S(2)}, u32[]{:S(2)}) async-start(bf16[4,128,512]{2,1,0:T(8,128)(2,1)} %get-tuple-element.93), calls=%async_computation.4 | async-start | bytes 1048576 | tf_op jit(solution)/shard_map/all_to_all | solution.py:359
  88.2 1.4 %collective-permute-start.13 = (bf16[4,128,256]{2,1,0:T(8,128)(2,1)S(1)}, bf16[4,128,256]{2,1,0:T(8,128)(2,1)S(1)}, u32[]{:S(2)}, u32[]{:S(2)}) collective-permute-start(bf16[4,128,256]{2,1,0:T(8,128)(2,1)S(1)} %copy-done.12), channel_id=1, source_target_pairs={{0,24},{2,26},{4,28},{6,30},{8,0},{10,2},{12,4},{14,6},{16,8},{18,... | collective-permute-start | bytes 786440 | tf_op jit(solution)/shard_map/ppermute | solution.py:362
  89.5 0.0 copy-done.1
  89.6 7.6 %forward.1 = (bf16[128,512]{1,0:T(8,128)(2,1)S(1)}, bf16[128,512]{1,0:T(8,128)(2,1)S(1)}, bf16[128,512]{1,0:T(8,128)(2,1)S(1)}, bf16[128,512]{1,0:T(8,128)(2,1)S(1)}) custom-call(s32[1,32]{1,0:T(1,128)S(1)} %copy-done.6, bf16[4,128,512]{2,1,0:T(8,128)(2,1)S(1)} %all-to-all-done.3.refs_0_, bf16[4,128,256]{2,1,0:T(8,128)(2,1)S(1)} %all_to_all.30.refs_1_, ...), custom_call_target="tpu_custom_call" | custom-call | bytes 2097280 | tf_op jit(solution)/shard_map/forward/pallas_call | solution.py:316
  97.2 0.0 copy-start.15
  97.2 0.0 copy-start.17
  97.2 0.0 copy-start.21
  97.2 0.0 collective-permute-done.7
  97.2 1.2 add_convert_fusion
  98.4 0.7 collective-permute-start.12
  99.2 0.0 collective-permute-done.13.c
  99.2 9.5 %collective-permute-done.12.b = bf16[4,128,256]{2,1,0:T(8,128)(2,1)S(1)} collective-permute-done((bf16[4,128,256]{2,1,0:T(8,128)(2,1)S(1)}, bf16[4,128,256]{2,1,0:T(8,128)(2,1)S(1)}, u32[]{:S(2)}, u32[]{:S(2)}) %collective-permute-start.12) | collective-permute-done | bytes 262176 | tf_op jit(solution)/shard_map/ppermute | solution.py:362
  108.6 0.8 sum_key_parts.1
  109.4 0.0 all-to-all-done.4.pieces
  109.5 3.5 %all-to-all-start.5 = ((bf16[4,128,256]{2,1,0:T(8,128)(2,1)}), bf16[4,128,256]{2,1,0:T(8,128)(2,1)S(1)}, u32[]{:S(2)}, u32[]{:S(2)}) async-start(bf16[4,128,256]{2,1,0:T(8,128)(2,1)} %sum_key_parts.1), calls=%async_computation.5 | async-start | bytes 524288 | tf_op jit(solution)/shard_map/all_to_all | solution.py:359
  113.0 2.9 %collective-permute-start.10 = (bf16[128,512]{1,0:T(8,128)(2,1)S(1)}, bf16[128,512]{1,0:T(8,128)(2,1)S(1)}, u32[]{:S(2)}, u32[]{:S(2)}) collective-permute-start(bf16[128,512]{1,0:T(8,128)(2,1)S(1)} %copy-done.22), channel_id=1, source_target_pairs={{0,5},{1,4},{2,7},{3,6},{4,1},{5,0},{6,3},{7,2},{8,13},{9,12},{10,... | collective-permute-start | bytes 393224 | tf_op jit(solution)/shard_map/ppermute | solution.py:373
  116.0 0.0 copy-done.20
  116.0 0.0 collective-permute-start.11
  116.0 1.3 %collective-permute-start.8 = (bf16[128,512]{1,0:T(8,128)(2,1)S(1)}, bf16[128,512]{1,0:T(8,128)(2,1)S(1)}, u32[]{:S(2)}, u32[]{:S(2)}) collective-permute-start(bf16[128,512]{1,0:T(8,128)(2,1)S(1)} %copy-done.18), channel_id=1, source_target_pairs={{0,1},{1,0},{2,3},{3,2},{4,5},{5,4},{6,7},{7,6},{8,9},{9,8},{10,11... | collective-permute-start | bytes 393224 | tf_op jit(solution)/shard_map/ppermute | solution.py:373
  117.3 0.2 collective-permute-start.9
  117.5 5.8 %collective-permute-done.10.refs_2_ = bf16[128,512]{1,0:T(8,128)(2,1)S(1)} collective-permute-done((bf16[128,512]{1,0:T(8,128)(2,1)S(1)}, bf16[128,512]{1,0:T(8,128)(2,1)S(1)}, u32[]{:S(2)}, u32[]{:S(2)}) %collective-permute-start.10) | collective-permute-done | bytes 131104 | tf_op jit(solution)/shard_map/ppermute | solution.py:373
  123.4 1.9 %collective-permute-done.11.refs_3_ = bf16[128,512]{1,0:T(8,128)(2,1)S(1)} collective-permute-done((bf16[128,512]{1,0:T(8,128)(2,1)S(1)}, bf16[128,512]{1,0:T(8,128)(2,1)S(1)}, u32[]{:S(2)}, u32[]{:S(2)}) %collective-permute-start.11) | collective-permute-done | bytes 131104 | tf_op jit(solution)/shard_map/ppermute | solution.py:373
  125.2 2.7 %collective-permute-done.8.refs_0_ = bf16[128,512]{1,0:T(8,128)(2,1)S(1)} collective-permute-done((bf16[128,512]{1,0:T(8,128)(2,1)S(1)}, bf16[128,512]{1,0:T(8,128)(2,1)S(1)}, u32[]{:S(2)}, u32[]{:S(2)}) %collective-permute-start.8) | collective-permute-done | bytes 131104 | tf_op jit(solution)/shard_map/ppermute | solution.py:373
  128.0 1.2 collective-permute-done.9.refs_1_
  129.2 1.2 gate.1
  130.4 0.8 query_grad.1
  131.2 0.0 all-to-all-done.5.pieces
  131.2 0.7 key_grad.1
  (31 shorter events, 0.1 us)
Async XLA Ops:
  2.7 10.3 %all-to-all-start = ((bf16[4,128,256]{2,1,0:T(8,128)(2,1)}), bf16[4,128,256]{2,1,0:T(8,128)(2,1)S(1)}, u32[]{:S(2)}, u32[]{:S(2)}) async-start(bf16[4,128,256]{2,1,0:T(8,128)(2,1)} %pack_keys_bwd.1), calls=%async_computation | async-start | bytes 524288 | tf_op jit(solution)/shard_map/all_to_all | solution.py:359
  12.9 20.5 %all-to-all-start.1 = ((bf16[4,128,1024]{2,1,0:T(8,128)(2,1)}), bf16[4,128,1024]{2,1,0:T(8,128)(2,1)S(1)}, u32[]{:S(2)}, u32[]{:S(2)}) async-start(bf16[4,128,1024]{2,1,0:T(8,128)(2,1)} %get-tuple-element.57), calls=%async_computation.1 | async-start | bytes 2097152 | tf_op jit(solution)/shard_map/all_to_all | solution.py:359
  16.4 11.5 %collective-permute-start = (bf16[4,128,256]{2,1,0:T(8,128)(2,1)S(1)}, bf16[4,128,256]{2,1,0:T(8,128)(2,1)S(1)}, u32[]{:S(2)}, u32[]{:S(2)}) collective-permute-start(bf16[4,128,256]{2,1,0:T(8,128)(2,1)S(1)} %all-to-all-done.refs_1_), channel_id=1, source_target_pairs={{0,8},{2,10},{4,12},{6,14},{8,16},{10,18},{12,20},{14,22},{16,24},... | collective-permute-start | bytes 786440 | tf_op jit(solution)/shard_map/ppermute | solution.py:362
  18.7 14.0 %collective-permute-start.1 = (bf16[4,128,256]{2,1,0:T(8,128)(2,1)S(1)}, bf16[4,128,256]{2,1,0:T(8,128)(2,1)S(1)}, u32[]{:S(2)}, u32[]{:S(2)}) collective-permute-start(bf16[4,128,256]{2,1,0:T(8,128)(2,1)S(1)} %all-to-all-done.refs_1_), channel_id=1, source_target_pairs={{0,24},{2,26},{4,28},{6,30},{8,0},{10,2},{12,4},{14,6},{16,8},{18,... | collective-permute-start | bytes 786440 | tf_op jit(solution)/shard_map/ppermute | solution.py:362
  22.8 24.8 %collective-permute-start.3 = (bf16[144,2048]{1,0:T(8,128)(2,1)}, bf16[144,2048]{1,0:T(8,128)(2,1)S(1)}, u32[]{:S(2)}, u32[]{:S(2)}) collective-permute-start(bf16[144,2048]{1,0:T(8,128)(2,1)} %get-tuple-element.67), channel_id=1, source_target_pairs={{0,1},{1,0},{2,3},{3,2},{4,5},{5,4},{6,7},{7,6},{8,9},{9,8},{10,11... | collective-permute-start | bytes 1769480 | tf_op jit(solution)/shard_map/ppermute | solution.py:373
  27.9 18.5 %copy-start.7 = (bf16[4,128,256]{2,1,0:T(8,128)(2,1)}, bf16[4,128,256]{2,1,0:T(8,128)(2,1)S(1)}, u32[]{:S(2)}) copy-start(bf16[4,128,256]{2,1,0:T(8,128)(2,1)S(1)} %collective-permute-done.refs_2_) | copy-start | bytes 786436
  32.7 0.7 copy-start.9
  42.8 18.7 %copy-start.6 = (s32[1,32]{1,0:T(1,128)S(1)}, s32[1,32]{1,0:T(1,128)}, u32[]{:S(2)}) copy-start(s32[1,32]{1,0:T(1,128)} %order_ref.3) | copy-start | bytes 388
  42.8 14.8 %all-to-all-start.3 = ((bf16[4,128,512]{2,1,0:T(8,128)(2,1)}), bf16[4,128,512]{2,1,0:T(8,128)(2,1)S(1)}, u32[]{:S(2)}, u32[]{:S(2)}) async-start(bf16[4,128,512]{2,1,0:T(8,128)(2,1)} %get-tuple-element.60), calls=%async_computation.3 | async-start | bytes 1048576 | tf_op jit(solution)/shard_map/all_to_all | solution.py:359
  46.4 10.5 %collective-permute-start.2 = (bf16[4,128,256]{2,1,0:T(8,128)(2,1)S(1)}, bf16[4,128,256]{2,1,0:T(8,128)(2,1)S(1)}, u32[]{:S(2)}, u32[]{:S(2)}) collective-permute-start(bf16[4,128,256]{2,1,0:T(8,128)(2,1)S(1)} %collective-permute-done.refs_2_), channel_id=1, source_target_pairs={{0,8},{2,10},{4,12},{6,14},{8,16},{10,18},{12,20},{14,22},{16,24},... | collective-permute-start | bytes 786440 | tf_op jit(solution)/shard_map/ppermute | solution.py:362
  56.9 0.7 copy-start.13
  57.6 22.3 %collective-permute-start.4 = (bf16[4,128,256]{2,1,0:T(8,128)(2,1)S(1)}, bf16[4,128,256]{2,1,0:T(8,128)(2,1)S(1)}, u32[]{:S(2)}, u32[]{:S(2)}) collective-permute-start(bf16[4,128,256]{2,1,0:T(8,128)(2,1)S(1)} %all_to_all.30.refs_1_), channel_id=1, source_target_pairs={{0,8},{2,10},{4,12},{6,14},{8,16},{10,18},{12,20},{14,22},{16,24},... | collective-permute-start | bytes 786440 | tf_op jit(solution)/shard_map/ppermute | solution.py:362
  57.6 23.0 %collective-permute-start.5 = (bf16[4,128,256]{2,1,0:T(8,128)(2,1)S(1)}, bf16[4,128,256]{2,1,0:T(8,128)(2,1)S(1)}, u32[]{:S(2)}, u32[]{:S(2)}) collective-permute-start(bf16[4,128,256]{2,1,0:T(8,128)(2,1)S(1)} %all_to_all.30.refs_1_), channel_id=1, source_target_pairs={{0,16},{2,18},{4,20},{6,22},{8,24},{10,26},{12,28},{14,30},{16,0},... | collective-permute-start | bytes 786440 | tf_op jit(solution)/shard_map/ppermute | solution.py:362
  58.7 22.6 %collective-permute-start.6 = (bf16[4,128,256]{2,1,0:T(8,128)(2,1)S(1)}, bf16[4,128,256]{2,1,0:T(8,128)(2,1)S(1)}, u32[]{:S(2)}, u32[]{:S(2)}) collective-permute-start(bf16[4,128,256]{2,1,0:T(8,128)(2,1)S(1)} %all_to_all.30.refs_1_), channel_id=1, source_target_pairs={{0,24},{2,26},{4,28},{6,30},{8,0},{10,2},{12,4},{14,6},{16,8},{18,... | collective-permute-start | bytes 786440 | tf_op jit(solution)/shard_map/ppermute | solution.py:362
  61.4 1.0 copy-start.8
  62.4 0.9 copy-start.10
  63.3 0.9 copy-start.14
  79.2 0.7 copy-start.11
  79.9 0.7 copy-start
  80.6 0.7 copy-start.2
  81.3 0.7 copy-start.4
  82.0 15.2 %collective-permute-start.7 = (bf16[4,128,256]{2,1,0:T(8,128)(2,1)}, bf16[4,128,256]{2,1,0:T(8,128)(2,1)}, u32[]{:S(2)}, u32[]{:S(2)}) collective-permute-start(bf16[4,128,256]{2,1,0:T(8,128)(2,1)} %get-tuple-element.87), channel_id=1, source_target_pairs={{0,8},{2,10},{4,12},{6,14},{8,16},{10,18},{12,20},{14,22},{16,24},... | collective-permute-start | bytes 786440 | tf_op jit(solution)/shard_map/ppermute | solution.py:362
  84.5 3.6 %copy-start.12 = (bf16[4,128,256]{2,1,0:T(8,128)(2,1)S(1)}, bf16[4,128,256]{2,1,0:T(8,128)(2,1)}, u32[]{:S(2)}) copy-start(bf16[4,128,256]{2,1,0:T(8,128)(2,1)} %copy-done.11) | copy-start | bytes 786436
  84.5 5.0 %copy-start.1 = (bf16[4,128,256]{2,1,0:T(8,128)(2,1)S(1)}, bf16[4,128,256]{2,1,0:T(8,128)(2,1)}, u32[]{:S(2)}) copy-start(bf16[4,128,256]{2,1,0:T(8,128)(2,1)} %copy-done) | copy-start | bytes 786436
  84.5 5.0 %copy-start.3 = (bf16[4,128,256]{2,1,0:T(8,128)(2,1)S(1)}, bf16[4,128,256]{2,1,0:T(8,128)(2,1)}, u32[]{:S(2)}) copy-start(bf16[4,128,256]{2,1,0:T(8,128)(2,1)} %copy-done.2) | copy-start | bytes 786436
  84.5 5.0 %copy-start.5 = (bf16[4,128,256]{2,1,0:T(8,128)(2,1)S(1)}, bf16[4,128,256]{2,1,0:T(8,128)(2,1)}, u32[]{:S(2)}) copy-start(bf16[4,128,256]{2,1,0:T(8,128)(2,1)} %copy-done.4) | copy-start | bytes 786436
  84.5 24.9 %all-to-all-start.4 = ((bf16[4,128,512]{2,1,0:T(8,128)(2,1)}), bf16[4,128,512]{2,1,0:T(8,128)(2,1)S(1)}, u32[]{:S(2)}, u32[]{:S(2)}) async-start(bf16[4,128,512]{2,1,0:T(8,128)(2,1)} %get-tuple-element.93), calls=%async_computation.4 | async-start | bytes 1048576 | tf_op jit(solution)/shard_map/all_to_all | solution.py:359
  88.2 11.0 %collective-permute-start.13 = (bf16[4,128,256]{2,1,0:T(8,128)(2,1)S(1)}, bf16[4,128,256]{2,1,0:T(8,128)(2,1)S(1)}, u32[]{:S(2)}, u32[]{:S(2)}) collective-permute-start(bf16[4,128,256]{2,1,0:T(8,128)(2,1)S(1)} %copy-done.12), channel_id=1, source_target_pairs={{0,24},{2,26},{4,28},{6,30},{8,0},{10,2},{12,4},{14,6},{16,8},{18,... | collective-permute-start | bytes 786440 | tf_op jit(solution)/shard_map/ppermute | solution.py:362
  97.2 1.2 copy-start.15
  97.2 1.2 copy-start.17
  97.2 1.2 copy-start.19
  97.2 1.2 copy-start.21
  98.4 10.2 %collective-permute-start.12 = (bf16[4,128,256]{2,1,0:T(8,128)(2,1)S(1)}, bf16[4,128,256]{2,1,0:T(8,128)(2,1)S(1)}, u32[]{:S(2)}, u32[]{:S(2)}) collective-permute-start(bf16[4,128,256]{2,1,0:T(8,128)(2,1)S(1)} %add_convert_fusion), channel_id=1, source_target_pairs={{0,8},{2,10},{4,12},{6,14},{8,16},{10,18},{12,20},{14,22},{16,24},... | collective-permute-start | bytes 786440 | tf_op jit(solution)/shard_map/ppermute | solution.py:362
  109.4 3.6 %copy-start.22 = (bf16[128,512]{1,0:T(8,128)(2,1)S(1)}, bf16[128,512]{1,0:T(8,128)(2,1)}, u32[]{:S(2)}) copy-start(bf16[128,512]{1,0:T(8,128)(2,1)} %copy-done.21) | copy-start | bytes 393220
  109.4 6.5 %copy-start.20 = (bf16[128,512]{1,0:T(8,128)(2,1)S(1)}, bf16[128,512]{1,0:T(8,128)(2,1)}, u32[]{:S(2)}) copy-start(bf16[128,512]{1,0:T(8,128)(2,1)} %copy-done.19) | copy-start | bytes 393220
  109.4 6.5 %copy-start.18 = (bf16[128,512]{1,0:T(8,128)(2,1)S(1)}, bf16[128,512]{1,0:T(8,128)(2,1)}, u32[]{:S(2)}) copy-start(bf16[128,512]{1,0:T(8,128)(2,1)} %copy-done.17) | copy-start | bytes 393220
  109.4 7.9 %copy-start.16 = (bf16[128,512]{1,0:T(8,128)(2,1)S(1)}, bf16[128,512]{1,0:T(8,128)(2,1)}, u32[]{:S(2)}) copy-start(bf16[128,512]{1,0:T(8,128)(2,1)} %copy-done.15) | copy-start | bytes 393220
  109.5 21.7 %all-to-all-start.5 = ((bf16[4,128,256]{2,1,0:T(8,128)(2,1)}), bf16[4,128,256]{2,1,0:T(8,128)(2,1)S(1)}, u32[]{:S(2)}, u32[]{:S(2)}) async-start(bf16[4,128,256]{2,1,0:T(8,128)(2,1)} %sum_key_parts.1), calls=%async_computation.5 | async-start | bytes 524288 | tf_op jit(solution)/shard_map/all_to_all | solution.py:359
  113.0 10.3 %collective-permute-start.10 = (bf16[128,512]{1,0:T(8,128)(2,1)S(1)}, bf16[128,512]{1,0:T(8,128)(2,1)S(1)}, u32[]{:S(2)}, u32[]{:S(2)}) collective-permute-start(bf16[128,512]{1,0:T(8,128)(2,1)S(1)} %copy-done.22), channel_id=1, source_target_pairs={{0,5},{1,4},{2,7},{3,6},{4,1},{5,0},{6,3},{7,2},{8,13},{9,12},{10,... | collective-permute-start | bytes 393224 | tf_op jit(solution)/shard_map/ppermute | solution.py:373
  116.0 9.3 %collective-permute-start.11 = (bf16[128,512]{1,0:T(8,128)(2,1)S(1)}, bf16[128,512]{1,0:T(8,128)(2,1)S(1)}, u32[]{:S(2)}, u32[]{:S(2)}) collective-permute-start(bf16[128,512]{1,0:T(8,128)(2,1)S(1)} %copy-done.20), channel_id=1, source_target_pairs={{0,7},{1,6},{2,5},{3,4},{4,3},{5,2},{6,1},{7,0},{8,15},{9,14},{10,... | collective-permute-start | bytes 393224 | tf_op jit(solution)/shard_map/ppermute | solution.py:373
  116.0 12.0 %collective-permute-start.8 = (bf16[128,512]{1,0:T(8,128)(2,1)S(1)}, bf16[128,512]{1,0:T(8,128)(2,1)S(1)}, u32[]{:S(2)}, u32[]{:S(2)}) collective-permute-start(bf16[128,512]{1,0:T(8,128)(2,1)S(1)} %copy-done.18), channel_id=1, source_target_pairs={{0,1},{1,0},{2,3},{3,2},{4,5},{5,4},{6,7},{7,6},{8,9},{9,8},{10,11... | collective-permute-start | bytes 393224 | tf_op jit(solution)/shard_map/ppermute | solution.py:373
  117.3 11.9 %collective-permute-start.9 = (bf16[128,512]{1,0:T(8,128)(2,1)S(1)}, bf16[128,512]{1,0:T(8,128)(2,1)S(1)}, u32[]{:S(2)}, u32[]{:S(2)}) collective-permute-start(bf16[128,512]{1,0:T(8,128)(2,1)S(1)} %copy-done.16), channel_id=1, source_target_pairs={{0,3},{1,2},{2,1},{3,0},{4,7},{5,6},{6,5},{7,4},{8,11},{9,10},{10,... | collective-permute-start | bytes 393224 | tf_op jit(solution)/shard_map/ppermute | solution.py:373

commit v2 on v0

--- a/solution.py
+++ b/solution.py
@@ -42,52 +42,74 @@
     return pl.ds(pl.multiple_of(index * width, width), width)
 
 
-def pack_keys(key_ref, value_ref, types_ref, table_ref, *refs):
-    pieces, (keys, types, table, typed, arrived, placed) = refs[:QUAD], refs[QUAD:]
+def pack_keys(
+    back_key, back_value, back_types, key, value, types, table_ref, *refs
+):
+    pieces, (keys, event_types, table, typed, arrived, placed) = refs[:QUAD], refs[QUAD:]
     _, member = place()
+    copies = [pltpu.make_async_copy(table_ref.at[0], table, arrived.at[4])]
+    for i, (key_ref, types_ref) in enumerate([(back_key, back_types), (key, types)]):
+        copies += [
+            pltpu.make_async_copy(types_ref, event_types.at[i], arrived.at[2 * i]),
+            pltpu.make_async_copy(key_ref.at[0], keys.at[i], arrived.at[2 * i + 1]),
+        ]
+    placements = [
+        pltpu.make_async_copy(
+            value_ref.at[0, :, columns(member ^ d, HEAD)],
+            pieces[d].at[:, (2 * i + 1) * HEAD : (2 * i + 2) * HEAD],
+            placed.at[i * QUAD + d],
+        )
+        for i, value_ref in enumerate([back_value, value])
+        for d in range(QUAD)
+    ]
+    for copy in copies + placements:
+        copy.start()
+    for copy in copies:
+        copy.wait()
+    for i in range(2):
+        onehot = (
+            lax.broadcasted_iota(jnp.int32, (table.shape[0], types.shape[1]), 0) == event_types[i]
+        ).astype(jnp.float32).astype(jnp.bfloat16)
+        type_rows = dot(onehot, table[...], TN)
+        typed[...] = (keys[i].astype(jnp.float32) + type_rows).astype(jnp.bfloat16)
+        for d in range(QUAD):
+            pieces[d][:, 2 * i * HEAD : (2 * i + 1) * HEAD] = typed[:, columns(member ^ d, HEAD)]
+    for copy in placements:
+        copy.wait()
+
+
+def stack_keys(*refs):
+    pieces, (back, front, placed) = refs[:QUAD], refs[QUAD:]
+    rows = pieces[0].shape[0]
     copies = [
-        pltpu.make_async_copy(source, target, arrived.at[i])
-        for i, (source, target) in enumerate(
-            [(types_ref, types), (table_ref.at[0], table), (key_ref.at[0], keys)]
+        pltpu.make_async_copy(
+            pieces[d].at[:, 2 * i * HEAD : (2 * i + 2) * HEAD],
+            out.at[d * rows : (d + 1) * rows, :],
+            placed.at[i * QUAD + d],
         )
-    ]
-    copies += [
-        pltpu.make_async_copy(
-            value_ref.at[0, :, columns(member ^ d, HEAD)], pieces[d].at[:, HEAD:], placed.at[d]
-        )
+        for i, out in enumerate([back, front])
         for d in range(QUAD)
     ]
     for copy in copies:
         copy.start()
-    for copy in copies[:3]:
+    for copy in copies:
         copy.wait()
-    onehot = (
-        lax.broadcasted_iota(jnp.int32, (table.shape[0], types.shape[1]), 0) == types[...]
-    ).astype(jnp.float32).astype(jnp.bfloat16)
-    type_rows = dot(onehot, table[...], TN)
-    typed[...] = (keys[...].astype(jnp.float32) + type_rows).astype(jnp.bfloat16)
-    for d in range(QUAD):
-        pieces[d][:, :HEAD] = typed[:, columns(member ^ d, HEAD)]
-    for copy in copies[3:]:
-        copy.wait()
 
 
 def pack_queries(query_ref, grad_ref, forward_ref, gate_ref, gain_ref, *refs):
-    pieces, forward_pieces, (gate_out, placed) = refs[:QUAD], refs[QUAD : 2 * QUAD], refs[2 * QUAD :]
+    pieces, (gate_out, placed) = refs[:QUAD], refs[QUAD:]
     _, member = place()
     width = query_ref.shape[2] // QUAD
     rows = gate_ref.shape[1]
-    copies = []
-    for d in reversed(range(QUAD)):
-        for i, (source, target) in enumerate(
-            [
-                (query_ref, pieces[d].at[:, :width]),
-                (grad_ref, pieces[d].at[:, width:]),
-                (forward_ref, forward_pieces[d]),
-            ]
-        ):
-            source = source.at[0, :, columns(member ^ d, width)]
-            copies.append(pltpu.make_async_copy(source, target, placed.at[3 * d + i]))
+    copies = [
+        pltpu.make_async_copy(
+            source.at[0, :, columns(member ^ d, width)],
+            pieces[d].at[:, i * width : (i + 1) * width],
+            placed.at[3 * d + i],
+        )
+        for d in reversed(range(QUAD))
+        for i, source in enumerate([query_ref, grad_ref, forward_ref])
+    ]
     copies.append(
         pltpu.make_async_copy(gate_ref.at[0], gate_out.at[:rows, :], placed.at[3 * QUAD])
     )
@@ -156,12 +178,13 @@
     block_rows = groups * stretch_rows
     steps = keys.shape[0] // block_rows + 1
     in_sequence(order_ref, stacks, stretch_rows, keys, values)
+    offset = 2 * groups * HEAD
     for d in range(QUAD):
         for e in range(2):
             for g in range(groups):
                 stacked[2 * d + e, g * stretch_rows : (g + 1) * stretch_rows, :] = queries[d][
                     e * stretch_rows : (e + 1) * stretch_rows,
-                    g * HEAD : (g + 1) * HEAD,
+                    offset + g * HEAD : offset + (g + 1) * HEAD,
                 ]
     total[...] = jnp.zeros_like(total)
     gap[...] = lax.broadcasted_iota(jnp.int32, gap.shape, 1) - lax.rem(
@@ -202,7 +225,7 @@
     keys, values, keys_t, stacked, grads, total_t, key_total, value_total, gap = refs
     z, member = place()
     stretch_rows = queries[0].shape[0] // 2
-    groups = queries[0].shape[1] // (2 * HEAD)
+    groups = query_outs[0].shape[1] // HEAD
     block_rows = groups * stretch_rows
     blocks = keys.shape[0] // block_rows
     steps = blocks + 1
@@ -379,27 +402,6 @@
         ]
         return lax.ppermute(block, ("ctx", "pipe"), route)
 
-    def pack(key, value, types, name):
-        return call(
-            pack_keys,
-            name,
-            [bf16(rows, 2 * HEAD)] * QUAD,
-            [HBM] * 4,
-            key,
-            value,
-            types,
-            type_key,
-            scratch=[
-                pltpu.VMEM(key.shape[1:], jnp.bfloat16),
-                pltpu.VMEM(types.shape, jnp.int32),
-                pltpu.VMEM(type_key.shape[1:], jnp.bfloat16),
-                pltpu.VMEM(key.shape[1:], jnp.bfloat16),
-                pltpu.SemaphoreType.DMA((3,)),
-                pltpu.SemaphoreType.DMA((QUAD,)),
-            ],
-            vmem=60,
-        )
-
     ahead = nz // 2
 
     def ring_up(block):
@@ -412,6 +414,7 @@
         return [stack, ring_up(stack)], [ring_down(stack)]
 
     def gather_rest(up, down):
+        up, down = lax.optimization_barrier((up, down))
         while len(up) <= ahead:
             up = up + [ring_up(up[-1])]
         while len(up) + len(down) < nz:
@@ -431,13 +434,34 @@
             down = ring_down(add(down, parts[s]))
         return parts[0], up, down
 
-    back_pieces = swap(pack(key_bwd, value_bwd, types_bwd, "pack_keys_bwd"))
+    pieces = swap(
+        call(
+            pack_keys,
+            "pack_keys",
+            [bf16(rows, 4 * HEAD)] * QUAD,
+            [HBM] * 7,
+            key_bwd,
+            value_bwd,
+            types_bwd,
+            key_fwd,
+            value_fwd,
+            types_fwd,
+            type_key,
+            scratch=[
+                pltpu.VMEM((2, *key_fwd.shape[1:]), jnp.bfloat16),
+                pltpu.VMEM((2, *types_fwd.shape), jnp.int32),
+                pltpu.VMEM(type_key.shape[1:], jnp.bfloat16),
+                pltpu.VMEM(key_fwd.shape[1:], jnp.bfloat16),
+                pltpu.SemaphoreType.DMA((5,)),
+                pltpu.SemaphoreType.DMA((2 * QUAD,)),
+            ],
+            vmem=60,
+        )
+    )
     packed = call(
         pack_queries,
         "pack_queries",
-        [bf16(rows, 2 * width)] * QUAD
-        + [bf16(rows, width)] * QUAD
-        + [bf16(rows + GAIN_ROWS, QUAD * width)],
+        [bf16(rows, 3 * width)] * QUAD + [bf16(rows + GAIN_ROWS, QUAD * width)],
         [HBM] * 4 + [VMEM],
         query_bwd,
         grad_out,
@@ -447,18 +471,22 @@
         scratch=[pltpu.SemaphoreType.DMA((3 * QUAD + 1,))],
         vmem=60,
     )
-    back_pieces, packed = lax.optimization_barrier((back_pieces, packed))
-    back_queries, queries, gate_before = swap(packed[:QUAD]), packed[QUAD:-1], packed[-1]
-    back_stacks = gather_rest(*gather_first(jnp.concatenate(back_pieces, axis=0)))
-    pieces = pack(key_fwd, value_fwd, types_fwd, "pack_keys_fwd")
+    pieces, packed = lax.optimization_barrier((pieces, packed))
+    back_stack, stack = call(
+        stack_keys,
+        "stack_keys",
+        [bf16(QUAD * rows, 2 * HEAD)] * 2,
+        [HBM] * QUAD,
+        *pieces,
+        scratch=[pltpu.SemaphoreType.DMA((2 * QUAD,))],
+    )
+    queries = swap(packed[:QUAD])
+    up, down = gather_first(back_stack)
+    up, down, gate_before = lax.optimization_barrier((up, down, packed[QUAD]))
+    back_stacks = gather_rest(up, down)
     gate_before = hand(gate_before, 0)
-    back_queries, pieces, queries = lax.optimization_barrier((back_queries, pieces, queries))
-    stack = jnp.concatenate(swap(pieces), axis=0)
-    stack, queries, back_stacks, gate_before = lax.optimization_barrier(
-        (stack, queries, back_stacks, gate_before)
-    )
+    stack, back_stacks = lax.optimization_barrier((stack, back_stacks))
     stacks = [stack] + [turn(stack, s) for s in range(1, nz)]
-    queries = swap(queries)
 
     sequence = [pltpu.VMEM((total_rows, HEAD), jnp.bfloat16)] * 2
     stacked = pltpu.VMEM((2 * QUAD, block_rows, HEAD), jnp.bfloat16)
@@ -469,7 +497,7 @@
         [bf16(rows, width)] * QUAD + [bf16(QUAD * rows, 2 * HEAD)] * nz,
         [SMEM] + [VMEM] * (QUAD + nz),
         stretch_order,
-        *back_queries,
+        *queries,
         *back_stacks,
         scratch=sequence
         + [
@@ -485,11 +513,12 @@
         transcendentals=2 * pairs,
     )
     query_pieces, key_parts = outs[:QUAD], outs[QUAD:]
-    query_pieces, key_parts, stacks, queries = lax.optimization_barrier(
-        (query_pieces, key_parts, stacks, queries)
+    query_pieces, key_parts, gate_before = lax.optimization_barrier(
+        (query_pieces, key_parts, gate_before)
     )
     key_sums = reduce_first(key_parts)
     query_pieces = swap(query_pieces)
+    query_pieces, stacks = lax.optimization_barrier((query_pieces, stacks))
     attended = call(
         functools.partial(forward_kernel, nz),
         "forward",
@@ -520,7 +549,6 @@
             *key_sums,
         )
     )
-    handed, query_pieces = lax.optimization_barrier((handed, query_pieces))
     (query_grad,) = call(
         query_grad_kernel,
         "query_grad",

time: 99 us -> 96.4 us (0.974)
  Pallas kernels: 32.2 us -> 30.8 us
    ppermute x9, waiting for transfers between devices: 13.4 us -> 21.8 us  [turn(): lax.ppermute(block, 'ctx', [(i, (i + s * QUAD) % devices) for i in range(...]
    ppermute x5, waiting for transfers between devices: 8.19 us -> 3.46 us  [hand(): return lax.ppermute(block, ('ctx', 'pipe'), route)]
    ppermute x18 -> x12, waiting for transfers between devices: 9.18 us -> 4.74 us  [swap(): lax.ppermute(pieces[d], 'ctx', [(i, i ^ d) for i in range(devices)])]
    ppermute x9, starting transfers between devices: 15.1 us -> 19.4 us  [turn(): lax.ppermute(block, 'ctx', [(i, (i + s * QUAD) % devices) for i in range(...]
    ppermute x18 -> x12, starting transfers between devices: 12.8 us -> 9.26 us  [swap(): lax.ppermute(pieces[d], 'ctx', [(i, i ^ d) for i in range(devices)])]
    pallas_call x9, Pallas kernels: 32.2 us -> 30.8 us  [call(): pl.pallas_call(kernel, name=name, out_shape=out_shape, in_specs=specs, ou...]
  transfers between devices with their start and end apart: 32 -> 26, of which waited for: 12 -> 9; matrix products, arithmetic and copies ran while one was open for 1% -> 0% of each run, Pallas kernels for 30% -> 29%
where the time goes in v2:
time: 96.4 us; the launch traced here: 96.2 us
  starting transfers between devices  34.6 us (36%)
  Pallas kernels  30.8 us (32%)
  waiting for transfers between devices  30 us (31%)
    pallas_call x9, Pallas kernels, call(): pl.pallas_call(kernel, name=name, out_shape=out_shape, in_specs=specs, ou...  30.8 us
    ppermute x9, waiting for transfers between devices, turn(): lax.ppermute(block, 'ctx', [(i, (i + s * QUAD) % devices) for i in range(...  21.8 us
    ppermute x9, starting transfers between devices, turn(): lax.ppermute(block, 'ctx', [(i, (i + s * QUAD) % devices) for i in range(...  19.4 us
    ppermute x12, starting transfers between devices, swap(): lax.ppermute(pieces[d], 'ctx', [(i, i ^ d) for i in range(devices)])  9.26 us
    ppermute x5, starting transfers between devices, hand(): return lax.ppermute(block, ('ctx', 'pipe'), route)  5.91 us
    ppermute x12, waiting for transfers between devices, swap(): lax.ppermute(pieces[d], 'ctx', [(i, i ^ d) for i in range(devices)])  4.74 us
    ppermute x5, waiting for transfers between devices, hand(): return lax.ppermute(block, ('ctx', 'pipe'), route)  3.46 us
  transfers between devices with their start and end apart: 26, of which 9 were waited for; matrix products, arithmetic and copies ran while one was open for 0% of the time, Pallas kernels for 29%

profile of v2, /device:TPU:0, one launch (start us, length us, event | category | flops | bytes accessed | tf_op | source)
XLA Modules:
  0.0 96.2 jit_solution(2606277999940754228)
XLA Ops:
  0.6 2.4 %pack_keys.1 = (bf16[128,512]{1,0:T(8,128)(2,1)}, bf16[128,512]{1,0:T(8,128)(2,1)}, bf16[128,512]{1,0:T(8,128)(2,1)}, bf16[128,512]{1,0:T(8,128)(2,1)}) custom-call(bf16[1,128,512]{2,1,0:T(8,128)(2,1)} %back_key.1, bf16[1,128,512]{2,1,0:T(8,128)(2,1)} %back_value.1, s32[1,128]{1,0:T(1,128)} %back_types.1, bf16[1,128,512]{2,1,0:T(8,128)(2,1)} %key.1, ...), custom_call_target="tpu_custom_call" | custom-call | bytes 1115136 | tf_op jit(solution)/shard_map/pack_keys/pallas_call | solution.py:345
  3.0 0.5 collective-permute-start
  3.5 2.6 %collective-permute-start.1 = (bf16[128,512]{1,0:T(8,128)(2,1)}, bf16[128,512]{1,0:T(8,128)(2,1)S(1)}, u32[]{:S(2)}, u32[]{:S(2)}) collective-permute-start(bf16[128,512]{1,0:T(8,128)(2,1)} %get-tuple-element.78), channel_id=1, source_target_pairs={{0,4},{2,6},{4,0},{6,2},{8,12},{10,14},{12,8},{14,10},{16,20},{18,... | collective-permute-start | bytes 393224 | tf_op jit(solution)/shard_map/ppermute | solution.py:387
  6.1 0.1 collective-permute-start.2
  6.2 3.8 %pack_queries.1 = (bf16[128,1536]{1,0:T(8,128)(2,1)}, bf16[128,1536]{1,0:T(8,128)(2,1)}, bf16[128,1536]{1,0:T(8,128)(2,1)}, bf16[128,1536]{1,0:T(8,128)(2,1)}, bf16[144,2048]{1,0:T(8,128)(2,1)}) custom-call(bf16[1,128,2048]{2,1,0:T(8,128)(2,1)} %query_ref.1, bf16[1,128,2048]{2,1,0:T(8,128)(2,1)} %grad_ref.1, bf16[1,128,2048]{2,1,0:T(8,128)(2,1)} %forward_ref.1, ...), custom_call_target="tpu_custom_call" | custom-call | bytes 4268032 | tf_op jit(solution)/shard_map/pack_queries/pallas_call | solution.py:345
  9.9 0.0 copy-start
  10.0 0.0 collective-permute-done.refs_1_
  10.0 0.7 collective-permute-done.1.refs_2_
  10.6 2.3 %collective-permute-done.2.refs_3_ = bf16[128,512]{1,0:T(8,128)(2,1)S(1)} collective-permute-done((bf16[128,512]{1,0:T(8,128)(2,1)}, bf16[128,512]{1,0:T(8,128)(2,1)S(1)}, u32[]{:S(2)}, u32[]{:S(2)}) %collective-permute-start.2) | collective-permute-done | bytes 131104 | tf_op jit(solution)/shard_map/ppermute | solution.py:387
  12.9 0.1 stack_keys.1
  13.1 0.0 copy-start.2
  13.1 1.7 %collective-permute-start.6 = (bf16[512,256]{1,0:T(8,128)(2,1)S(1)}, bf16[512,256]{1,0:T(8,128)(2,1)S(1)}, u32[]{:S(2)}, u32[]{:S(2)}) collective-permute-start(bf16[512,256]{1,0:T(8,128)(2,1)S(1)} %get-tuple-element.102.refs_4_), channel_id=1, source_target_pairs={{0,8},{2,10},{4,12},{6,14},{8,16},{10,18},{12,20},{14,22},{16,24},... | collective-permute-start | bytes 786440 | tf_op jit(solution)/shard_map/ppermute | solution.py:392
  14.8 2.2 %collective-permute-start.7 = (bf16[512,256]{1,0:T(8,128)(2,1)S(1)}, bf16[512,256]{1,0:T(8,128)(2,1)S(1)}, u32[]{:S(2)}, u32[]{:S(2)}) collective-permute-start(bf16[512,256]{1,0:T(8,128)(2,1)S(1)} %get-tuple-element.102.refs_4_), channel_id=1, source_target_pairs={{0,24},{2,26},{4,28},{6,30},{8,0},{10,2},{12,4},{14,6},{16,8},{18,... | collective-permute-start | bytes 786440 | tf_op jit(solution)/shard_map/ppermute | solution.py:392
  17.0 0.0 collective-permute-start.3
  17.0 1.6 %collective-permute-start.4 = (bf16[128,1536]{1,0:T(8,128)(2,1)}, bf16[128,1536]{1,0:T(8,128)(2,1)S(1)}, u32[]{:S(2)}, u32[]{:S(2)}) collective-permute-start(bf16[128,1536]{1,0:T(8,128)(2,1)} %get-tuple-element.87), channel_id=1, source_target_pairs={{0,4},{2,6},{4,0},{6,2},{8,12},{10,14},{12,8},{14,10},{16,20},{18,... | collective-permute-start | bytes 1179656 | tf_op jit(solution)/shard_map/ppermute | solution.py:387
  18.5 0.3 collective-permute-start.5
  18.8 5.3 %collective-permute-done.6.refs_5_ = bf16[512,256]{1,0:T(8,128)(2,1)S(1)} collective-permute-done((bf16[512,256]{1,0:T(8,128)(2,1)S(1)}, bf16[512,256]{1,0:T(8,128)(2,1)S(1)}, u32[]{:S(2)}, u32[]{:S(2)}) %collective-permute-start.6) | collective-permute-done | bytes 262176 | tf_op jit(solution)/shard_map/ppermute | solution.py:392
  24.1 4.5 %collective-permute-done.7.refs_7_ = bf16[512,256]{1,0:T(8,128)(2,1)S(1)} collective-permute-done((bf16[512,256]{1,0:T(8,128)(2,1)S(1)}, bf16[512,256]{1,0:T(8,128)(2,1)S(1)}, u32[]{:S(2)}, u32[]{:S(2)}) %collective-permute-start.7) | collective-permute-done | bytes 262176 | tf_op jit(solution)/shard_map/ppermute | solution.py:392
  28.6 1.5 %collective-permute-start.9 = (bf16[144,2048]{1,0:T(8,128)(2,1)}, bf16[144,2048]{1,0:T(8,128)(2,1)S(1)}, u32[]{:S(2)}, u32[]{:S(2)}) collective-permute-start(bf16[144,2048]{1,0:T(8,128)(2,1)} %get-tuple-element.114), channel_id=1, source_target_pairs={{0,1},{1,0},{2,3},{3,2},{4,5},{5,4},{6,7},{7,6},{8,9},{9,8},{10,11... | collective-permute-start | bytes 1769480 | tf_op jit(solution)/shard_map/ppermute | solution.py:403
  30.1 1.1 %collective-permute-start.8 = (bf16[512,256]{1,0:T(8,128)(2,1)S(1)}, bf16[512,256]{1,0:T(8,128)(2,1)S(1)}, u32[]{:S(2)}, u32[]{:S(2)}) collective-permute-start(bf16[512,256]{1,0:T(8,128)(2,1)S(1)} %collective-permute-done.6.refs_5_), channel_id=1, source_target_pairs={{0,8},{2,10},{4,12},{6,14},{8,16},{10,18},{12,20},{14,22},{16,24},... | collective-permute-start | bytes 786440 | tf_op jit(solution)/shard_map/ppermute | solution.py:392
  31.3 8.1 %collective-permute-done.8.refs_6_ = bf16[512,256]{1,0:T(8,128)(2,1)S(1)} collective-permute-done((bf16[512,256]{1,0:T(8,128)(2,1)S(1)}, bf16[512,256]{1,0:T(8,128)(2,1)S(1)}, u32[]{:S(2)}, u32[]{:S(2)}) %collective-permute-start.8) | collective-permute-done | bytes 262176 | tf_op jit(solution)/shard_map/ppermute | solution.py:392
  39.3 0.0 collective-permute-start.13
  39.3 0.0 collective-permute-done.3.refs_1_
  39.3 0.9 collective-permute-start.14
  40.2 0.0 collective-permute-done.4.refs_2_
  40.2 3.0 %collective-permute-start.15 = (bf16[512,256]{1,0:T(8,128)(2,1)S(1)}, bf16[512,256]{1,0:T(8,128)(2,1)S(1)}, u32[]{:S(2)}, u32[]{:S(2)}) collective-permute-start(bf16[512,256]{1,0:T(8,128)(2,1)S(1)} %get-tuple-element.120.refs_4_), channel_id=1, source_target_pairs={{0,24},{2,26},{4,28},{6,30},{8,0},{10,2},{12,4},{14,6},{16,8},{18,... | collective-permute-start | bytes 786440 | tf_op jit(solution)/shard_map/ppermute | solution.py:392
  43.2 0.0 collective-permute-done.5.refs_3_
  43.2 14.1 %backward.1 = (bf16[128,512]{1,0:T(8,128)(2,1)S(1)}, bf16[128,512]{1,0:T(8,128)(2,1)S(1)}, bf16[128,512]{1,0:T(8,128)(2,1)S(1)}, bf16[128,512]{1,0:T(8,128)(2,1)...) custom-call(s32[1,32]{1,0:T(1,128)S(1)} %copy-done.2, ...), custom_call_target="tpu_custom_call" | custom-call | flops 3019898880 | bytes 4194432 | tf_op jit(solution)/shard_map/backward/pallas_call | solution.py:345
  57.3 0.0 collective-permute-done.9.refs_4_
  57.3 0.6 collective-permute-start.16
  57.9 0.0 collective-permute-start.10
  57.9 0.0 collective-permute-done.13.refs_5_
  57.9 1.5 %collective-permute-start.11 = (bf16[128,512]{1,0:T(8,128)(2,1)S(1)}, bf16[128,512]{1,0:T(8,128)(2,1)S(1)}, u32[]{:S(2)}, u32[]{:S(2)}) collective-permute-start(bf16[128,512]{1,0:T(8,128)(2,1)S(1)} %get-tuple-element.117), channel_id=1, source_target_pairs={{0,4},{2,6},{4,0},{6,2},{8,12},{10,14},{12,8},{14,10},{16,20},{18,... | collective-permute-start | bytes 393224 | tf_op jit(solution)/shard_map/ppermute | solution.py:387
  59.4 0.0 collective-permute-done.14.refs_6_
  59.4 0.4 collective-permute-start.12
  59.8 0.0 collective-permute-done.15.refs_7_
  59.8 6.2 %collective-permute-start.22 = (bf16[512,256]{1,0:T(8,128)(2,1)S(1)}, bf16[512,256]{1,0:T(8,128)(2,1)S(1)}, u32[]{:S(2)}, u32[]{:S(2)}) collective-permute-start(bf16[512,256]{1,0:T(8,128)(2,1)S(1)} %get-tuple-element.141), channel_id=1, source_target_pairs={{0,24},{2,26},{4,28},{6,30},{8,0},{10,2},{12,4},{14,6},{16,8},{18,... | collective-permute-start | bytes 786440 | tf_op jit(solution)/shard_map/ppermute | solution.py:392
  65.9 0.0 collective-permute-done.10.refs_1_
  65.9 0.0 collective-permute-done.11.refs_2_
  65.9 0.3 collective-permute-done.12.refs_3_
  66.2 7.6 %forward.1 = (bf16[128,512]{1,0:T(8,128)(2,1)S(1)}, bf16[128,512]{1,0:T(8,128)(2,1)S(1)}, bf16[128,512]{1,0:T(8,128)(2,1)S(1)}, bf16[128,512]{1,0:T(8,128)(2,1)S(1)}) custom-call(s32[1,32]{1,0:T(1,128)S(1)} %copy-done.2, bf16[128,1536]{1,0:T(8,128)(2,1)S(1)} %copy-done, bf16[128,1536]{1,0:T(8,128)(2,1)S(1)} %collective-permute-done.3.refs_1_, ...), custom_call_target="tpu_custom_call" | custom-call | bytes 3145856 | tf_op jit(solution)/shard_map/forward/pallas_call | solution.py:345
  73.8 0.0 collective-permute-done.16
  73.8 0.1 add_convert_fusion
  73.9 3.8 %collective-permute-start.21 = (bf16[512,256]{1,0:T(8,128)(2,1)S(1)}, bf16[512,256]{1,0:T(8,128)(2,1)S(1)}, u32[]{:S(2)}, u32[]{:S(2)}) collective-permute-start(bf16[512,256]{1,0:T(8,128)(2,1)S(1)} %add_convert_fusion), channel_id=1, source_target_pairs={{0,8},{2,10},{4,12},{6,14},{8,16},{10,18},{12,20},{14,22},{16,24},... | collective-permute-start | bytes 786440 | tf_op jit(solution)/shard_map/ppermute | solution.py:392
  77.7 0.5 collective-permute-start.17
  78.2 0.0 collective-permute-start.18
  78.2 2.5 %collective-permute-start.19 = (bf16[128,512]{1,0:T(8,128)(2,1)S(1)}, bf16[128,512]{1,0:T(8,128)(2,1)S(1)}, u32[]{:S(2)}, u32[]{:S(2)}) collective-permute-start(bf16[128,512]{1,0:T(8,128)(2,1)S(1)} %get-tuple-element.131), channel_id=1, source_target_pairs={{0,5},{1,4},{2,7},{3,6},{4,1},{5,0},{6,3},{7,2},{8,13},{9,12},{10,... | collective-permute-start | bytes 393224 | tf_op jit(solution)/shard_map/ppermute | solution.py:403
  80.7 0.0 collective-permute-done.22.refs_2_
  80.7 1.4 %collective-permute-start.20 = (bf16[128,512]{1,0:T(8,128)(2,1)S(1)}, bf16[128,512]{1,0:T(8,128)(2,1)S(1)}, u32[]{:S(2)}, u32[]{:S(2)}) collective-permute-start(bf16[128,512]{1,0:T(8,128)(2,1)S(1)} %get-tuple-element.132), channel_id=1, source_target_pairs={{0,7},{1,6},{2,5},{3,4},{4,3},{5,2},{6,1},{7,0},{8,15},{9,14},{10,... | collective-permute-start | bytes 393224 | tf_op jit(solution)/shard_map/ppermute | solution.py:403
  82.1 3.9 %collective-permute-done.21.refs_1_ = bf16[512,256]{1,0:T(8,128)(2,1)S(1)} collective-permute-done((bf16[512,256]{1,0:T(8,128)(2,1)S(1)}, bf16[512,256]{1,0:T(8,128)(2,1)S(1)}, u32[]{:S(2)}, u32[]{:S(2)}) %collective-permute-start.21) | collective-permute-done | bytes 262176 | tf_op jit(solution)/shard_map/ppermute | solution.py:392
  86.0 0.1 sum_key_parts.1
  86.1 0.1 collective-permute-start.23
  86.2 3.4 %collective-permute-done.17.refs_0_ = bf16[128,512]{1,0:T(8,128)(2,1)S(1)} collective-permute-done((bf16[128,512]{1,0:T(8,128)(2,1)S(1)}, bf16[128,512]{1,0:T(8,128)(2,1)S(1)}, u32[]{:S(2)}, u32[]{:S(2)}) %collective-permute-start.17) | collective-permute-done | bytes 131104 | tf_op jit(solution)/shard_map/ppermute | solution.py:403
  89.7 1.5 %collective-permute-start.24 = (bf16[128,256]{1,0:T(8,128)(2,1)S(1)}, bf16[128,256]{1,0:T(8,128)(2,1)S(1)}, u32[]{:S(2)}, u32[]{:S(2)}) collective-permute-start(bf16[128,256]{1,0:T(8,128)(2,1)S(1)} %get-tuple-element.144), channel_id=1, source_target_pairs={{0,4},{2,6},{4,0},{6,2},{8,12},{10,14},{12,8},{14,10},{16,20},{18,... | collective-permute-start | bytes 196616 | tf_op jit(solution)/shard_map/ppermute | solution.py:387
  91.2 0.0 collective-permute-done.18.refs_1_
  91.2 0.8 collective-permute-start.25
  92.0 0.8 query_grad.1
  92.8 0.0 collective-permute-done.19.refs_2_
  92.8 0.0 collective-permute-done.20.refs_3_
  92.8 1.2 %gate.1 = bf16[1,128,2048]{2,1,0:T(8,128)(2,1)} custom-call(bf16[128,512]{1,0:T(8,128)(2,1)S(1)} %collective-permute-done.17.refs_0_, bf16[128,512]{1,0:T(8,128)(2,1)S(1)} %collective-permute-done.18.refs_1_, bf16[128,512]{1,0:T(8,128)(2,1)S(1)} %collective-permute-done.19.refs_2_, bf16[128,512]{1,0:T(8,128)(2,1)S(1)} %collective-permute-done.20.refs_3_, ...), custom_call_target="tpu_custom_call" | custom-call | bytes 1638400 | tf_op jit(solution)/shard_map/gate/pallas_call | solution.py:345
  94.0 0.0 collective-permute-done.23.refs_1_
  94.0 0.0 collective-permute-done.24.refs_2_
  94.0 1.5 %collective-permute-done.25.refs_3_ = bf16[128,256]{1,0:T(8,128)(2,1)S(1)} collective-permute-done((bf16[128,256]{1,0:T(8,128)(2,1)S(1)}, bf16[128,256]{1,0:T(8,128)(2,1)S(1)}, u32[]{:S(2)}, u32[]{:S(2)}) %collective-permute-start.25) | collective-permute-done | bytes 65568 | tf_op jit(solution)/shard_map/ppermute | solution.py:387
  95.5 0.8 key_grad.1
  (4 shorter events, 0.0 us)
Async XLA Ops:
  3.0 7.0 %collective-permute-start = (bf16[128,512]{1,0:T(8,128)(2,1)}, bf16[128,512]{1,0:T(8,128)(2,1)S(1)}, u32[]{:S(2)}, u32[]{:S(2)}) collective-permute-start(bf16[128,512]{1,0:T(8,128)(2,1)} %get-tuple-element.77), channel_id=1, source_target_pairs={{0,2},{2,0},{4,6},{6,4},{8,10},{10,8},{12,14},{14,12},{16,18},{18,... | collective-permute-start | bytes 393224 | tf_op jit(solution)/shard_map/ppermute | solution.py:387
  3.5 7.1 %collective-permute-start.1 = (bf16[128,512]{1,0:T(8,128)(2,1)}, bf16[128,512]{1,0:T(8,128)(2,1)S(1)}, u32[]{:S(2)}, u32[]{:S(2)}) collective-permute-start(bf16[128,512]{1,0:T(8,128)(2,1)} %get-tuple-element.78), channel_id=1, source_target_pairs={{0,4},{2,6},{4,0},{6,2},{8,12},{10,14},{12,8},{14,10},{16,20},{18,... | collective-permute-start | bytes 393224 | tf_op jit(solution)/shard_map/ppermute | solution.py:387
  6.1 6.8 %copy-start.1 = (bf16[128,512]{1,0:T(8,128)(2,1)S(1)}, bf16[128,512]{1,0:T(8,128)(2,1)}, u32[]{:S(2)}) copy-start(bf16[128,512]{1,0:T(8,128)(2,1)} %get-tuple-element.89.refs_0_) | copy-start | bytes 393220
  6.1 6.8 %collective-permute-start.2 = (bf16[128,512]{1,0:T(8,128)(2,1)}, bf16[128,512]{1,0:T(8,128)(2,1)S(1)}, u32[]{:S(2)}, u32[]{:S(2)}) collective-permute-start(bf16[128,512]{1,0:T(8,128)(2,1)} %get-tuple-element.79), channel_id=1, source_target_pairs={{0,6},{2,4},{4,2},{6,0},{8,14},{10,12},{12,10},{14,8},{16,22},{18,... | collective-permute-start | bytes 393224 | tf_op jit(solution)/shard_map/ppermute | solution.py:387
  9.9 33.3 %copy-start = (bf16[128,1536]{1,0:T(8,128)(2,1)S(1)}, bf16[128,1536]{1,0:T(8,128)(2,1)}, u32[]{:S(2)}) copy-start(bf16[128,1536]{1,0:T(8,128)(2,1)} %get-tuple-element.85.refs_0_) | copy-start | bytes 1179652
  13.1 30.2 %copy-start.2 = (s32[1,32]{1,0:T(1,128)S(1)}, s32[1,32]{1,0:T(1,128)}, u32[]{:S(2)}) copy-start(s32[1,32]{1,0:T(1,128)} %order_ref.3) | copy-start | bytes 388
  13.1 11.0 %collective-permute-start.6 = (bf16[512,256]{1,0:T(8,128)(2,1)S(1)}, bf16[512,256]{1,0:T(8,128)(2,1)S(1)}, u32[]{:S(2)}, u32[]{:S(2)}) collective-permute-start(bf16[512,256]{1,0:T(8,128)(2,1)S(1)} %get-tuple-element.102.refs_4_), channel_id=1, source_target_pairs={{0,8},{2,10},{4,12},{6,14},{8,16},{10,18},{12,20},{14,22},{16,24},... | collective-permute-start | bytes 786440 | tf_op jit(solution)/shard_map/ppermute | solution.py:392
  14.8 13.8 %collective-permute-start.7 = (bf16[512,256]{1,0:T(8,128)(2,1)S(1)}, bf16[512,256]{1,0:T(8,128)(2,1)S(1)}, u32[]{:S(2)}, u32[]{:S(2)}) collective-permute-start(bf16[512,256]{1,0:T(8,128)(2,1)S(1)} %get-tuple-element.102.refs_4_), channel_id=1, source_target_pairs={{0,24},{2,26},{4,28},{6,30},{8,0},{10,2},{12,4},{14,6},{16,8},{18,... | collective-permute-start | bytes 786440 | tf_op jit(solution)/shard_map/ppermute | solution.py:392
  17.0 22.4 %collective-permute-start.3 = (bf16[128,1536]{1,0:T(8,128)(2,1)}, bf16[128,1536]{1,0:T(8,128)(2,1)S(1)}, u32[]{:S(2)}, u32[]{:S(2)}) collective-permute-start(bf16[128,1536]{1,0:T(8,128)(2,1)} %get-tuple-element.86), channel_id=1, source_target_pairs={{0,2},{2,0},{4,6},{6,4},{8,10},{10,8},{12,14},{14,12},{16,18},{18,... | collective-permute-start | bytes 1179656 | tf_op jit(solution)/shard_map/ppermute | solution.py:387
  17.0 23.3 %collective-permute-start.4 = (bf16[128,1536]{1,0:T(8,128)(2,1)}, bf16[128,1536]{1,0:T(8,128)(2,1)S(1)}, u32[]{:S(2)}, u32[]{:S(2)}) collective-permute-start(bf16[128,1536]{1,0:T(8,128)(2,1)} %get-tuple-element.87), channel_id=1, source_target_pairs={{0,4},{2,6},{4,0},{6,2},{8,12},{10,14},{12,8},{14,10},{16,20},{18,... | collective-permute-start | bytes 1179656 | tf_op jit(solution)/shard_map/ppermute | solution.py:387
  18.5 24.7 %collective-permute-start.5 = (bf16[128,1536]{1,0:T(8,128)(2,1)}, bf16[128,1536]{1,0:T(8,128)(2,1)S(1)}, u32[]{:S(2)}, u32[]{:S(2)}) collective-permute-start(bf16[128,1536]{1,0:T(8,128)(2,1)} %get-tuple-element.88), channel_id=1, source_target_pairs={{0,6},{2,4},{4,2},{6,0},{8,14},{10,12},{12,10},{14,8},{16,22},{18,... | collective-permute-start | bytes 1179656 | tf_op jit(solution)/shard_map/ppermute | solution.py:387
  28.6 28.7 %collective-permute-start.9 = (bf16[144,2048]{1,0:T(8,128)(2,1)}, bf16[144,2048]{1,0:T(8,128)(2,1)S(1)}, u32[]{:S(2)}, u32[]{:S(2)}) collective-permute-start(bf16[144,2048]{1,0:T(8,128)(2,1)} %get-tuple-element.114), channel_id=1, source_target_pairs={{0,1},{1,0},{2,3},{3,2},{4,5},{5,4},{6,7},{7,6},{8,9},{9,8},{10,11... | collective-permute-start | bytes 1769480 | tf_op jit(solution)/shard_map/ppermute | solution.py:403
  30.1 9.2 %collective-permute-start.8 = (bf16[512,256]{1,0:T(8,128)(2,1)S(1)}, bf16[512,256]{1,0:T(8,128)(2,1)S(1)}, u32[]{:S(2)}, u32[]{:S(2)}) collective-permute-start(bf16[512,256]{1,0:T(8,128)(2,1)S(1)} %collective-permute-done.6.refs_5_), channel_id=1, source_target_pairs={{0,8},{2,10},{4,12},{6,14},{8,16},{10,18},{12,20},{14,22},{16,24},... | collective-permute-start | bytes 786440 | tf_op jit(solution)/shard_map/ppermute | solution.py:392
  39.3 18.6 %collective-permute-start.13 = (bf16[512,256]{1,0:T(8,128)(2,1)S(1)}, bf16[512,256]{1,0:T(8,128)(2,1)S(1)}, u32[]{:S(2)}, u32[]{:S(2)}) collective-permute-start(bf16[512,256]{1,0:T(8,128)(2,1)S(1)} %get-tuple-element.120.refs_4_), channel_id=1, source_target_pairs={{0,8},{2,10},{4,12},{6,14},{8,16},{10,18},{12,20},{14,22},{16,24},... | collective-permute-start | bytes 786440 | tf_op jit(solution)/shard_map/ppermute | solution.py:392
  39.3 20.1 %collective-permute-start.14 = (bf16[512,256]{1,0:T(8,128)(2,1)S(1)}, bf16[512,256]{1,0:T(8,128)(2,1)S(1)}, u32[]{:S(2)}, u32[]{:S(2)}) collective-permute-start(bf16[512,256]{1,0:T(8,128)(2,1)S(1)} %get-tuple-element.120.refs_4_), channel_id=1, source_target_pairs={{0,16},{2,18},{4,20},{6,22},{8,24},{10,26},{12,28},{14,30},{16,0},... | collective-permute-start | bytes 786440 | tf_op jit(solution)/shard_map/ppermute | solution.py:392
  40.2 19.6 %collective-permute-start.15 = (bf16[512,256]{1,0:T(8,128)(2,1)S(1)}, bf16[512,256]{1,0:T(8,128)(2,1)S(1)}, u32[]{:S(2)}, u32[]{:S(2)}) collective-permute-start(bf16[512,256]{1,0:T(8,128)(2,1)S(1)} %get-tuple-element.120.refs_4_), channel_id=1, source_target_pairs={{0,24},{2,26},{4,28},{6,30},{8,0},{10,2},{12,4},{14,6},{16,8},{18,... | collective-permute-start | bytes 786440 | tf_op jit(solution)/shard_map/ppermute | solution.py:392
  57.3 16.5 %collective-permute-start.16 = (bf16[512,256]{1,0:T(8,128)(2,1)S(1)}, bf16[512,256]{1,0:T(8,128)(2,1)S(1)}, u32[]{:S(2)}, u32[]{:S(2)}) collective-permute-start(bf16[512,256]{1,0:T(8,128)(2,1)S(1)} %get-tuple-element.128), channel_id=1, source_target_pairs={{0,8},{2,10},{4,12},{6,14},{8,16},{10,18},{12,20},{14,22},{16,24},... | collective-permute-start | bytes 786440 | tf_op jit(solution)/shard_map/ppermute | solution.py:392
  57.9 8.0 %collective-permute-start.10 = (bf16[128,512]{1,0:T(8,128)(2,1)S(1)}, bf16[128,512]{1,0:T(8,128)(2,1)S(1)}, u32[]{:S(2)}, u32[]{:S(2)}) collective-permute-start(bf16[128,512]{1,0:T(8,128)(2,1)S(1)} %get-tuple-element.116), channel_id=1, source_target_pairs={{0,2},{2,0},{4,6},{6,4},{8,10},{10,8},{12,14},{14,12},{16,18},{18,... | collective-permute-start | bytes 393224 | tf_op jit(solution)/shard_map/ppermute | solution.py:387
  57.9 8.0 %collective-permute-start.11 = (bf16[128,512]{1,0:T(8,128)(2,1)S(1)}, bf16[128,512]{1,0:T(8,128)(2,1)S(1)}, u32[]{:S(2)}, u32[]{:S(2)}) collective-permute-start(bf16[128,512]{1,0:T(8,128)(2,1)S(1)} %get-tuple-element.117), channel_id=1, source_target_pairs={{0,4},{2,6},{4,0},{6,2},{8,12},{10,14},{12,8},{14,10},{16,20},{18,... | collective-permute-start | bytes 393224 | tf_op jit(solution)/shard_map/ppermute | solution.py:387
  59.4 6.8 %collective-permute-start.12 = (bf16[128,512]{1,0:T(8,128)(2,1)S(1)}, bf16[128,512]{1,0:T(8,128)(2,1)S(1)}, u32[]{:S(2)}, u32[]{:S(2)}) collective-permute-start(bf16[128,512]{1,0:T(8,128)(2,1)S(1)} %get-tuple-element.118), channel_id=1, source_target_pairs={{0,6},{2,4},{4,2},{6,0},{8,14},{10,12},{12,10},{14,8},{16,22},{18,... | collective-permute-start | bytes 393224 | tf_op jit(solution)/shard_map/ppermute | solution.py:387
  59.8 20.9 %collective-permute-start.22 = (bf16[512,256]{1,0:T(8,128)(2,1)S(1)}, bf16[512,256]{1,0:T(8,128)(2,1)S(1)}, u32[]{:S(2)}, u32[]{:S(2)}) collective-permute-start(bf16[512,256]{1,0:T(8,128)(2,1)S(1)} %get-tuple-element.141), channel_id=1, source_target_pairs={{0,24},{2,26},{4,28},{6,30},{8,0},{10,2},{12,4},{14,6},{16,8},{18,... | collective-permute-start | bytes 786440 | tf_op jit(solution)/shard_map/ppermute | solution.py:392
  73.9 12.1 %collective-permute-start.21 = (bf16[512,256]{1,0:T(8,128)(2,1)S(1)}, bf16[512,256]{1,0:T(8,128)(2,1)S(1)}, u32[]{:S(2)}, u32[]{:S(2)}) collective-permute-start(bf16[512,256]{1,0:T(8,128)(2,1)S(1)} %add_convert_fusion), channel_id=1, source_target_pairs={{0,8},{2,10},{4,12},{6,14},{8,16},{10,18},{12,20},{14,22},{16,24},... | collective-permute-start | bytes 786440 | tf_op jit(solution)/shard_map/ppermute | solution.py:392
  77.7 11.9 %collective-permute-start.17 = (bf16[128,512]{1,0:T(8,128)(2,1)S(1)}, bf16[128,512]{1,0:T(8,128)(2,1)S(1)}, u32[]{:S(2)}, u32[]{:S(2)}) collective-permute-start(bf16[128,512]{1,0:T(8,128)(2,1)S(1)} %get-tuple-element.129), channel_id=1, source_target_pairs={{0,1},{1,0},{2,3},{3,2},{4,5},{5,4},{6,7},{7,6},{8,9},{9,8},{10,11... | collective-permute-start | bytes 393224 | tf_op jit(solution)/shard_map/ppermute | solution.py:403
  78.2 12.9 %collective-permute-start.18 = (bf16[128,512]{1,0:T(8,128)(2,1)S(1)}, bf16[128,512]{1,0:T(8,128)(2,1)S(1)}, u32[]{:S(2)}, u32[]{:S(2)}) collective-permute-start(bf16[128,512]{1,0:T(8,128)(2,1)S(1)} %get-tuple-element.130), channel_id=1, source_target_pairs={{0,3},{1,2},{2,1},{3,0},{4,7},{5,6},{6,5},{7,4},{8,11},{9,10},{10,... | collective-permute-start | bytes 393224 | tf_op jit(solution)/shard_map/ppermute | solution.py:403
  78.2 14.6 %collective-permute-start.19 = (bf16[128,512]{1,0:T(8,128)(2,1)S(1)}, bf16[128,512]{1,0:T(8,128)(2,1)S(1)}, u32[]{:S(2)}, u32[]{:S(2)}) collective-permute-start(bf16[128,512]{1,0:T(8,128)(2,1)S(1)} %get-tuple-element.131), channel_id=1, source_target_pairs={{0,5},{1,4},{2,7},{3,6},{4,1},{5,0},{6,3},{7,2},{8,13},{9,12},{10,... | collective-permute-start | bytes 393224 | tf_op jit(solution)/shard_map/ppermute | solution.py:403
  80.7 12.1 %collective-permute-start.20 = (bf16[128,512]{1,0:T(8,128)(2,1)S(1)}, bf16[128,512]{1,0:T(8,128)(2,1)S(1)}, u32[]{:S(2)}, u32[]{:S(2)}) collective-permute-start(bf16[128,512]{1,0:T(8,128)(2,1)S(1)} %get-tuple-element.132), channel_id=1, source_target_pairs={{0,7},{1,6},{2,5},{3,4},{4,3},{5,2},{6,1},{7,0},{8,15},{9,14},{10,... | collective-permute-start | bytes 393224 | tf_op jit(solution)/shard_map/ppermute | solution.py:403
  86.1 7.9 %collective-permute-start.23 = (bf16[128,256]{1,0:T(8,128)(2,1)S(1)}, bf16[128,256]{1,0:T(8,128)(2,1)S(1)}, u32[]{:S(2)}, u32[]{:S(2)}) collective-permute-start(bf16[128,256]{1,0:T(8,128)(2,1)S(1)} %get-tuple-element.143), channel_id=1, source_target_pairs={{0,2},{2,0},{4,6},{6,4},{8,10},{10,8},{12,14},{14,12},{16,18},{18,... | collective-permute-start | bytes 196616 | tf_op jit(solution)/shard_map/ppermute | solution.py:387
  89.7 4.3 %collective-permute-start.24 = (bf16[128,256]{1,0:T(8,128)(2,1)S(1)}, bf16[128,256]{1,0:T(8,128)(2,1)S(1)}, u32[]{:S(2)}, u32[]{:S(2)}) collective-permute-start(bf16[128,256]{1,0:T(8,128)(2,1)S(1)} %get-tuple-element.144), channel_id=1, source_target_pairs={{0,4},{2,6},{4,0},{6,2},{8,12},{10,14},{12,8},{14,10},{16,20},{18,... | collective-permute-start | bytes 196616 | tf_op jit(solution)/shard_map/ppermute | solution.py:387
  91.2 4.3 %collective-permute-start.25 = (bf16[128,256]{1,0:T(8,128)(2,1)S(1)}, bf16[128,256]{1,0:T(8,128)(2,1)S(1)}, u32[]{:S(2)}, u32[]{:S(2)}) collective-permute-start(bf16[128,256]{1,0:T(8,128)(2,1)S(1)} %get-tuple-element.145), channel_id=1, source_target_pairs={{0,6},{2,4},{4,2},{6,0},{8,14},{10,12},{12,10},{14,8},{16,22},{18,... | collective-permute-start | bytes 196616 | tf_op jit(solution)/shard_map/ppermute | solution.py:387

commit v3 on v2

--- a/solution.py
+++ b/solution.py
@@ -299,7 +299,7 @@
 
 
 def sum_kernel(*refs):
-    parts, pieces = refs[:3], refs[3:]
+    parts, pieces = refs[:-QUAD], refs[-QUAD:]
     rows = pieces[0].shape[0]
     for d in range(QUAD):
         lower = d * rows
@@ -402,37 +402,8 @@
         ]
         return lax.ppermute(block, ("ctx", "pipe"), route)
 
-    ahead = nz // 2
-
-    def ring_up(block):
-        return turn(block, 1)
-
-    def ring_down(block):
-        return turn(block, nz - 1)
-
-    def gather_first(stack):
-        return [stack, ring_up(stack)], [ring_down(stack)]
-
-    def gather_rest(up, down):
-        up, down = lax.optimization_barrier((up, down))
-        while len(up) <= ahead:
-            up = up + [ring_up(up[-1])]
-        while len(up) + len(down) < nz:
-            down = down + [ring_down(down[-1])]
-        return up + down[::-1]
-
-    def reduce_first(parts):
-        return ring_up(parts[ahead]), ring_down(parts[ahead + 1])
-
-    def add(a, b):
-        return (a.astype(jnp.float32) + b.astype(jnp.float32)).astype(jnp.bfloat16)
-
-    def reduce_rest(parts, up, down):
-        for s in range(ahead - 1, 0, -1):
-            up = ring_up(add(up, parts[s]))
-        for s in range(ahead + 2, nz):
-            down = ring_down(add(down, parts[s]))
-        return parts[0], up, down
+    def gather(stack):
+        return [stack] + [turn(stack, s) for s in range(1, nz)]
 
     pieces = swap(
         call(
@@ -471,7 +442,7 @@
         scratch=[pltpu.SemaphoreType.DMA((3 * QUAD + 1,))],
         vmem=60,
     )
-    pieces, packed = lax.optimization_barrier((pieces, packed))
+    pieces, packed = lax.optimization_barrier((pieces, list(packed)))
     back_stack, stack = call(
         stack_keys,
         "stack_keys",
@@ -480,13 +451,12 @@
         *pieces,
         scratch=[pltpu.SemaphoreType.DMA((2 * QUAD,))],
     )
+    back_stacks = gather(back_stack)
+    back_stacks, packed[1] = lax.optimization_barrier((back_stacks, packed[1]))
     queries = swap(packed[:QUAD])
-    up, down = gather_first(back_stack)
-    up, down, gate_before = lax.optimization_barrier((up, down, packed[QUAD]))
-    back_stacks = gather_rest(up, down)
-    gate_before = hand(gate_before, 0)
+    gate_before = hand(packed[QUAD], 0)
     stack, back_stacks = lax.optimization_barrier((stack, back_stacks))
-    stacks = [stack] + [turn(stack, s) for s in range(1, nz)]
+    stacks = gather(stack)
 
     sequence = [pltpu.VMEM((total_rows, HEAD), jnp.bfloat16)] * 2
     stacked = pltpu.VMEM((2 * QUAD, block_rows, HEAD), jnp.bfloat16)
@@ -516,9 +486,8 @@
     query_pieces, key_parts, gate_before = lax.optimization_barrier(
         (query_pieces, key_parts, gate_before)
     )
-    key_sums = reduce_first(key_parts)
+    key_parts = [key_parts[0]] + [turn(key_parts[s], s) for s in range(1, nz)]
     query_pieces = swap(query_pieces)
-    query_pieces, stacks = lax.optimization_barrier((query_pieces, stacks))
     attended = call(
         functools.partial(forward_kernel, nz),
         "forward",
@@ -530,7 +499,7 @@
         scratch=sequence
         + [stacked, pltpu.VMEM((2 * QUAD, block_rows, HEAD), jnp.float32), gap],
     )
-    attended, key_up = lax.optimization_barrier((attended, key_sums[0]))
+    attended, query_pieces = lax.optimization_barrier((attended, query_pieces))
     (handed,) = call(
         gate_kernel,
         "gate",
@@ -539,14 +508,13 @@
         *[hand(attended[d], d) for d in range(QUAD)],
         gate_before,
     )
-    key_sums = reduce_rest(key_parts, key_up, key_sums[1])
     key_pieces = swap(
         call(
             sum_kernel,
             "sum_key_parts",
             [bf16(rows, 2 * HEAD)] * QUAD,
-            [VMEM] * 3,
-            *key_sums,
+            [VMEM] * nz,
+            *key_parts,
         )
     )
     (query_grad,) = call(

time: 96.4 us -> 103 us (1.068)
  the two profiles are of different devices: /device:TPU:0 before, /device:TPU:19 now
where the time goes in v3:
time: 103 us
  waiting for transfers between devices  36.4 us (35%)
  starting transfers between devices  35.2 us (34%)
  Pallas kernels  30.8 us (30%)
    pallas_call x9, Pallas kernels, call(): pl.pallas_call(kernel, name=name, out_shape=out_shape, in_specs=specs, ou...  30.8 us
    ppermute x9, waiting for transfers between devices, turn(): lax.ppermute(block, 'ctx', [(i, (i + s * QUAD) % devices) for i in range(...  22.6 us
    ppermute x12, starting transfers between devices, swap(): lax.ppermute(pieces[d], 'ctx', [(i, i ^ d) for i in range(devices)])  17.7 us
    ppermute x9, starting transfers between devices, turn(): lax.ppermute(block, 'ctx', [(i, (i + s * QUAD) % devices) for i in range(...  11.7 us
    ppermute x5, waiting for transfers between devices, hand(): return lax.ppermute(block, ('ctx', 'pipe'), route)  8.84 us
    ppermute x5, starting transfers between devices, hand(): return lax.ppermute(block, ('ctx', 'pipe'), route)  5.7 us
    ppermute x12, waiting for transfers between devices, swap(): lax.ppermute(pieces[d], 'ctx', [(i, i ^ d) for i in range(devices)])  4.92 us
  transfers between devices with their start and end apart: 26, of which 9 were waited for; matrix products, arithmetic and copies ran while one was open for 0% of the time, Pallas kernels for 27%

profile of v3, /device:TPU:19, one launch (start us, length us, event | category | flops | bytes accessed | tf_op | source)
XLA Modules:
  0.0 103.2 jit_solution(12707607991131511377)
XLA Ops:
  0.6 2.4 %pack_keys.1 = (bf16[128,512]{1,0:T(8,128)(2,1)}, bf16[128,512]{1,0:T(8,128)(2,1)}, bf16[128,512]{1,0:T(8,128)(2,1)}, bf16[128,512]{1,0:T(8,128)(2,1)}) custom-call(bf16[1,128,512]{2,1,0:T(8,128)(2,1)} %back_key.1, bf16[1,128,512]{2,1,0:T(8,128)(2,1)} %back_value.1, s32[1,128]{1,0:T(1,128)} %back_types.1, bf16[1,128,512]{2,1,0:T(8,128)(2,1)} %key.1, ...), custom_call_target="tpu_custom_call" | custom-call | bytes 1115136 | tf_op jit(solution)/shard_map/pack_keys/pallas_call | solution.py:345
  3.0 0.7 collective-permute-start
  3.7 0.3 collective-permute-start.1
  4.0 1.4 %collective-permute-start.2 = (bf16[128,512]{1,0:T(8,128)(2,1)}, bf16[128,512]{1,0:T(8,128)(2,1)S(1)}, u32[]{:S(2)}, u32[]{:S(2)}) collective-permute-start(bf16[128,512]{1,0:T(8,128)(2,1)} %get-tuple-element.72), channel_id=1, source_target_pairs={{0,6},{2,4},{4,2},{6,0},{8,14},{10,12},{12,10},{14,8},{16,22},{18,... | collective-permute-start | bytes 393224 | tf_op jit(solution)/shard_map/ppermute | solution.py:387
  5.5 3.8 %pack_queries.1 = (bf16[128,1536]{1,0:T(8,128)(2,1)}, bf16[128,1536]{1,0:T(8,128)(2,1)}, bf16[128,1536]{1,0:T(8,128)(2,1)}, bf16[128,1536]{1,0:T(8,128)(2,1)}, bf16[144,2048]{1,0:T(8,128)(2,1)}) custom-call(bf16[1,128,2048]{2,1,0:T(8,128)(2,1)} %query_ref.1, bf16[1,128,2048]{2,1,0:T(8,128)(2,1)} %grad_ref.1, bf16[1,128,2048]{2,1,0:T(8,128)(2,1)} %forward_ref.1, ...), custom_call_target="tpu_custom_call" | custom-call | bytes 4268032 | tf_op jit(solution)/shard_map/pack_queries/pallas_call | solution.py:345
  9.2 0.0 copy-start
  9.3 0.0 collective-permute-done.refs_1_
  9.3 0.0 collective-permute-done.1.refs_2_
  9.3 2.7 %collective-permute-done.2.refs_3_ = bf16[128,512]{1,0:T(8,128)(2,1)S(1)} collective-permute-done((bf16[128,512]{1,0:T(8,128)(2,1)}, bf16[128,512]{1,0:T(8,128)(2,1)S(1)}, u32[]{:S(2)}, u32[]{:S(2)}) %collective-permute-start.2) | collective-permute-done | bytes 131104 | tf_op jit(solution)/shard_map/ppermute | solution.py:387
  12.0 0.0 copy-done.1
  12.0 0.1 stack_keys.1
  12.1 0.0 copy-start.2
  12.2 1.3 %collective-permute-start.3 = (bf16[512,256]{1,0:T(8,128)(2,1)S(1)}, bf16[512,256]{1,0:T(8,128)(2,1)S(1)}, u32[]{:S(2)}, u32[]{:S(2)}) collective-permute-start(bf16[512,256]{1,0:T(8,128)(2,1)S(1)} %get-tuple-element.98.refs_4_), channel_id=1, source_target_pairs={{0,8},{2,10},{4,12},{6,14},{8,16},{10,18},{12,20},{14,22},{16,24},... | collective-permute-start | bytes 786440 | tf_op jit(solution)/shard_map/ppermute | solution.py:392
  13.5 0.1 collective-permute-start.4
  13.6 1.2 %collective-permute-start.5 = (bf16[512,256]{1,0:T(8,128)(2,1)S(1)}, bf16[512,256]{1,0:T(8,128)(2,1)S(1)}, u32[]{:S(2)}, u32[]{:S(2)}) collective-permute-start(bf16[512,256]{1,0:T(8,128)(2,1)S(1)} %get-tuple-element.98.refs_4_), channel_id=1, source_target_pairs={{0,24},{2,26},{4,28},{6,30},{8,0},{10,2},{12,4},{14,6},{16,8},{18,... | collective-permute-start | bytes 786440 | tf_op jit(solution)/shard_map/ppermute | solution.py:392
  14.8 0.2 collective-permute-start.7
  15.0 2.3 %collective-permute-start.8 = (bf16[128,1536]{1,0:T(8,128)(2,1)}, bf16[128,1536]{1,0:T(8,128)(2,1)S(1)}, u32[]{:S(2)}, u32[]{:S(2)}) collective-permute-start(bf16[128,1536]{1,0:T(8,128)(2,1)} %get-tuple-element.87), channel_id=1, source_target_pairs={{0,6},{2,4},{4,2},{6,0},{8,14},{10,12},{12,10},{14,8},{16,22},{18,... | collective-permute-start | bytes 1179656 | tf_op jit(solution)/shard_map/ppermute | solution.py:387
  17.3 2.7 %collective-permute-done.3.refs_5_ = bf16[512,256]{1,0:T(8,128)(2,1)S(1)} collective-permute-done((bf16[512,256]{1,0:T(8,128)(2,1)S(1)}, bf16[512,256]{1,0:T(8,128)(2,1)S(1)}, u32[]{:S(2)}, u32[]{:S(2)}) %collective-permute-start.3) | collective-permute-done | bytes 262176 | tf_op jit(solution)/shard_map/ppermute | solution.py:392
  20.0 10.6 %collective-permute-done.4.refs_6_ = bf16[512,256]{1,0:T(8,128)(2,1)S(1)} collective-permute-done((bf16[512,256]{1,0:T(8,128)(2,1)S(1)}, bf16[512,256]{1,0:T(8,128)(2,1)S(1)}, u32[]{:S(2)}, u32[]{:S(2)}) %collective-permute-start.4) | collective-permute-done | bytes 262176 | tf_op jit(solution)/shard_map/ppermute | solution.py:392
  30.5 5.6 %collective-permute-done.5.refs_7_ = bf16[512,256]{1,0:T(8,128)(2,1)S(1)} collective-permute-done((bf16[512,256]{1,0:T(8,128)(2,1)S(1)}, bf16[512,256]{1,0:T(8,128)(2,1)S(1)}, u32[]{:S(2)}, u32[]{:S(2)}) %collective-permute-start.5) | collective-permute-done | bytes 262176 | tf_op jit(solution)/shard_map/ppermute | solution.py:392
  36.2 0.5 collective-permute-start.6
  36.6 1.2 %collective-permute-start.12 = (bf16[144,2048]{1,0:T(8,128)(2,1)}, bf16[144,2048]{1,0:T(8,128)(2,1)S(1)}, u32[]{:S(2)}, u32[]{:S(2)}) collective-permute-start(bf16[144,2048]{1,0:T(8,128)(2,1)} %get-tuple-element.110), channel_id=1, source_target_pairs={{0,1},{1,0},{2,3},{3,2},{4,5},{5,4},{6,7},{7,6},{8,9},{9,8},{10,11... | collective-permute-start | bytes 1769480 | tf_op jit(solution)/shard_map/ppermute | solution.py:403
  37.9 0.0 collective-permute-start.10
  37.9 0.0 collective-permute-done.7.refs_2_
  37.9 3.5 %collective-permute-start.11 = (bf16[512,256]{1,0:T(8,128)(2,1)S(1)}, bf16[512,256]{1,0:T(8,128)(2,1)S(1)}, u32[]{:S(2)}, u32[]{:S(2)}) collective-permute-start(bf16[512,256]{1,0:T(8,128)(2,1)S(1)} %get-tuple-element.93.refs_4_), channel_id=1, source_target_pairs={{0,24},{2,26},{4,28},{6,30},{8,0},{10,2},{12,4},{14,6},{16,8},{18,... | collective-permute-start | bytes 786440 | tf_op jit(solution)/shard_map/ppermute | solution.py:392
  41.4 0.0 collective-permute-done.8.refs_3_
  41.4 0.0 collective-permute-start.9
  41.4 0.0 collective-permute-done.6.refs_1_
  41.4 14.1 %backward.1 = (bf16[128,512]{1,0:T(8,128)(2,1)S(1)}, bf16[128,512]{1,0:T(8,128)(2,1)S(1)}, bf16[128,512]{1,0:T(8,128)(2,1)S(1)}, bf16[128,512]{1,0:T(8,128)(2,1)...) custom-call(s32[1,32]{1,0:T(1,128)S(1)} %copy-done.2, ...), custom_call_target="tpu_custom_call" | custom-call | flops 3019898880 | bytes 4194432 | tf_op jit(solution)/shard_map/backward/pallas_call | solution.py:345
  55.5 0.0 collective-permute-done.12.refs_4_
  55.5 0.9 collective-permute-start.13
  56.4 3.4 %collective-permute-start.20 = (bf16[512,256]{1,0:T(8,128)(2,1)S(1)}, bf16[512,256]{1,0:T(8,128)(2,1)S(1)}, u32[]{:S(2)}, u32[]{:S(2)}) collective-permute-start(bf16[512,256]{1,0:T(8,128)(2,1)S(1)} %get-tuple-element.125), channel_id=1, source_target_pairs={{0,8},{2,10},{4,12},{6,14},{8,16},{10,18},{12,20},{14,22},{16,24},... | collective-permute-start | bytes 786440 | tf_op jit(solution)/shard_map/ppermute | solution.py:392
  59.9 0.0 collective-permute-done.10.refs_6_
  59.9 0.0 collective-permute-start.21
  59.9 0.5 collective-permute-done.11.refs_7_
  60.3 0.2 collective-permute-start.14
  60.6 3.4 %collective-permute-done.9.refs_5_ = bf16[512,256]{1,0:T(8,128)(2,1)S(1)} collective-permute-done((bf16[512,256]{1,0:T(8,128)(2,1)S(1)}, bf16[512,256]{1,0:T(8,128)(2,1)S(1)}, u32[]{:S(2)}, u32[]{:S(2)}) %collective-permute-start.9) | collective-permute-done | bytes 262176 | tf_op jit(solution)/shard_map/ppermute | solution.py:392
  63.9 10.6 %collective-permute-start.15 = (bf16[128,512]{1,0:T(8,128)(2,1)S(1)}, bf16[128,512]{1,0:T(8,128)(2,1)S(1)}, u32[]{:S(2)}, u32[]{:S(2)}) collective-permute-start(bf16[128,512]{1,0:T(8,128)(2,1)S(1)} %get-tuple-element.114), channel_id=1, source_target_pairs={{0,6},{2,4},{4,2},{6,0},{8,14},{10,12},{12,10},{14,8},{16,22},{18,... | collective-permute-start | bytes 393224 | tf_op jit(solution)/shard_map/ppermute | solution.py:387
  74.5 0.0 collective-permute-done.13.refs_1_
  74.5 2.2 %collective-permute-start.22 = (bf16[512,256]{1,0:T(8,128)(2,1)S(1)}, bf16[512,256]{1,0:T(8,128)(2,1)S(1)}, u32[]{:S(2)}, u32[]{:S(2)}) collective-permute-start(bf16[512,256]{1,0:T(8,128)(2,1)S(1)} %get-tuple-element.127), channel_id=1, source_target_pairs={{0,24},{2,26},{4,28},{6,30},{8,0},{10,2},{12,4},{14,6},{16,8},{18,... | collective-permute-start | bytes 786440 | tf_op jit(solution)/shard_map/ppermute | solution.py:392
  76.7 7.6 %forward.1 = (bf16[128,512]{1,0:T(8,128)(2,1)S(1)}, bf16[128,512]{1,0:T(8,128)(2,1)S(1)}, bf16[128,512]{1,0:T(8,128)(2,1)S(1)}, bf16[128,512]{1,0:T(8,128)(2,1)S(1)}) custom-call(s32[1,32]{1,0:T(1,128)S(1)} %copy-done.2, bf16[128,1536]{1,0:T(8,128)(2,1)S(1)} %copy-done, bf16[128,1536]{1,0:T(8,128)(2,1)S(1)} %collective-permute-done.6.refs_1_, ...), custom_call_target="tpu_custom_call" | custom-call | bytes 3145856 | tf_op jit(solution)/shard_map/forward/pallas_call | solution.py:345
  84.3 0.0 collective-permute-done.14.refs_2_
  84.3 0.0 collective-permute-done.15.refs_3_
  84.3 0.3 collective-permute-start.16
  84.6 0.7 collective-permute-start.17
  85.3 0.0 collective-permute-done.20.refs_1_
  85.3 1.1 %collective-permute-start.18 = (bf16[128,512]{1,0:T(8,128)(2,1)S(1)}, bf16[128,512]{1,0:T(8,128)(2,1)S(1)}, u32[]{:S(2)}, u32[]{:S(2)}) collective-permute-start(bf16[128,512]{1,0:T(8,128)(2,1)S(1)} %get-tuple-element.117), channel_id=1, source_target_pairs={{0,5},{1,4},{2,7},{3,6},{4,1},{5,0},{6,3},{7,2},{8,13},{9,12},{10,... | collective-permute-start | bytes 393224 | tf_op jit(solution)/shard_map/ppermute | solution.py:403
  86.4 0.0 collective-permute-done.21.refs_2_
  86.4 2.4 %collective-permute-start.19 = (bf16[128,512]{1,0:T(8,128)(2,1)S(1)}, bf16[128,512]{1,0:T(8,128)(2,1)S(1)}, u32[]{:S(2)}, u32[]{:S(2)}) collective-permute-start(bf16[128,512]{1,0:T(8,128)(2,1)S(1)} %get-tuple-element.118), channel_id=1, source_target_pairs={{0,7},{1,6},{2,5},{3,4},{4,3},{5,2},{6,1},{7,0},{8,15},{9,14},{10,... | collective-permute-start | bytes 393224 | tf_op jit(solution)/shard_map/ppermute | solution.py:403
  88.8 0.0 collective-permute-done.22.refs_3_
  88.8 0.1 sum_key_parts.1
  88.9 0.1 collective-permute-start.23
  89.0 6.2 %collective-permute-done.16.refs_0_ = bf16[128,512]{1,0:T(8,128)(2,1)S(1)} collective-permute-done((bf16[128,512]{1,0:T(8,128)(2,1)S(1)}, bf16[128,512]{1,0:T(8,128)(2,1)S(1)}, u32[]{:S(2)}, u32[]{:S(2)}) %collective-permute-start.16) | collective-permute-done | bytes 131104 | tf_op jit(solution)/shard_map/ppermute | solution.py:403
  95.2 0.0 collective-permute-start.24
  95.2 2.6 %collective-permute-done.17.refs_1_ = bf16[128,512]{1,0:T(8,128)(2,1)S(1)} collective-permute-done((bf16[128,512]{1,0:T(8,128)(2,1)S(1)}, bf16[128,512]{1,0:T(8,128)(2,1)S(1)}, u32[]{:S(2)}, u32[]{:S(2)}) %collective-permute-start.17) | collective-permute-done | bytes 131104 | tf_op jit(solution)/shard_map/ppermute | solution.py:403
  97.9 0.4 collective-permute-start.25
  98.3 0.8 query_grad.1
  99.1 0.0 collective-permute-done.18.refs_2_
  99.1 0.0 collective-permute-done.19.refs_3_
  99.1 1.2 %gate.1 = bf16[1,128,2048]{2,1,0:T(8,128)(2,1)} custom-call(bf16[128,512]{1,0:T(8,128)(2,1)S(1)} %collective-permute-done.16.refs_0_, bf16[128,512]{1,0:T(8,128)(2,1)S(1)} %collective-permute-done.17.refs_1_, bf16[128,512]{1,0:T(8,128)(2,1)S(1)} %collective-permute-done.18.refs_2_, bf16[128,512]{1,0:T(8,128)(2,1)S(1)} %collective-permute-done.19.refs_3_, ...), custom_call_target="tpu_custom_call" | custom-call | bytes 1638400 | tf_op jit(solution)/shard_map/gate/pallas_call | solution.py:345
  100.3 0.0 collective-permute-done.23.refs_1_
  100.3 0.0 collective-permute-done.24.refs_2_
  100.3 2.2 %collective-permute-done.25.refs_3_ = bf16[128,256]{1,0:T(8,128)(2,1)S(1)} collective-permute-done((bf16[128,256]{1,0:T(8,128)(2,1)S(1)}, bf16[128,256]{1,0:T(8,128)(2,1)S(1)}, u32[]{:S(2)}, u32[]{:S(2)}) %collective-permute-start.25) | collective-permute-done | bytes 65568 | tf_op jit(solution)/shard_map/ppermute | solution.py:387
  102.5 0.8 key_grad.1
  (3 shorter events, 0.0 us)
Async XLA Ops:
  3.0 6.3 %collective-permute-start = (bf16[128,512]{1,0:T(8,128)(2,1)}, bf16[128,512]{1,0:T(8,128)(2,1)S(1)}, u32[]{:S(2)}, u32[]{:S(2)}) collective-permute-start(bf16[128,512]{1,0:T(8,128)(2,1)} %get-tuple-element.70), channel_id=1, source_target_pairs={{0,2},{2,0},{4,6},{6,4},{8,10},{10,8},{12,14},{14,12},{16,18},{18,... | collective-permute-start | bytes 393224 | tf_op jit(solution)/shard_map/ppermute | solution.py:387
  3.7 5.5 %collective-permute-start.1 = (bf16[128,512]{1,0:T(8,128)(2,1)}, bf16[128,512]{1,0:T(8,128)(2,1)S(1)}, u32[]{:S(2)}, u32[]{:S(2)}) collective-permute-start(bf16[128,512]{1,0:T(8,128)(2,1)} %get-tuple-element.71), channel_id=1, source_target_pairs={{0,4},{2,6},{4,0},{6,2},{8,12},{10,14},{12,8},{14,10},{16,20},{18,... | collective-permute-start | bytes 393224 | tf_op jit(solution)/shard_map/ppermute | solution.py:387
  4.0 8.0 %copy-start.1 = (bf16[128,512]{1,0:T(8,128)(2,1)S(1)}, bf16[128,512]{1,0:T(8,128)(2,1)}, u32[]{:S(2)}) copy-start(bf16[128,512]{1,0:T(8,128)(2,1)} %get-tuple-element.79.refs_0_) | copy-start | bytes 393220
  4.0 8.0 %collective-permute-start.2 = (bf16[128,512]{1,0:T(8,128)(2,1)}, bf16[128,512]{1,0:T(8,128)(2,1)S(1)}, u32[]{:S(2)}, u32[]{:S(2)}) collective-permute-start(bf16[128,512]{1,0:T(8,128)(2,1)} %get-tuple-element.72), channel_id=1, source_target_pairs={{0,6},{2,4},{4,2},{6,0},{8,14},{10,12},{12,10},{14,8},{16,22},{18,... | collective-permute-start | bytes 393224 | tf_op jit(solution)/shard_map/ppermute | solution.py:387
  9.2 32.2 %copy-start = (bf16[128,1536]{1,0:T(8,128)(2,1)S(1)}, bf16[128,1536]{1,0:T(8,128)(2,1)}, u32[]{:S(2)}) copy-start(bf16[128,1536]{1,0:T(8,128)(2,1)} %get-tuple-element.78.refs_0_) | copy-start | bytes 1179652
  12.1 29.3 %copy-start.2 = (s32[1,32]{1,0:T(1,128)S(1)}, s32[1,32]{1,0:T(1,128)}, u32[]{:S(2)}) copy-start(s32[1,32]{1,0:T(1,128)} %order_ref.3) | copy-start | bytes 388
  12.2 7.8 %collective-permute-start.3 = (bf16[512,256]{1,0:T(8,128)(2,1)S(1)}, bf16[512,256]{1,0:T(8,128)(2,1)S(1)}, u32[]{:S(2)}, u32[]{:S(2)}) collective-permute-start(bf16[512,256]{1,0:T(8,128)(2,1)S(1)} %get-tuple-element.98.refs_4_), channel_id=1, source_target_pairs={{0,8},{2,10},{4,12},{6,14},{8,16},{10,18},{12,20},{14,22},{16,24},... | collective-permute-start | bytes 786440 | tf_op jit(solution)/shard_map/ppermute | solution.py:392
  13.5 17.0 %collective-permute-start.4 = (bf16[512,256]{1,0:T(8,128)(2,1)S(1)}, bf16[512,256]{1,0:T(8,128)(2,1)S(1)}, u32[]{:S(2)}, u32[]{:S(2)}) collective-permute-start(bf16[512,256]{1,0:T(8,128)(2,1)S(1)} %get-tuple-element.98.refs_4_), channel_id=1, source_target_pairs={{0,16},{2,18},{4,20},{6,22},{8,24},{10,26},{12,28},{14,30},{16,0},... | collective-permute-start | bytes 786440 | tf_op jit(solution)/shard_map/ppermute | solution.py:392
  13.6 22.6 %collective-permute-start.5 = (bf16[512,256]{1,0:T(8,128)(2,1)S(1)}, bf16[512,256]{1,0:T(8,128)(2,1)S(1)}, u32[]{:S(2)}, u32[]{:S(2)}) collective-permute-start(bf16[512,256]{1,0:T(8,128)(2,1)S(1)} %get-tuple-element.98.refs_4_), channel_id=1, source_target_pairs={{0,24},{2,26},{4,28},{6,30},{8,0},{10,2},{12,4},{14,6},{16,8},{18,... | collective-permute-start | bytes 786440 | tf_op jit(solution)/shard_map/ppermute | solution.py:392
  14.8 23.1 %collective-permute-start.7 = (bf16[128,1536]{1,0:T(8,128)(2,1)}, bf16[128,1536]{1,0:T(8,128)(2,1)S(1)}, u32[]{:S(2)}, u32[]{:S(2)}) collective-permute-start(bf16[128,1536]{1,0:T(8,128)(2,1)} %get-tuple-element.86), channel_id=1, source_target_pairs={{0,4},{2,6},{4,0},{6,2},{8,12},{10,14},{12,8},{14,10},{16,20},{18,... | collective-permute-start | bytes 1179656 | tf_op jit(solution)/shard_map/ppermute | solution.py:387
  15.0 26.4 %collective-permute-start.8 = (bf16[128,1536]{1,0:T(8,128)(2,1)}, bf16[128,1536]{1,0:T(8,128)(2,1)S(1)}, u32[]{:S(2)}, u32[]{:S(2)}) collective-permute-start(bf16[128,1536]{1,0:T(8,128)(2,1)} %get-tuple-element.87), channel_id=1, source_target_pairs={{0,6},{2,4},{4,2},{6,0},{8,14},{10,12},{12,10},{14,8},{16,22},{18,... | collective-permute-start | bytes 1179656 | tf_op jit(solution)/shard_map/ppermute | solution.py:387
  36.2 5.2 %collective-permute-start.6 = (bf16[128,1536]{1,0:T(8,128)(2,1)}, bf16[128,1536]{1,0:T(8,128)(2,1)S(1)}, u32[]{:S(2)}, u32[]{:S(2)}) collective-permute-start(bf16[128,1536]{1,0:T(8,128)(2,1)} %get-tuple-element.85), channel_id=1, source_target_pairs={{0,2},{2,0},{4,6},{6,4},{8,10},{10,8},{12,14},{14,12},{16,18},{18,... | collective-permute-start | bytes 1179656 | tf_op jit(solution)/shard_map/ppermute | solution.py:387
  36.6 18.9 %collective-permute-start.12 = (bf16[144,2048]{1,0:T(8,128)(2,1)}, bf16[144,2048]{1,0:T(8,128)(2,1)S(1)}, u32[]{:S(2)}, u32[]{:S(2)}) collective-permute-start(bf16[144,2048]{1,0:T(8,128)(2,1)} %get-tuple-element.110), channel_id=1, source_target_pairs={{0,1},{1,0},{2,3},{3,2},{4,5},{5,4},{6,7},{7,6},{8,9},{9,8},{10,11... | collective-permute-start | bytes 1769480 | tf_op jit(solution)/shard_map/ppermute | solution.py:403
  37.9 22.0 %collective-permute-start.10 = (bf16[512,256]{1,0:T(8,128)(2,1)S(1)}, bf16[512,256]{1,0:T(8,128)(2,1)S(1)}, u32[]{:S(2)}, u32[]{:S(2)}) collective-permute-start(bf16[512,256]{1,0:T(8,128)(2,1)S(1)} %get-tuple-element.93.refs_4_), channel_id=1, source_target_pairs={{0,16},{2,18},{4,20},{6,22},{8,24},{10,26},{12,28},{14,30},{16,0},... | collective-permute-start | bytes 786440 | tf_op jit(solution)/shard_map/ppermute | solution.py:392
  37.9 22.4 %collective-permute-start.11 = (bf16[512,256]{1,0:T(8,128)(2,1)S(1)}, bf16[512,256]{1,0:T(8,128)(2,1)S(1)}, u32[]{:S(2)}, u32[]{:S(2)}) collective-permute-start(bf16[512,256]{1,0:T(8,128)(2,1)S(1)} %get-tuple-element.93.refs_4_), channel_id=1, source_target_pairs={{0,24},{2,26},{4,28},{6,30},{8,0},{10,2},{12,4},{14,6},{16,8},{18,... | collective-permute-start | bytes 786440 | tf_op jit(solution)/shard_map/ppermute | solution.py:392
  41.4 22.5 %collective-permute-start.9 = (bf16[512,256]{1,0:T(8,128)(2,1)S(1)}, bf16[512,256]{1,0:T(8,128)(2,1)S(1)}, u32[]{:S(2)}, u32[]{:S(2)}) collective-permute-start(bf16[512,256]{1,0:T(8,128)(2,1)S(1)} %get-tuple-element.93.refs_4_), channel_id=1, source_target_pairs={{0,8},{2,10},{4,12},{6,14},{8,16},{10,18},{12,20},{14,22},{16,24},... | collective-permute-start | bytes 786440 | tf_op jit(solution)/shard_map/ppermute | solution.py:392
  55.5 19.0 %collective-permute-start.13 = (bf16[128,512]{1,0:T(8,128)(2,1)S(1)}, bf16[128,512]{1,0:T(8,128)(2,1)S(1)}, u32[]{:S(2)}, u32[]{:S(2)}) collective-permute-start(bf16[128,512]{1,0:T(8,128)(2,1)S(1)} %get-tuple-element.112), channel_id=1, source_target_pairs={{0,2},{2,0},{4,6},{6,4},{8,10},{10,8},{12,14},{14,12},{16,18},{18,... | collective-permute-start | bytes 393224 | tf_op jit(solution)/shard_map/ppermute | solution.py:387
  56.4 28.9 %collective-permute-start.20 = (bf16[512,256]{1,0:T(8,128)(2,1)S(1)}, bf16[512,256]{1,0:T(8,128)(2,1)S(1)}, u32[]{:S(2)}, u32[]{:S(2)}) collective-permute-start(bf16[512,256]{1,0:T(8,128)(2,1)S(1)} %get-tuple-element.125), channel_id=1, source_target_pairs={{0,8},{2,10},{4,12},{6,14},{8,16},{10,18},{12,20},{14,22},{16,24},... | collective-permute-start | bytes 786440 | tf_op jit(solution)/shard_map/ppermute | solution.py:392
  59.9 26.6 %collective-permute-start.21 = (bf16[512,256]{1,0:T(8,128)(2,1)S(1)}, bf16[512,256]{1,0:T(8,128)(2,1)S(1)}, u32[]{:S(2)}, u32[]{:S(2)}) collective-permute-start(bf16[512,256]{1,0:T(8,128)(2,1)S(1)} %get-tuple-element.126), channel_id=1, source_target_pairs={{0,16},{2,18},{4,20},{6,22},{8,24},{10,26},{12,28},{14,30},{16,0},... | collective-permute-start | bytes 786440 | tf_op jit(solution)/shard_map/ppermute | solution.py:392
  60.3 24.0 %collective-permute-start.14 = (bf16[128,512]{1,0:T(8,128)(2,1)S(1)}, bf16[128,512]{1,0:T(8,128)(2,1)S(1)}, u32[]{:S(2)}, u32[]{:S(2)}) collective-permute-start(bf16[128,512]{1,0:T(8,128)(2,1)S(1)} %get-tuple-element.113), channel_id=1, source_target_pairs={{0,4},{2,6},{4,0},{6,2},{8,12},{10,14},{12,8},{14,10},{16,20},{18,... | collective-permute-start | bytes 393224 | tf_op jit(solution)/shard_map/ppermute | solution.py:387
  63.9 20.4 %collective-permute-start.15 = (bf16[128,512]{1,0:T(8,128)(2,1)S(1)}, bf16[128,512]{1,0:T(8,128)(2,1)S(1)}, u32[]{:S(2)}, u32[]{:S(2)}) collective-permute-start(bf16[128,512]{1,0:T(8,128)(2,1)S(1)} %get-tuple-element.114), channel_id=1, source_target_pairs={{0,6},{2,4},{4,2},{6,0},{8,14},{10,12},{12,10},{14,8},{16,22},{18,... | collective-permute-start | bytes 393224 | tf_op jit(solution)/shard_map/ppermute | solution.py:387
  74.5 14.3 %collective-permute-start.22 = (bf16[512,256]{1,0:T(8,128)(2,1)S(1)}, bf16[512,256]{1,0:T(8,128)(2,1)S(1)}, u32[]{:S(2)}, u32[]{:S(2)}) collective-permute-start(bf16[512,256]{1,0:T(8,128)(2,1)S(1)} %get-tuple-element.127), channel_id=1, source_target_pairs={{0,24},{2,26},{4,28},{6,30},{8,0},{10,2},{12,4},{14,6},{16,8},{18,... | collective-permute-start | bytes 786440 | tf_op jit(solution)/shard_map/ppermute | solution.py:392
  84.3 10.9 %collective-permute-start.16 = (bf16[128,512]{1,0:T(8,128)(2,1)S(1)}, bf16[128,512]{1,0:T(8,128)(2,1)S(1)}, u32[]{:S(2)}, u32[]{:S(2)}) collective-permute-start(bf16[128,512]{1,0:T(8,128)(2,1)S(1)} %get-tuple-element.115), channel_id=1, source_target_pairs={{0,1},{1,0},{2,3},{3,2},{4,5},{5,4},{6,7},{7,6},{8,9},{9,8},{10,11... | collective-permute-start | bytes 393224 | tf_op jit(solution)/shard_map/ppermute | solution.py:403
  84.6 13.2 %collective-permute-start.17 = (bf16[128,512]{1,0:T(8,128)(2,1)S(1)}, bf16[128,512]{1,0:T(8,128)(2,1)S(1)}, u32[]{:S(2)}, u32[]{:S(2)}) collective-permute-start(bf16[128,512]{1,0:T(8,128)(2,1)S(1)} %get-tuple-element.116), channel_id=1, source_target_pairs={{0,3},{1,2},{2,1},{3,0},{4,7},{5,6},{6,5},{7,4},{8,11},{9,10},{10,... | collective-permute-start | bytes 393224 | tf_op jit(solution)/shard_map/ppermute | solution.py:403
  85.3 13.8 %collective-permute-start.18 = (bf16[128,512]{1,0:T(8,128)(2,1)S(1)}, bf16[128,512]{1,0:T(8,128)(2,1)S(1)}, u32[]{:S(2)}, u32[]{:S(2)}) collective-permute-start(bf16[128,512]{1,0:T(8,128)(2,1)S(1)} %get-tuple-element.117), channel_id=1, source_target_pairs={{0,5},{1,4},{2,7},{3,6},{4,1},{5,0},{6,3},{7,2},{8,13},{9,12},{10,... | collective-permute-start | bytes 393224 | tf_op jit(solution)/shard_map/ppermute | solution.py:403
  86.4 12.7 %collective-permute-start.19 = (bf16[128,512]{1,0:T(8,128)(2,1)S(1)}, bf16[128,512]{1,0:T(8,128)(2,1)S(1)}, u32[]{:S(2)}, u32[]{:S(2)}) collective-permute-start(bf16[128,512]{1,0:T(8,128)(2,1)S(1)} %get-tuple-element.118), channel_id=1, source_target_pairs={{0,7},{1,6},{2,5},{3,4},{4,3},{5,2},{6,1},{7,0},{8,15},{9,14},{10,... | collective-permute-start | bytes 393224 | tf_op jit(solution)/shard_map/ppermute | solution.py:403
  88.9 11.3 %collective-permute-start.23 = (bf16[128,256]{1,0:T(8,128)(2,1)S(1)}, bf16[128,256]{1,0:T(8,128)(2,1)S(1)}, u32[]{:S(2)}, u32[]{:S(2)}) collective-permute-start(bf16[128,256]{1,0:T(8,128)(2,1)S(1)} %get-tuple-element.129), channel_id=1, source_target_pairs={{0,2},{2,0},{4,6},{6,4},{8,10},{10,8},{12,14},{14,12},{16,18},{18,... | collective-permute-start | bytes 196616 | tf_op jit(solution)/shard_map/ppermute | solution.py:387
  95.2 5.0 %collective-permute-start.24 = (bf16[128,256]{1,0:T(8,128)(2,1)S(1)}, bf16[128,256]{1,0:T(8,128)(2,1)S(1)}, u32[]{:S(2)}, u32[]{:S(2)}) collective-permute-start(bf16[128,256]{1,0:T(8,128)(2,1)S(1)} %get-tuple-element.130), channel_id=1, source_target_pairs={{0,4},{2,6},{4,0},{6,2},{8,12},{10,14},{12,8},{14,10},{16,20},{18,... | collective-permute-start | bytes 196616 | tf_op jit(solution)/shard_map/ppermute | solution.py:387
  97.9 4.6 %collective-permute-start.25 = (bf16[128,256]{1,0:T(8,128)(2,1)S(1)}, bf16[128,256]{1,0:T(8,128)(2,1)S(1)}, u32[]{:S(2)}, u32[]{:S(2)}) collective-permute-start(bf16[128,256]{1,0:T(8,128)(2,1)S(1)} %get-tuple-element.131), channel_id=1, source_target_pairs={{0,6},{2,4},{4,2},{6,0},{8,14},{10,12},{12,10},{14,8},{16,22},{18,... | collective-permute-start | bytes 196616 | tf_op jit(solution)/shard_map/ppermute | solution.py:387

commit v4 on v2

--- a/solution.py
+++ b/solution.py
@@ -9,6 +9,7 @@
 from jax.sharding import PartitionSpec as P
 
 HEAD = 128
+UNROLL = 3
 QUAD = 4
 SCALE = HEAD ** (-0.5)
 EXP2_SCALE = -SCALE / math.log(2.0)
@@ -167,10 +168,21 @@
     return jnp.where(visible, part, 0.0)
 
 
-def forward_kernel(nz, order_ref, *refs):
-    queries, refs = refs[:QUAD], refs[QUAD:]
+def repeat(steps, advance):
+    def several(i, _):
+        for j in range(UNROLL):
+            advance(i * UNROLL + j)
+        return 0
+
+    lax.fori_loop(0, steps // UNROLL, several, 0)
+    for step in range(steps // UNROLL * UNROLL, steps):
+        advance(step)
+
+
+def forward_kernel(nz, parts, order_ref, *refs):
+    queries, refs = refs[: len(parts)], refs[len(parts) :]
     stacks, refs = refs[:nz], refs[nz:]
-    outs, refs = refs[:QUAD], refs[QUAD:]
+    outs, refs = refs[: len(parts)], refs[len(parts) :]
     keys, values, stacked, total, gap = refs
     z, member = place()
     stretch_rows = queries[0].shape[0] // 2
@@ -179,10 +191,10 @@
     steps = keys.shape[0] // block_rows + 1
     in_sequence(order_ref, stacks, stretch_rows, keys, values)
     offset = 2 * groups * HEAD
-    for d in range(QUAD):
+    for i in range(len(parts)):
         for e in range(2):
             for g in range(groups):
-                stacked[2 * d + e, g * stretch_rows : (g + 1) * stretch_rows, :] = queries[d][
+                stacked[2 * i + e, g * stretch_rows : (g + 1) * stretch_rows, :] = queries[i][
                     e * stretch_rows : (e + 1) * stretch_rows,
                     offset + g * HEAD : offset + (g + 1) * HEAD,
                 ]
@@ -191,29 +203,28 @@
         lax.broadcasted_iota(jnp.int32, gap.shape, 0), stretch_rows
     )
 
-    def advance(step, _):
-        for d in range(QUAD):
+    def advance(step):
+        for i, d in enumerate(parts):
             row, stretch, block = step_place(
                 stretch_of(order_ref, z, member, d, 0),
                 stretch_of(order_ref, z, member, d, 1),
                 step,
-                d,
+                i,
                 groups,
             )
             rows = rows_at(block, block_rows)
             raw = dot(stacked[row], keys[rows, :], NT)
             visible = gap[...] <= stretch * stretch_rows - block * block_rows
-            weights = (raw * SCALE * sigmoid_of(raw, visible)).astype(jnp.bfloat16)
+            weights = (raw * sigmoid_of(raw, visible)).astype(jnp.bfloat16)
             total[row] += dot(weights, values[rows, :], NN)
-        return 0
-
-    lax.fori_loop(0, steps, advance, 0)
-    for d in range(QUAD):
+
+    repeat(steps, advance)
+    for i, d in enumerate(parts):
         for e in range(2):
-            shrink = shrink_of(stretch_of(order_ref, z, member, d, e), stretch_rows)
+            shrink = SCALE * shrink_of(stretch_of(order_ref, z, member, d, e), stretch_rows)
             for g in range(groups):
-                outs[d][e * stretch_rows : (e + 1) * stretch_rows, g * HEAD : (g + 1) * HEAD] = (
-                    total[2 * d + e, g * stretch_rows : (g + 1) * stretch_rows, :] * shrink
+                outs[i][e * stretch_rows : (e + 1) * stretch_rows, g * HEAD : (g + 1) * HEAD] = (
+                    total[2 * i + e, g * stretch_rows : (g + 1) * stretch_rows, :] * shrink
                 ).astype(jnp.bfloat16)
 
 
@@ -254,7 +265,7 @@
         lax.broadcasted_iota(jnp.int32, gap.shape, 1), stretch_rows
     )
 
-    def advance(step, _):
+    def advance(step):
         for d in range(QUAD):
             row, stretch, block = step_place(
                 stretch_of(order_ref, z, member, d, 0),
@@ -274,9 +285,8 @@
             total_t[row] += dot(keys_t[block], score_grad, NN)
             key_total[rows, :] += dot(score_grad, stacked[row], NN)
             value_total[rows, :] += dot(weights, grads[row], NN)
-        return 0
-
-    lax.fori_loop(0, steps, advance, 0)
+
+    repeat(steps, advance)
     for d in range(QUAD):
         for e in range(2):
             query_grad = (total_t[2 * d + e].T * SCALE).astype(jnp.bfloat16)
@@ -518,28 +528,39 @@
     )
     key_sums = reduce_first(key_parts)
     query_pieces = swap(query_pieces)
-    query_pieces, stacks = lax.optimization_barrier((query_pieces, stacks))
-    attended = call(
-        functools.partial(forward_kernel, nz),
-        "forward",
-        [bf16(rows, width)] * QUAD,
-        [SMEM] + [VMEM] * (QUAD + nz),
-        stretch_order,
-        *queries,
-        *stacks,
-        scratch=sequence
-        + [stacked, pltpu.VMEM((2 * QUAD, block_rows, HEAD), jnp.float32), gap],
-    )
-    attended, key_up = lax.optimization_barrier((attended, key_sums[0]))
+    def attend(parts, name):
+        return call(
+            functools.partial(forward_kernel, nz, parts),
+            name,
+            [bf16(rows, width)] * len(parts),
+            [SMEM] + [VMEM] * (len(parts) + nz),
+            stretch_order,
+            *[queries[d] for d in parts],
+            *stacks,
+            scratch=sequence
+            + [
+                pltpu.VMEM((2 * len(parts), block_rows, HEAD), jnp.bfloat16),
+                pltpu.VMEM((2 * len(parts), block_rows, HEAD), jnp.float32),
+                gap,
+            ],
+        )
+
+    far = attend((2, 3), "forward_far")
+    far, query_pieces, key_sums = lax.optimization_barrier((far, query_pieces, key_sums))
+    far = [hand(piece, d) for d, piece in zip((2, 3), far)]
+    far, stacks = lax.optimization_barrier((far, stacks))
+    near = attend((0, 1), "forward_near")
+    near = [hand(piece, d) for d, piece in zip((0, 1), near)]
     (handed,) = call(
         gate_kernel,
         "gate",
         [bf16(*gate_fwd.shape)],
         [VMEM] * (QUAD + 1),
-        *[hand(attended[d], d) for d in range(QUAD)],
+        *near,
+        *far,
         gate_before,
     )
-    key_sums = reduce_rest(key_parts, key_up, key_sums[1])
+    key_sums = reduce_rest(key_parts, *key_sums)
     key_pieces = swap(
         call(
             sum_kernel,

time: 96.4 us -> 103 us (1.068)
  waiting for transfers between devices: 30 us -> 36.2 us
  starting transfers between devices: 34.6 us -> 37.2 us
  Pallas kernels: 30.8 us -> 28.9 us
    ppermute x5, waiting for transfers between devices: 3.46 us -> 9.77 us  [hand(): return lax.ppermute(block, ('ctx', 'pipe'), route)]
    ppermute x9, starting transfers between devices: 19.4 us -> 22.9 us  [turn(): lax.ppermute(block, 'ctx', [(i, (i + s * QUAD) % devices) for i in range(...]
    pallas_call x9 -> x10, Pallas kernels: 30.8 us -> 28.9 us  [call(): pl.pallas_call(kernel, name=name, out_shape=out_shape, in_specs=specs, ou...]
    ppermute x9, waiting for transfers between devices: 21.8 us -> 20.5 us  [turn(): lax.ppermute(block, 'ctx', [(i, (i + s * QUAD) % devices) for i in range(...]
    ppermute x12, waiting for transfers between devices: 4.74 us -> 5.88 us  [swap(): lax.ppermute(pieces[d], 'ctx', [(i, i ^ d) for i in range(devices)])]
  transfers between devices with their start and end apart: 26 -> 26, of which waited for: 9 -> 12; matrix products, arithmetic and copies ran while one was open for 0% -> 0% of each run, Pallas kernels for 29% -> 25%
where the time goes in v4:
time: 103 us
  starting transfers between devices  37.2 us (36%)
  waiting for transfers between devices  36.2 us (35%)
  Pallas kernels  28.9 us (28%)
    pallas_call x10, Pallas kernels, call(): pl.pallas_call(kernel, name=name, out_shape=out_shape, in_specs=specs, ou...  28.9 us
    ppermute x9, starting transfers between devices, turn(): lax.ppermute(block, 'ctx', [(i, (i + s * QUAD) % devices) for i in range(...  22.9 us
    ppermute x9, waiting for transfers between devices, turn(): lax.ppermute(block, 'ctx', [(i, (i + s * QUAD) % devices) for i in range(...  20.5 us
    ppermute x5, waiting for transfers between devices, hand(): return lax.ppermute(block, ('ctx', 'pipe'), route)  9.77 us
    ppermute x12, starting transfers between devices, swap(): lax.ppermute(pieces[d], 'ctx', [(i, i ^ d) for i in range(devices)])  8.79 us
    ppermute x12, waiting for transfers between devices, swap(): lax.ppermute(pieces[d], 'ctx', [(i, i ^ d) for i in range(devices)])  5.88 us
    ppermute x5, starting transfers between devices, hand(): return lax.ppermute(block, ('ctx', 'pipe'), route)  5.48 us
  transfers between devices with their start and end apart: 26, of which 12 were waited for; matrix products, arithmetic and copies ran while one was open for 0% of the time, Pallas kernels for 25%

profile of v4, /device:TPU:0, one launch (start us, length us, event | category | flops | bytes accessed | tf_op | source)
XLA Modules:
  0.0 103.0 jit_solution(3248912211482705629)
XLA Ops:
  0.6 2.4 %pack_keys.1 = (bf16[128,512]{1,0:T(8,128)(2,1)}, bf16[128,512]{1,0:T(8,128)(2,1)}, bf16[128,512]{1,0:T(8,128)(2,1)}, bf16[128,512]{1,0:T(8,128)(2,1)}) custom-call(bf16[1,128,512]{2,1,0:T(8,128)(2,1)} %back_key.1, bf16[1,128,512]{2,1,0:T(8,128)(2,1)} %back_value.1, s32[1,128]{1,0:T(1,128)} %back_types.1, bf16[1,128,512]{2,1,0:T(8,128)(2,1)} %key.1, ...), custom_call_target="tpu_custom_call" | custom-call | bytes 1115136 | tf_op jit(solution)/shard_map/pack_keys/pallas_call | solution.py:355
  3.0 0.5 collective-permute-start
  3.5 2.6 %collective-permute-start.1 = (bf16[128,512]{1,0:T(8,128)(2,1)}, bf16[128,512]{1,0:T(8,128)(2,1)S(1)}, u32[]{:S(2)}, u32[]{:S(2)}) collective-permute-start(bf16[128,512]{1,0:T(8,128)(2,1)} %get-tuple-element.79), channel_id=1, source_target_pairs={{0,4},{2,6},{4,0},{6,2},{8,12},{10,14},{12,8},{14,10},{16,20},{18,... | collective-permute-start | bytes 393224 | tf_op jit(solution)/shard_map/ppermute | solution.py:397
  6.1 0.1 collective-permute-start.2
  6.2 3.8 %pack_queries.1 = (bf16[128,1536]{1,0:T(8,128)(2,1)}, bf16[128,1536]{1,0:T(8,128)(2,1)}, bf16[128,1536]{1,0:T(8,128)(2,1)}, bf16[128,1536]{1,0:T(8,128)(2,1)}, bf16[144,2048]{1,0:T(8,128)(2,1)}) custom-call(bf16[1,128,2048]{2,1,0:T(8,128)(2,1)} %query_ref.1, bf16[1,128,2048]{2,1,0:T(8,128)(2,1)} %grad_ref.1, bf16[1,128,2048]{2,1,0:T(8,128)(2,1)} %forward_ref.1, ...), custom_call_target="tpu_custom_call" | custom-call | bytes 4268032 | tf_op jit(solution)/shard_map/pack_queries/pallas_call | solution.py:355
  10.0 0.0 copy-start
  10.0 0.0 collective-permute-done.refs_1_
  10.0 0.7 collective-permute-done.1.refs_2_
  10.7 2.3 %collective-permute-done.2.refs_3_ = bf16[128,512]{1,0:T(8,128)(2,1)S(1)} collective-permute-done((bf16[128,512]{1,0:T(8,128)(2,1)}, bf16[128,512]{1,0:T(8,128)(2,1)S(1)}, u32[]{:S(2)}, u32[]{:S(2)}) %collective-permute-start.2) | collective-permute-done | bytes 131104 | tf_op jit(solution)/shard_map/ppermute | solution.py:397
  12.9 0.1 stack_keys.1
  13.1 0.0 copy-start.2
  13.1 1.7 %collective-permute-start.6 = (bf16[512,256]{1,0:T(8,128)(2,1)S(1)}, bf16[512,256]{1,0:T(8,128)(2,1)S(1)}, u32[]{:S(2)}, u32[]{:S(2)}) collective-permute-start(bf16[512,256]{1,0:T(8,128)(2,1)S(1)} %get-tuple-element.106.refs_4_), channel_id=1, source_target_pairs={{0,8},{2,10},{4,12},{6,14},{8,16},{10,18},{12,20},{14,22},{16,24},... | collective-permute-start | bytes 786440 | tf_op jit(solution)/shard_map/ppermute | solution.py:402
  14.8 2.2 %collective-permute-start.7 = (bf16[512,256]{1,0:T(8,128)(2,1)S(1)}, bf16[512,256]{1,0:T(8,128)(2,1)S(1)}, u32[]{:S(2)}, u32[]{:S(2)}) collective-permute-start(bf16[512,256]{1,0:T(8,128)(2,1)S(1)} %get-tuple-element.106.refs_4_), channel_id=1, source_target_pairs={{0,24},{2,26},{4,28},{6,30},{8,0},{10,2},{12,4},{14,6},{16,8},{18,... | collective-permute-start | bytes 786440 | tf_op jit(solution)/shard_map/ppermute | solution.py:402
  17.0 0.0 collective-permute-start.3
  17.0 1.6 %collective-permute-start.4 = (bf16[128,1536]{1,0:T(8,128)(2,1)}, bf16[128,1536]{1,0:T(8,128)(2,1)S(1)}, u32[]{:S(2)}, u32[]{:S(2)}) collective-permute-start(bf16[128,1536]{1,0:T(8,128)(2,1)} %get-tuple-element.88), channel_id=1, source_target_pairs={{0,4},{2,6},{4,0},{6,2},{8,12},{10,14},{12,8},{14,10},{16,20},{18,... | collective-permute-start | bytes 1179656 | tf_op jit(solution)/shard_map/ppermute | solution.py:397
  18.5 0.3 collective-permute-start.5
  18.8 5.3 %collective-permute-done.6.refs_5_ = bf16[512,256]{1,0:T(8,128)(2,1)S(1)} collective-permute-done((bf16[512,256]{1,0:T(8,128)(2,1)S(1)}, bf16[512,256]{1,0:T(8,128)(2,1)S(1)}, u32[]{:S(2)}, u32[]{:S(2)}) %collective-permute-start.6) | collective-permute-done | bytes 262176 | tf_op jit(solution)/shard_map/ppermute | solution.py:402
  24.1 4.5 %collective-permute-done.7.refs_7_ = bf16[512,256]{1,0:T(8,128)(2,1)S(1)} collective-permute-done((bf16[512,256]{1,0:T(8,128)(2,1)S(1)}, bf16[512,256]{1,0:T(8,128)(2,1)S(1)}, u32[]{:S(2)}, u32[]{:S(2)}) %collective-permute-start.7) | collective-permute-done | bytes 262176 | tf_op jit(solution)/shard_map/ppermute | solution.py:402
  28.6 1.5 %collective-permute-start.12 = (bf16[144,2048]{1,0:T(8,128)(2,1)}, bf16[144,2048]{1,0:T(8,128)(2,1)S(1)}, u32[]{:S(2)}, u32[]{:S(2)}) collective-permute-start(bf16[144,2048]{1,0:T(8,128)(2,1)} %get-tuple-element.118), channel_id=1, source_target_pairs={{0,1},{1,0},{2,3},{3,2},{4,5},{5,4},{6,7},{7,6},{8,9},{9,8},{10,11... | collective-permute-start | bytes 1769480 | tf_op jit(solution)/shard_map/ppermute | solution.py:413
  30.2 1.1 %collective-permute-start.8 = (bf16[512,256]{1,0:T(8,128)(2,1)S(1)}, bf16[512,256]{1,0:T(8,128)(2,1)S(1)}, u32[]{:S(2)}, u32[]{:S(2)}) collective-permute-start(bf16[512,256]{1,0:T(8,128)(2,1)S(1)} %collective-permute-done.6.refs_5_), channel_id=1, source_target_pairs={{0,8},{2,10},{4,12},{6,14},{8,16},{10,18},{12,20},{14,22},{16,24},... | collective-permute-start | bytes 786440 | tf_op jit(solution)/shard_map/ppermute | solution.py:402
  31.3 8.1 %collective-permute-done.8.refs_6_ = bf16[512,256]{1,0:T(8,128)(2,1)S(1)} collective-permute-done((bf16[512,256]{1,0:T(8,128)(2,1)S(1)}, bf16[512,256]{1,0:T(8,128)(2,1)S(1)}, u32[]{:S(2)}, u32[]{:S(2)}) %collective-permute-start.8) | collective-permute-done | bytes 262176 | tf_op jit(solution)/shard_map/ppermute | solution.py:402
  39.3 0.0 collective-permute-start.10
  39.3 0.0 collective-permute-done.3.refs_1_
  39.3 2.2 %collective-permute-start.11 = (bf16[512,256]{1,0:T(8,128)(2,1)S(1)}, bf16[512,256]{1,0:T(8,128)(2,1)S(1)}, u32[]{:S(2)}, u32[]{:S(2)}) collective-permute-start(bf16[512,256]{1,0:T(8,128)(2,1)S(1)} %get-tuple-element.127.refs_2_), channel_id=1, source_target_pairs={{0,24},{2,26},{4,28},{6,30},{8,0},{10,2},{12,4},{14,6},{16,8},{18,... | collective-permute-start | bytes 786440 | tf_op jit(solution)/shard_map/ppermute | solution.py:402
  41.6 0.0 collective-permute-done.4.refs_0_.refs_2_
  41.6 0.0 collective-permute-start.9
  41.6 0.0 collective-permute-done.5.refs_1_.refs_3_
  41.6 12.8 %backward.1 = (bf16[128,512]{1,0:T(8,128)(2,1)S(1)}, bf16[128,512]{1,0:T(8,128)(2,1)S(1)}, bf16[128,512]{1,0:T(8,128)(2,1)S(1)}, bf16[128,512]{1,0:T(8,128)(2,1)...) custom-call(s32[1,32]{1,0:T(1,128)S(1)} %copy-done.2, ...), custom_call_target="tpu_custom_call" | custom-call | flops 3019898880 | bytes 4194432 | tf_op jit(solution)/shard_map/backward/pallas_call | solution.py:355
  54.4 0.0 collective-permute-done.12.refs_4_
  54.4 1.3 %collective-permute-start.16 = (bf16[512,256]{1,0:T(8,128)(2,1)S(1)}, bf16[512,256]{1,0:T(8,128)(2,1)S(1)}, u32[]{:S(2)}, u32[]{:S(2)}) collective-permute-start(bf16[512,256]{1,0:T(8,128)(2,1)S(1)} %get-tuple-element.123), channel_id=1, source_target_pairs={{0,8},{2,10},{4,12},{6,14},{8,16},{10,18},{12,20},{14,22},{16,24},... | collective-permute-start | bytes 786440 | tf_op jit(solution)/shard_map/ppermute | solution.py:402
  55.8 2.6 %collective-permute-start.17 = (bf16[512,256]{1,0:T(8,128)(2,1)S(1)}, bf16[512,256]{1,0:T(8,128)(2,1)S(1)}, u32[]{:S(2)}, u32[]{:S(2)}) collective-permute-start(bf16[512,256]{1,0:T(8,128)(2,1)S(1)} %get-tuple-element.124), channel_id=1, source_target_pairs={{0,24},{2,26},{4,28},{6,30},{8,0},{10,2},{12,4},{14,6},{16,8},{18,... | collective-permute-start | bytes 786440 | tf_op jit(solution)/shard_map/ppermute | solution.py:402
  58.4 0.0 collective-permute-done.10.refs_4_
  58.4 0.0 collective-permute-start.13
  58.4 0.0 collective-permute-done.11.refs_5_
  58.4 1.6 %collective-permute-start.14 = (bf16[128,512]{1,0:T(8,128)(2,1)S(1)}, bf16[128,512]{1,0:T(8,128)(2,1)S(1)}, u32[]{:S(2)}, u32[]{:S(2)}) collective-permute-start(bf16[128,512]{1,0:T(8,128)(2,1)S(1)} %get-tuple-element.121), channel_id=1, source_target_pairs={{0,4},{2,6},{4,0},{6,2},{8,12},{10,14},{12,8},{14,10},{16,20},{18,... | collective-permute-start | bytes 393224 | tf_op jit(solution)/shard_map/ppermute | solution.py:397
  59.9 0.0 collective-permute-done.9.refs_3_
  59.9 0.3 collective-permute-start.15
  60.2 3.5 %forward_far.1 = (bf16[128,512]{1,0:T(8,128)(2,1)S(1)}, bf16[128,512]{1,0:T(8,128)(2,1)S(1)}) custom-call(s32[1,32]{1,0:T(1,128)S(1)} %copy-done.2, bf16[128,1536]{1,0:T(8,128)(2,1)S(1)} %collective-permute-done.4.refs_0_.refs_2_, bf16[128,1536]{1,0:T(8,128)(2,1)S(1)} %collective-permute-done.5.refs_1_.refs_3_, ...), custom_call_target="tpu_custom_call" | custom-call | bytes 2097280 | tf_op jit(solution)/shard_map/forward_far/pallas_call | solution.py:355
  63.7 0.0 collective-permute-done.13.refs_1_
  63.7 1.0 collective-permute-done.14.refs_2_
  64.7 1.9 %collective-permute-done.15.refs_3_ = bf16[128,512]{1,0:T(8,128)(2,1)S(1)} collective-permute-done((bf16[128,512]{1,0:T(8,128)(2,1)S(1)}, bf16[128,512]{1,0:T(8,128)(2,1)S(1)}, u32[]{:S(2)}, u32[]{:S(2)}) %collective-permute-start.15) | collective-permute-done | bytes 131104 | tf_op jit(solution)/shard_map/ppermute | solution.py:397
  66.6 0.0 collective-permute-done.16
  66.6 2.6 %collective-permute-done.17.refs_2_ = bf16[512,256]{1,0:T(8,128)(2,1)S(1)} collective-permute-done((bf16[512,256]{1,0:T(8,128)(2,1)S(1)}, bf16[512,256]{1,0:T(8,128)(2,1)S(1)}, u32[]{:S(2)}, u32[]{:S(2)}) %collective-permute-start.17) | collective-permute-done | bytes 262176 | tf_op jit(solution)/shard_map/ppermute | solution.py:402
  69.2 0.1 add_convert_fusion
  69.3 11.7 %collective-permute-start.22 = (bf16[512,256]{1,0:T(8,128)(2,1)S(1)}, bf16[512,256]{1,0:T(8,128)(2,1)S(1)}, u32[]{:S(2)}, u32[]{:S(2)}) collective-permute-start(bf16[512,256]{1,0:T(8,128)(2,1)S(1)} %add_convert_fusion), channel_id=1, source_target_pairs={{0,8},{2,10},{4,12},{6,14},{8,16},{10,18},{12,20},{14,22},{16,24},... | collective-permute-start | bytes 786440 | tf_op jit(solution)/shard_map/ppermute | solution.py:402
  81.0 1.4 %collective-permute-start.18 = (bf16[128,512]{1,0:T(8,128)(2,1)S(1)}, bf16[128,512]{1,0:T(8,128)(2,1)S(1)}, u32[]{:S(2)}, u32[]{:S(2)}) collective-permute-start(bf16[128,512]{1,0:T(8,128)(2,1)S(1)} %get-tuple-element.125), channel_id=1, source_target_pairs={{0,5},{1,4},{2,7},{3,6},{4,1},{5,0},{6,3},{7,2},{8,13},{9,12},{10,... | collective-permute-start | bytes 393224 | tf_op jit(solution)/shard_map/ppermute | solution.py:413
  82.5 0.5 collective-permute-start.19
  83.0 4.8 %collective-permute-done.18.refs_2_ = bf16[128,512]{1,0:T(8,128)(2,1)S(1)} collective-permute-done((bf16[128,512]{1,0:T(8,128)(2,1)S(1)}, bf16[128,512]{1,0:T(8,128)(2,1)S(1)}, u32[]{:S(2)}, u32[]{:S(2)}) %collective-permute-start.18) | collective-permute-done | bytes 131104 | tf_op jit(solution)/shard_map/ppermute | solution.py:413
  87.8 1.3 %collective-permute-done.19.refs_3_ = bf16[128,512]{1,0:T(8,128)(2,1)S(1)} collective-permute-done((bf16[128,512]{1,0:T(8,128)(2,1)S(1)}, bf16[128,512]{1,0:T(8,128)(2,1)S(1)}, u32[]{:S(2)}, u32[]{:S(2)}) %collective-permute-start.19) | collective-permute-done | bytes 131104 | tf_op jit(solution)/shard_map/ppermute | solution.py:413
  89.1 3.5 %forward_near.1 = (bf16[128,512]{1,0:T(8,128)(2,1)S(1)}, bf16[128,512]{1,0:T(8,128)(2,1)S(1)}) custom-call(s32[1,32]{1,0:T(1,128)S(1)} %copy-done.2, bf16[128,1536]{1,0:T(8,128)(2,1)S(1)} %copy-done, bf16[128,1536]{1,0:T(8,128)(2,1)S(1)} %collective-permute-done.3.refs_1_, bf16[512,256]{1,0:T(8,128)(2,1)S(1)} %get-tuple-element.127.refs_2_, ...), custom_call_target="tpu_custom_call" | custom-call | bytes 2097280 | tf_op jit(solution)/shard_map/forward_near/pallas_call | solution.py:355
  92.6 1.3 %collective-permute-start.20 = (bf16[128,512]{1,0:T(8,128)(2,1)S(1)}, bf16[128,512]{1,0:T(8,128)(2,1)S(1)}, u32[]{:S(2)}, u32[]{:S(2)}) collective-permute-start(bf16[128,512]{1,0:T(8,128)(2,1)S(1)} %get-tuple-element.131), channel_id=1, source_target_pairs={{0,1},{1,0},{2,3},{3,2},{4,5},{5,4},{6,7},{7,6},{8,9},{9,8},{10,11... | collective-permute-start | bytes 393224 | tf_op jit(solution)/shard_map/ppermute | solution.py:413
  93.9 0.7 collective-permute-start.21
  94.6 0.0 collective-permute-done.22.refs_1_
  94.6 0.1 sum_key_parts.1
  94.7 0.3 collective-permute-start.23
  95.0 1.3 %collective-permute-start.24 = (bf16[128,256]{1,0:T(8,128)(2,1)S(1)}, bf16[128,256]{1,0:T(8,128)(2,1)S(1)}, u32[]{:S(2)}, u32[]{:S(2)}) collective-permute-start(bf16[128,256]{1,0:T(8,128)(2,1)S(1)} %get-tuple-element.146), channel_id=1, source_target_pairs={{0,4},{2,6},{4,0},{6,2},{8,12},{10,14},{12,8},{14,10},{16,20},{18,... | collective-permute-start | bytes 196616 | tf_op jit(solution)/shard_map/ppermute | solution.py:397
  96.3 0.3 collective-permute-start.25
  96.6 0.8 query_grad.1
  97.4 1.5 %collective-permute-done.20.refs_0_ = bf16[128,512]{1,0:T(8,128)(2,1)S(1)} collective-permute-done((bf16[128,512]{1,0:T(8,128)(2,1)S(1)}, bf16[128,512]{1,0:T(8,128)(2,1)S(1)}, u32[]{:S(2)}, u32[]{:S(2)}) %collective-permute-start.20) | collective-permute-done | bytes 131104 | tf_op jit(solution)/shard_map/ppermute | solution.py:413
  99.0 2.1 %collective-permute-done.21.refs_1_ = bf16[128,512]{1,0:T(8,128)(2,1)S(1)} collective-permute-done((bf16[128,512]{1,0:T(8,128)(2,1)S(1)}, bf16[128,512]{1,0:T(8,128)(2,1)S(1)}, u32[]{:S(2)}, u32[]{:S(2)}) %collective-permute-start.21) | collective-permute-done | bytes 131104 | tf_op jit(solution)/shard_map/ppermute | solution.py:413
  101.1 1.2 %gate.1 = bf16[1,128,2048]{2,1,0:T(8,128)(2,1)} custom-call(bf16[128,512]{1,0:T(8,128)(2,1)S(1)} %collective-permute-done.20.refs_0_, bf16[128,512]{1,0:T(8,128)(2,1)S(1)} %collective-permute-done.21.refs_1_, bf16[128,512]{1,0:T(8,128)(2,1)S(1)} %collective-permute-done.18.refs_2_, bf16[128,512]{1,0:T(8,128)(2,1)S(1)} %collective-permute-done.19.refs_3_, ...), custom_call_target="tpu_custom_call" | custom-call | bytes 1638400 | tf_op jit(solution)/shard_map/gate/pallas_call | solution.py:355
  102.3 0.0 collective-permute-done.24.refs_2_
  102.3 0.0 collective-permute-done.25.refs_3_
  102.3 0.8 key_grad.1
  (5 shorter events, 0.0 us)
Async XLA Ops:
  3.0 7.0 %collective-permute-start = (bf16[128,512]{1,0:T(8,128)(2,1)}, bf16[128,512]{1,0:T(8,128)(2,1)S(1)}, u32[]{:S(2)}, u32[]{:S(2)}) collective-permute-start(bf16[128,512]{1,0:T(8,128)(2,1)} %get-tuple-element.78), channel_id=1, source_target_pairs={{0,2},{2,0},{4,6},{6,4},{8,10},{10,8},{12,14},{14,12},{16,18},{18,... | collective-permute-start | bytes 393224 | tf_op jit(solution)/shard_map/ppermute | solution.py:397
  3.5 7.1 %collective-permute-start.1 = (bf16[128,512]{1,0:T(8,128)(2,1)}, bf16[128,512]{1,0:T(8,128)(2,1)S(1)}, u32[]{:S(2)}, u32[]{:S(2)}) collective-permute-start(bf16[128,512]{1,0:T(8,128)(2,1)} %get-tuple-element.79), channel_id=1, source_target_pairs={{0,4},{2,6},{4,0},{6,2},{8,12},{10,14},{12,8},{14,10},{16,20},{18,... | collective-permute-start | bytes 393224 | tf_op jit(solution)/shard_map/ppermute | solution.py:397
  6.1 6.8 %copy-start.1 = (bf16[128,512]{1,0:T(8,128)(2,1)S(1)}, bf16[128,512]{1,0:T(8,128)(2,1)}, u32[]{:S(2)}) copy-start(bf16[128,512]{1,0:T(8,128)(2,1)} %get-tuple-element.90.refs_0_) | copy-start | bytes 393220
  6.1 6.8 %collective-permute-start.2 = (bf16[128,512]{1,0:T(8,128)(2,1)}, bf16[128,512]{1,0:T(8,128)(2,1)S(1)}, u32[]{:S(2)}, u32[]{:S(2)}) collective-permute-start(bf16[128,512]{1,0:T(8,128)(2,1)} %get-tuple-element.80), channel_id=1, source_target_pairs={{0,6},{2,4},{4,2},{6,0},{8,14},{10,12},{12,10},{14,8},{16,22},{18,... | collective-permute-start | bytes 393224 | tf_op jit(solution)/shard_map/ppermute | solution.py:397
  10.0 31.6 %copy-start = (bf16[128,1536]{1,0:T(8,128)(2,1)S(1)}, bf16[128,1536]{1,0:T(8,128)(2,1)}, u32[]{:S(2)}) copy-start(bf16[128,1536]{1,0:T(8,128)(2,1)} %get-tuple-element.86.refs_0_) | copy-start | bytes 1179652
  13.1 28.5 %copy-start.2 = (s32[1,32]{1,0:T(1,128)S(1)}, s32[1,32]{1,0:T(1,128)}, u32[]{:S(2)}) copy-start(s32[1,32]{1,0:T(1,128)} %order_ref.5) | copy-start | bytes 388
  13.1 11.0 %collective-permute-start.6 = (bf16[512,256]{1,0:T(8,128)(2,1)S(1)}, bf16[512,256]{1,0:T(8,128)(2,1)S(1)}, u32[]{:S(2)}, u32[]{:S(2)}) collective-permute-start(bf16[512,256]{1,0:T(8,128)(2,1)S(1)} %get-tuple-element.106.refs_4_), channel_id=1, source_target_pairs={{0,8},{2,10},{4,12},{6,14},{8,16},{10,18},{12,20},{14,22},{16,24},... | collective-permute-start | bytes 786440 | tf_op jit(solution)/shard_map/ppermute | solution.py:402
  14.8 13.8 %collective-permute-start.7 = (bf16[512,256]{1,0:T(8,128)(2,1)S(1)}, bf16[512,256]{1,0:T(8,128)(2,1)S(1)}, u32[]{:S(2)}, u32[]{:S(2)}) collective-permute-start(bf16[512,256]{1,0:T(8,128)(2,1)S(1)} %get-tuple-element.106.refs_4_), channel_id=1, source_target_pairs={{0,24},{2,26},{4,28},{6,30},{8,0},{10,2},{12,4},{14,6},{16,8},{18,... | collective-permute-start | bytes 786440 | tf_op jit(solution)/shard_map/ppermute | solution.py:402
  17.0 22.4 %collective-permute-start.3 = (bf16[128,1536]{1,0:T(8,128)(2,1)}, bf16[128,1536]{1,0:T(8,128)(2,1)S(1)}, u32[]{:S(2)}, u32[]{:S(2)}) collective-permute-start(bf16[128,1536]{1,0:T(8,128)(2,1)} %get-tuple-element.87), channel_id=1, source_target_pairs={{0,2},{2,0},{4,6},{6,4},{8,10},{10,8},{12,14},{14,12},{16,18},{18,... | collective-permute-start | bytes 1179656 | tf_op jit(solution)/shard_map/ppermute | solution.py:397
  17.0 24.6 %collective-permute-start.4 = (bf16[128,1536]{1,0:T(8,128)(2,1)}, bf16[128,1536]{1,0:T(8,128)(2,1)S(1)}, u32[]{:S(2)}, u32[]{:S(2)}) collective-permute-start(bf16[128,1536]{1,0:T(8,128)(2,1)} %get-tuple-element.88), channel_id=1, source_target_pairs={{0,4},{2,6},{4,0},{6,2},{8,12},{10,14},{12,8},{14,10},{16,20},{18,... | collective-permute-start | bytes 1179656 | tf_op jit(solution)/shard_map/ppermute | solution.py:397
  18.5 23.1 %collective-permute-start.5 = (bf16[128,1536]{1,0:T(8,128)(2,1)}, bf16[128,1536]{1,0:T(8,128)(2,1)S(1)}, u32[]{:S(2)}, u32[]{:S(2)}) collective-permute-start(bf16[128,1536]{1,0:T(8,128)(2,1)} %get-tuple-element.89), channel_id=1, source_target_pairs={{0,6},{2,4},{4,2},{6,0},{8,14},{10,12},{12,10},{14,8},{16,22},{18,... | collective-permute-start | bytes 1179656 | tf_op jit(solution)/shard_map/ppermute | solution.py:397
  28.6 25.8 %collective-permute-start.12 = (bf16[144,2048]{1,0:T(8,128)(2,1)}, bf16[144,2048]{1,0:T(8,128)(2,1)S(1)}, u32[]{:S(2)}, u32[]{:S(2)}) collective-permute-start(bf16[144,2048]{1,0:T(8,128)(2,1)} %get-tuple-element.118), channel_id=1, source_target_pairs={{0,1},{1,0},{2,3},{3,2},{4,5},{5,4},{6,7},{7,6},{8,9},{9,8},{10,11... | collective-permute-start | bytes 1769480 | tf_op jit(solution)/shard_map/ppermute | solution.py:413
  30.2 9.2 %collective-permute-start.8 = (bf16[512,256]{1,0:T(8,128)(2,1)S(1)}, bf16[512,256]{1,0:T(8,128)(2,1)S(1)}, u32[]{:S(2)}, u32[]{:S(2)}) collective-permute-start(bf16[512,256]{1,0:T(8,128)(2,1)S(1)} %collective-permute-done.6.refs_5_), channel_id=1, source_target_pairs={{0,8},{2,10},{4,12},{6,14},{8,16},{10,18},{12,20},{14,22},{16,24},... | collective-permute-start | bytes 786440 | tf_op jit(solution)/shard_map/ppermute | solution.py:402
  39.3 19.0 %collective-permute-start.10 = (bf16[512,256]{1,0:T(8,128)(2,1)S(1)}, bf16[512,256]{1,0:T(8,128)(2,1)S(1)}, u32[]{:S(2)}, u32[]{:S(2)}) collective-permute-start(bf16[512,256]{1,0:T(8,128)(2,1)S(1)} %get-tuple-element.127.refs_2_), channel_id=1, source_target_pairs={{0,16},{2,18},{4,20},{6,22},{8,24},{10,26},{12,28},{14,30},{16,0},... | collective-permute-start | bytes 786440 | tf_op jit(solution)/shard_map/ppermute | solution.py:402
  39.3 19.0 %collective-permute-start.11 = (bf16[512,256]{1,0:T(8,128)(2,1)S(1)}, bf16[512,256]{1,0:T(8,128)(2,1)S(1)}, u32[]{:S(2)}, u32[]{:S(2)}) collective-permute-start(bf16[512,256]{1,0:T(8,128)(2,1)S(1)} %get-tuple-element.127.refs_2_), channel_id=1, source_target_pairs={{0,24},{2,26},{4,28},{6,30},{8,0},{10,2},{12,4},{14,6},{16,8},{18,... | collective-permute-start | bytes 786440 | tf_op jit(solution)/shard_map/ppermute | solution.py:402
  41.6 18.3 %collective-permute-start.9 = (bf16[512,256]{1,0:T(8,128)(2,1)S(1)}, bf16[512,256]{1,0:T(8,128)(2,1)S(1)}, u32[]{:S(2)}, u32[]{:S(2)}) collective-permute-start(bf16[512,256]{1,0:T(8,128)(2,1)S(1)} %get-tuple-element.127.refs_2_), channel_id=1, source_target_pairs={{0,8},{2,10},{4,12},{6,14},{8,16},{10,18},{12,20},{14,22},{16,24},... | collective-permute-start | bytes 786440 | tf_op jit(solution)/shard_map/ppermute | solution.py:402
  54.4 12.2 %collective-permute-start.16 = (bf16[512,256]{1,0:T(8,128)(2,1)S(1)}, bf16[512,256]{1,0:T(8,128)(2,1)S(1)}, u32[]{:S(2)}, u32[]{:S(2)}) collective-permute-start(bf16[512,256]{1,0:T(8,128)(2,1)S(1)} %get-tuple-element.123), channel_id=1, source_target_pairs={{0,8},{2,10},{4,12},{6,14},{8,16},{10,18},{12,20},{14,22},{16,24},... | collective-permute-start | bytes 786440 | tf_op jit(solution)/shard_map/ppermute | solution.py:402
  55.8 13.5 %collective-permute-start.17 = (bf16[512,256]{1,0:T(8,128)(2,1)S(1)}, bf16[512,256]{1,0:T(8,128)(2,1)S(1)}, u32[]{:S(2)}, u32[]{:S(2)}) collective-permute-start(bf16[512,256]{1,0:T(8,128)(2,1)S(1)} %get-tuple-element.124), channel_id=1, source_target_pairs={{0,24},{2,26},{4,28},{6,30},{8,0},{10,2},{12,4},{14,6},{16,8},{18,... | collective-permute-start | bytes 786440 | tf_op jit(solution)/shard_map/ppermute | solution.py:402
  58.4 5.3 %collective-permute-start.13 = (bf16[128,512]{1,0:T(8,128)(2,1)S(1)}, bf16[128,512]{1,0:T(8,128)(2,1)S(1)}, u32[]{:S(2)}, u32[]{:S(2)}) collective-permute-start(bf16[128,512]{1,0:T(8,128)(2,1)S(1)} %get-tuple-element.120), channel_id=1, source_target_pairs={{0,2},{2,0},{4,6},{6,4},{8,10},{10,8},{12,14},{14,12},{16,18},{18,... | collective-permute-start | bytes 393224 | tf_op jit(solution)/shard_map/ppermute | solution.py:397
  58.4 6.4 %collective-permute-start.14 = (bf16[128,512]{1,0:T(8,128)(2,1)S(1)}, bf16[128,512]{1,0:T(8,128)(2,1)S(1)}, u32[]{:S(2)}, u32[]{:S(2)}) collective-permute-start(bf16[128,512]{1,0:T(8,128)(2,1)S(1)} %get-tuple-element.121), channel_id=1, source_target_pairs={{0,4},{2,6},{4,0},{6,2},{8,12},{10,14},{12,8},{14,10},{16,20},{18,... | collective-permute-start | bytes 393224 | tf_op jit(solution)/shard_map/ppermute | solution.py:397
  59.9 6.7 %collective-permute-start.15 = (bf16[128,512]{1,0:T(8,128)(2,1)S(1)}, bf16[128,512]{1,0:T(8,128)(2,1)S(1)}, u32[]{:S(2)}, u32[]{:S(2)}) collective-permute-start(bf16[128,512]{1,0:T(8,128)(2,1)S(1)} %get-tuple-element.122), channel_id=1, source_target_pairs={{0,6},{2,4},{4,2},{6,0},{8,14},{10,12},{12,10},{14,8},{16,22},{18,... | collective-permute-start | bytes 393224 | tf_op jit(solution)/shard_map/ppermute | solution.py:397
  69.3 25.3 %collective-permute-start.22 = (bf16[512,256]{1,0:T(8,128)(2,1)S(1)}, bf16[512,256]{1,0:T(8,128)(2,1)S(1)}, u32[]{:S(2)}, u32[]{:S(2)}) collective-permute-start(bf16[512,256]{1,0:T(8,128)(2,1)S(1)} %add_convert_fusion), channel_id=1, source_target_pairs={{0,8},{2,10},{4,12},{6,14},{8,16},{10,18},{12,20},{14,22},{16,24},... | collective-permute-start | bytes 786440 | tf_op jit(solution)/shard_map/ppermute | solution.py:402
  81.0 6.8 %collective-permute-start.18 = (bf16[128,512]{1,0:T(8,128)(2,1)S(1)}, bf16[128,512]{1,0:T(8,128)(2,1)S(1)}, u32[]{:S(2)}, u32[]{:S(2)}) collective-permute-start(bf16[128,512]{1,0:T(8,128)(2,1)S(1)} %get-tuple-element.125), channel_id=1, source_target_pairs={{0,5},{1,4},{2,7},{3,6},{4,1},{5,0},{6,3},{7,2},{8,13},{9,12},{10,... | collective-permute-start | bytes 393224 | tf_op jit(solution)/shard_map/ppermute | solution.py:413
  82.5 6.7 %collective-permute-start.19 = (bf16[128,512]{1,0:T(8,128)(2,1)S(1)}, bf16[128,512]{1,0:T(8,128)(2,1)S(1)}, u32[]{:S(2)}, u32[]{:S(2)}) collective-permute-start(bf16[128,512]{1,0:T(8,128)(2,1)S(1)} %get-tuple-element.126), channel_id=1, source_target_pairs={{0,7},{1,6},{2,5},{3,4},{4,3},{5,2},{6,1},{7,0},{8,15},{9,14},{10,... | collective-permute-start | bytes 393224 | tf_op jit(solution)/shard_map/ppermute | solution.py:413
  92.6 6.4 %collective-permute-start.20 = (bf16[128,512]{1,0:T(8,128)(2,1)S(1)}, bf16[128,512]{1,0:T(8,128)(2,1)S(1)}, u32[]{:S(2)}, u32[]{:S(2)}) collective-permute-start(bf16[128,512]{1,0:T(8,128)(2,1)S(1)} %get-tuple-element.131), channel_id=1, source_target_pairs={{0,1},{1,0},{2,3},{3,2},{4,5},{5,4},{6,7},{7,6},{8,9},{9,8},{10,11... | collective-permute-start | bytes 393224 | tf_op jit(solution)/shard_map/ppermute | solution.py:413
  93.9 7.2 %collective-permute-start.21 = (bf16[128,512]{1,0:T(8,128)(2,1)S(1)}, bf16[128,512]{1,0:T(8,128)(2,1)S(1)}, u32[]{:S(2)}, u32[]{:S(2)}) collective-permute-start(bf16[128,512]{1,0:T(8,128)(2,1)S(1)} %get-tuple-element.132), channel_id=1, source_target_pairs={{0,3},{1,2},{2,1},{3,0},{4,7},{5,6},{6,5},{7,4},{8,11},{9,10},{10,... | collective-permute-start | bytes 393224 | tf_op jit(solution)/shard_map/ppermute | solution.py:413
  94.7 7.6 %collective-permute-start.23 = (bf16[128,256]{1,0:T(8,128)(2,1)S(1)}, bf16[128,256]{1,0:T(8,128)(2,1)S(1)}, u32[]{:S(2)}, u32[]{:S(2)}) collective-permute-start(bf16[128,256]{1,0:T(8,128)(2,1)S(1)} %get-tuple-element.145), channel_id=1, source_target_pairs={{0,2},{2,0},{4,6},{6,4},{8,10},{10,8},{12,14},{14,12},{16,18},{18,... | collective-permute-start | bytes 196616 | tf_op jit(solution)/shard_map/ppermute | solution.py:397
  95.0 7.3 %collective-permute-start.24 = (bf16[128,256]{1,0:T(8,128)(2,1)S(1)}, bf16[128,256]{1,0:T(8,128)(2,1)S(1)}, u32[]{:S(2)}, u32[]{:S(2)}) collective-permute-start(bf16[128,256]{1,0:T(8,128)(2,1)S(1)} %get-tuple-element.146), channel_id=1, source_target_pairs={{0,4},{2,6},{4,0},{6,2},{8,12},{10,14},{12,8},{14,10},{16,20},{18,... | collective-permute-start | bytes 196616 | tf_op jit(solution)/shard_map/ppermute | solution.py:397
  96.3 5.9 %collective-permute-start.25 = (bf16[128,256]{1,0:T(8,128)(2,1)S(1)}, bf16[128,256]{1,0:T(8,128)(2,1)S(1)}, u32[]{:S(2)}, u32[]{:S(2)}) collective-permute-start(bf16[128,256]{1,0:T(8,128)(2,1)S(1)} %get-tuple-element.147), channel_id=1, source_target_pairs={{0,6},{2,4},{4,2},{6,0},{8,14},{10,12},{12,10},{14,8},{16,22},{18,... | collective-permute-start | bytes 196616 | tf_op jit(solution)/shard_map/ppermute | solution.py:397

commit v5 on v4

--- a/solution.py
+++ b/solution.py
@@ -43,52 +43,41 @@
     return pl.ds(pl.multiple_of(index * width, width), width)
 
 
-def pack_keys(
-    back_key, back_value, back_types, key, value, types, table_ref, *refs
-):
-    pieces, (keys, event_types, table, typed, arrived, placed) = refs[:QUAD], refs[QUAD:]
+def pack_keys(key_ref, value_ref, types_ref, table_ref, *refs):
+    pieces, (keys, types, table, typed, arrived, placed) = refs[:QUAD], refs[QUAD:]
     _, member = place()
-    copies = [pltpu.make_async_copy(table_ref.at[0], table, arrived.at[4])]
-    for i, (key_ref, types_ref) in enumerate([(back_key, back_types), (key, types)]):
-        copies += [
-            pltpu.make_async_copy(types_ref, event_types.at[i], arrived.at[2 * i]),
-            pltpu.make_async_copy(key_ref.at[0], keys.at[i], arrived.at[2 * i + 1]),
-        ]
+    copies = [
+        pltpu.make_async_copy(source, target, arrived.at[i])
+        for i, (source, target) in enumerate(
+            [(types_ref, types), (table_ref.at[0], table), (key_ref.at[0], keys)]
+        )
+    ]
     placements = [
         pltpu.make_async_copy(
-            value_ref.at[0, :, columns(member ^ d, HEAD)],
-            pieces[d].at[:, (2 * i + 1) * HEAD : (2 * i + 2) * HEAD],
-            placed.at[i * QUAD + d],
+            value_ref.at[0, :, columns(member ^ d, HEAD)], pieces[d].at[:, HEAD:], placed.at[d]
         )
-        for i, value_ref in enumerate([back_value, value])
         for d in range(QUAD)
     ]
     for copy in copies + placements:
         copy.start()
     for copy in copies:
         copy.wait()
-    for i in range(2):
-        onehot = (
-            lax.broadcasted_iota(jnp.int32, (table.shape[0], types.shape[1]), 0) == event_types[i]
-        ).astype(jnp.float32).astype(jnp.bfloat16)
-        type_rows = dot(onehot, table[...], TN)
-        typed[...] = (keys[i].astype(jnp.float32) + type_rows).astype(jnp.bfloat16)
-        for d in range(QUAD):
-            pieces[d][:, 2 * i * HEAD : (2 * i + 1) * HEAD] = typed[:, columns(member ^ d, HEAD)]
+    onehot = (
+        lax.broadcasted_iota(jnp.int32, (table.shape[0], types.shape[1]), 0) == types[...]
+    ).astype(jnp.float32).astype(jnp.bfloat16)
+    type_rows = dot(onehot, table[...], TN)
+    typed[...] = (keys[...].astype(jnp.float32) + type_rows).astype(jnp.bfloat16)
+    for d in range(QUAD):
+        pieces[d][:, :HEAD] = typed[:, columns(member ^ d, HEAD)]
     for copy in placements:
         copy.wait()
 
 
 def stack_keys(*refs):
-    pieces, (back, front, placed) = refs[:QUAD], refs[QUAD:]
+    pieces, (out, placed) = refs[:QUAD], refs[QUAD:]
     rows = pieces[0].shape[0]
     copies = [
-        pltpu.make_async_copy(
-            pieces[d].at[:, 2 * i * HEAD : (2 * i + 2) * HEAD],
-            out.at[d * rows : (d + 1) * rows, :],
-            placed.at[i * QUAD + d],
-        )
-        for i, out in enumerate([back, front])
+        pltpu.make_async_copy(pieces[d], out.at[d * rows : (d + 1) * rows, :], placed.at[d])
         for d in range(QUAD)
     ]
     for copy in copies:
@@ -420,17 +409,6 @@
     def ring_down(block):
         return turn(block, nz - 1)
 
-    def gather_first(stack):
-        return [stack, ring_up(stack)], [ring_down(stack)]
-
-    def gather_rest(up, down):
-        up, down = lax.optimization_barrier((up, down))
-        while len(up) <= ahead:
-            up = up + [ring_up(up[-1])]
-        while len(up) + len(down) < nz:
-            down = down + [ring_down(down[-1])]
-        return up + down[::-1]
-
     def reduce_first(parts):
         return ring_up(parts[ahead]), ring_down(parts[ahead + 1])
 
@@ -444,30 +422,41 @@
             down = ring_down(add(down, parts[s]))
         return parts[0], up, down
 
-    pieces = swap(
-        call(
+    def gather(stack):
+        return [stack] + [turn(stack, s) for s in range(1, nz)]
+
+    def pack(key, value, types, name):
+        return call(
             pack_keys,
-            "pack_keys",
-            [bf16(rows, 4 * HEAD)] * QUAD,
-            [HBM] * 7,
-            key_bwd,
-            value_bwd,
-            types_bwd,
-            key_fwd,
-            value_fwd,
-            types_fwd,
+            name,
+            [bf16(rows, 2 * HEAD)] * QUAD,
+            [HBM] * 4,
+            key,
+            value,
+            types,
             type_key,
             scratch=[
-                pltpu.VMEM((2, *key_fwd.shape[1:]), jnp.bfloat16),
-                pltpu.VMEM((2, *types_fwd.shape), jnp.int32),
+                pltpu.VMEM(key.shape[1:], jnp.bfloat16),
+                pltpu.VMEM(types.shape, jnp.int32),
                 pltpu.VMEM(type_key.shape[1:], jnp.bfloat16),
-                pltpu.VMEM(key_fwd.shape[1:], jnp.bfloat16),
-                pltpu.SemaphoreType.DMA((5,)),
-                pltpu.SemaphoreType.DMA((2 * QUAD,)),
+                pltpu.VMEM(key.shape[1:], jnp.bfloat16),
+                pltpu.SemaphoreType.DMA((3,)),
+                pltpu.SemaphoreType.DMA((QUAD,)),
             ],
             vmem=60,
         )
-    )
+
+    def stacked_keys(pieces, name):
+        return call(
+            stack_keys,
+            name,
+            [bf16(QUAD * rows, 2 * HEAD)],
+            [HBM] * QUAD,
+            *pieces,
+            scratch=[pltpu.SemaphoreType.DMA((QUAD,))],
+        )[0]
+
+    back_pieces = swap(pack(key_bwd, value_bwd, types_bwd, "pack_keys_bwd"))
     packed = call(
         pack_queries,
         "pack_queries",
@@ -481,22 +470,16 @@
         scratch=[pltpu.SemaphoreType.DMA((3 * QUAD + 1,))],
         vmem=60,
     )
-    pieces, packed = lax.optimization_barrier((pieces, packed))
-    back_stack, stack = call(
-        stack_keys,
-        "stack_keys",
-        [bf16(QUAD * rows, 2 * HEAD)] * 2,
-        [HBM] * QUAD,
-        *pieces,
-        scratch=[pltpu.SemaphoreType.DMA((2 * QUAD,))],
-    )
+    back_pieces, packed = lax.optimization_barrier((back_pieces, list(packed)))
+    back_stacks = gather(stacked_keys(back_pieces, "stack_keys_bwd"))
+    pieces = swap(pack(key_fwd, value_fwd, types_fwd, "pack_keys_fwd"))
+    pieces, packed[2:QUAD] = lax.optimization_barrier((pieces, packed[2:QUAD]))
+    back_stacks, packed[1] = lax.optimization_barrier((back_stacks, packed[1]))
     queries = swap(packed[:QUAD])
-    up, down = gather_first(back_stack)
-    up, down, gate_before = lax.optimization_barrier((up, down, packed[QUAD]))
-    back_stacks = gather_rest(up, down)
-    gate_before = hand(gate_before, 0)
+    stack = stacked_keys(pieces, "stack_keys_fwd")
     stack, back_stacks = lax.optimization_barrier((stack, back_stacks))
-    stacks = [stack] + [turn(stack, s) for s in range(1, nz)]
+    stacks = gather(stack)
+    gate_before = hand(packed[QUAD], 0)
 
     sequence = [pltpu.VMEM((total_rows, HEAD), jnp.bfloat16)] * 2
     stacked = pltpu.VMEM((2 * QUAD, block_rows, HEAD), jnp.bfloat16)
@@ -526,41 +509,31 @@
     query_pieces, key_parts, gate_before = lax.optimization_barrier(
         (query_pieces, key_parts, gate_before)
     )
+    query_pieces = swap(query_pieces)
+    stacks, key_parts, query_pieces = lax.optimization_barrier((stacks, key_parts, query_pieces))
     key_sums = reduce_first(key_parts)
-    query_pieces = swap(query_pieces)
-    def attend(parts, name):
-        return call(
-            functools.partial(forward_kernel, nz, parts),
-            name,
-            [bf16(rows, width)] * len(parts),
-            [SMEM] + [VMEM] * (len(parts) + nz),
-            stretch_order,
-            *[queries[d] for d in parts],
-            *stacks,
-            scratch=sequence
-            + [
-                pltpu.VMEM((2 * len(parts), block_rows, HEAD), jnp.bfloat16),
-                pltpu.VMEM((2 * len(parts), block_rows, HEAD), jnp.float32),
-                gap,
-            ],
-        )
-
-    far = attend((2, 3), "forward_far")
-    far, query_pieces, key_sums = lax.optimization_barrier((far, query_pieces, key_sums))
-    far = [hand(piece, d) for d, piece in zip((2, 3), far)]
-    far, stacks = lax.optimization_barrier((far, stacks))
-    near = attend((0, 1), "forward_near")
-    near = [hand(piece, d) for d, piece in zip((0, 1), near)]
+    parts = tuple(range(QUAD))
+    attended = call(
+        functools.partial(forward_kernel, nz, parts),
+        "forward",
+        [bf16(rows, width)] * QUAD,
+        [SMEM] + [VMEM] * (QUAD + nz),
+        stretch_order,
+        *queries,
+        *stacks,
+        scratch=sequence
+        + [stacked, pltpu.VMEM((2 * QUAD, block_rows, HEAD), jnp.float32), gap],
+    )
+    attended, key_up = lax.optimization_barrier((attended, key_sums[0]))
     (handed,) = call(
         gate_kernel,
         "gate",
         [bf16(*gate_fwd.shape)],
         [VMEM] * (QUAD + 1),
-        *near,
-        *far,
+        *[hand(attended[d], d) for d in range(QUAD)],
         gate_before,
     )
-    key_sums = reduce_rest(key_parts, *key_sums)
+    key_sums = reduce_rest(key_parts, key_up, key_sums[1])
     key_pieces = swap(
         call(
             sum_kernel,

time: 103 us -> 93.5 us (0.908)
  waiting for transfers between devices: 36.2 us -> 26.5 us
  starting transfers between devices: 37.2 us -> 36 us
    ppermute x5, waiting for transfers between devices: 9.77 us -> 0.6 us  [hand(): return lax.ppermute(block, ('ctx', 'pipe'), route)]
    ppermute x9, starting transfers between devices: 22.9 us -> 17.2 us  [turn(): lax.ppermute(block, 'ctx', [(i, (i + s * QUAD) % devices) for i in range(...]
    ppermute x9, waiting for transfers between devices: 20.5 us -> 16.3 us  [turn(): lax.ppermute(block, 'ctx', [(i, (i + s * QUAD) % devices) for i in range(...]
    ppermute x12 -> x15, waiting for transfers between devices: 5.88 us -> 9.55 us  [swap(): lax.ppermute(pieces[d], 'ctx', [(i, i ^ d) for i in range(devices)])]
    ppermute x12 -> x15, starting transfers between devices: 8.79 us -> 12.3 us  [swap(): lax.ppermute(pieces[d], 'ctx', [(i, i ^ d) for i in range(devices)])]
    pallas_call x10 -> x11, Pallas kernels: 28.9 us -> 29 us  [call(): pl.pallas_call(kernel, name=name, out_shape=out_shape, in_specs=specs, ou...]
  transfers between devices with their start and end apart: 26 -> 29, of which waited for: 12 -> 14; matrix products, arithmetic and copies ran while one was open for 0% -> 0% of each run, Pallas kernels for 25% -> 28%
where the time goes in v5:
time: 93.5 us; the launch traced here: 93.2 us
  starting transfers between devices  36 us (39%)
  Pallas kernels  29 us (31%)
  waiting for transfers between devices  26.5 us (28%)
    pallas_call x11, Pallas kernels, call(): pl.pallas_call(kernel, name=name, out_shape=out_shape, in_specs=specs, ou...  29 us
    ppermute x9, starting transfers between devices, turn(): lax.ppermute(block, 'ctx', [(i, (i + s * QUAD) % devices) for i in range(...  17.2 us
    ppermute x9, waiting for transfers between devices, turn(): lax.ppermute(block, 'ctx', [(i, (i + s * QUAD) % devices) for i in range(...  16.3 us
    ppermute x15, starting transfers between devices, swap(): lax.ppermute(pieces[d], 'ctx', [(i, i ^ d) for i in range(devices)])  12.3 us
    ppermute x15, waiting for transfers between devices, swap(): lax.ppermute(pieces[d], 'ctx', [(i, i ^ d) for i in range(devices)])  9.55 us
    ppermute x5, starting transfers between devices, hand(): return lax.ppermute(block, ('ctx', 'pipe'), route)  6.5 us
  transfers between devices with their start and end apart: 29, of which 14 were waited for; matrix products, arithmetic and copies ran while one was open for 0% of the time, Pallas kernels for 28%

profile of v5, /device:TPU:0, one launch (start us, length us, event | category | flops | bytes accessed | tf_op | source)
XLA Modules:
  0.0 93.2 jit_solution(1581127900283707394)
XLA Ops:
  0.6 2.0 %pack_keys_bwd.1 = (bf16[128,256]{1,0:T(8,128)(2,1)}, bf16[128,256]{1,0:T(8,128)(2,1)}, bf16[128,256]{1,0:T(8,128)(2,1)}, bf16[128,256]{1,0:T(8,128)(2,1)}) custom-call(bf16[1,128,512]{2,1,0:T(8,128)(2,1)} %key_ref.2, bf16[1,128,512]{2,1,0:T(8,128)(2,1)} %value_ref.2, s32[1,128]{1,0:T(1,128)} %types_ref.2, bf16[1,64,512]{2,1,0:T(8,128)(2,1)} %table_ref.3), custom_call_target="tpu_custom_call" | custom-call | bytes 590336 | tf_op jit(solution)/shard_map/pack_keys_bwd/pallas_call | solution.py:344
  2.6 0.5 collective-permute-start
  3.1 2.6 %collective-permute-start.1 = (bf16[128,256]{1,0:T(8,128)(2,1)}, bf16[128,256]{1,0:T(8,128)(2,1)S(1)}, u32[]{:S(2)}, u32[]{:S(2)}) collective-permute-start(bf16[128,256]{1,0:T(8,128)(2,1)} %get-tuple-element.88), channel_id=1, source_target_pairs={{0,4},{2,6},{4,0},{6,2},{8,12},{10,14},{12,8},{14,10},{16,20},{18,... | collective-permute-start | bytes 196616 | tf_op jit(solution)/shard_map/ppermute | solution.py:386
  5.7 0.1 collective-permute-start.2
  5.8 3.8 %pack_queries.1 = (bf16[128,1536]{1,0:T(8,128)(2,1)}, bf16[128,1536]{1,0:T(8,128)(2,1)}, bf16[128,1536]{1,0:T(8,128)(2,1)}, bf16[128,1536]{1,0:T(8,128)(2,1)}, bf16[144,2048]{1,0:T(8,128)(2,1)}) custom-call(bf16[1,128,2048]{2,1,0:T(8,128)(2,1)} %query_ref.1, bf16[1,128,2048]{2,1,0:T(8,128)(2,1)} %grad_ref.1, bf16[1,128,2048]{2,1,0:T(8,128)(2,1)} %forward_ref.1, ...), custom_call_target="tpu_custom_call" | custom-call | bytes 4268032 | tf_op jit(solution)/shard_map/pack_queries/pallas_call | solution.py:344
  9.6 0.4 collective-permute-done.2.refs_3_
  10.0 0.4 stack_keys_bwd.1.refs_4_
  10.4 0.0 copy-start
  10.4 1.6 %collective-permute-start.3 = (bf16[512,256]{1,0:T(8,128)(2,1)S(1)}, bf16[512,256]{1,0:T(8,128)(2,1)S(1)}, u32[]{:S(2)}, u32[]{:S(2)}) collective-permute-start(bf16[512,256]{1,0:T(8,128)(2,1)S(1)} %stack_keys_bwd.1.refs_4_), channel_id=1, source_target_pairs={{0,8},{2,10},{4,12},{6,14},{8,16},{10,18},{12,20},{14,22},{16,24},... | collective-permute-start | bytes 786440 | tf_op jit(solution)/shard_map/ppermute | solution.py:391
  12.1 2.6 %collective-permute-start.4 = (bf16[512,256]{1,0:T(8,128)(2,1)S(1)}, bf16[512,256]{1,0:T(8,128)(2,1)S(1)}, u32[]{:S(2)}, u32[]{:S(2)}) collective-permute-start(bf16[512,256]{1,0:T(8,128)(2,1)S(1)} %stack_keys_bwd.1.refs_4_), channel_id=1, source_target_pairs={{0,16},{2,18},{4,20},{6,22},{8,24},{10,26},{12,28},{14,30},{16,0},... | collective-permute-start | bytes 786440 | tf_op jit(solution)/shard_map/ppermute | solution.py:391
  14.6 1.4 %collective-permute-start.5 = (bf16[512,256]{1,0:T(8,128)(2,1)S(1)}, bf16[512,256]{1,0:T(8,128)(2,1)S(1)}, u32[]{:S(2)}, u32[]{:S(2)}) collective-permute-start(bf16[512,256]{1,0:T(8,128)(2,1)S(1)} %stack_keys_bwd.1.refs_4_), channel_id=1, source_target_pairs={{0,24},{2,26},{4,28},{6,30},{8,0},{10,2},{12,4},{14,6},{16,8},{18,... | collective-permute-start | bytes 786440 | tf_op jit(solution)/shard_map/ppermute | solution.py:391
  16.0 2.0 %pack_keys_fwd.1 = (bf16[128,256]{1,0:T(8,128)(2,1)}, bf16[128,256]{1,0:T(8,128)(2,1)}, bf16[128,256]{1,0:T(8,128)(2,1)}, bf16[128,256]{1,0:T(8,128)(2,1)}) custom-call(bf16[1,128,512]{2,1,0:T(8,128)(2,1)} %key_ref.3, bf16[1,128,512]{2,1,0:T(8,128)(2,1)} %value_ref.3, s32[1,128]{1,0:T(1,128)} %types_ref.3, bf16[1,64,512]{2,1,0:T(8,128)(2,1)} %table_ref.3), custom_call_target="tpu_custom_call" | custom-call | bytes 590336 | tf_op jit(solution)/shard_map/pack_keys_fwd/pallas_call | solution.py:344
  18.0 0.1 collective-permute-start.7
  18.0 1.4 %collective-permute-start.8 = (bf16[128,256]{1,0:T(8,128)(2,1)}, bf16[128,256]{1,0:T(8,128)(2,1)S(1)}, u32[]{:S(2)}, u32[]{:S(2)}) collective-permute-start(bf16[128,256]{1,0:T(8,128)(2,1)} %get-tuple-element.104), channel_id=1, source_target_pairs={{0,4},{2,6},{4,0},{6,2},{8,12},{10,14},{12,8},{14,10},{16,20},{18,... | collective-permute-start | bytes 196616 | tf_op jit(solution)/shard_map/ppermute | solution.py:386
  19.4 0.0 collective-permute-done.7.refs_1_
  19.5 1.1 %collective-permute-start.9 = (bf16[128,256]{1,0:T(8,128)(2,1)}, bf16[128,256]{1,0:T(8,128)(2,1)S(1)}, u32[]{:S(2)}, u32[]{:S(2)}) collective-permute-start(bf16[128,256]{1,0:T(8,128)(2,1)} %get-tuple-element.105), channel_id=1, source_target_pairs={{0,6},{2,4},{4,2},{6,0},{8,14},{10,12},{12,10},{14,8},{16,22},{18,... | collective-permute-start | bytes 196616 | tf_op jit(solution)/shard_map/ppermute | solution.py:386
  20.6 2.3 %collective-permute-done.8.refs_2_ = bf16[128,256]{1,0:T(8,128)(2,1)S(1)} collective-permute-done((bf16[128,256]{1,0:T(8,128)(2,1)}, bf16[128,256]{1,0:T(8,128)(2,1)S(1)}, u32[]{:S(2)}, u32[]{:S(2)}) %collective-permute-start.8) | collective-permute-done | bytes 65568 | tf_op jit(solution)/shard_map/ppermute | solution.py:386
  22.9 1.0 %collective-permute-done.9.refs_3_ = bf16[128,256]{1,0:T(8,128)(2,1)S(1)} collective-permute-done((bf16[128,256]{1,0:T(8,128)(2,1)}, bf16[128,256]{1,0:T(8,128)(2,1)S(1)}, u32[]{:S(2)}, u32[]{:S(2)}) %collective-permute-start.9) | collective-permute-done | bytes 65568 | tf_op jit(solution)/shard_map/ppermute | solution.py:386
  23.9 1.4 %collective-permute-start.10 = (bf16[128,1536]{1,0:T(8,128)(2,1)}, bf16[128,1536]{1,0:T(8,128)(2,1)S(1)}, u32[]{:S(2)}, u32[]{:S(2)}) collective-permute-start(bf16[128,1536]{1,0:T(8,128)(2,1)} %get-tuple-element.108), channel_id=1, source_target_pairs={{0,4},{2,6},{4,0},{6,2},{8,12},{10,14},{12,8},{14,10},{16,20},{18,... | collective-permute-start | bytes 1179656 | tf_op jit(solution)/shard_map/ppermute | solution.py:386
  25.3 0.4 collective-permute-start.11
  25.6 6.5 %collective-permute-done.4.refs_6_ = bf16[512,256]{1,0:T(8,128)(2,1)S(1)} collective-permute-done((bf16[512,256]{1,0:T(8,128)(2,1)S(1)}, bf16[512,256]{1,0:T(8,128)(2,1)S(1)}, u32[]{:S(2)}, u32[]{:S(2)}) %collective-permute-start.4) | collective-permute-done | bytes 262176 | tf_op jit(solution)/shard_map/ppermute | solution.py:391
  32.1 0.0 collective-permute-start.6
  32.1 1.6 %collective-permute-start.15 = (bf16[144,2048]{1,0:T(8,128)(2,1)}, bf16[144,2048]{1,0:T(8,128)(2,1)S(1)}, u32[]{:S(2)}, u32[]{:S(2)}) collective-permute-start(bf16[144,2048]{1,0:T(8,128)(2,1)} %get-tuple-element.131), channel_id=1, source_target_pairs={{0,1},{1,0},{2,3},{3,2},{4,5},{5,4},{6,7},{7,6},{8,9},{9,8},{10,11... | collective-permute-start | bytes 1769480 | tf_op jit(solution)/shard_map/ppermute | solution.py:402
  33.7 0.8 copy-done.1
  34.6 0.4 stack_keys_fwd.1.refs_4_
  34.9 6.1 %collective-permute-start.12 = (bf16[512,256]{1,0:T(8,128)(2,1)S(1)}, bf16[512,256]{1,0:T(8,128)(2,1)S(1)}, u32[]{:S(2)}, u32[]{:S(2)}) collective-permute-start(bf16[512,256]{1,0:T(8,128)(2,1)S(1)} %stack_keys_fwd.1.refs_4_), channel_id=1, source_target_pairs={{0,8},{2,10},{4,12},{6,14},{8,16},{10,18},{12,20},{14,22},{16,24},... | collective-permute-start | bytes 786440 | tf_op jit(solution)/shard_map/ppermute | solution.py:391
  41.0 1.6 %collective-permute-start.13 = (bf16[512,256]{1,0:T(8,128)(2,1)S(1)}, bf16[512,256]{1,0:T(8,128)(2,1)S(1)}, u32[]{:S(2)}, u32[]{:S(2)}) collective-permute-start(bf16[512,256]{1,0:T(8,128)(2,1)S(1)} %stack_keys_fwd.1.refs_4_), channel_id=1, source_target_pairs={{0,16},{2,18},{4,20},{6,22},{8,24},{10,26},{12,28},{14,30},{16,0},... | collective-permute-start | bytes 786440 | tf_op jit(solution)/shard_map/ppermute | solution.py:391
  42.6 0.7 collective-permute-done.11.refs_3_
  43.4 0.1 collective-permute-start.14
  43.5 0.0 collective-permute-done.6.refs_1_
  43.5 12.8 %backward.1 = (bf16[128,512]{1,0:T(8,128)(2,1)S(1)}, bf16[128,512]{1,0:T(8,128)(2,1)S(1)}, bf16[128,512]{1,0:T(8,128)(2,1)S(1)}, bf16[128,512]{1,0:T(8,128)(2,1)...) custom-call(s32[1,32]{1,0:T(1,128)S(1)} %copy-done.3, ...), custom_call_target="tpu_custom_call" | custom-call | flops 3019898880 | bytes 4194432 | tf_op jit(solution)/shard_map/backward/pallas_call | solution.py:344
  56.3 0.0 collective-permute-done.15.refs_4_
  56.3 0.7 collective-permute-start.16
  57.0 1.3 %collective-permute-start.17 = (bf16[128,512]{1,0:T(8,128)(2,1)S(1)}, bf16[128,512]{1,0:T(8,128)(2,1)S(1)}, u32[]{:S(2)}, u32[]{:S(2)}) collective-permute-start(bf16[128,512]{1,0:T(8,128)(2,1)S(1)} %get-tuple-element.138), channel_id=1, source_target_pairs={{0,4},{2,6},{4,0},{6,2},{8,12},{10,14},{12,8},{14,10},{16,20},{18,... | collective-permute-start | bytes 393224 | tf_op jit(solution)/shard_map/ppermute | solution.py:386
  58.3 0.0 collective-permute-done.12.refs_5_
  58.3 0.1 collective-permute-start.18
  58.4 1.7 %collective-permute-done.13.refs_6_ = bf16[512,256]{1,0:T(8,128)(2,1)S(1)} collective-permute-done((bf16[512,256]{1,0:T(8,128)(2,1)S(1)}, bf16[512,256]{1,0:T(8,128)(2,1)S(1)}, u32[]{:S(2)}, u32[]{:S(2)}) %collective-permute-start.13) | collective-permute-done | bytes 262176 | tf_op jit(solution)/shard_map/ppermute | solution.py:391
  60.1 0.0 collective-permute-done.14.refs_7_
  60.1 3.2 %collective-permute-done.17.refs_2_ = bf16[128,512]{1,0:T(8,128)(2,1)S(1)} collective-permute-done((bf16[128,512]{1,0:T(8,128)(2,1)S(1)}, bf16[128,512]{1,0:T(8,128)(2,1)S(1)}, u32[]{:S(2)}, u32[]{:S(2)}) %collective-permute-start.17) | collective-permute-done | bytes 131104 | tf_op jit(solution)/shard_map/ppermute | solution.py:386
  63.3 1.1 %collective-permute-done.18.refs_3_ = bf16[128,512]{1,0:T(8,128)(2,1)S(1)} collective-permute-done((bf16[128,512]{1,0:T(8,128)(2,1)S(1)}, bf16[128,512]{1,0:T(8,128)(2,1)S(1)}, u32[]{:S(2)}, u32[]{:S(2)}) %collective-permute-start.18) | collective-permute-done | bytes 131104 | tf_op jit(solution)/shard_map/ppermute | solution.py:386
  64.4 1.8 %collective-permute-start.19 = (bf16[512,256]{1,0:T(8,128)(2,1)S(1)}, bf16[512,256]{1,0:T(8,128)(2,1)S(1)}, u32[]{:S(2)}, u32[]{:S(2)}) collective-permute-start(bf16[512,256]{1,0:T(8,128)(2,1)S(1)} %get-tuple-element.148), channel_id=1, source_target_pairs={{0,8},{2,10},{4,12},{6,14},{8,16},{10,18},{12,20},{14,22},{16,24},... | collective-permute-start | bytes 786440 | tf_op jit(solution)/shard_map/ppermute | solution.py:391
  66.2 2.0 %collective-permute-start.25 = (bf16[512,256]{1,0:T(8,128)(2,1)S(1)}, bf16[512,256]{1,0:T(8,128)(2,1)S(1)}, u32[]{:S(2)}, u32[]{:S(2)}) collective-permute-start(bf16[512,256]{1,0:T(8,128)(2,1)S(1)} %get-tuple-element.161), channel_id=1, source_target_pairs={{0,24},{2,26},{4,28},{6,30},{8,0},{10,2},{12,4},{14,6},{16,8},{18,... | collective-permute-start | bytes 786440 | tf_op jit(solution)/shard_map/ppermute | solution.py:391
  68.2 4.9 %forward.1 = (bf16[128,512]{1,0:T(8,128)(2,1)S(1)}, bf16[128,512]{1,0:T(8,128)(2,1)S(1)}, bf16[128,512]{1,0:T(8,128)(2,1)S(1)}, bf16[128,512]{1,0:T(8,128)(2,1)S(1)}) custom-call(s32[1,32]{1,0:T(1,128)S(1)} %copy-done.3, bf16[128,1536]{1,0:T(8,128)(2,1)S(1)} %copy-done, bf16[128,1536]{1,0:T(8,128)(2,1)S(1)} %collective-permute-done.6.refs_1_, ...), custom_call_target="tpu_custom_call" | custom-call | bytes 3145856 | tf_op jit(solution)/shard_map/forward/pallas_call | solution.py:344
  73.1 2.3 %collective-permute-done.19 = bf16[512,256]{1,0:T(8,128)(2,1)S(1)} collective-permute-done((bf16[512,256]{1,0:T(8,128)(2,1)S(1)}, bf16[512,256]{1,0:T(8,128)(2,1)S(1)}, u32[]{:S(2)}, u32[]{:S(2)}) %collective-permute-start.19) | collective-permute-done | bytes 262176 | tf_op jit(solution)/shard_map/ppermute | solution.py:391
  75.4 0.1 add_convert_fusion
  75.5 0.1 collective-permute-start.24
  75.5 1.6 %collective-permute-start.20 = (bf16[128,512]{1,0:T(8,128)(2,1)S(1)}, bf16[128,512]{1,0:T(8,128)(2,1)S(1)}, u32[]{:S(2)}, u32[]{:S(2)}) collective-permute-start(bf16[128,512]{1,0:T(8,128)(2,1)S(1)} %get-tuple-element.149), channel_id=1, source_target_pairs={{0,1},{1,0},{2,3},{3,2},{4,5},{5,4},{6,7},{7,6},{8,9},{9,8},{10,11... | collective-permute-start | bytes 393224 | tf_op jit(solution)/shard_map/ppermute | solution.py:402
  77.1 0.0 collective-permute-start.21
  77.1 1.7 %collective-permute-start.22 = (bf16[128,512]{1,0:T(8,128)(2,1)S(1)}, bf16[128,512]{1,0:T(8,128)(2,1)S(1)}, u32[]{:S(2)}, u32[]{:S(2)}) collective-permute-start(bf16[128,512]{1,0:T(8,128)(2,1)S(1)} %get-tuple-element.151), channel_id=1, source_target_pairs={{0,5},{1,4},{2,7},{3,6},{4,1},{5,0},{6,3},{7,2},{8,13},{9,12},{10,... | collective-permute-start | bytes 393224 | tf_op jit(solution)/shard_map/ppermute | solution.py:402
  78.8 1.6 %collective-permute-done.25.refs_2_ = bf16[512,256]{1,0:T(8,128)(2,1)S(1)} collective-permute-done((bf16[512,256]{1,0:T(8,128)(2,1)S(1)}, bf16[512,256]{1,0:T(8,128)(2,1)S(1)}, u32[]{:S(2)}, u32[]{:S(2)}) %collective-permute-start.25) | collective-permute-done | bytes 262176 | tf_op jit(solution)/shard_map/ppermute | solution.py:391
  80.4 1.6 %collective-permute-start.23 = (bf16[128,512]{1,0:T(8,128)(2,1)S(1)}, bf16[128,512]{1,0:T(8,128)(2,1)S(1)}, u32[]{:S(2)}, u32[]{:S(2)}) collective-permute-start(bf16[128,512]{1,0:T(8,128)(2,1)S(1)} %get-tuple-element.152), channel_id=1, source_target_pairs={{0,7},{1,6},{2,5},{3,4},{4,3},{5,2},{6,1},{7,0},{8,15},{9,14},{10,... | collective-permute-start | bytes 393224 | tf_op jit(solution)/shard_map/ppermute | solution.py:402
  82.0 4.3 %collective-permute-done.24.refs_1_ = bf16[512,256]{1,0:T(8,128)(2,1)S(1)} collective-permute-done((bf16[512,256]{1,0:T(8,128)(2,1)S(1)}, bf16[512,256]{1,0:T(8,128)(2,1)S(1)}, u32[]{:S(2)}, u32[]{:S(2)}) %collective-permute-start.24) | collective-permute-done | bytes 262176 | tf_op jit(solution)/shard_map/ppermute | solution.py:391
  86.4 0.1 sum_key_parts.1
  86.5 0.1 collective-permute-start.26
  86.5 0.1 collective-permute-done.20.refs_0_
  86.6 1.4 %collective-permute-start.27 = (bf16[128,256]{1,0:T(8,128)(2,1)S(1)}, bf16[128,256]{1,0:T(8,128)(2,1)S(1)}, u32[]{:S(2)}, u32[]{:S(2)}) collective-permute-start(bf16[128,256]{1,0:T(8,128)(2,1)S(1)} %get-tuple-element.164), channel_id=1, source_target_pairs={{0,4},{2,6},{4,0},{6,2},{8,12},{10,14},{12,8},{14,10},{16,20},{18,... | collective-permute-start | bytes 196616 | tf_op jit(solution)/shard_map/ppermute | solution.py:386
  88.0 0.5 collective-permute-done.21.refs_1_
  88.5 1.3 %collective-permute-start.28 = (bf16[128,256]{1,0:T(8,128)(2,1)S(1)}, bf16[128,256]{1,0:T(8,128)(2,1)S(1)}, u32[]{:S(2)}, u32[]{:S(2)}) collective-permute-start(bf16[128,256]{1,0:T(8,128)(2,1)S(1)} %get-tuple-element.165), channel_id=1, source_target_pairs={{0,6},{2,4},{4,2},{6,0},{8,14},{10,12},{12,10},{14,8},{16,22},{18,... | collective-permute-start | bytes 196616 | tf_op jit(solution)/shard_map/ppermute | solution.py:386
  89.8 0.8 query_grad.1
  90.6 0.0 collective-permute-done.22.refs_2_
  90.6 1.2 %gate.1 = bf16[1,128,2048]{2,1,0:T(8,128)(2,1)} custom-call(bf16[128,512]{1,0:T(8,128)(2,1)S(1)} %collective-permute-done.20.refs_0_, bf16[128,512]{1,0:T(8,128)(2,1)S(1)} %collective-permute-done.21.refs_1_, bf16[128,512]{1,0:T(8,128)(2,1)S(1)} %collective-permute-done.22.refs_2_, bf16[128,512]{1,0:T(8,128)(2,1)S(1)} %collective-permute-done.23.refs_3_, ...), custom_call_target="tpu_custom_call" | custom-call | bytes 1638400 | tf_op jit(solution)/shard_map/gate/pallas_call | solution.py:344
  91.8 0.0 collective-permute-done.26.refs_1_
  91.8 0.7 collective-permute-done.28.refs_3_
  92.5 0.8 key_grad.1
  (16 shorter events, 0.0 us)
Async XLA Ops:
  2.6 7.0 %collective-permute-start = (bf16[128,256]{1,0:T(8,128)(2,1)}, bf16[128,256]{1,0:T(8,128)(2,1)S(1)}, u32[]{:S(2)}, u32[]{:S(2)}) collective-permute-start(bf16[128,256]{1,0:T(8,128)(2,1)} %get-tuple-element.87), channel_id=1, source_target_pairs={{0,2},{2,0},{4,6},{6,4},{8,10},{10,8},{12,14},{14,12},{16,18},{18,... | collective-permute-start | bytes 196616 | tf_op jit(solution)/shard_map/ppermute | solution.py:386
  3.1 6.5 %collective-permute-start.1 = (bf16[128,256]{1,0:T(8,128)(2,1)}, bf16[128,256]{1,0:T(8,128)(2,1)S(1)}, u32[]{:S(2)}, u32[]{:S(2)}) collective-permute-start(bf16[128,256]{1,0:T(8,128)(2,1)} %get-tuple-element.88), channel_id=1, source_target_pairs={{0,4},{2,6},{4,0},{6,2},{8,12},{10,14},{12,8},{14,10},{16,20},{18,... | collective-permute-start | bytes 196616 | tf_op jit(solution)/shard_map/ppermute | solution.py:386
  5.7 4.4 %copy-start.2 = (bf16[128,256]{1,0:T(8,128)(2,1)S(1)}, bf16[128,256]{1,0:T(8,128)(2,1)}, u32[]{:S(2)}) copy-start(bf16[128,256]{1,0:T(8,128)(2,1)} %get-tuple-element.96.refs_0_) | copy-start | bytes 196612
  5.7 4.3 %collective-permute-start.2 = (bf16[128,256]{1,0:T(8,128)(2,1)}, bf16[128,256]{1,0:T(8,128)(2,1)S(1)}, u32[]{:S(2)}, u32[]{:S(2)}) collective-permute-start(bf16[128,256]{1,0:T(8,128)(2,1)} %get-tuple-element.89), channel_id=1, source_target_pairs={{0,6},{2,4},{4,2},{6,0},{8,14},{10,12},{12,10},{14,8},{16,22},{18,... | collective-permute-start | bytes 196616 | tf_op jit(solution)/shard_map/ppermute | solution.py:386
  10.0 22.1 %copy-start.4 = (bf16[128,1536]{1,0:T(8,128)(2,1)S(1)}, bf16[128,1536]{1,0:T(8,128)(2,1)}, u32[]{:S(2)}) copy-start(bf16[128,1536]{1,0:T(8,128)(2,1)} %get-tuple-element.101) | copy-start | bytes 1179652
  10.4 33.0 %copy-start = (bf16[128,1536]{1,0:T(8,128)(2,1)S(1)}, bf16[128,1536]{1,0:T(8,128)(2,1)}, u32[]{:S(2)}) copy-start(bf16[128,1536]{1,0:T(8,128)(2,1)} %get-tuple-element.95.refs_0_) | copy-start | bytes 1179652
  10.4 15.2 %collective-permute-start.3 = (bf16[512,256]{1,0:T(8,128)(2,1)S(1)}, bf16[512,256]{1,0:T(8,128)(2,1)S(1)}, u32[]{:S(2)}, u32[]{:S(2)}) collective-permute-start(bf16[512,256]{1,0:T(8,128)(2,1)S(1)} %stack_keys_bwd.1.refs_4_), channel_id=1, source_target_pairs={{0,8},{2,10},{4,12},{6,14},{8,16},{10,18},{12,20},{14,22},{16,24},... | collective-permute-start | bytes 786440 | tf_op jit(solution)/shard_map/ppermute | solution.py:391
  12.1 20.1 %collective-permute-start.4 = (bf16[512,256]{1,0:T(8,128)(2,1)S(1)}, bf16[512,256]{1,0:T(8,128)(2,1)S(1)}, u32[]{:S(2)}, u32[]{:S(2)}) collective-permute-start(bf16[512,256]{1,0:T(8,128)(2,1)S(1)} %stack_keys_bwd.1.refs_4_), channel_id=1, source_target_pairs={{0,16},{2,18},{4,20},{6,22},{8,24},{10,26},{12,28},{14,30},{16,0},... | collective-permute-start | bytes 786440 | tf_op jit(solution)/shard_map/ppermute | solution.py:391
  14.6 17.5 %collective-permute-start.5 = (bf16[512,256]{1,0:T(8,128)(2,1)S(1)}, bf16[512,256]{1,0:T(8,128)(2,1)S(1)}, u32[]{:S(2)}, u32[]{:S(2)}) collective-permute-start(bf16[512,256]{1,0:T(8,128)(2,1)S(1)} %stack_keys_bwd.1.refs_4_), channel_id=1, source_target_pairs={{0,24},{2,26},{4,28},{6,30},{8,0},{10,2},{12,4},{14,6},{16,8},{18,... | collective-permute-start | bytes 786440 | tf_op jit(solution)/shard_map/ppermute | solution.py:391
  18.0 1.5 %collective-permute-start.7 = (bf16[128,256]{1,0:T(8,128)(2,1)}, bf16[128,256]{1,0:T(8,128)(2,1)S(1)}, u32[]{:S(2)}, u32[]{:S(2)}) collective-permute-start(bf16[128,256]{1,0:T(8,128)(2,1)} %get-tuple-element.103), channel_id=1, source_target_pairs={{0,2},{2,0},{4,6},{6,4},{8,10},{10,8},{12,14},{14,12},{16,18},{18,... | collective-permute-start | bytes 196616 | tf_op jit(solution)/shard_map/ppermute | solution.py:386
  18.0 4.8 %collective-permute-start.8 = (bf16[128,256]{1,0:T(8,128)(2,1)}, bf16[128,256]{1,0:T(8,128)(2,1)S(1)}, u32[]{:S(2)}, u32[]{:S(2)}) collective-permute-start(bf16[128,256]{1,0:T(8,128)(2,1)} %get-tuple-element.104), channel_id=1, source_target_pairs={{0,4},{2,6},{4,0},{6,2},{8,12},{10,14},{12,8},{14,10},{16,20},{18,... | collective-permute-start | bytes 196616 | tf_op jit(solution)/shard_map/ppermute | solution.py:386
  19.5 4.4 %collective-permute-start.9 = (bf16[128,256]{1,0:T(8,128)(2,1)}, bf16[128,256]{1,0:T(8,128)(2,1)S(1)}, u32[]{:S(2)}, u32[]{:S(2)}) collective-permute-start(bf16[128,256]{1,0:T(8,128)(2,1)} %get-tuple-element.105), channel_id=1, source_target_pairs={{0,6},{2,4},{4,2},{6,0},{8,14},{10,12},{12,10},{14,8},{16,22},{18,... | collective-permute-start | bytes 196616 | tf_op jit(solution)/shard_map/ppermute | solution.py:386
  23.9 17.1 %collective-permute-start.10 = (bf16[128,1536]{1,0:T(8,128)(2,1)}, bf16[128,1536]{1,0:T(8,128)(2,1)S(1)}, u32[]{:S(2)}, u32[]{:S(2)}) collective-permute-start(bf16[128,1536]{1,0:T(8,128)(2,1)} %get-tuple-element.108), channel_id=1, source_target_pairs={{0,4},{2,6},{4,0},{6,2},{8,12},{10,14},{12,8},{14,10},{16,20},{18,... | collective-permute-start | bytes 1179656 | tf_op jit(solution)/shard_map/ppermute | solution.py:386
  25.3 18.1 %collective-permute-start.11 = (bf16[128,1536]{1,0:T(8,128)(2,1)}, bf16[128,1536]{1,0:T(8,128)(2,1)S(1)}, u32[]{:S(2)}, u32[]{:S(2)}) collective-permute-start(bf16[128,1536]{1,0:T(8,128)(2,1)} %get-tuple-element.109), channel_id=1, source_target_pairs={{0,6},{2,4},{4,2},{6,0},{8,14},{10,12},{12,10},{14,8},{16,22},{18,... | collective-permute-start | bytes 1179656 | tf_op jit(solution)/shard_map/ppermute | solution.py:386
  32.1 11.3 %collective-permute-start.6 = (bf16[128,1536]{1,0:T(8,128)(2,1)S(1)}, bf16[128,1536]{1,0:T(8,128)(2,1)S(1)}, u32[]{:S(2)}, u32[]{:S(2)}) collective-permute-start(bf16[128,1536]{1,0:T(8,128)(2,1)S(1)} %copy-done.4), channel_id=1, source_target_pairs={{0,2},{2,0},{4,6},{6,4},{8,10},{10,8},{12,14},{14,12},{16,18},{18,... | collective-permute-start | bytes 1179656 | tf_op jit(solution)/shard_map/ppermute | solution.py:386
  32.1 24.1 %collective-permute-start.15 = (bf16[144,2048]{1,0:T(8,128)(2,1)}, bf16[144,2048]{1,0:T(8,128)(2,1)S(1)}, u32[]{:S(2)}, u32[]{:S(2)}) collective-permute-start(bf16[144,2048]{1,0:T(8,128)(2,1)} %get-tuple-element.131), channel_id=1, source_target_pairs={{0,1},{1,0},{2,3},{3,2},{4,5},{5,4},{6,7},{7,6},{8,9},{9,8},{10,11... | collective-permute-start | bytes 1769480 | tf_op jit(solution)/shard_map/ppermute | solution.py:402
  33.7 0.8 copy-start.1
  34.6 8.9 %copy-start.3 = (s32[1,32]{1,0:T(1,128)S(1)}, s32[1,32]{1,0:T(1,128)}, u32[]{:S(2)}) copy-start(s32[1,32]{1,0:T(1,128)} %order_ref.3) | copy-start | bytes 388
  34.9 23.4 %collective-permute-start.12 = (bf16[512,256]{1,0:T(8,128)(2,1)S(1)}, bf16[512,256]{1,0:T(8,128)(2,1)S(1)}, u32[]{:S(2)}, u32[]{:S(2)}) collective-permute-start(bf16[512,256]{1,0:T(8,128)(2,1)S(1)} %stack_keys_fwd.1.refs_4_), channel_id=1, source_target_pairs={{0,8},{2,10},{4,12},{6,14},{8,16},{10,18},{12,20},{14,22},{16,24},... | collective-permute-start | bytes 786440 | tf_op jit(solution)/shard_map/ppermute | solution.py:391
  41.0 19.1 %collective-permute-start.13 = (bf16[512,256]{1,0:T(8,128)(2,1)S(1)}, bf16[512,256]{1,0:T(8,128)(2,1)S(1)}, u32[]{:S(2)}, u32[]{:S(2)}) collective-permute-start(bf16[512,256]{1,0:T(8,128)(2,1)S(1)} %stack_keys_fwd.1.refs_4_), channel_id=1, source_target_pairs={{0,16},{2,18},{4,20},{6,22},{8,24},{10,26},{12,28},{14,30},{16,0},... | collective-permute-start | bytes 786440 | tf_op jit(solution)/shard_map/ppermute | solution.py:391
  43.4 16.7 %collective-permute-start.14 = (bf16[512,256]{1,0:T(8,128)(2,1)S(1)}, bf16[512,256]{1,0:T(8,128)(2,1)S(1)}, u32[]{:S(2)}, u32[]{:S(2)}) collective-permute-start(bf16[512,256]{1,0:T(8,128)(2,1)S(1)} %stack_keys_fwd.1.refs_4_), channel_id=1, source_target_pairs={{0,24},{2,26},{4,28},{6,30},{8,0},{10,2},{12,4},{14,6},{16,8},{18,... | collective-permute-start | bytes 786440 | tf_op jit(solution)/shard_map/ppermute | solution.py:391
  56.3 3.8 %collective-permute-start.16 = (bf16[128,512]{1,0:T(8,128)(2,1)S(1)}, bf16[128,512]{1,0:T(8,128)(2,1)S(1)}, u32[]{:S(2)}, u32[]{:S(2)}) collective-permute-start(bf16[128,512]{1,0:T(8,128)(2,1)S(1)} %get-tuple-element.137), channel_id=1, source_target_pairs={{0,2},{2,0},{4,6},{6,4},{8,10},{10,8},{12,14},{14,12},{16,18},{18,... | collective-permute-start | bytes 393224 | tf_op jit(solution)/shard_map/ppermute | solution.py:386
  57.0 6.4 %collective-permute-start.17 = (bf16[128,512]{1,0:T(8,128)(2,1)S(1)}, bf16[128,512]{1,0:T(8,128)(2,1)S(1)}, u32[]{:S(2)}, u32[]{:S(2)}) collective-permute-start(bf16[128,512]{1,0:T(8,128)(2,1)S(1)} %get-tuple-element.138), channel_id=1, source_target_pairs={{0,4},{2,6},{4,0},{6,2},{8,12},{10,14},{12,8},{14,10},{16,20},{18,... | collective-permute-start | bytes 393224 | tf_op jit(solution)/shard_map/ppermute | solution.py:386
  58.3 6.1 %collective-permute-start.18 = (bf16[128,512]{1,0:T(8,128)(2,1)S(1)}, bf16[128,512]{1,0:T(8,128)(2,1)S(1)}, u32[]{:S(2)}, u32[]{:S(2)}) collective-permute-start(bf16[128,512]{1,0:T(8,128)(2,1)S(1)} %get-tuple-element.139), channel_id=1, source_target_pairs={{0,6},{2,4},{4,2},{6,0},{8,14},{10,12},{12,10},{14,8},{16,22},{18,... | collective-permute-start | bytes 393224 | tf_op jit(solution)/shard_map/ppermute | solution.py:386
  64.4 11.0 %collective-permute-start.19 = (bf16[512,256]{1,0:T(8,128)(2,1)S(1)}, bf16[512,256]{1,0:T(8,128)(2,1)S(1)}, u32[]{:S(2)}, u32[]{:S(2)}) collective-permute-start(bf16[512,256]{1,0:T(8,128)(2,1)S(1)} %get-tuple-element.148), channel_id=1, source_target_pairs={{0,8},{2,10},{4,12},{6,14},{8,16},{10,18},{12,20},{14,22},{16,24},... | collective-permute-start | bytes 786440 | tf_op jit(solution)/shard_map/ppermute | solution.py:391
  66.2 14.2 %collective-permute-start.25 = (bf16[512,256]{1,0:T(8,128)(2,1)S(1)}, bf16[512,256]{1,0:T(8,128)(2,1)S(1)}, u32[]{:S(2)}, u32[]{:S(2)}) collective-permute-start(bf16[512,256]{1,0:T(8,128)(2,1)S(1)} %get-tuple-element.161), channel_id=1, source_target_pairs={{0,24},{2,26},{4,28},{6,30},{8,0},{10,2},{12,4},{14,6},{16,8},{18,... | collective-permute-start | bytes 786440 | tf_op jit(solution)/shard_map/ppermute | solution.py:391
  75.5 10.9 %collective-permute-start.24 = (bf16[512,256]{1,0:T(8,128)(2,1)S(1)}, bf16[512,256]{1,0:T(8,128)(2,1)S(1)}, u32[]{:S(2)}, u32[]{:S(2)}) collective-permute-start(bf16[512,256]{1,0:T(8,128)(2,1)S(1)} %add_convert_fusion), channel_id=1, source_target_pairs={{0,8},{2,10},{4,12},{6,14},{8,16},{10,18},{12,20},{14,22},{16,24},... | collective-permute-start | bytes 786440 | tf_op jit(solution)/shard_map/ppermute | solution.py:391
  75.5 11.1 %collective-permute-start.20 = (bf16[128,512]{1,0:T(8,128)(2,1)S(1)}, bf16[128,512]{1,0:T(8,128)(2,1)S(1)}, u32[]{:S(2)}, u32[]{:S(2)}) collective-permute-start(bf16[128,512]{1,0:T(8,128)(2,1)S(1)} %get-tuple-element.149), channel_id=1, source_target_pairs={{0,1},{1,0},{2,3},{3,2},{4,5},{5,4},{6,7},{7,6},{8,9},{9,8},{10,11... | collective-permute-start | bytes 393224 | tf_op jit(solution)/shard_map/ppermute | solution.py:402
  77.1 11.4 %collective-permute-start.21 = (bf16[128,512]{1,0:T(8,128)(2,1)S(1)}, bf16[128,512]{1,0:T(8,128)(2,1)S(1)}, u32[]{:S(2)}, u32[]{:S(2)}) collective-permute-start(bf16[128,512]{1,0:T(8,128)(2,1)S(1)} %get-tuple-element.150), channel_id=1, source_target_pairs={{0,3},{1,2},{2,1},{3,0},{4,7},{5,6},{6,5},{7,4},{8,11},{9,10},{10,... | collective-permute-start | bytes 393224 | tf_op jit(solution)/shard_map/ppermute | solution.py:402
  77.1 13.5 %collective-permute-start.22 = (bf16[128,512]{1,0:T(8,128)(2,1)S(1)}, bf16[128,512]{1,0:T(8,128)(2,1)S(1)}, u32[]{:S(2)}, u32[]{:S(2)}) collective-permute-start(bf16[128,512]{1,0:T(8,128)(2,1)S(1)} %get-tuple-element.151), channel_id=1, source_target_pairs={{0,5},{1,4},{2,7},{3,6},{4,1},{5,0},{6,3},{7,2},{8,13},{9,12},{10,... | collective-permute-start | bytes 393224 | tf_op jit(solution)/shard_map/ppermute | solution.py:402
  80.4 10.2 %collective-permute-start.23 = (bf16[128,512]{1,0:T(8,128)(2,1)S(1)}, bf16[128,512]{1,0:T(8,128)(2,1)S(1)}, u32[]{:S(2)}, u32[]{:S(2)}) collective-permute-start(bf16[128,512]{1,0:T(8,128)(2,1)S(1)} %get-tuple-element.152), channel_id=1, source_target_pairs={{0,7},{1,6},{2,5},{3,4},{4,3},{5,2},{6,1},{7,0},{8,15},{9,14},{10,... | collective-permute-start | bytes 393224 | tf_op jit(solution)/shard_map/ppermute | solution.py:402
  86.5 5.3 %collective-permute-start.26 = (bf16[128,256]{1,0:T(8,128)(2,1)S(1)}, bf16[128,256]{1,0:T(8,128)(2,1)S(1)}, u32[]{:S(2)}, u32[]{:S(2)}) collective-permute-start(bf16[128,256]{1,0:T(8,128)(2,1)S(1)} %get-tuple-element.163), channel_id=1, source_target_pairs={{0,2},{2,0},{4,6},{6,4},{8,10},{10,8},{12,14},{14,12},{16,18},{18,... | collective-permute-start | bytes 196616 | tf_op jit(solution)/shard_map/ppermute | solution.py:386
  86.6 5.1 %collective-permute-start.27 = (bf16[128,256]{1,0:T(8,128)(2,1)S(1)}, bf16[128,256]{1,0:T(8,128)(2,1)S(1)}, u32[]{:S(2)}, u32[]{:S(2)}) collective-permute-start(bf16[128,256]{1,0:T(8,128)(2,1)S(1)} %get-tuple-element.164), channel_id=1, source_target_pairs={{0,4},{2,6},{4,0},{6,2},{8,12},{10,14},{12,8},{14,10},{16,20},{18,... | collective-permute-start | bytes 196616 | tf_op jit(solution)/shard_map/ppermute | solution.py:386
  88.5 4.0 %collective-permute-start.28 = (bf16[128,256]{1,0:T(8,128)(2,1)S(1)}, bf16[128,256]{1,0:T(8,128)(2,1)S(1)}, u32[]{:S(2)}, u32[]{:S(2)}) collective-permute-start(bf16[128,256]{1,0:T(8,128)(2,1)S(1)} %get-tuple-element.165), channel_id=1, source_target_pairs={{0,6},{2,4},{4,2},{6,0},{8,14},{10,12},{12,10},{14,8},{16,22},{18,... | collective-permute-start | bytes 196616 | tf_op jit(solution)/shard_map/ppermute | solution.py:386

commit v6 on v5

--- a/solution.py
+++ b/solution.py
@@ -9,7 +9,6 @@
 from jax.sharding import PartitionSpec as P
 
 HEAD = 128
-UNROLL = 3
 QUAD = 4
 SCALE = HEAD ** (-0.5)
 EXP2_SCALE = -SCALE / math.log(2.0)
@@ -157,14 +156,14 @@
     return jnp.where(visible, part, 0.0)
 
 
-def repeat(steps, advance):
+def repeat(steps, together, advance):
     def several(i, _):
-        for j in range(UNROLL):
-            advance(i * UNROLL + j)
+        for j in range(together):
+            advance(i * together + j)
         return 0
 
-    lax.fori_loop(0, steps // UNROLL, several, 0)
-    for step in range(steps // UNROLL * UNROLL, steps):
+    lax.fori_loop(0, steps // together, several, 0)
+    for step in range(steps // together * together, steps):
         advance(step)
 
 
@@ -207,7 +206,7 @@
             weights = (raw * sigmoid_of(raw, visible)).astype(jnp.bfloat16)
             total[row] += dot(weights, values[rows, :], NN)
 
-    repeat(steps, advance)
+    repeat(steps, 9, advance)
     for i, d in enumerate(parts):
         for e in range(2):
             shrink = SCALE * shrink_of(stretch_of(order_ref, z, member, d, e), stretch_rows)
@@ -275,7 +274,7 @@
             key_total[rows, :] += dot(score_grad, stacked[row], NN)
             value_total[rows, :] += dot(weights, grads[row], NN)
 
-    repeat(steps, advance)
+    repeat(steps, 3, advance)
     for d in range(QUAD):
         for e in range(2):
             query_grad = (total_t[2 * d + e].T * SCALE).astype(jnp.bfloat16)
@@ -381,11 +380,11 @@
     steps = total_rows // block_rows + 1
     pairs = steps * QUAD * block_rows * block_rows
 
+    def swap_one(piece, d):
+        return lax.ppermute(piece, "ctx", [(i, i ^ d) for i in range(devices)])
+
     def swap(pieces):
-        return [pieces[0]] + [
-            lax.ppermute(pieces[d], "ctx", [(i, i ^ d) for i in range(devices)])
-            for d in range(1, QUAD)
-        ]
+        return [pieces[0]] + [swap_one(pieces[d], d) for d in range(1, QUAD)]
 
     def turn(block, s):
         return lax.ppermute(
@@ -509,8 +508,9 @@
     query_pieces, key_parts, gate_before = lax.optimization_barrier(
         (query_pieces, key_parts, gate_before)
     )
-    query_pieces = swap(query_pieces)
-    stacks, key_parts, query_pieces = lax.optimization_barrier((stacks, key_parts, query_pieces))
+    query_pieces = list(query_pieces)
+    query_pieces[2:] = [swap_one(query_pieces[d], d) for d in range(2, QUAD)]
+    stacks, key_parts = lax.optimization_barrier((stacks, key_parts))
     key_sums = reduce_first(key_parts)
     parts = tuple(range(QUAD))
     attended = call(
@@ -524,7 +524,10 @@
         scratch=sequence
         + [stacked, pltpu.VMEM((2 * QUAD, block_rows, HEAD), jnp.float32), gap],
     )
-    attended, key_up = lax.optimization_barrier((attended, key_sums[0]))
+    attended, key_up, query_pieces = lax.optimization_barrier(
+        (attended, key_sums[0], query_pieces)
+    )
+    query_pieces[1] = swap_one(query_pieces[1], 1)
     (handed,) = call(
         gate_kernel,
         "gate",

time: 93.5 us -> 93.8 us (level)
  starting transfers between devices: 36 us -> 38.7 us
  waiting for transfers between devices: 26.5 us -> 25 us
    ppermute x9, starting transfers between devices: 17.2 us -> 21.5 us  [turn(): lax.ppermute(block, 'ctx', [(i, (i + s * QUAD) % devices) for i in range(...]
    ppermute x15, waiting for transfers between devices: 9.55 us -> 6.6 us  [swap_one(): return lax.ppermute(piece, 'ctx', [(i, i ^ d) for i in range(devices)])]
    ppermute x5, starting transfers between devices: 6.5 us -> 5.13 us  [hand(): return lax.ppermute(block, ('ctx', 'pipe'), route)]
    ppermute x5, waiting for transfers between devices: 0.6 us -> 1.8 us  [hand(): return lax.ppermute(block, ('ctx', 'pipe'), route)]
  transfers between devices with their start and end apart: 29 -> 29, of which waited for: 14 -> 12; matrix products, arithmetic and copies ran while one was open for 0% -> 0% of each run, Pallas kernels for 28% -> 27%
where the time goes in v6:
time: 93.8 us; the launch traced here: 93.6 us
  starting transfers between devices  38.7 us (41%)
  Pallas kernels  28.2 us (30%)
  waiting for transfers between devices  25 us (27%)
    pallas_call x11, Pallas kernels, call(): pl.pallas_call(kernel, name=name, out_shape=out_shape, in_specs=specs, ou...  28.2 us
    ppermute x9, starting transfers between devices, turn(): lax.ppermute(block, 'ctx', [(i, (i + s * QUAD) % devices) for i in range(...  21.5 us
    ppermute x9, waiting for transfers between devices, turn(): lax.ppermute(block, 'ctx', [(i, (i + s * QUAD) % devices) for i in range(...  16.6 us
    ppermute x15, starting transfers between devices, swap_one(): return lax.ppermute(piece, 'ctx', [(i, i ^ d) for i in range(devices)])  12.1 us
    ppermute x15, waiting for transfers between devices, swap_one(): return lax.ppermute(piece, 'ctx', [(i, i ^ d) for i in range(devices)])  6.6 us
    ppermute x5, starting transfers between devices, hand(): return lax.ppermute(block, ('ctx', 'pipe'), route)  5.13 us
  transfers between devices with their start and end apart: 29, of which 12 were waited for; matrix products, arithmetic and copies ran while one was open for 0% of the time, Pallas kernels for 27%

profile of v6, /device:TPU:0, one launch (start us, length us, event | category | flops | bytes accessed | tf_op | source)
XLA Modules:
  0.0 93.6 jit_solution(3632243995405922457)
XLA Ops:
  0.6 2.0 %pack_keys_bwd.1 = (bf16[128,256]{1,0:T(8,128)(2,1)}, bf16[128,256]{1,0:T(8,128)(2,1)}, bf16[128,256]{1,0:T(8,128)(2,1)}, bf16[128,256]{1,0:T(8,128)(2,1)}) custom-call(bf16[1,128,512]{2,1,0:T(8,128)(2,1)} %key_ref.2, bf16[1,128,512]{2,1,0:T(8,128)(2,1)} %value_ref.2, s32[1,128]{1,0:T(1,128)} %types_ref.2, bf16[1,64,512]{2,1,0:T(8,128)(2,1)} %table_ref.3), custom_call_target="tpu_custom_call" | custom-call | bytes 590336 | tf_op jit(solution)/shard_map/pack_keys_bwd/pallas_call | solution.py:343
  2.6 0.5 collective-permute-start
  3.1 2.6 %collective-permute-start.1 = (bf16[128,256]{1,0:T(8,128)(2,1)}, bf16[128,256]{1,0:T(8,128)(2,1)S(1)}, u32[]{:S(2)}, u32[]{:S(2)}) collective-permute-start(bf16[128,256]{1,0:T(8,128)(2,1)} %get-tuple-element.88), channel_id=1, source_target_pairs={{0,4},{2,6},{4,0},{6,2},{8,12},{10,14},{12,8},{14,10},{16,20},{18,... | collective-permute-start | bytes 196616 | tf_op jit(solution)/shard_map/ppermute | solution.py:384
  5.7 0.1 collective-permute-start.2
  5.8 3.8 %pack_queries.1 = (bf16[128,1536]{1,0:T(8,128)(2,1)}, bf16[128,1536]{1,0:T(8,128)(2,1)}, bf16[128,1536]{1,0:T(8,128)(2,1)}, bf16[128,1536]{1,0:T(8,128)(2,1)}, bf16[144,2048]{1,0:T(8,128)(2,1)}) custom-call(bf16[1,128,2048]{2,1,0:T(8,128)(2,1)} %query_ref.1, bf16[1,128,2048]{2,1,0:T(8,128)(2,1)} %grad_ref.1, bf16[1,128,2048]{2,1,0:T(8,128)(2,1)} %forward_ref.1, ...), custom_call_target="tpu_custom_call" | custom-call | bytes 4268032 | tf_op jit(solution)/shard_map/pack_queries/pallas_call | solution.py:343
  9.6 0.0 collective-permute-done.refs_1_
  9.6 0.0 collective-permute-done.1.refs_2_
  9.6 0.4 collective-permute-done.2.refs_3_
  10.0 0.4 stack_keys_bwd.1.refs_4_
  10.4 0.0 copy-start
  10.4 1.6 %collective-permute-start.3 = (bf16[512,256]{1,0:T(8,128)(2,1)S(1)}, bf16[512,256]{1,0:T(8,128)(2,1)S(1)}, u32[]{:S(2)}, u32[]{:S(2)}) collective-permute-start(bf16[512,256]{1,0:T(8,128)(2,1)S(1)} %stack_keys_bwd.1.refs_4_), channel_id=1, source_target_pairs={{0,8},{2,10},{4,12},{6,14},{8,16},{10,18},{12,20},{14,22},{16,24},... | collective-permute-start | bytes 786440 | tf_op jit(solution)/shard_map/ppermute | solution.py:390
  12.1 2.6 %collective-permute-start.4 = (bf16[512,256]{1,0:T(8,128)(2,1)S(1)}, bf16[512,256]{1,0:T(8,128)(2,1)S(1)}, u32[]{:S(2)}, u32[]{:S(2)}) collective-permute-start(bf16[512,256]{1,0:T(8,128)(2,1)S(1)} %stack_keys_bwd.1.refs_4_), channel_id=1, source_target_pairs={{0,16},{2,18},{4,20},{6,22},{8,24},{10,26},{12,28},{14,30},{16,0},... | collective-permute-start | bytes 786440 | tf_op jit(solution)/shard_map/ppermute | solution.py:390
  14.6 1.4 %collective-permute-start.5 = (bf16[512,256]{1,0:T(8,128)(2,1)S(1)}, bf16[512,256]{1,0:T(8,128)(2,1)S(1)}, u32[]{:S(2)}, u32[]{:S(2)}) collective-permute-start(bf16[512,256]{1,0:T(8,128)(2,1)S(1)} %stack_keys_bwd.1.refs_4_), channel_id=1, source_target_pairs={{0,24},{2,26},{4,28},{6,30},{8,0},{10,2},{12,4},{14,6},{16,8},{18,... | collective-permute-start | bytes 786440 | tf_op jit(solution)/shard_map/ppermute | solution.py:390
  16.0 2.0 %pack_keys_fwd.1 = (bf16[128,256]{1,0:T(8,128)(2,1)}, bf16[128,256]{1,0:T(8,128)(2,1)}, bf16[128,256]{1,0:T(8,128)(2,1)}, bf16[128,256]{1,0:T(8,128)(2,1)}) custom-call(bf16[1,128,512]{2,1,0:T(8,128)(2,1)} %key_ref.3, bf16[1,128,512]{2,1,0:T(8,128)(2,1)} %value_ref.3, s32[1,128]{1,0:T(1,128)} %types_ref.3, bf16[1,64,512]{2,1,0:T(8,128)(2,1)} %table_ref.3), custom_call_target="tpu_custom_call" | custom-call | bytes 590336 | tf_op jit(solution)/shard_map/pack_keys_fwd/pallas_call | solution.py:343
  18.0 0.1 collective-permute-start.7
  18.0 1.4 %collective-permute-start.8 = (bf16[128,256]{1,0:T(8,128)(2,1)}, bf16[128,256]{1,0:T(8,128)(2,1)S(1)}, u32[]{:S(2)}, u32[]{:S(2)}) collective-permute-start(bf16[128,256]{1,0:T(8,128)(2,1)} %get-tuple-element.104), channel_id=1, source_target_pairs={{0,4},{2,6},{4,0},{6,2},{8,12},{10,14},{12,8},{14,10},{16,20},{18,... | collective-permute-start | bytes 196616 | tf_op jit(solution)/shard_map/ppermute | solution.py:384
  19.4 0.0 collective-permute-done.7.refs_1_
  19.5 1.1 %collective-permute-start.9 = (bf16[128,256]{1,0:T(8,128)(2,1)}, bf16[128,256]{1,0:T(8,128)(2,1)S(1)}, u32[]{:S(2)}, u32[]{:S(2)}) collective-permute-start(bf16[128,256]{1,0:T(8,128)(2,1)} %get-tuple-element.105), channel_id=1, source_target_pairs={{0,6},{2,4},{4,2},{6,0},{8,14},{10,12},{12,10},{14,8},{16,22},{18,... | collective-permute-start | bytes 196616 | tf_op jit(solution)/shard_map/ppermute | solution.py:384
  20.6 2.3 %collective-permute-done.8.refs_2_ = bf16[128,256]{1,0:T(8,128)(2,1)S(1)} collective-permute-done((bf16[128,256]{1,0:T(8,128)(2,1)}, bf16[128,256]{1,0:T(8,128)(2,1)S(1)}, u32[]{:S(2)}, u32[]{:S(2)}) %collective-permute-start.8) | collective-permute-done | bytes 65568 | tf_op jit(solution)/shard_map/ppermute | solution.py:384
  22.9 1.0 %collective-permute-done.9.refs_3_ = bf16[128,256]{1,0:T(8,128)(2,1)S(1)} collective-permute-done((bf16[128,256]{1,0:T(8,128)(2,1)}, bf16[128,256]{1,0:T(8,128)(2,1)S(1)}, u32[]{:S(2)}, u32[]{:S(2)}) %collective-permute-start.9) | collective-permute-done | bytes 65568 | tf_op jit(solution)/shard_map/ppermute | solution.py:384
  23.9 1.4 %collective-permute-start.10 = (bf16[128,1536]{1,0:T(8,128)(2,1)}, bf16[128,1536]{1,0:T(8,128)(2,1)S(1)}, u32[]{:S(2)}, u32[]{:S(2)}) collective-permute-start(bf16[128,1536]{1,0:T(8,128)(2,1)} %get-tuple-element.108), channel_id=1, source_target_pairs={{0,4},{2,6},{4,0},{6,2},{8,12},{10,14},{12,8},{14,10},{16,20},{18,... | collective-permute-start | bytes 1179656 | tf_op jit(solution)/shard_map/ppermute | solution.py:384
  25.3 0.4 collective-permute-start.11
  25.6 0.0 collective-permute-done.3.refs_5_
  25.6 6.5 %collective-permute-done.4.refs_6_ = bf16[512,256]{1,0:T(8,128)(2,1)S(1)} collective-permute-done((bf16[512,256]{1,0:T(8,128)(2,1)S(1)}, bf16[512,256]{1,0:T(8,128)(2,1)S(1)}, u32[]{:S(2)}, u32[]{:S(2)}) %collective-permute-start.4) | collective-permute-done | bytes 262176 | tf_op jit(solution)/shard_map/ppermute | solution.py:390
  32.1 0.0 collective-permute-done.5.refs_7_
  32.1 1.6 %collective-permute-start.15 = (bf16[144,2048]{1,0:T(8,128)(2,1)}, bf16[144,2048]{1,0:T(8,128)(2,1)S(1)}, u32[]{:S(2)}, u32[]{:S(2)}) collective-permute-start(bf16[144,2048]{1,0:T(8,128)(2,1)} %get-tuple-element.131), channel_id=1, source_target_pairs={{0,1},{1,0},{2,3},{3,2},{4,5},{5,4},{6,7},{7,6},{8,9},{9,8},{10,11... | collective-permute-start | bytes 1769480 | tf_op jit(solution)/shard_map/ppermute | solution.py:401
  33.7 0.8 copy-done.1
  34.6 0.4 stack_keys_fwd.1.refs_4_
  34.9 6.1 %collective-permute-start.12 = (bf16[512,256]{1,0:T(8,128)(2,1)S(1)}, bf16[512,256]{1,0:T(8,128)(2,1)S(1)}, u32[]{:S(2)}, u32[]{:S(2)}) collective-permute-start(bf16[512,256]{1,0:T(8,128)(2,1)S(1)} %stack_keys_fwd.1.refs_4_), channel_id=1, source_target_pairs={{0,8},{2,10},{4,12},{6,14},{8,16},{10,18},{12,20},{14,22},{16,24},... | collective-permute-start | bytes 786440 | tf_op jit(solution)/shard_map/ppermute | solution.py:390
  41.0 0.0 collective-permute-done.10.refs_2_
  41.0 1.6 %collective-permute-start.13 = (bf16[512,256]{1,0:T(8,128)(2,1)S(1)}, bf16[512,256]{1,0:T(8,128)(2,1)S(1)}, u32[]{:S(2)}, u32[]{:S(2)}) collective-permute-start(bf16[512,256]{1,0:T(8,128)(2,1)S(1)} %stack_keys_fwd.1.refs_4_), channel_id=1, source_target_pairs={{0,16},{2,18},{4,20},{6,22},{8,24},{10,26},{12,28},{14,30},{16,0},... | collective-permute-start | bytes 786440 | tf_op jit(solution)/shard_map/ppermute | solution.py:390
  42.6 0.7 collective-permute-done.11.refs_3_
  43.4 0.1 collective-permute-start.14
  43.5 0.0 collective-permute-done.6.refs_1_
  43.5 12.8 %backward.1 = (bf16[128,512]{1,0:T(8,128)(2,1)S(1)}, bf16[128,512]{1,0:T(8,128)(2,1)S(1)}, bf16[128,512]{1,0:T(8,128)(2,1)S(1)}, bf16[128,512]{1,0:T(8,128)(2,1)...) custom-call(s32[1,32]{1,0:T(1,128)S(1)} %copy-done.3, ...), custom_call_target="tpu_custom_call" | custom-call | flops 3019898880 | bytes 4194432 | tf_op jit(solution)/shard_map/backward/pallas_call | solution.py:343
  56.3 0.0 collective-permute-done.12.refs_5_
  56.3 3.8 %collective-permute-done.13.refs_6_ = bf16[512,256]{1,0:T(8,128)(2,1)S(1)} collective-permute-done((bf16[512,256]{1,0:T(8,128)(2,1)S(1)}, bf16[512,256]{1,0:T(8,128)(2,1)S(1)}, u32[]{:S(2)}, u32[]{:S(2)}) %collective-permute-start.13) | collective-permute-done | bytes 262176 | tf_op jit(solution)/shard_map/ppermute | solution.py:390
  60.1 6.1 %collective-permute-start.16 = (bf16[512,256]{1,0:T(8,128)(2,1)S(1)}, bf16[512,256]{1,0:T(8,128)(2,1)S(1)}, u32[]{:S(2)}, u32[]{:S(2)}) collective-permute-start(bf16[512,256]{1,0:T(8,128)(2,1)S(1)} %get-tuple-element.144), channel_id=1, source_target_pairs={{0,8},{2,10},{4,12},{6,14},{8,16},{10,18},{12,20},{14,22},{16,24},... | collective-permute-start | bytes 786440 | tf_op jit(solution)/shard_map/ppermute | solution.py:390
  66.1 1.5 %collective-permute-start.17 = (bf16[128,512]{1,0:T(8,128)(2,1)S(1)}, bf16[128,512]{1,0:T(8,128)(2,1)S(1)}, u32[]{:S(2)}, u32[]{:S(2)}) collective-permute-start(bf16[128,512]{1,0:T(8,128)(2,1)S(1)} %get-tuple-element.147), channel_id=1, source_target_pairs={{0,4},{2,6},{4,0},{6,2},{8,12},{10,14},{12,8},{14,10},{16,20},{18,... | collective-permute-start | bytes 393224 | tf_op jit(solution)/shard_map/ppermute | solution.py:384
  67.7 0.0 collective-permute-start.18
  67.7 0.7 collective-permute-start.25
  68.4 4.1 %forward.1 = (bf16[128,512]{1,0:T(8,128)(2,1)S(1)}, bf16[128,512]{1,0:T(8,128)(2,1)S(1)}, bf16[128,512]{1,0:T(8,128)(2,1)S(1)}, bf16[128,512]{1,0:T(8,128)(2,1)S(1)}) custom-call(s32[1,32]{1,0:T(1,128)S(1)} %copy-done.3, bf16[128,1536]{1,0:T(8,128)(2,1)S(1)} %copy-done, bf16[128,1536]{1,0:T(8,128)(2,1)S(1)} %collective-permute-done.6.refs_1_, ...), custom_call_target="tpu_custom_call" | custom-call | bytes 3145856 | tf_op jit(solution)/shard_map/forward/pallas_call | solution.py:343
  72.5 1.0 %collective-permute-done.18.refs_3_ = bf16[128,512]{1,0:T(8,128)(2,1)S(1)} collective-permute-done((bf16[128,512]{1,0:T(8,128)(2,1)S(1)}, bf16[128,512]{1,0:T(8,128)(2,1)S(1)}, u32[]{:S(2)}, u32[]{:S(2)}) %collective-permute-start.18) | collective-permute-done | bytes 131104 | tf_op jit(solution)/shard_map/ppermute | solution.py:384
  73.4 0.6 collective-permute-done.16
  74.1 0.1 add_convert_fusion
  74.1 1.3 %collective-permute-start.24 = (bf16[512,256]{1,0:T(8,128)(2,1)S(1)}, bf16[512,256]{1,0:T(8,128)(2,1)S(1)}, u32[]{:S(2)}, u32[]{:S(2)}) collective-permute-start(bf16[512,256]{1,0:T(8,128)(2,1)S(1)} %add_convert_fusion), channel_id=1, source_target_pairs={{0,8},{2,10},{4,12},{6,14},{8,16},{10,18},{12,20},{14,22},{16,24},... | collective-permute-start | bytes 786440 | tf_op jit(solution)/shard_map/ppermute | solution.py:390
  75.4 0.0 collective-permute-start.23
  75.4 0.5 collective-permute-start.19
  75.9 1.4 %collective-permute-start.20 = (bf16[128,512]{1,0:T(8,128)(2,1)S(1)}, bf16[128,512]{1,0:T(8,128)(2,1)S(1)}, u32[]{:S(2)}, u32[]{:S(2)}) collective-permute-start(bf16[128,512]{1,0:T(8,128)(2,1)S(1)} %get-tuple-element.150), channel_id=1, source_target_pairs={{0,3},{1,2},{2,1},{3,0},{4,7},{5,6},{6,5},{7,4},{8,11},{9,10},{10,... | collective-permute-start | bytes 393224 | tf_op jit(solution)/shard_map/ppermute | solution.py:401
  77.3 1.5 %collective-permute-done.25.refs_2_ = bf16[512,256]{1,0:T(8,128)(2,1)S(1)} collective-permute-done((bf16[512,256]{1,0:T(8,128)(2,1)S(1)}, bf16[512,256]{1,0:T(8,128)(2,1)S(1)}, u32[]{:S(2)}, u32[]{:S(2)}) %collective-permute-start.25) | collective-permute-done | bytes 262176 | tf_op jit(solution)/shard_map/ppermute | solution.py:390
  78.8 1.4 %collective-permute-start.21 = (bf16[128,512]{1,0:T(8,128)(2,1)S(1)}, bf16[128,512]{1,0:T(8,128)(2,1)S(1)}, u32[]{:S(2)}, u32[]{:S(2)}) collective-permute-start(bf16[128,512]{1,0:T(8,128)(2,1)S(1)} %get-tuple-element.151), channel_id=1, source_target_pairs={{0,5},{1,4},{2,7},{3,6},{4,1},{5,0},{6,3},{7,2},{8,13},{9,12},{10,... | collective-permute-start | bytes 393224 | tf_op jit(solution)/shard_map/ppermute | solution.py:401
  80.1 4.2 %collective-permute-done.24.refs_1_ = bf16[512,256]{1,0:T(8,128)(2,1)S(1)} collective-permute-done((bf16[512,256]{1,0:T(8,128)(2,1)S(1)}, bf16[512,256]{1,0:T(8,128)(2,1)S(1)}, u32[]{:S(2)}, u32[]{:S(2)}) %collective-permute-start.24) | collective-permute-done | bytes 262176 | tf_op jit(solution)/shard_map/ppermute | solution.py:390
  84.4 0.3 collective-permute-start.22
  84.7 0.1 sum_key_parts.1
  84.8 0.0 collective-permute-done.23.refs_1_
  84.8 1.3 %collective-permute-start.26 = (bf16[128,256]{1,0:T(8,128)(2,1)S(1)}, bf16[128,256]{1,0:T(8,128)(2,1)S(1)}, u32[]{:S(2)}, u32[]{:S(2)}) collective-permute-start(bf16[128,256]{1,0:T(8,128)(2,1)S(1)} %get-tuple-element.163), channel_id=1, source_target_pairs={{0,2},{2,0},{4,6},{6,4},{8,10},{10,8},{12,14},{14,12},{16,18},{18,... | collective-permute-start | bytes 196616 | tf_op jit(solution)/shard_map/ppermute | solution.py:384
  86.1 0.0 collective-permute-done.19.refs_0_
  86.1 0.6 collective-permute-start.27
  86.6 1.3 %collective-permute-start.28 = (bf16[128,256]{1,0:T(8,128)(2,1)S(1)}, bf16[128,256]{1,0:T(8,128)(2,1)S(1)}, u32[]{:S(2)}, u32[]{:S(2)}) collective-permute-start(bf16[128,256]{1,0:T(8,128)(2,1)S(1)} %get-tuple-element.165), channel_id=1, source_target_pairs={{0,6},{2,4},{4,2},{6,0},{8,14},{10,12},{12,10},{14,8},{16,22},{18,... | collective-permute-start | bytes 196616 | tf_op jit(solution)/shard_map/ppermute | solution.py:384
  87.9 0.8 query_grad.1
  88.7 1.8 %collective-permute-done.22.refs_3_ = bf16[128,512]{1,0:T(8,128)(2,1)S(1)} collective-permute-done((bf16[128,512]{1,0:T(8,128)(2,1)S(1)}, bf16[128,512]{1,0:T(8,128)(2,1)S(1)}, u32[]{:S(2)}, u32[]{:S(2)}) %collective-permute-start.22) | collective-permute-done | bytes 131104 | tf_op jit(solution)/shard_map/ppermute | solution.py:401
  90.5 1.2 %gate.1 = bf16[1,128,2048]{2,1,0:T(8,128)(2,1)} custom-call(bf16[128,512]{1,0:T(8,128)(2,1)S(1)} %collective-permute-done.19.refs_0_, bf16[128,512]{1,0:T(8,128)(2,1)S(1)} %collective-permute-done.20.refs_1_, bf16[128,512]{1,0:T(8,128)(2,1)S(1)} %collective-permute-done.21.refs_2_, bf16[128,512]{1,0:T(8,128)(2,1)S(1)} %collective-permute-done.22.refs_3_, ...), custom_call_target="tpu_custom_call" | custom-call | bytes 1638400 | tf_op jit(solution)/shard_map/gate/pallas_call | solution.py:343
  91.7 1.1 %collective-permute-done.28.refs_3_ = bf16[128,256]{1,0:T(8,128)(2,1)S(1)} collective-permute-done((bf16[128,256]{1,0:T(8,128)(2,1)S(1)}, bf16[128,256]{1,0:T(8,128)(2,1)S(1)}, u32[]{:S(2)}, u32[]{:S(2)}) %collective-permute-start.28) | collective-permute-done | bytes 65568 | tf_op jit(solution)/shard_map/ppermute | solution.py:384
  92.8 0.8 key_grad.1
  (16 shorter events, 0.0 us)
Async XLA Ops:
  2.6 7.0 %collective-permute-start = (bf16[128,256]{1,0:T(8,128)(2,1)}, bf16[128,256]{1,0:T(8,128)(2,1)S(1)}, u32[]{:S(2)}, u32[]{:S(2)}) collective-permute-start(bf16[128,256]{1,0:T(8,128)(2,1)} %get-tuple-element.87), channel_id=1, source_target_pairs={{0,2},{2,0},{4,6},{6,4},{8,10},{10,8},{12,14},{14,12},{16,18},{18,... | collective-permute-start | bytes 196616 | tf_op jit(solution)/shard_map/ppermute | solution.py:384
  3.1 6.5 %collective-permute-start.1 = (bf16[128,256]{1,0:T(8,128)(2,1)}, bf16[128,256]{1,0:T(8,128)(2,1)S(1)}, u32[]{:S(2)}, u32[]{:S(2)}) collective-permute-start(bf16[128,256]{1,0:T(8,128)(2,1)} %get-tuple-element.88), channel_id=1, source_target_pairs={{0,4},{2,6},{4,0},{6,2},{8,12},{10,14},{12,8},{14,10},{16,20},{18,... | collective-permute-start | bytes 196616 | tf_op jit(solution)/shard_map/ppermute | solution.py:384
  5.7 4.4 %copy-start.2 = (bf16[128,256]{1,0:T(8,128)(2,1)S(1)}, bf16[128,256]{1,0:T(8,128)(2,1)}, u32[]{:S(2)}) copy-start(bf16[128,256]{1,0:T(8,128)(2,1)} %get-tuple-element.96.refs_0_) | copy-start | bytes 196612
  5.7 4.3 %collective-permute-start.2 = (bf16[128,256]{1,0:T(8,128)(2,1)}, bf16[128,256]{1,0:T(8,128)(2,1)S(1)}, u32[]{:S(2)}, u32[]{:S(2)}) collective-permute-start(bf16[128,256]{1,0:T(8,128)(2,1)} %get-tuple-element.89), channel_id=1, source_target_pairs={{0,6},{2,4},{4,2},{6,0},{8,14},{10,12},{12,10},{14,8},{16,22},{18,... | collective-permute-start | bytes 196616 | tf_op jit(solution)/shard_map/ppermute | solution.py:384
  10.0 22.1 %copy-start.4 = (bf16[128,1536]{1,0:T(8,128)(2,1)S(1)}, bf16[128,1536]{1,0:T(8,128)(2,1)}, u32[]{:S(2)}) copy-start(bf16[128,1536]{1,0:T(8,128)(2,1)} %get-tuple-element.101) | copy-start | bytes 1179652
  10.4 33.0 %copy-start = (bf16[128,1536]{1,0:T(8,128)(2,1)S(1)}, bf16[128,1536]{1,0:T(8,128)(2,1)}, u32[]{:S(2)}) copy-start(bf16[128,1536]{1,0:T(8,128)(2,1)} %get-tuple-element.95.refs_0_) | copy-start | bytes 1179652
  10.4 15.2 %collective-permute-start.3 = (bf16[512,256]{1,0:T(8,128)(2,1)S(1)}, bf16[512,256]{1,0:T(8,128)(2,1)S(1)}, u32[]{:S(2)}, u32[]{:S(2)}) collective-permute-start(bf16[512,256]{1,0:T(8,128)(2,1)S(1)} %stack_keys_bwd.1.refs_4_), channel_id=1, source_target_pairs={{0,8},{2,10},{4,12},{6,14},{8,16},{10,18},{12,20},{14,22},{16,24},... | collective-permute-start | bytes 786440 | tf_op jit(solution)/shard_map/ppermute | solution.py:390
  12.1 20.1 %collective-permute-start.4 = (bf16[512,256]{1,0:T(8,128)(2,1)S(1)}, bf16[512,256]{1,0:T(8,128)(2,1)S(1)}, u32[]{:S(2)}, u32[]{:S(2)}) collective-permute-start(bf16[512,256]{1,0:T(8,128)(2,1)S(1)} %stack_keys_bwd.1.refs_4_), channel_id=1, source_target_pairs={{0,16},{2,18},{4,20},{6,22},{8,24},{10,26},{12,28},{14,30},{16,0},... | collective-permute-start | bytes 786440 | tf_op jit(solution)/shard_map/ppermute | solution.py:390
  14.6 17.5 %collective-permute-start.5 = (bf16[512,256]{1,0:T(8,128)(2,1)S(1)}, bf16[512,256]{1,0:T(8,128)(2,1)S(1)}, u32[]{:S(2)}, u32[]{:S(2)}) collective-permute-start(bf16[512,256]{1,0:T(8,128)(2,1)S(1)} %stack_keys_bwd.1.refs_4_), channel_id=1, source_target_pairs={{0,24},{2,26},{4,28},{6,30},{8,0},{10,2},{12,4},{14,6},{16,8},{18,... | collective-permute-start | bytes 786440 | tf_op jit(solution)/shard_map/ppermute | solution.py:390
  18.0 1.5 %collective-permute-start.7 = (bf16[128,256]{1,0:T(8,128)(2,1)}, bf16[128,256]{1,0:T(8,128)(2,1)S(1)}, u32[]{:S(2)}, u32[]{:S(2)}) collective-permute-start(bf16[128,256]{1,0:T(8,128)(2,1)} %get-tuple-element.103), channel_id=1, source_target_pairs={{0,2},{2,0},{4,6},{6,4},{8,10},{10,8},{12,14},{14,12},{16,18},{18,... | collective-permute-start | bytes 196616 | tf_op jit(solution)/shard_map/ppermute | solution.py:384
  18.0 4.8 %collective-permute-start.8 = (bf16[128,256]{1,0:T(8,128)(2,1)}, bf16[128,256]{1,0:T(8,128)(2,1)S(1)}, u32[]{:S(2)}, u32[]{:S(2)}) collective-permute-start(bf16[128,256]{1,0:T(8,128)(2,1)} %get-tuple-element.104), channel_id=1, source_target_pairs={{0,4},{2,6},{4,0},{6,2},{8,12},{10,14},{12,8},{14,10},{16,20},{18,... | collective-permute-start | bytes 196616 | tf_op jit(solution)/shard_map/ppermute | solution.py:384
  19.5 4.4 %collective-permute-start.9 = (bf16[128,256]{1,0:T(8,128)(2,1)}, bf16[128,256]{1,0:T(8,128)(2,1)S(1)}, u32[]{:S(2)}, u32[]{:S(2)}) collective-permute-start(bf16[128,256]{1,0:T(8,128)(2,1)} %get-tuple-element.105), channel_id=1, source_target_pairs={{0,6},{2,4},{4,2},{6,0},{8,14},{10,12},{12,10},{14,8},{16,22},{18,... | collective-permute-start | bytes 196616 | tf_op jit(solution)/shard_map/ppermute | solution.py:384
  23.9 17.1 %collective-permute-start.10 = (bf16[128,1536]{1,0:T(8,128)(2,1)}, bf16[128,1536]{1,0:T(8,128)(2,1)S(1)}, u32[]{:S(2)}, u32[]{:S(2)}) collective-permute-start(bf16[128,1536]{1,0:T(8,128)(2,1)} %get-tuple-element.108), channel_id=1, source_target_pairs={{0,4},{2,6},{4,0},{6,2},{8,12},{10,14},{12,8},{14,10},{16,20},{18,... | collective-permute-start | bytes 1179656 | tf_op jit(solution)/shard_map/ppermute | solution.py:384
  25.3 18.1 %collective-permute-start.11 = (bf16[128,1536]{1,0:T(8,128)(2,1)}, bf16[128,1536]{1,0:T(8,128)(2,1)S(1)}, u32[]{:S(2)}, u32[]{:S(2)}) collective-permute-start(bf16[128,1536]{1,0:T(8,128)(2,1)} %get-tuple-element.109), channel_id=1, source_target_pairs={{0,6},{2,4},{4,2},{6,0},{8,14},{10,12},{12,10},{14,8},{16,22},{18,... | collective-permute-start | bytes 1179656 | tf_op jit(solution)/shard_map/ppermute | solution.py:384
  32.1 11.3 %collective-permute-start.6 = (bf16[128,1536]{1,0:T(8,128)(2,1)S(1)}, bf16[128,1536]{1,0:T(8,128)(2,1)S(1)}, u32[]{:S(2)}, u32[]{:S(2)}) collective-permute-start(bf16[128,1536]{1,0:T(8,128)(2,1)S(1)} %copy-done.4), channel_id=1, source_target_pairs={{0,2},{2,0},{4,6},{6,4},{8,10},{10,8},{12,14},{14,12},{16,18},{18,... | collective-permute-start | bytes 1179656 | tf_op jit(solution)/shard_map/ppermute | solution.py:384
  32.1 24.1 %collective-permute-start.15 = (bf16[144,2048]{1,0:T(8,128)(2,1)}, bf16[144,2048]{1,0:T(8,128)(2,1)S(1)}, u32[]{:S(2)}, u32[]{:S(2)}) collective-permute-start(bf16[144,2048]{1,0:T(8,128)(2,1)} %get-tuple-element.131), channel_id=1, source_target_pairs={{0,1},{1,0},{2,3},{3,2},{4,5},{5,4},{6,7},{7,6},{8,9},{9,8},{10,11... | collective-permute-start | bytes 1769480 | tf_op jit(solution)/shard_map/ppermute | solution.py:401
  33.7 0.8 copy-start.1
  34.6 8.9 %copy-start.3 = (s32[1,32]{1,0:T(1,128)S(1)}, s32[1,32]{1,0:T(1,128)}, u32[]{:S(2)}) copy-start(s32[1,32]{1,0:T(1,128)} %order_ref.3) | copy-start | bytes 388
  34.9 21.4 %collective-permute-start.12 = (bf16[512,256]{1,0:T(8,128)(2,1)S(1)}, bf16[512,256]{1,0:T(8,128)(2,1)S(1)}, u32[]{:S(2)}, u32[]{:S(2)}) collective-permute-start(bf16[512,256]{1,0:T(8,128)(2,1)S(1)} %stack_keys_fwd.1.refs_4_), channel_id=1, source_target_pairs={{0,8},{2,10},{4,12},{6,14},{8,16},{10,18},{12,20},{14,22},{16,24},... | collective-permute-start | bytes 786440 | tf_op jit(solution)/shard_map/ppermute | solution.py:390
  41.0 19.1 %collective-permute-start.13 = (bf16[512,256]{1,0:T(8,128)(2,1)S(1)}, bf16[512,256]{1,0:T(8,128)(2,1)S(1)}, u32[]{:S(2)}, u32[]{:S(2)}) collective-permute-start(bf16[512,256]{1,0:T(8,128)(2,1)S(1)} %stack_keys_fwd.1.refs_4_), channel_id=1, source_target_pairs={{0,16},{2,18},{4,20},{6,22},{8,24},{10,26},{12,28},{14,30},{16,0},... | collective-permute-start | bytes 786440 | tf_op jit(solution)/shard_map/ppermute | solution.py:390
  43.4 16.7 %collective-permute-start.14 = (bf16[512,256]{1,0:T(8,128)(2,1)S(1)}, bf16[512,256]{1,0:T(8,128)(2,1)S(1)}, u32[]{:S(2)}, u32[]{:S(2)}) collective-permute-start(bf16[512,256]{1,0:T(8,128)(2,1)S(1)} %stack_keys_fwd.1.refs_4_), channel_id=1, source_target_pairs={{0,24},{2,26},{4,28},{6,30},{8,0},{10,2},{12,4},{14,6},{16,8},{18,... | collective-permute-start | bytes 786440 | tf_op jit(solution)/shard_map/ppermute | solution.py:390
  60.1 14.0 %collective-permute-start.16 = (bf16[512,256]{1,0:T(8,128)(2,1)S(1)}, bf16[512,256]{1,0:T(8,128)(2,1)S(1)}, u32[]{:S(2)}, u32[]{:S(2)}) collective-permute-start(bf16[512,256]{1,0:T(8,128)(2,1)S(1)} %get-tuple-element.144), channel_id=1, source_target_pairs={{0,8},{2,10},{4,12},{6,14},{8,16},{10,18},{12,20},{14,22},{16,24},... | collective-permute-start | bytes 786440 | tf_op jit(solution)/shard_map/ppermute | solution.py:390
  66.1 6.3 %collective-permute-start.17 = (bf16[128,512]{1,0:T(8,128)(2,1)S(1)}, bf16[128,512]{1,0:T(8,128)(2,1)S(1)}, u32[]{:S(2)}, u32[]{:S(2)}) collective-permute-start(bf16[128,512]{1,0:T(8,128)(2,1)S(1)} %get-tuple-element.147), channel_id=1, source_target_pairs={{0,4},{2,6},{4,0},{6,2},{8,12},{10,14},{12,8},{14,10},{16,20},{18,... | collective-permute-start | bytes 393224 | tf_op jit(solution)/shard_map/ppermute | solution.py:384
  67.7 5.8 %collective-permute-start.18 = (bf16[128,512]{1,0:T(8,128)(2,1)S(1)}, bf16[128,512]{1,0:T(8,128)(2,1)S(1)}, u32[]{:S(2)}, u32[]{:S(2)}) collective-permute-start(bf16[128,512]{1,0:T(8,128)(2,1)S(1)} %get-tuple-element.148), channel_id=1, source_target_pairs={{0,6},{2,4},{4,2},{6,0},{8,14},{10,12},{12,10},{14,8},{16,22},{18,... | collective-permute-start | bytes 393224 | tf_op jit(solution)/shard_map/ppermute | solution.py:384
  67.7 11.1 %collective-permute-start.25 = (bf16[512,256]{1,0:T(8,128)(2,1)S(1)}, bf16[512,256]{1,0:T(8,128)(2,1)S(1)}, u32[]{:S(2)}, u32[]{:S(2)}) collective-permute-start(bf16[512,256]{1,0:T(8,128)(2,1)S(1)} %get-tuple-element.161), channel_id=1, source_target_pairs={{0,24},{2,26},{4,28},{6,30},{8,0},{10,2},{12,4},{14,6},{16,8},{18,... | collective-permute-start | bytes 786440 | tf_op jit(solution)/shard_map/ppermute | solution.py:390
  74.1 10.2 %collective-permute-start.24 = (bf16[512,256]{1,0:T(8,128)(2,1)S(1)}, bf16[512,256]{1,0:T(8,128)(2,1)S(1)}, u32[]{:S(2)}, u32[]{:S(2)}) collective-permute-start(bf16[512,256]{1,0:T(8,128)(2,1)S(1)} %add_convert_fusion), channel_id=1, source_target_pairs={{0,8},{2,10},{4,12},{6,14},{8,16},{10,18},{12,20},{14,22},{16,24},... | collective-permute-start | bytes 786440 | tf_op jit(solution)/shard_map/ppermute | solution.py:390
  75.4 9.3 %collective-permute-start.23 = (bf16[128,512]{1,0:T(8,128)(2,1)S(1)}, bf16[128,512]{1,0:T(8,128)(2,1)S(1)}, u32[]{:S(2)}, u32[]{:S(2)}) collective-permute-start(bf16[128,512]{1,0:T(8,128)(2,1)S(1)} %get-tuple-element.155), channel_id=1, source_target_pairs={{0,2},{2,0},{4,6},{6,4},{8,10},{10,8},{12,14},{14,12},{16,18},{18,... | collective-permute-start | bytes 393224 | tf_op jit(solution)/shard_map/ppermute | solution.py:384
  75.4 10.6 %collective-permute-start.19 = (bf16[128,512]{1,0:T(8,128)(2,1)S(1)}, bf16[128,512]{1,0:T(8,128)(2,1)S(1)}, u32[]{:S(2)}, u32[]{:S(2)}) collective-permute-start(bf16[128,512]{1,0:T(8,128)(2,1)S(1)} %get-tuple-element.149), channel_id=1, source_target_pairs={{0,1},{1,0},{2,3},{3,2},{4,5},{5,4},{6,7},{7,6},{8,9},{9,8},{10,11... | collective-permute-start | bytes 393224 | tf_op jit(solution)/shard_map/ppermute | solution.py:401
  75.9 10.7 %collective-permute-start.20 = (bf16[128,512]{1,0:T(8,128)(2,1)S(1)}, bf16[128,512]{1,0:T(8,128)(2,1)S(1)}, u32[]{:S(2)}, u32[]{:S(2)}) collective-permute-start(bf16[128,512]{1,0:T(8,128)(2,1)S(1)} %get-tuple-element.150), channel_id=1, source_target_pairs={{0,3},{1,2},{2,1},{3,0},{4,7},{5,6},{6,5},{7,4},{8,11},{9,10},{10,... | collective-permute-start | bytes 393224 | tf_op jit(solution)/shard_map/ppermute | solution.py:401
  78.8 10.0 %collective-permute-start.21 = (bf16[128,512]{1,0:T(8,128)(2,1)S(1)}, bf16[128,512]{1,0:T(8,128)(2,1)S(1)}, u32[]{:S(2)}, u32[]{:S(2)}) collective-permute-start(bf16[128,512]{1,0:T(8,128)(2,1)S(1)} %get-tuple-element.151), channel_id=1, source_target_pairs={{0,5},{1,4},{2,7},{3,6},{4,1},{5,0},{6,3},{7,2},{8,13},{9,12},{10,... | collective-permute-start | bytes 393224 | tf_op jit(solution)/shard_map/ppermute | solution.py:401
  84.4 6.2 %collective-permute-start.22 = (bf16[128,512]{1,0:T(8,128)(2,1)S(1)}, bf16[128,512]{1,0:T(8,128)(2,1)S(1)}, u32[]{:S(2)}, u32[]{:S(2)}) collective-permute-start(bf16[128,512]{1,0:T(8,128)(2,1)S(1)} %get-tuple-element.152), channel_id=1, source_target_pairs={{0,7},{1,6},{2,5},{3,4},{4,3},{5,2},{6,1},{7,0},{8,15},{9,14},{10,... | collective-permute-start | bytes 393224 | tf_op jit(solution)/shard_map/ppermute | solution.py:401
  84.8 6.9 %collective-permute-start.26 = (bf16[128,256]{1,0:T(8,128)(2,1)S(1)}, bf16[128,256]{1,0:T(8,128)(2,1)S(1)}, u32[]{:S(2)}, u32[]{:S(2)}) collective-permute-start(bf16[128,256]{1,0:T(8,128)(2,1)S(1)} %get-tuple-element.163), channel_id=1, source_target_pairs={{0,2},{2,0},{4,6},{6,4},{8,10},{10,8},{12,14},{14,12},{16,18},{18,... | collective-permute-start | bytes 196616 | tf_op jit(solution)/shard_map/ppermute | solution.py:384
  86.1 5.6 %collective-permute-start.27 = (bf16[128,256]{1,0:T(8,128)(2,1)S(1)}, bf16[128,256]{1,0:T(8,128)(2,1)S(1)}, u32[]{:S(2)}, u32[]{:S(2)}) collective-permute-start(bf16[128,256]{1,0:T(8,128)(2,1)S(1)} %get-tuple-element.164), channel_id=1, source_target_pairs={{0,4},{2,6},{4,0},{6,2},{8,12},{10,14},{12,8},{14,10},{16,20},{18,... | collective-permute-start | bytes 196616 | tf_op jit(solution)/shard_map/ppermute | solution.py:384
  86.6 6.2 %collective-permute-start.28 = (bf16[128,256]{1,0:T(8,128)(2,1)S(1)}, bf16[128,256]{1,0:T(8,128)(2,1)S(1)}, u32[]{:S(2)}, u32[]{:S(2)}) collective-permute-start(bf16[128,256]{1,0:T(8,128)(2,1)S(1)} %get-tuple-element.165), channel_id=1, source_target_pairs={{0,6},{2,4},{4,2},{6,0},{8,14},{10,12},{12,10},{14,8},{16,22},{18,... | collective-permute-start | bytes 196616 | tf_op jit(solution)/shard_map/ppermute | solution.py:384

commit v7 on v6

--- a/solution.py
+++ b/solution.py
@@ -424,6 +424,14 @@
     def gather(stack):
         return [stack] + [turn(stack, s) for s in range(1, nz)]
 
+    def gather_ring(up):
+        down = [ring_down(up[0])]
+        while len(up) <= ahead:
+            up.append(ring_up(up[-1]))
+        while len(up) + len(down) < nz:
+            down.append(ring_down(down[-1]))
+        return up + down[::-1]
+
     def pack(key, value, types, name):
         return call(
             pack_keys,
@@ -456,6 +464,9 @@
         )[0]
 
     back_pieces = swap(pack(key_bwd, value_bwd, types_bwd, "pack_keys_bwd"))
+    pieces = pack(key_fwd, value_fwd, types_fwd, "pack_keys_fwd")
+    back_pieces, pieces = lax.optimization_barrier((back_pieces, pieces))
+    pieces = swap(pieces)
     packed = call(
         pack_queries,
         "pack_queries",
@@ -469,14 +480,16 @@
         scratch=[pltpu.SemaphoreType.DMA((3 * QUAD + 1,))],
         vmem=60,
     )
-    back_pieces, packed = lax.optimization_barrier((back_pieces, list(packed)))
-    back_stacks = gather(stacked_keys(back_pieces, "stack_keys_bwd"))
-    pieces = swap(pack(key_fwd, value_fwd, types_fwd, "pack_keys_fwd"))
-    pieces, packed[2:QUAD] = lax.optimization_barrier((pieces, packed[2:QUAD]))
-    back_stacks, packed[1] = lax.optimization_barrier((back_stacks, packed[1]))
+    packed = list(packed)
+    back_stack = stacked_keys(back_pieces, "stack_keys_bwd")
+    up = [back_stack, ring_up(back_stack)]
+    up, pieces, packed = lax.optimization_barrier((up, pieces, packed))
+    back_stacks = gather_ring(up)
+    stack = stacked_keys(pieces, "stack_keys_fwd")
+    back_stacks, stack, packed[1], packed[QUAD] = lax.optimization_barrier(
+        (back_stacks, stack, packed[1], packed[QUAD])
+    )
     queries = swap(packed[:QUAD])
-    stack = stacked_keys(pieces, "stack_keys_fwd")
-    stack, back_stacks = lax.optimization_barrier((stack, back_stacks))
     stacks = gather(stack)
     gate_before = hand(packed[QUAD], 0)
 
@@ -527,13 +540,15 @@
     attended, key_up, query_pieces = lax.optimization_barrier(
         (attended, key_sums[0], query_pieces)
     )
+    attended = [hand(attended[d], d) for d in range(QUAD)]
+    attended[0], query_pieces[1] = lax.optimization_barrier((attended[0], query_pieces[1]))
     query_pieces[1] = swap_one(query_pieces[1], 1)
     (handed,) = call(
         gate_kernel,
         "gate",
         [bf16(*gate_fwd.shape)],
         [VMEM] * (QUAD + 1),
-        *[hand(attended[d], d) for d in range(QUAD)],
+        *attended,
         gate_before,
     )
     key_sums = reduce_rest(key_parts, key_up, key_sums[1])

time: 93.8 us -> 89.7 us (0.956)
  starting transfers between devices: 38.7 us -> 32.4 us
  waiting for transfers between devices: 25 us -> 28 us
    ppermute x5, waiting for transfers between devices: 1.8 us -> 7.73 us  [hand(): return lax.ppermute(block, ('ctx', 'pipe'), route)]
    ppermute x9, starting transfers between devices: 21.5 us -> 16.4 us  [turn(): lax.ppermute(block, 'ctx', [(i, (i + s * QUAD) % devices) for i in range(...]
    ppermute x9, waiting for transfers between devices: 16.6 us -> 13 us  [turn(): lax.ppermute(block, 'ctx', [(i, (i + s * QUAD) % devices) for i in range(...]
  transfers between devices with their start and end apart: 29 -> 29, of which waited for: 12 -> 13; matrix products, arithmetic and copies ran while one was open for 0% -> 0% of each run, Pallas kernels for 27% -> 28%
where the time goes in v7:
time: 89.7 us; the launch traced here: 89.5 us
  starting transfers between devices  32.4 us (36%)
  Pallas kernels  28.2 us (31%)
  waiting for transfers between devices  28 us (31%)
    pallas_call x11, Pallas kernels, call(): pl.pallas_call(kernel, name=name, out_shape=out_shape, in_specs=specs, ou...  28.2 us
    ppermute x9, starting transfers between devices, turn(): lax.ppermute(block, 'ctx', [(i, (i + s * QUAD) % devices) for i in range(...  16.4 us
    ppermute x9, waiting for transfers between devices, turn(): lax.ppermute(block, 'ctx', [(i, (i + s * QUAD) % devices) for i in range(...  13 us
    ppermute x15, starting transfers between devices, swap_one(): return lax.ppermute(piece, 'ctx', [(i, i ^ d) for i in range(devices)])  11.5 us
    ppermute x5, waiting for transfers between devices, hand(): return lax.ppermute(block, ('ctx', 'pipe'), route)  7.73 us
    ppermute x15, waiting for transfers between devices, swap_one(): return lax.ppermute(piece, 'ctx', [(i, i ^ d) for i in range(devices)])  7.27 us
    ppermute x5, starting transfers between devices, hand(): return lax.ppermute(block, ('ctx', 'pipe'), route)  4.45 us
  transfers between devices with their start and end apart: 29, of which 13 were waited for; matrix products, arithmetic and copies ran while one was open for 0% of the time, Pallas kernels for 28%

profile of v7, /device:TPU:0, one launch (start us, length us, event | category | flops | bytes accessed | tf_op | source)
XLA Modules:
  0.0 89.5 jit_solution(7516463215175516242)
XLA Ops:
  0.6 2.0 %pack_keys_bwd.1 = (bf16[128,256]{1,0:T(8,128)(2,1)}, bf16[128,256]{1,0:T(8,128)(2,1)}, bf16[128,256]{1,0:T(8,128)(2,1)}, bf16[128,256]{1,0:T(8,128)(2,1)}) custom-call(bf16[1,128,512]{2,1,0:T(8,128)(2,1)} %key_ref.2, bf16[1,128,512]{2,1,0:T(8,128)(2,1)} %value_ref.2, s32[1,128]{1,0:T(1,128)} %types_ref.2, bf16[1,64,512]{2,1,0:T(8,128)(2,1)} %table_ref.3), custom_call_target="tpu_custom_call" | custom-call | bytes 590336 | tf_op jit(solution)/shard_map/pack_keys_bwd/pallas_call | solution.py:343
  2.6 0.5 collective-permute-start
  3.1 2.6 %collective-permute-start.1 = (bf16[128,256]{1,0:T(8,128)(2,1)}, bf16[128,256]{1,0:T(8,128)(2,1)S(1)}, u32[]{:S(2)}, u32[]{:S(2)}) collective-permute-start(bf16[128,256]{1,0:T(8,128)(2,1)} %get-tuple-element.91), channel_id=1, source_target_pairs={{0,4},{2,6},{4,0},{6,2},{8,12},{10,14},{12,8},{14,10},{16,20},{18,... | collective-permute-start | bytes 196616 | tf_op jit(solution)/shard_map/ppermute | solution.py:384
  5.7 0.1 collective-permute-start.2
  5.8 2.0 %pack_keys_fwd.1 = (bf16[128,256]{1,0:T(8,128)(2,1)}, bf16[128,256]{1,0:T(8,128)(2,1)}, bf16[128,256]{1,0:T(8,128)(2,1)}, bf16[128,256]{1,0:T(8,128)(2,1)}) custom-call(bf16[1,128,512]{2,1,0:T(8,128)(2,1)} %key_ref.3, bf16[1,128,512]{2,1,0:T(8,128)(2,1)} %value_ref.3, s32[1,128]{1,0:T(1,128)} %types_ref.3, bf16[1,64,512]{2,1,0:T(8,128)(2,1)} %table_ref.3), custom_call_target="tpu_custom_call" | custom-call | bytes 590336 | tf_op jit(solution)/shard_map/pack_keys_fwd/pallas_call | solution.py:343
  7.7 0.0 collective-permute-done.refs_1_
  7.7 0.9 collective-permute-done.1.refs_2_
  8.6 1.5 %collective-permute-done.2.refs_3_ = bf16[128,256]{1,0:T(8,128)(2,1)S(1)} collective-permute-done((bf16[128,256]{1,0:T(8,128)(2,1)}, bf16[128,256]{1,0:T(8,128)(2,1)S(1)}, u32[]{:S(2)}, u32[]{:S(2)}) %collective-permute-start.2) | collective-permute-done | bytes 65568 | tf_op jit(solution)/shard_map/ppermute | solution.py:384
  10.1 0.4 stack_keys_bwd.1.refs_4_
  10.4 0.0 copy-start.1
  10.5 1.6 %collective-permute-start.3 = (bf16[512,256]{1,0:T(8,128)(2,1)S(1)}, bf16[512,256]{1,0:T(8,128)(2,1)S(1)}, u32[]{:S(2)}, u32[]{:S(2)}) collective-permute-start(bf16[512,256]{1,0:T(8,128)(2,1)S(1)} %stack_keys_bwd.1.refs_4_), channel_id=1, source_target_pairs={{0,8},{2,10},{4,12},{6,14},{8,16},{10,18},{12,20},{14,22},{16,24},... | collective-permute-start | bytes 786440 | tf_op jit(solution)/shard_map/ppermute | solution.py:390
  12.1 0.0 collective-permute-start.4
  12.1 1.3 %collective-permute-start.5 = (bf16[128,256]{1,0:T(8,128)(2,1)S(1)}, bf16[128,256]{1,0:T(8,128)(2,1)S(1)}, u32[]{:S(2)}, u32[]{:S(2)}) collective-permute-start(bf16[128,256]{1,0:T(8,128)(2,1)S(1)} %copy-done.5), channel_id=1, source_target_pairs={{0,4},{2,6},{4,0},{6,2},{8,12},{10,14},{12,8},{14,10},{16,20},{18,... | collective-permute-start | bytes 196616 | tf_op jit(solution)/shard_map/ppermute | solution.py:384
  13.4 0.5 collective-permute-start.6
  14.0 3.8 %pack_queries.1 = (bf16[128,1536]{1,0:T(8,128)(2,1)}, bf16[128,1536]{1,0:T(8,128)(2,1)}, bf16[128,1536]{1,0:T(8,128)(2,1)}, bf16[128,1536]{1,0:T(8,128)(2,1)}, bf16[144,2048]{1,0:T(8,128)(2,1)}) custom-call(bf16[1,128,2048]{2,1,0:T(8,128)(2,1)} %query_ref.1, bf16[1,128,2048]{2,1,0:T(8,128)(2,1)} %grad_ref.1, bf16[1,128,2048]{2,1,0:T(8,128)(2,1)} %forward_ref.1, ...), custom_call_target="tpu_custom_call" | custom-call | bytes 4268032 | tf_op jit(solution)/shard_map/pack_queries/pallas_call | solution.py:343
  17.8 0.0 copy-start
  17.8 0.0 collective-permute-done.4.refs_1_
  17.8 0.0 collective-permute-done.5.refs_2_
  17.8 2.9 %collective-permute-done.3.refs_5_ = bf16[512,256]{1,0:T(8,128)(2,1)S(1)} collective-permute-done((bf16[512,256]{1,0:T(8,128)(2,1)S(1)}, bf16[512,256]{1,0:T(8,128)(2,1)S(1)}, u32[]{:S(2)}, u32[]{:S(2)}) %collective-permute-start.3) | collective-permute-done | bytes 262176 | tf_op jit(solution)/shard_map/ppermute | solution.py:390
  20.7 3.8 %collective-permute-start.8 = (bf16[512,256]{1,0:T(8,128)(2,1)S(1)}, bf16[512,256]{1,0:T(8,128)(2,1)S(1)}, u32[]{:S(2)}, u32[]{:S(2)}) collective-permute-start(bf16[512,256]{1,0:T(8,128)(2,1)S(1)} %stack_keys_bwd.1.refs_4_), channel_id=1, source_target_pairs={{0,24},{2,26},{4,28},{6,30},{8,0},{10,2},{12,4},{14,6},{16,8},{18,... | collective-permute-start | bytes 786440 | tf_op jit(solution)/shard_map/ppermute | solution.py:390
  24.5 1.4 %collective-permute-start.10 = (bf16[128,1536]{1,0:T(8,128)(2,1)}, bf16[128,1536]{1,0:T(8,128)(2,1)S(1)}, u32[]{:S(2)}, u32[]{:S(2)}) collective-permute-start(bf16[128,1536]{1,0:T(8,128)(2,1)} %get-tuple-element.120), channel_id=1, source_target_pairs={{0,4},{2,6},{4,0},{6,2},{8,12},{10,14},{12,8},{14,10},{16,20},{18,... | collective-permute-start | bytes 1179656 | tf_op jit(solution)/shard_map/ppermute | solution.py:384
  25.9 0.0 collective-permute-start.11
  25.9 0.4 stack_keys_fwd.1.refs_4_
  26.3 5.4 %collective-permute-done.7.refs_6_ = bf16[512,256]{1,0:T(8,128)(2,1)S(1)} collective-permute-done((bf16[512,256]{1,0:T(8,128)(2,1)S(1)}, bf16[512,256]{1,0:T(8,128)(2,1)S(1)}, u32[]{:S(2)}, u32[]{:S(2)}) %collective-permute-start.7) | collective-permute-done | bytes 262176 | tf_op jit(solution)/shard_map/ppermute | solution.py:390
  31.7 2.1 %collective-permute-done.8.refs_7_ = bf16[512,256]{1,0:T(8,128)(2,1)S(1)} collective-permute-done((bf16[512,256]{1,0:T(8,128)(2,1)S(1)}, bf16[512,256]{1,0:T(8,128)(2,1)S(1)}, u32[]{:S(2)}, u32[]{:S(2)}) %collective-permute-start.8) | collective-permute-done | bytes 262176 | tf_op jit(solution)/shard_map/ppermute | solution.py:390
  33.9 0.0 collective-permute-start.9
  33.9 1.5 %collective-permute-start.15 = (bf16[144,2048]{1,0:T(8,128)(2,1)}, bf16[144,2048]{1,0:T(8,128)(2,1)S(1)}, u32[]{:S(2)}, u32[]{:S(2)}) collective-permute-start(bf16[144,2048]{1,0:T(8,128)(2,1)} %get-tuple-element.135), channel_id=1, source_target_pairs={{0,1},{1,0},{2,3},{3,2},{4,5},{5,4},{6,7},{7,6},{8,9},{9,8},{10,11... | collective-permute-start | bytes 1769480 | tf_op jit(solution)/shard_map/ppermute | solution.py:401
  35.4 1.1 %collective-permute-start.12 = (bf16[512,256]{1,0:T(8,128)(2,1)S(1)}, bf16[512,256]{1,0:T(8,128)(2,1)S(1)}, u32[]{:S(2)}, u32[]{:S(2)}) collective-permute-start(bf16[512,256]{1,0:T(8,128)(2,1)S(1)} %stack_keys_fwd.1.refs_4_), channel_id=1, source_target_pairs={{0,8},{2,10},{4,12},{6,14},{8,16},{10,18},{12,20},{14,22},{16,24},... | collective-permute-start | bytes 786440 | tf_op jit(solution)/shard_map/ppermute | solution.py:390
  36.5 0.3 collective-permute-done.10.refs_2_
  36.8 1.3 %collective-permute-start.13 = (bf16[512,256]{1,0:T(8,128)(2,1)S(1)}, bf16[512,256]{1,0:T(8,128)(2,1)S(1)}, u32[]{:S(2)}, u32[]{:S(2)}) collective-permute-start(bf16[512,256]{1,0:T(8,128)(2,1)S(1)} %stack_keys_fwd.1.refs_4_), channel_id=1, source_target_pairs={{0,16},{2,18},{4,20},{6,22},{8,24},{10,26},{12,28},{14,30},{16,0},... | collective-permute-start | bytes 786440 | tf_op jit(solution)/shard_map/ppermute | solution.py:390
  38.1 4.1 %collective-permute-done.11.refs_3_ = bf16[128,1536]{1,0:T(8,128)(2,1)S(1)} collective-permute-done((bf16[128,1536]{1,0:T(8,128)(2,1)}, bf16[128,1536]{1,0:T(8,128)(2,1)S(1)}, u32[]{:S(2)}, u32[]{:S(2)}) %collective-permute-start.11) | collective-permute-done | bytes 393248 | tf_op jit(solution)/shard_map/ppermute | solution.py:384
  42.2 0.3 collective-permute-start.14
  42.5 0.0 collective-permute-done.9.refs_1_
  42.5 12.8 %backward.1 = (bf16[128,512]{1,0:T(8,128)(2,1)S(1)}, bf16[128,512]{1,0:T(8,128)(2,1)S(1)}, bf16[128,512]{1,0:T(8,128)(2,1)S(1)}, bf16[128,512]{1,0:T(8,128)(2,1)...) custom-call(s32[1,32]{1,0:T(1,128)S(1)} %copy-done.3, ...), custom_call_target="tpu_custom_call" | custom-call | flops 3019898880 | bytes 4194432 | tf_op jit(solution)/shard_map/backward/pallas_call | solution.py:343
  55.3 0.0 collective-permute-done.12.refs_5_
  55.3 1.7 %collective-permute-done.13.refs_6_ = bf16[512,256]{1,0:T(8,128)(2,1)S(1)} collective-permute-done((bf16[512,256]{1,0:T(8,128)(2,1)S(1)}, bf16[512,256]{1,0:T(8,128)(2,1)S(1)}, u32[]{:S(2)}, u32[]{:S(2)}) %collective-permute-start.13) | collective-permute-done | bytes 262176 | tf_op jit(solution)/shard_map/ppermute | solution.py:390
  57.0 0.1 collective-permute-done.14.refs_7_
  57.1 5.9 %collective-permute-start.16 = (bf16[512,256]{1,0:T(8,128)(2,1)S(1)}, bf16[512,256]{1,0:T(8,128)(2,1)S(1)}, u32[]{:S(2)}, u32[]{:S(2)}) collective-permute-start(bf16[512,256]{1,0:T(8,128)(2,1)S(1)} %get-tuple-element.148), channel_id=1, source_target_pairs={{0,8},{2,10},{4,12},{6,14},{8,16},{10,18},{12,20},{14,22},{16,24},... | collective-permute-start | bytes 786440 | tf_op jit(solution)/shard_map/ppermute | solution.py:390
  63.0 1.4 %collective-permute-start.17 = (bf16[128,512]{1,0:T(8,128)(2,1)S(1)}, bf16[128,512]{1,0:T(8,128)(2,1)S(1)}, u32[]{:S(2)}, u32[]{:S(2)}) collective-permute-start(bf16[128,512]{1,0:T(8,128)(2,1)S(1)} %get-tuple-element.151), channel_id=1, source_target_pairs={{0,4},{2,6},{4,0},{6,2},{8,12},{10,14},{12,8},{14,10},{16,20},{18,... | collective-permute-start | bytes 393224 | tf_op jit(solution)/shard_map/ppermute | solution.py:384
  64.4 0.0 collective-permute-start.18
  64.4 1.2 %collective-permute-start.25 = (bf16[512,256]{1,0:T(8,128)(2,1)S(1)}, bf16[512,256]{1,0:T(8,128)(2,1)S(1)}, u32[]{:S(2)}, u32[]{:S(2)}) collective-permute-start(bf16[512,256]{1,0:T(8,128)(2,1)S(1)} %get-tuple-element.167), channel_id=1, source_target_pairs={{0,24},{2,26},{4,28},{6,30},{8,0},{10,2},{12,4},{14,6},{16,8},{18,... | collective-permute-start | bytes 786440 | tf_op jit(solution)/shard_map/ppermute | solution.py:390
  65.6 4.1 %forward.1 = (bf16[128,512]{1,0:T(8,128)(2,1)S(1)}, bf16[128,512]{1,0:T(8,128)(2,1)S(1)}, bf16[128,512]{1,0:T(8,128)(2,1)S(1)}, bf16[128,512]{1,0:T(8,128)(2,1)S(1)}) custom-call(s32[1,32]{1,0:T(1,128)S(1)} %copy-done.3, bf16[128,1536]{1,0:T(8,128)(2,1)S(1)} %copy-done, bf16[128,1536]{1,0:T(8,128)(2,1)S(1)} %collective-permute-done.9.refs_1_, ...), custom_call_target="tpu_custom_call" | custom-call | bytes 3145856 | tf_op jit(solution)/shard_map/forward/pallas_call | solution.py:343
  69.7 0.5 collective-permute-done.18.refs_3_
  70.2 0.8 collective-permute-done.16
  71.0 0.1 add_convert_fusion
  71.0 1.3 %collective-permute-start.24 = (bf16[512,256]{1,0:T(8,128)(2,1)S(1)}, bf16[512,256]{1,0:T(8,128)(2,1)S(1)}, u32[]{:S(2)}, u32[]{:S(2)}) collective-permute-start(bf16[512,256]{1,0:T(8,128)(2,1)S(1)} %add_convert_fusion), channel_id=1, source_target_pairs={{0,8},{2,10},{4,12},{6,14},{8,16},{10,18},{12,20},{14,22},{16,24},... | collective-permute-start | bytes 786440 | tf_op jit(solution)/shard_map/ppermute | solution.py:390
  72.3 0.5 collective-permute-start.19
  72.8 2.4 %collective-permute-start.21 = (bf16[128,512]{1,0:T(8,128)(2,1)S(1)}, bf16[128,512]{1,0:T(8,128)(2,1)S(1)}, u32[]{:S(2)}, u32[]{:S(2)}) collective-permute-start(bf16[128,512]{1,0:T(8,128)(2,1)S(1)} %get-tuple-element.157), channel_id=1, source_target_pairs={{0,5},{1,4},{2,7},{3,6},{4,1},{5,0},{6,3},{7,2},{8,13},{9,12},{10,... | collective-permute-start | bytes 393224 | tf_op jit(solution)/shard_map/ppermute | solution.py:401
  75.2 6.2 %collective-permute-done.19.refs_0_ = bf16[128,512]{1,0:T(8,128)(2,1)S(1)} collective-permute-done((bf16[128,512]{1,0:T(8,128)(2,1)S(1)}, bf16[128,512]{1,0:T(8,128)(2,1)S(1)}, u32[]{:S(2)}, u32[]{:S(2)}) %collective-permute-start.19) | collective-permute-done | bytes 131104 | tf_op jit(solution)/shard_map/ppermute | solution.py:401
  81.4 0.0 collective-permute-start.22
  81.4 0.6 collective-permute-start.23
  82.0 0.1 sum_key_parts.1
  82.1 0.1 collective-permute-start.26
  82.2 0.0 collective-permute-done.20.refs_1_
  82.2 1.4 %collective-permute-start.27 = (bf16[128,256]{1,0:T(8,128)(2,1)S(1)}, bf16[128,256]{1,0:T(8,128)(2,1)S(1)}, u32[]{:S(2)}, u32[]{:S(2)}) collective-permute-start(bf16[128,256]{1,0:T(8,128)(2,1)S(1)} %get-tuple-element.170), channel_id=1, source_target_pairs={{0,4},{2,6},{4,0},{6,2},{8,12},{10,14},{12,8},{14,10},{16,20},{18,... | collective-permute-start | bytes 196616 | tf_op jit(solution)/shard_map/ppermute | solution.py:384
  83.6 0.0 collective-permute-done.21.refs_2_
  83.6 1.6 %collective-permute-start.28 = (bf16[128,256]{1,0:T(8,128)(2,1)S(1)}, bf16[128,256]{1,0:T(8,128)(2,1)S(1)}, u32[]{:S(2)}, u32[]{:S(2)}) collective-permute-start(bf16[128,256]{1,0:T(8,128)(2,1)S(1)} %get-tuple-element.171), channel_id=1, source_target_pairs={{0,6},{2,4},{4,2},{6,0},{8,14},{10,12},{12,10},{14,8},{16,22},{18,... | collective-permute-start | bytes 196616 | tf_op jit(solution)/shard_map/ppermute | solution.py:384
  85.2 1.5 %collective-permute-done.22.refs_3_ = bf16[128,512]{1,0:T(8,128)(2,1)S(1)} collective-permute-done((bf16[128,512]{1,0:T(8,128)(2,1)S(1)}, bf16[128,512]{1,0:T(8,128)(2,1)S(1)}, u32[]{:S(2)}, u32[]{:S(2)}) %collective-permute-start.22) | collective-permute-done | bytes 131104 | tf_op jit(solution)/shard_map/ppermute | solution.py:401
  86.7 1.2 %gate.1 = bf16[1,128,2048]{2,1,0:T(8,128)(2,1)} custom-call(bf16[128,512]{1,0:T(8,128)(2,1)S(1)} %collective-permute-done.19.refs_0_, bf16[128,512]{1,0:T(8,128)(2,1)S(1)} %collective-permute-done.20.refs_1_, bf16[128,512]{1,0:T(8,128)(2,1)S(1)} %collective-permute-done.21.refs_2_, bf16[128,512]{1,0:T(8,128)(2,1)S(1)} %collective-permute-done.22.refs_3_, ...), custom_call_target="tpu_custom_call" | custom-call | bytes 1638400 | tf_op jit(solution)/shard_map/gate/pallas_call | solution.py:343
  87.9 0.0 collective-permute-done.23.refs_1_
  87.9 0.8 query_grad.1
  88.7 0.0 collective-permute-done.26.refs_1_
  88.7 0.0 collective-permute-done.27.refs_2_
  88.7 0.8 key_grad.1
  (20 shorter events, 0.0 us)
Async XLA Ops:
  2.6 5.1 %collective-permute-start = (bf16[128,256]{1,0:T(8,128)(2,1)}, bf16[128,256]{1,0:T(8,128)(2,1)S(1)}, u32[]{:S(2)}, u32[]{:S(2)}) collective-permute-start(bf16[128,256]{1,0:T(8,128)(2,1)} %get-tuple-element.90), channel_id=1, source_target_pairs={{0,2},{2,0},{4,6},{6,4},{8,10},{10,8},{12,14},{14,12},{16,18},{18,... | collective-permute-start | bytes 196616 | tf_op jit(solution)/shard_map/ppermute | solution.py:384
  3.1 5.5 %collective-permute-start.1 = (bf16[128,256]{1,0:T(8,128)(2,1)}, bf16[128,256]{1,0:T(8,128)(2,1)S(1)}, u32[]{:S(2)}, u32[]{:S(2)}) collective-permute-start(bf16[128,256]{1,0:T(8,128)(2,1)} %get-tuple-element.91), channel_id=1, source_target_pairs={{0,4},{2,6},{4,0},{6,2},{8,12},{10,14},{12,8},{14,10},{16,20},{18,... | collective-permute-start | bytes 196616 | tf_op jit(solution)/shard_map/ppermute | solution.py:384
  5.7 4.4 %copy-start.2 = (bf16[128,256]{1,0:T(8,128)(2,1)S(1)}, bf16[128,256]{1,0:T(8,128)(2,1)}, u32[]{:S(2)}) copy-start(bf16[128,256]{1,0:T(8,128)(2,1)} %get-tuple-element.97.refs_0_) | copy-start | bytes 196612
  5.7 4.3 %collective-permute-start.2 = (bf16[128,256]{1,0:T(8,128)(2,1)}, bf16[128,256]{1,0:T(8,128)(2,1)S(1)}, u32[]{:S(2)}, u32[]{:S(2)}) collective-permute-start(bf16[128,256]{1,0:T(8,128)(2,1)} %get-tuple-element.92), channel_id=1, source_target_pairs={{0,6},{2,4},{4,2},{6,0},{8,14},{10,12},{12,10},{14,8},{16,22},{18,... | collective-permute-start | bytes 196616 | tf_op jit(solution)/shard_map/ppermute | solution.py:384
  10.0 2.0 %copy-start.6 = (bf16[128,256]{1,0:T(8,128)(2,1)S(1)}, bf16[128,256]{1,0:T(8,128)(2,1)}, u32[]{:S(2)}) copy-start(bf16[128,256]{1,0:T(8,128)(2,1)} %get-tuple-element.102) | copy-start | bytes 196612
  10.0 2.0 %copy-start.5 = (bf16[128,256]{1,0:T(8,128)(2,1)S(1)}, bf16[128,256]{1,0:T(8,128)(2,1)}, u32[]{:S(2)}) copy-start(bf16[128,256]{1,0:T(8,128)(2,1)} %get-tuple-element.103) | copy-start | bytes 196612
  10.0 3.4 %copy-start.4 = (bf16[128,256]{1,0:T(8,128)(2,1)S(1)}, bf16[128,256]{1,0:T(8,128)(2,1)}, u32[]{:S(2)}) copy-start(bf16[128,256]{1,0:T(8,128)(2,1)} %get-tuple-element.104) | copy-start | bytes 196612
  10.4 15.5 %copy-start.1 = (bf16[128,256]{1,0:T(8,128)(2,1)S(1)}, bf16[128,256]{1,0:T(8,128)(2,1)}, u32[]{:S(2)}) copy-start(bf16[128,256]{1,0:T(8,128)(2,1)} %get-tuple-element.113.refs_0_) | copy-start | bytes 196612
  10.5 10.2 %collective-permute-start.3 = (bf16[512,256]{1,0:T(8,128)(2,1)S(1)}, bf16[512,256]{1,0:T(8,128)(2,1)S(1)}, u32[]{:S(2)}, u32[]{:S(2)}) collective-permute-start(bf16[512,256]{1,0:T(8,128)(2,1)S(1)} %stack_keys_bwd.1.refs_4_), channel_id=1, source_target_pairs={{0,8},{2,10},{4,12},{6,14},{8,16},{10,18},{12,20},{14,22},{16,24},... | collective-permute-start | bytes 786440 | tf_op jit(solution)/shard_map/ppermute | solution.py:390
  12.1 5.7 %collective-permute-start.4 = (bf16[128,256]{1,0:T(8,128)(2,1)S(1)}, bf16[128,256]{1,0:T(8,128)(2,1)S(1)}, u32[]{:S(2)}, u32[]{:S(2)}) collective-permute-start(bf16[128,256]{1,0:T(8,128)(2,1)S(1)} %copy-done.6), channel_id=1, source_target_pairs={{0,2},{2,0},{4,6},{6,4},{8,10},{10,8},{12,14},{14,12},{16,18},{18,... | collective-permute-start | bytes 196616 | tf_op jit(solution)/shard_map/ppermute | solution.py:384
  12.1 5.7 %collective-permute-start.5 = (bf16[128,256]{1,0:T(8,128)(2,1)S(1)}, bf16[128,256]{1,0:T(8,128)(2,1)S(1)}, u32[]{:S(2)}, u32[]{:S(2)}) collective-permute-start(bf16[128,256]{1,0:T(8,128)(2,1)S(1)} %copy-done.5), channel_id=1, source_target_pairs={{0,4},{2,6},{4,0},{6,2},{8,12},{10,14},{12,8},{14,10},{16,20},{18,... | collective-permute-start | bytes 196616 | tf_op jit(solution)/shard_map/ppermute | solution.py:384
  13.4 4.4 %collective-permute-start.6 = (bf16[128,256]{1,0:T(8,128)(2,1)S(1)}, bf16[128,256]{1,0:T(8,128)(2,1)S(1)}, u32[]{:S(2)}, u32[]{:S(2)}) collective-permute-start(bf16[128,256]{1,0:T(8,128)(2,1)S(1)} %copy-done.4), channel_id=1, source_target_pairs={{0,6},{2,4},{4,2},{6,0},{8,14},{10,12},{12,10},{14,8},{16,22},{18,... | collective-permute-start | bytes 196616 | tf_op jit(solution)/shard_map/ppermute | solution.py:384
  17.8 24.7 %copy-start = (bf16[128,1536]{1,0:T(8,128)(2,1)S(1)}, bf16[128,1536]{1,0:T(8,128)(2,1)}, u32[]{:S(2)}) copy-start(bf16[128,1536]{1,0:T(8,128)(2,1)} %get-tuple-element.110.refs_0_) | copy-start | bytes 1179652
  20.7 21.8 %copy-start.3 = (s32[1,32]{1,0:T(1,128)S(1)}, s32[1,32]{1,0:T(1,128)}, u32[]{:S(2)}) copy-start(s32[1,32]{1,0:T(1,128)} %order_ref.3) | copy-start | bytes 388
  20.7 11.0 %collective-permute-start.7 = (bf16[512,256]{1,0:T(8,128)(2,1)S(1)}, bf16[512,256]{1,0:T(8,128)(2,1)S(1)}, u32[]{:S(2)}, u32[]{:S(2)}) collective-permute-start(bf16[512,256]{1,0:T(8,128)(2,1)S(1)} %collective-permute-done.3.refs_5_), channel_id=1, source_target_pairs={{0,8},{2,10},{4,12},{6,14},{8,16},{10,18},{12,20},{14,22},{16,24},... | collective-permute-start | bytes 786440 | tf_op jit(solution)/shard_map/ppermute | solution.py:390
  20.7 13.2 %collective-permute-start.8 = (bf16[512,256]{1,0:T(8,128)(2,1)S(1)}, bf16[512,256]{1,0:T(8,128)(2,1)S(1)}, u32[]{:S(2)}, u32[]{:S(2)}) collective-permute-start(bf16[512,256]{1,0:T(8,128)(2,1)S(1)} %stack_keys_bwd.1.refs_4_), channel_id=1, source_target_pairs={{0,24},{2,26},{4,28},{6,30},{8,0},{10,2},{12,4},{14,6},{16,8},{18,... | collective-permute-start | bytes 786440 | tf_op jit(solution)/shard_map/ppermute | solution.py:390
  24.5 12.3 %collective-permute-start.10 = (bf16[128,1536]{1,0:T(8,128)(2,1)}, bf16[128,1536]{1,0:T(8,128)(2,1)S(1)}, u32[]{:S(2)}, u32[]{:S(2)}) collective-permute-start(bf16[128,1536]{1,0:T(8,128)(2,1)} %get-tuple-element.120), channel_id=1, source_target_pairs={{0,4},{2,6},{4,0},{6,2},{8,12},{10,14},{12,8},{14,10},{16,20},{18,... | collective-permute-start | bytes 1179656 | tf_op jit(solution)/shard_map/ppermute | solution.py:384
  25.9 16.3 %collective-permute-start.11 = (bf16[128,1536]{1,0:T(8,128)(2,1)}, bf16[128,1536]{1,0:T(8,128)(2,1)S(1)}, u32[]{:S(2)}, u32[]{:S(2)}) collective-permute-start(bf16[128,1536]{1,0:T(8,128)(2,1)} %get-tuple-element.121), channel_id=1, source_target_pairs={{0,6},{2,4},{4,2},{6,0},{8,14},{10,12},{12,10},{14,8},{16,22},{18,... | collective-permute-start | bytes 1179656 | tf_op jit(solution)/shard_map/ppermute | solution.py:384
  33.9 8.6 %collective-permute-start.9 = (bf16[128,1536]{1,0:T(8,128)(2,1)}, bf16[128,1536]{1,0:T(8,128)(2,1)S(1)}, u32[]{:S(2)}, u32[]{:S(2)}) collective-permute-start(bf16[128,1536]{1,0:T(8,128)(2,1)} %get-tuple-element.119), channel_id=1, source_target_pairs={{0,2},{2,0},{4,6},{6,4},{8,10},{10,8},{12,14},{14,12},{16,18},{18,... | collective-permute-start | bytes 1179656 | tf_op jit(solution)/shard_map/ppermute | solution.py:384
  33.9 21.4 %collective-permute-start.15 = (bf16[144,2048]{1,0:T(8,128)(2,1)}, bf16[144,2048]{1,0:T(8,128)(2,1)S(1)}, u32[]{:S(2)}, u32[]{:S(2)}) collective-permute-start(bf16[144,2048]{1,0:T(8,128)(2,1)} %get-tuple-element.135), channel_id=1, source_target_pairs={{0,1},{1,0},{2,3},{3,2},{4,5},{5,4},{6,7},{7,6},{8,9},{9,8},{10,11... | collective-permute-start | bytes 1769480 | tf_op jit(solution)/shard_map/ppermute | solution.py:401
  35.4 19.9 %collective-permute-start.12 = (bf16[512,256]{1,0:T(8,128)(2,1)S(1)}, bf16[512,256]{1,0:T(8,128)(2,1)S(1)}, u32[]{:S(2)}, u32[]{:S(2)}) collective-permute-start(bf16[512,256]{1,0:T(8,128)(2,1)S(1)} %stack_keys_fwd.1.refs_4_), channel_id=1, source_target_pairs={{0,8},{2,10},{4,12},{6,14},{8,16},{10,18},{12,20},{14,22},{16,24},... | collective-permute-start | bytes 786440 | tf_op jit(solution)/shard_map/ppermute | solution.py:390
  36.8 20.2 %collective-permute-start.13 = (bf16[512,256]{1,0:T(8,128)(2,1)S(1)}, bf16[512,256]{1,0:T(8,128)(2,1)S(1)}, u32[]{:S(2)}, u32[]{:S(2)}) collective-permute-start(bf16[512,256]{1,0:T(8,128)(2,1)S(1)} %stack_keys_fwd.1.refs_4_), channel_id=1, source_target_pairs={{0,16},{2,18},{4,20},{6,22},{8,24},{10,26},{12,28},{14,30},{16,0},... | collective-permute-start | bytes 786440 | tf_op jit(solution)/shard_map/ppermute | solution.py:390
  42.2 14.9 %collective-permute-start.14 = (bf16[512,256]{1,0:T(8,128)(2,1)S(1)}, bf16[512,256]{1,0:T(8,128)(2,1)S(1)}, u32[]{:S(2)}, u32[]{:S(2)}) collective-permute-start(bf16[512,256]{1,0:T(8,128)(2,1)S(1)} %stack_keys_fwd.1.refs_4_), channel_id=1, source_target_pairs={{0,24},{2,26},{4,28},{6,30},{8,0},{10,2},{12,4},{14,6},{16,8},{18,... | collective-permute-start | bytes 786440 | tf_op jit(solution)/shard_map/ppermute | solution.py:390
  57.1 13.9 %collective-permute-start.16 = (bf16[512,256]{1,0:T(8,128)(2,1)S(1)}, bf16[512,256]{1,0:T(8,128)(2,1)S(1)}, u32[]{:S(2)}, u32[]{:S(2)}) collective-permute-start(bf16[512,256]{1,0:T(8,128)(2,1)S(1)} %get-tuple-element.148), channel_id=1, source_target_pairs={{0,8},{2,10},{4,12},{6,14},{8,16},{10,18},{12,20},{14,22},{16,24},... | collective-permute-start | bytes 786440 | tf_op jit(solution)/shard_map/ppermute | solution.py:390
  63.0 6.7 %collective-permute-start.17 = (bf16[128,512]{1,0:T(8,128)(2,1)S(1)}, bf16[128,512]{1,0:T(8,128)(2,1)S(1)}, u32[]{:S(2)}, u32[]{:S(2)}) collective-permute-start(bf16[128,512]{1,0:T(8,128)(2,1)S(1)} %get-tuple-element.151), channel_id=1, source_target_pairs={{0,4},{2,6},{4,0},{6,2},{8,12},{10,14},{12,8},{14,10},{16,20},{18,... | collective-permute-start | bytes 393224 | tf_op jit(solution)/shard_map/ppermute | solution.py:384
  64.4 5.8 %collective-permute-start.18 = (bf16[128,512]{1,0:T(8,128)(2,1)S(1)}, bf16[128,512]{1,0:T(8,128)(2,1)S(1)}, u32[]{:S(2)}, u32[]{:S(2)}) collective-permute-start(bf16[128,512]{1,0:T(8,128)(2,1)S(1)} %get-tuple-element.152), channel_id=1, source_target_pairs={{0,6},{2,4},{4,2},{6,0},{8,14},{10,12},{12,10},{14,8},{16,22},{18,... | collective-permute-start | bytes 393224 | tf_op jit(solution)/shard_map/ppermute | solution.py:384
  64.4 17.0 %collective-permute-start.25 = (bf16[512,256]{1,0:T(8,128)(2,1)S(1)}, bf16[512,256]{1,0:T(8,128)(2,1)S(1)}, u32[]{:S(2)}, u32[]{:S(2)}) collective-permute-start(bf16[512,256]{1,0:T(8,128)(2,1)S(1)} %get-tuple-element.167), channel_id=1, source_target_pairs={{0,24},{2,26},{4,28},{6,30},{8,0},{10,2},{12,4},{14,6},{16,8},{18,... | collective-permute-start | bytes 786440 | tf_op jit(solution)/shard_map/ppermute | solution.py:390
  71.0 11.0 %collective-permute-start.24 = (bf16[512,256]{1,0:T(8,128)(2,1)S(1)}, bf16[512,256]{1,0:T(8,128)(2,1)S(1)}, u32[]{:S(2)}, u32[]{:S(2)}) collective-permute-start(bf16[512,256]{1,0:T(8,128)(2,1)S(1)} %add_convert_fusion), channel_id=1, source_target_pairs={{0,8},{2,10},{4,12},{6,14},{8,16},{10,18},{12,20},{14,22},{16,24},... | collective-permute-start | bytes 786440 | tf_op jit(solution)/shard_map/ppermute | solution.py:390
  72.3 9.1 %collective-permute-start.19 = (bf16[128,512]{1,0:T(8,128)(2,1)S(1)}, bf16[128,512]{1,0:T(8,128)(2,1)S(1)}, u32[]{:S(2)}, u32[]{:S(2)}) collective-permute-start(bf16[128,512]{1,0:T(8,128)(2,1)S(1)} %get-tuple-element.153), channel_id=1, source_target_pairs={{0,1},{1,0},{2,3},{3,2},{4,5},{5,4},{6,7},{7,6},{8,9},{9,8},{10,11... | collective-permute-start | bytes 393224 | tf_op jit(solution)/shard_map/ppermute | solution.py:401
  72.8 9.4 %collective-permute-start.20 = (bf16[128,512]{1,0:T(8,128)(2,1)S(1)}, bf16[128,512]{1,0:T(8,128)(2,1)S(1)}, u32[]{:S(2)}, u32[]{:S(2)}) collective-permute-start(bf16[128,512]{1,0:T(8,128)(2,1)S(1)} %get-tuple-element.156), channel_id=1, source_target_pairs={{0,3},{1,2},{2,1},{3,0},{4,7},{5,6},{6,5},{7,4},{8,11},{9,10},{10,... | collective-permute-start | bytes 393224 | tf_op jit(solution)/shard_map/ppermute | solution.py:401
  72.8 10.8 %collective-permute-start.21 = (bf16[128,512]{1,0:T(8,128)(2,1)S(1)}, bf16[128,512]{1,0:T(8,128)(2,1)S(1)}, u32[]{:S(2)}, u32[]{:S(2)}) collective-permute-start(bf16[128,512]{1,0:T(8,128)(2,1)S(1)} %get-tuple-element.157), channel_id=1, source_target_pairs={{0,5},{1,4},{2,7},{3,6},{4,1},{5,0},{6,3},{7,2},{8,13},{9,12},{10,... | collective-permute-start | bytes 393224 | tf_op jit(solution)/shard_map/ppermute | solution.py:401
  81.4 5.3 %collective-permute-start.22 = (bf16[128,512]{1,0:T(8,128)(2,1)S(1)}, bf16[128,512]{1,0:T(8,128)(2,1)S(1)}, u32[]{:S(2)}, u32[]{:S(2)}) collective-permute-start(bf16[128,512]{1,0:T(8,128)(2,1)S(1)} %get-tuple-element.158), channel_id=1, source_target_pairs={{0,7},{1,6},{2,5},{3,4},{4,3},{5,2},{6,1},{7,0},{8,15},{9,14},{10,... | collective-permute-start | bytes 393224 | tf_op jit(solution)/shard_map/ppermute | solution.py:401
  81.4 6.5 %collective-permute-start.23 = (bf16[128,512]{1,0:T(8,128)(2,1)S(1)}, bf16[128,512]{1,0:T(8,128)(2,1)S(1)}, u32[]{:S(2)}, u32[]{:S(2)}) collective-permute-start(bf16[128,512]{1,0:T(8,128)(2,1)S(1)} %get-tuple-element.161), channel_id=1, source_target_pairs={{0,2},{2,0},{4,6},{6,4},{8,10},{10,8},{12,14},{14,12},{16,18},{18,... | collective-permute-start | bytes 393224 | tf_op jit(solution)/shard_map/ppermute | solution.py:384
  82.1 6.6 %collective-permute-start.26 = (bf16[128,256]{1,0:T(8,128)(2,1)S(1)}, bf16[128,256]{1,0:T(8,128)(2,1)S(1)}, u32[]{:S(2)}, u32[]{:S(2)}) collective-permute-start(bf16[128,256]{1,0:T(8,128)(2,1)S(1)} %get-tuple-element.169), channel_id=1, source_target_pairs={{0,2},{2,0},{4,6},{6,4},{8,10},{10,8},{12,14},{14,12},{16,18},{18,... | collective-permute-start | bytes 196616 | tf_op jit(solution)/shard_map/ppermute | solution.py:384
  82.2 6.5 %collective-permute-start.27 = (bf16[128,256]{1,0:T(8,128)(2,1)S(1)}, bf16[128,256]{1,0:T(8,128)(2,1)S(1)}, u32[]{:S(2)}, u32[]{:S(2)}) collective-permute-start(bf16[128,256]{1,0:T(8,128)(2,1)S(1)} %get-tuple-element.170), channel_id=1, source_target_pairs={{0,4},{2,6},{4,0},{6,2},{8,12},{10,14},{12,8},{14,10},{16,20},{18,... | collective-permute-start | bytes 196616 | tf_op jit(solution)/shard_map/ppermute | solution.py:384
  83.6 5.1 %collective-permute-start.28 = (bf16[128,256]{1,0:T(8,128)(2,1)S(1)}, bf16[128,256]{1,0:T(8,128)(2,1)S(1)}, u32[]{:S(2)}, u32[]{:S(2)}) collective-permute-start(bf16[128,256]{1,0:T(8,128)(2,1)S(1)} %get-tuple-element.171), channel_id=1, source_target_pairs={{0,6},{2,4},{4,2},{6,0},{8,14},{10,12},{12,10},{14,8},{16,22},{18,... | collective-permute-start | bytes 196616 | tf_op jit(solution)/shard_map/ppermute | solution.py:384

commit v8 on v7

--- a/solution.py
+++ b/solution.py
@@ -467,6 +467,7 @@
     pieces = pack(key_fwd, value_fwd, types_fwd, "pack_keys_fwd")
     back_pieces, pieces = lax.optimization_barrier((back_pieces, pieces))
     pieces = swap(pieces)
+    back_stack = stacked_keys(back_pieces, "stack_keys_bwd")
     packed = call(
         pack_queries,
         "pack_queries",
@@ -481,17 +482,16 @@
         vmem=60,
     )
     packed = list(packed)
-    back_stack = stacked_keys(back_pieces, "stack_keys_bwd")
     up = [back_stack, ring_up(back_stack)]
     up, pieces, packed = lax.optimization_barrier((up, pieces, packed))
     back_stacks = gather_ring(up)
     stack = stacked_keys(pieces, "stack_keys_fwd")
-    back_stacks, stack, packed[1], packed[QUAD] = lax.optimization_barrier(
-        (back_stacks, stack, packed[1], packed[QUAD])
-    )
     queries = swap(packed[:QUAD])
+    back_stacks, stack, queries[1], gate_before = lax.optimization_barrier(
+        (back_stacks, stack, queries[1], packed[QUAD])
+    )
     stacks = gather(stack)
-    gate_before = hand(packed[QUAD], 0)
+    gate_before = hand(gate_before, 0)
 
     sequence = [pltpu.VMEM((total_rows, HEAD), jnp.bfloat16)] * 2
     stacked = pltpu.VMEM((2 * QUAD, block_rows, HEAD), jnp.bfloat16)
@@ -540,6 +540,8 @@
     attended, key_up, query_pieces = lax.optimization_barrier(
         (attended, key_sums[0], query_pieces)
     )
+    attended = list(attended)
+    attended[3], key_down = lax.optimization_barrier((attended[3], key_sums[1]))
     attended = [hand(attended[d], d) for d in range(QUAD)]
     attended[0], query_pieces[1] = lax.optimization_barrier((attended[0], query_pieces[1]))
     query_pieces[1] = swap_one(query_pieces[1], 1)
@@ -551,7 +553,7 @@
         *attended,
         gate_before,
     )
-    key_sums = reduce_rest(key_parts, key_up, key_sums[1])
+    key_sums = reduce_rest(key_parts, key_up, key_down)
     key_pieces = swap(
         call(
             sum_kernel,

time: 89.7 us -> 92.6 us (1.032)
  starting transfers between devices: 32.4 us -> 34.7 us
    ppermute x9, waiting for transfers between devices: 13 us -> 18 us  [turn(): lax.ppermute(block, 'ctx', [(i, (i + s * QUAD) % devices) for i in range(...]
    ppermute x9, starting transfers between devices: 16.4 us -> 19.9 us  [turn(): lax.ppermute(block, 'ctx', [(i, (i + s * QUAD) % devices) for i in range(...]
    ppermute x5, waiting for transfers between devices: 7.73 us -> 4.77 us  [hand(): return lax.ppermute(block, ('ctx', 'pipe'), route)]
    ppermute x15, starting transfers between devices: 11.5 us -> 9.6 us  [swap_one(): return lax.ppermute(piece, 'ctx', [(i, i ^ d) for i in range(devices)])]
    ppermute x15, waiting for transfers between devices: 7.27 us -> 5.79 us  [swap_one(): return lax.ppermute(piece, 'ctx', [(i, i ^ d) for i in range(devices)])]
  transfers between devices with their start and end apart: 29 -> 29, of which waited for: 13 -> 13; matrix products, arithmetic and copies ran while one was open for 0% -> 0% of each run, Pallas kernels for 28% -> 27%
where the time goes in v8:
time: 92.6 us; the launch traced here: 92.4 us
  starting transfers between devices  34.7 us (37%)
  waiting for transfers between devices  28.6 us (31%)
  Pallas kernels  28.2 us (30%)
    pallas_call x11, Pallas kernels, call(): pl.pallas_call(kernel, name=name, out_shape=out_shape, in_specs=specs, ou...  28.2 us
    ppermute x9, starting transfers between devices, turn(): lax.ppermute(block, 'ctx', [(i, (i + s * QUAD) % devices) for i in range(...  19.9 us
    ppermute x9, waiting for transfers between devices, turn(): lax.ppermute(block, 'ctx', [(i, (i + s * QUAD) % devices) for i in range(...  18 us
    ppermute x15, starting transfers between devices, swap_one(): return lax.ppermute(piece, 'ctx', [(i, i ^ d) for i in range(devices)])  9.6 us
    ppermute x15, waiting for transfers between devices, swap_one(): return lax.ppermute(piece, 'ctx', [(i, i ^ d) for i in range(devices)])  5.79 us
    ppermute x5, starting transfers between devices, hand(): return lax.ppermute(block, ('ctx', 'pipe'), route)  5.18 us
    ppermute x5, waiting for transfers between devices, hand(): return lax.ppermute(block, ('ctx', 'pipe'), route)  4.77 us
  transfers between devices with their start and end apart: 29, of which 13 were waited for; matrix products, arithmetic and copies ran while one was open for 0% of the time, Pallas kernels for 27%

profile of v8, /device:TPU:0, one launch (start us, length us, event | category | flops | bytes accessed | tf_op | source)
XLA Modules:
  0.0 92.4 jit_solution(10479284656479278516)
XLA Ops:
  0.6 2.0 %pack_keys_bwd.1 = (bf16[128,256]{1,0:T(8,128)(2,1)}, bf16[128,256]{1,0:T(8,128)(2,1)}, bf16[128,256]{1,0:T(8,128)(2,1)}, bf16[128,256]{1,0:T(8,128)(2,1)}) custom-call(bf16[1,128,512]{2,1,0:T(8,128)(2,1)} %key_ref.2, bf16[1,128,512]{2,1,0:T(8,128)(2,1)} %value_ref.2, s32[1,128]{1,0:T(1,128)} %types_ref.2, bf16[1,64,512]{2,1,0:T(8,128)(2,1)} %table_ref.3), custom_call_target="tpu_custom_call" | custom-call | bytes 590336 | tf_op jit(solution)/shard_map/pack_keys_bwd/pallas_call | solution.py:343
  2.6 0.5 collective-permute-start
  3.1 2.6 %collective-permute-start.1 = (bf16[128,256]{1,0:T(8,128)(2,1)}, bf16[128,256]{1,0:T(8,128)(2,1)S(1)}, u32[]{:S(2)}, u32[]{:S(2)}) collective-permute-start(bf16[128,256]{1,0:T(8,128)(2,1)} %get-tuple-element.93), channel_id=1, source_target_pairs={{0,4},{2,6},{4,0},{6,2},{8,12},{10,14},{12,8},{14,10},{16,20},{18,... | collective-permute-start | bytes 196616 | tf_op jit(solution)/shard_map/ppermute | solution.py:384
  5.7 0.1 collective-permute-start.2
  5.8 2.0 %pack_keys_fwd.1 = (bf16[128,256]{1,0:T(8,128)(2,1)}, bf16[128,256]{1,0:T(8,128)(2,1)}, bf16[128,256]{1,0:T(8,128)(2,1)}, bf16[128,256]{1,0:T(8,128)(2,1)}) custom-call(bf16[1,128,512]{2,1,0:T(8,128)(2,1)} %key_ref.3, bf16[1,128,512]{2,1,0:T(8,128)(2,1)} %value_ref.3, s32[1,128]{1,0:T(1,128)} %types_ref.3, bf16[1,64,512]{2,1,0:T(8,128)(2,1)} %table_ref.3), custom_call_target="tpu_custom_call" | custom-call | bytes 590336 | tf_op jit(solution)/shard_map/pack_keys_fwd/pallas_call | solution.py:343
  7.7 0.0 collective-permute-done.refs_1_
  7.7 0.9 collective-permute-done.1.refs_2_
  8.6 1.5 %collective-permute-done.2.refs_3_ = bf16[128,256]{1,0:T(8,128)(2,1)S(1)} collective-permute-done((bf16[128,256]{1,0:T(8,128)(2,1)}, bf16[128,256]{1,0:T(8,128)(2,1)S(1)}, u32[]{:S(2)}, u32[]{:S(2)}) %collective-permute-start.2) | collective-permute-done | bytes 65568 | tf_op jit(solution)/shard_map/ppermute | solution.py:384
  10.1 0.4 stack_keys_bwd.1.refs_4_
  10.4 0.0 copy-start.1
  10.5 1.6 %collective-permute-start.3 = (bf16[512,256]{1,0:T(8,128)(2,1)S(1)}, bf16[512,256]{1,0:T(8,128)(2,1)S(1)}, u32[]{:S(2)}, u32[]{:S(2)}) collective-permute-start(bf16[512,256]{1,0:T(8,128)(2,1)S(1)} %stack_keys_bwd.1.refs_4_), channel_id=1, source_target_pairs={{0,8},{2,10},{4,12},{6,14},{8,16},{10,18},{12,20},{14,22},{16,24},... | collective-permute-start | bytes 786440 | tf_op jit(solution)/shard_map/ppermute | solution.py:390
  12.1 0.0 collective-permute-start.4
  12.1 1.3 %collective-permute-start.5 = (bf16[128,256]{1,0:T(8,128)(2,1)S(1)}, bf16[128,256]{1,0:T(8,128)(2,1)S(1)}, u32[]{:S(2)}, u32[]{:S(2)}) collective-permute-start(bf16[128,256]{1,0:T(8,128)(2,1)S(1)} %copy-done.5), channel_id=1, source_target_pairs={{0,4},{2,6},{4,0},{6,2},{8,12},{10,14},{12,8},{14,10},{16,20},{18,... | collective-permute-start | bytes 196616 | tf_op jit(solution)/shard_map/ppermute | solution.py:384
  13.4 0.5 collective-permute-start.6
  14.0 3.8 %pack_queries.1 = (bf16[128,1536]{1,0:T(8,128)(2,1)}, bf16[128,1536]{1,0:T(8,128)(2,1)}, bf16[128,1536]{1,0:T(8,128)(2,1)}, bf16[128,1536]{1,0:T(8,128)(2,1)}, bf16[144,2048]{1,0:T(8,128)(2,1)}) custom-call(bf16[1,128,2048]{2,1,0:T(8,128)(2,1)} %query_ref.1, bf16[1,128,2048]{2,1,0:T(8,128)(2,1)} %grad_ref.1, bf16[1,128,2048]{2,1,0:T(8,128)(2,1)} %forward_ref.1, ...), custom_call_target="tpu_custom_call" | custom-call | bytes 4268032 | tf_op jit(solution)/shard_map/pack_queries/pallas_call | solution.py:343
  17.8 0.0 copy-start
  17.8 0.0 collective-permute-done.4.refs_1_
  17.8 0.0 collective-permute-done.5.refs_2_
  17.8 0.0 collective-permute-done.6.refs_3_
  17.8 2.9 %collective-permute-done.3.refs_5_ = bf16[512,256]{1,0:T(8,128)(2,1)S(1)} collective-permute-done((bf16[512,256]{1,0:T(8,128)(2,1)S(1)}, bf16[512,256]{1,0:T(8,128)(2,1)S(1)}, u32[]{:S(2)}, u32[]{:S(2)}) %collective-permute-start.3) | collective-permute-done | bytes 262176 | tf_op jit(solution)/shard_map/ppermute | solution.py:390
  20.7 0.0 collective-permute-start.9
  20.7 0.0 collective-permute-start.7
  20.7 3.8 %collective-permute-start.8 = (bf16[512,256]{1,0:T(8,128)(2,1)S(1)}, bf16[512,256]{1,0:T(8,128)(2,1)S(1)}, u32[]{:S(2)}, u32[]{:S(2)}) collective-permute-start(bf16[512,256]{1,0:T(8,128)(2,1)S(1)} %stack_keys_bwd.1.refs_4_), channel_id=1, source_target_pairs={{0,24},{2,26},{4,28},{6,30},{8,0},{10,2},{12,4},{14,6},{16,8},{18,... | collective-permute-start | bytes 786440 | tf_op jit(solution)/shard_map/ppermute | solution.py:390
  24.5 1.4 %collective-permute-start.10 = (bf16[128,1536]{1,0:T(8,128)(2,1)}, bf16[128,1536]{1,0:T(8,128)(2,1)S(1)}, u32[]{:S(2)}, u32[]{:S(2)}) collective-permute-start(bf16[128,1536]{1,0:T(8,128)(2,1)} %get-tuple-element.122), channel_id=1, source_target_pairs={{0,4},{2,6},{4,0},{6,2},{8,12},{10,14},{12,8},{14,10},{16,20},{18,... | collective-permute-start | bytes 1179656 | tf_op jit(solution)/shard_map/ppermute | solution.py:384
  25.9 0.0 collective-permute-start.11
  25.9 0.4 stack_keys_fwd.1.refs_4_
  26.3 5.3 %collective-permute-done.7.refs_6_ = bf16[512,256]{1,0:T(8,128)(2,1)S(1)} collective-permute-done((bf16[512,256]{1,0:T(8,128)(2,1)S(1)}, bf16[512,256]{1,0:T(8,128)(2,1)S(1)}, u32[]{:S(2)}, u32[]{:S(2)}) %collective-permute-start.7) | collective-permute-done | bytes 262176 | tf_op jit(solution)/shard_map/ppermute | solution.py:390
  31.6 3.4 %collective-permute-done.8.refs_7_ = bf16[512,256]{1,0:T(8,128)(2,1)S(1)} collective-permute-done((bf16[512,256]{1,0:T(8,128)(2,1)S(1)}, bf16[512,256]{1,0:T(8,128)(2,1)S(1)}, u32[]{:S(2)}, u32[]{:S(2)}) %collective-permute-start.8) | collective-permute-done | bytes 262176 | tf_op jit(solution)/shard_map/ppermute | solution.py:390
  35.0 0.0 collective-permute-done.9.refs_1_
  35.0 1.5 %collective-permute-start.15 = (bf16[144,2048]{1,0:T(8,128)(2,1)}, bf16[144,2048]{1,0:T(8,128)(2,1)S(1)}, u32[]{:S(2)}, u32[]{:S(2)}) collective-permute-start(bf16[144,2048]{1,0:T(8,128)(2,1)} %get-tuple-element.137), channel_id=1, source_target_pairs={{0,1},{1,0},{2,3},{3,2},{4,5},{5,4},{6,7},{7,6},{8,9},{9,8},{10,11... | collective-permute-start | bytes 1769480 | tf_op jit(solution)/shard_map/ppermute | solution.py:401
  36.6 1.0 %collective-permute-start.12 = (bf16[512,256]{1,0:T(8,128)(2,1)S(1)}, bf16[512,256]{1,0:T(8,128)(2,1)S(1)}, u32[]{:S(2)}, u32[]{:S(2)}) collective-permute-start(bf16[512,256]{1,0:T(8,128)(2,1)S(1)} %stack_keys_fwd.1.refs_4_), channel_id=1, source_target_pairs={{0,8},{2,10},{4,12},{6,14},{8,16},{10,18},{12,20},{14,22},{16,24},... | collective-permute-start | bytes 786440 | tf_op jit(solution)/shard_map/ppermute | solution.py:390
  37.6 1.6 %collective-permute-start.13 = (bf16[512,256]{1,0:T(8,128)(2,1)S(1)}, bf16[512,256]{1,0:T(8,128)(2,1)S(1)}, u32[]{:S(2)}, u32[]{:S(2)}) collective-permute-start(bf16[512,256]{1,0:T(8,128)(2,1)S(1)} %stack_keys_fwd.1.refs_4_), channel_id=1, source_target_pairs={{0,16},{2,18},{4,20},{6,22},{8,24},{10,26},{12,28},{14,30},{16,0},... | collective-permute-start | bytes 786440 | tf_op jit(solution)/shard_map/ppermute | solution.py:390
  39.2 0.0 collective-permute-done.10.refs_2_
  39.2 2.7 %collective-permute-start.14 = (bf16[512,256]{1,0:T(8,128)(2,1)S(1)}, bf16[512,256]{1,0:T(8,128)(2,1)S(1)}, u32[]{:S(2)}, u32[]{:S(2)}) collective-permute-start(bf16[512,256]{1,0:T(8,128)(2,1)S(1)} %stack_keys_fwd.1.refs_4_), channel_id=1, source_target_pairs={{0,24},{2,26},{4,28},{6,30},{8,0},{10,2},{12,4},{14,6},{16,8},{18,... | collective-permute-start | bytes 786440 | tf_op jit(solution)/shard_map/ppermute | solution.py:390
  41.9 1.3 %collective-permute-done.11.refs_3_ = bf16[128,1536]{1,0:T(8,128)(2,1)S(1)} collective-permute-done((bf16[128,1536]{1,0:T(8,128)(2,1)}, bf16[128,1536]{1,0:T(8,128)(2,1)S(1)}, u32[]{:S(2)}, u32[]{:S(2)}) %collective-permute-start.11) | collective-permute-done | bytes 393248 | tf_op jit(solution)/shard_map/ppermute | solution.py:384
  43.2 12.8 %backward.1 = (bf16[128,512]{1,0:T(8,128)(2,1)S(1)}, bf16[128,512]{1,0:T(8,128)(2,1)S(1)}, bf16[128,512]{1,0:T(8,128)(2,1)S(1)}, bf16[128,512]{1,0:T(8,128)(2,1)...) custom-call(s32[1,32]{1,0:T(1,128)S(1)} %copy-done.3, ...), custom_call_target="tpu_custom_call" | custom-call | flops 3019898880 | bytes 4194432 | tf_op jit(solution)/shard_map/backward/pallas_call | solution.py:343
  56.0 1.4 %collective-permute-done.13.refs_6_ = bf16[512,256]{1,0:T(8,128)(2,1)S(1)} collective-permute-done((bf16[512,256]{1,0:T(8,128)(2,1)S(1)}, bf16[512,256]{1,0:T(8,128)(2,1)S(1)}, u32[]{:S(2)}, u32[]{:S(2)}) %collective-permute-start.13) | collective-permute-done | bytes 262176 | tf_op jit(solution)/shard_map/ppermute | solution.py:390
  57.4 0.0 collective-permute-done.14.refs_7_
  57.4 5.6 %collective-permute-start.16 = (bf16[512,256]{1,0:T(8,128)(2,1)S(1)}, bf16[512,256]{1,0:T(8,128)(2,1)S(1)}, u32[]{:S(2)}, u32[]{:S(2)}) collective-permute-start(bf16[512,256]{1,0:T(8,128)(2,1)S(1)} %get-tuple-element.150), channel_id=1, source_target_pairs={{0,8},{2,10},{4,12},{6,14},{8,16},{10,18},{12,20},{14,22},{16,24},... | collective-permute-start | bytes 786440 | tf_op jit(solution)/shard_map/ppermute | solution.py:390
  63.0 1.4 %collective-permute-start.17 = (bf16[128,512]{1,0:T(8,128)(2,1)S(1)}, bf16[128,512]{1,0:T(8,128)(2,1)S(1)}, u32[]{:S(2)}, u32[]{:S(2)}) collective-permute-start(bf16[128,512]{1,0:T(8,128)(2,1)S(1)} %get-tuple-element.153), channel_id=1, source_target_pairs={{0,4},{2,6},{4,0},{6,2},{8,12},{10,14},{12,8},{14,10},{16,20},{18,... | collective-permute-start | bytes 393224 | tf_op jit(solution)/shard_map/ppermute | solution.py:384
  64.4 1.4 %collective-permute-start.22 = (bf16[512,256]{1,0:T(8,128)(2,1)S(1)}, bf16[512,256]{1,0:T(8,128)(2,1)S(1)}, u32[]{:S(2)}, u32[]{:S(2)}) collective-permute-start(bf16[512,256]{1,0:T(8,128)(2,1)S(1)} %get-tuple-element.161), channel_id=1, source_target_pairs={{0,24},{2,26},{4,28},{6,30},{8,0},{10,2},{12,4},{14,6},{16,8},{18,... | collective-permute-start | bytes 786440 | tf_op jit(solution)/shard_map/ppermute | solution.py:390
  65.8 4.1 %forward.1 = (bf16[128,512]{1,0:T(8,128)(2,1)S(1)}, bf16[128,512]{1,0:T(8,128)(2,1)S(1)}, bf16[128,512]{1,0:T(8,128)(2,1)S(1)}, bf16[128,512]{1,0:T(8,128)(2,1)S(1)}) custom-call(s32[1,32]{1,0:T(1,128)S(1)} %copy-done.3, bf16[128,1536]{1,0:T(8,128)(2,1)S(1)} %copy-done, bf16[128,1536]{1,0:T(8,128)(2,1)S(1)} %collective-permute-done.9.refs_1_, ...), custom_call_target="tpu_custom_call" | custom-call | bytes 3145856 | tf_op jit(solution)/shard_map/forward/pallas_call | solution.py:343
  69.9 0.0 collective-permute-done.17.refs_2_
  69.9 0.3 collective-permute-done.18.refs_3_
  70.2 0.0 collective-permute-done.16
  70.2 0.1 add_convert_fusion
  70.2 2.1 %collective-permute-start.25 = (bf16[512,256]{1,0:T(8,128)(2,1)S(1)}, bf16[512,256]{1,0:T(8,128)(2,1)S(1)}, u32[]{:S(2)}, u32[]{:S(2)}) collective-permute-start(bf16[512,256]{1,0:T(8,128)(2,1)S(1)} %add_convert_fusion), channel_id=1, source_target_pairs={{0,8},{2,10},{4,12},{6,14},{8,16},{10,18},{12,20},{14,22},{16,24},... | collective-permute-start | bytes 786440 | tf_op jit(solution)/shard_map/ppermute | solution.py:390
  72.3 0.5 collective-permute-start.19
  72.9 2.5 %collective-permute-done.22.refs_2_ = bf16[512,256]{1,0:T(8,128)(2,1)S(1)} collective-permute-done((bf16[512,256]{1,0:T(8,128)(2,1)S(1)}, bf16[512,256]{1,0:T(8,128)(2,1)S(1)}, u32[]{:S(2)}, u32[]{:S(2)}) %collective-permute-start.22) | collective-permute-done | bytes 262176 | tf_op jit(solution)/shard_map/ppermute | solution.py:390
  75.4 0.7 collective-permute-start.23
  76.0 1.9 %collective-permute-start.20 = (bf16[128,512]{1,0:T(8,128)(2,1)S(1)}, bf16[128,512]{1,0:T(8,128)(2,1)S(1)}, u32[]{:S(2)}, u32[]{:S(2)}) collective-permute-start(bf16[128,512]{1,0:T(8,128)(2,1)S(1)} %get-tuple-element.158), channel_id=1, source_target_pairs={{0,3},{1,2},{2,1},{3,0},{4,7},{5,6},{6,5},{7,4},{8,11},{9,10},{10,... | collective-permute-start | bytes 393224 | tf_op jit(solution)/shard_map/ppermute | solution.py:401
  78.0 0.6 collective-permute-start.21
  78.5 2.5 %collective-permute-done.25.refs_1_ = bf16[512,256]{1,0:T(8,128)(2,1)S(1)} collective-permute-done((bf16[512,256]{1,0:T(8,128)(2,1)S(1)}, bf16[512,256]{1,0:T(8,128)(2,1)S(1)}, u32[]{:S(2)}, u32[]{:S(2)}) %collective-permute-start.25) | collective-permute-done | bytes 262176 | tf_op jit(solution)/shard_map/ppermute | solution.py:390
  81.0 0.1 sum_key_parts.1
  81.1 0.1 collective-permute-start.26
  81.2 0.8 collective-permute-done.23.refs_3_
  82.1 1.5 %collective-permute-start.27 = (bf16[128,256]{1,0:T(8,128)(2,1)S(1)}, bf16[128,256]{1,0:T(8,128)(2,1)S(1)}, u32[]{:S(2)}, u32[]{:S(2)}) collective-permute-start(bf16[128,256]{1,0:T(8,128)(2,1)S(1)} %get-tuple-element.174), channel_id=1, source_target_pairs={{0,4},{2,6},{4,0},{6,2},{8,12},{10,14},{12,8},{14,10},{16,20},{18,... | collective-permute-start | bytes 196616 | tf_op jit(solution)/shard_map/ppermute | solution.py:384
  83.6 3.9 %collective-permute-done.20.refs_1_ = bf16[128,512]{1,0:T(8,128)(2,1)S(1)} collective-permute-done((bf16[128,512]{1,0:T(8,128)(2,1)S(1)}, bf16[128,512]{1,0:T(8,128)(2,1)S(1)}, u32[]{:S(2)}, u32[]{:S(2)}) %collective-permute-start.20) | collective-permute-done | bytes 131104 | tf_op jit(solution)/shard_map/ppermute | solution.py:401
  87.5 0.2 collective-permute-start.28
  87.7 1.2 %gate.1 = bf16[1,128,2048]{2,1,0:T(8,128)(2,1)} custom-call(bf16[128,512]{1,0:T(8,128)(2,1)S(1)} %collective-permute-done.19.refs_0_, bf16[128,512]{1,0:T(8,128)(2,1)S(1)} %collective-permute-done.20.refs_1_, bf16[128,512]{1,0:T(8,128)(2,1)S(1)} %collective-permute-done.21.refs_2_, bf16[128,512]{1,0:T(8,128)(2,1)S(1)} %collective-permute-done.23.refs_3_, ...), custom_call_target="tpu_custom_call" | custom-call | bytes 1638400 | tf_op jit(solution)/shard_map/gate/pallas_call | solution.py:343
  88.8 0.0 collective-permute-done.24.refs_1_
  88.8 0.8 query_grad.1
  89.7 1.9 %collective-permute-done.28.refs_3_ = bf16[128,256]{1,0:T(8,128)(2,1)S(1)} collective-permute-done((bf16[128,256]{1,0:T(8,128)(2,1)S(1)}, bf16[128,256]{1,0:T(8,128)(2,1)S(1)}, u32[]{:S(2)}, u32[]{:S(2)}) %collective-permute-start.28) | collective-permute-done | bytes 65568 | tf_op jit(solution)/shard_map/ppermute | solution.py:384
  91.6 0.8 key_grad.1
  (20 shorter events, 0.0 us)
Async XLA Ops:
  2.6 5.1 %collective-permute-start = (bf16[128,256]{1,0:T(8,128)(2,1)}, bf16[128,256]{1,0:T(8,128)(2,1)S(1)}, u32[]{:S(2)}, u32[]{:S(2)}) collective-permute-start(bf16[128,256]{1,0:T(8,128)(2,1)} %get-tuple-element.92), channel_id=1, source_target_pairs={{0,2},{2,0},{4,6},{6,4},{8,10},{10,8},{12,14},{14,12},{16,18},{18,... | collective-permute-start | bytes 196616 | tf_op jit(solution)/shard_map/ppermute | solution.py:384
  3.1 5.5 %collective-permute-start.1 = (bf16[128,256]{1,0:T(8,128)(2,1)}, bf16[128,256]{1,0:T(8,128)(2,1)S(1)}, u32[]{:S(2)}, u32[]{:S(2)}) collective-permute-start(bf16[128,256]{1,0:T(8,128)(2,1)} %get-tuple-element.93), channel_id=1, source_target_pairs={{0,4},{2,6},{4,0},{6,2},{8,12},{10,14},{12,8},{14,10},{16,20},{18,... | collective-permute-start | bytes 196616 | tf_op jit(solution)/shard_map/ppermute | solution.py:384
  5.7 4.4 %copy-start.2 = (bf16[128,256]{1,0:T(8,128)(2,1)S(1)}, bf16[128,256]{1,0:T(8,128)(2,1)}, u32[]{:S(2)}) copy-start(bf16[128,256]{1,0:T(8,128)(2,1)} %get-tuple-element.99.refs_0_) | copy-start | bytes 196612
  5.7 4.3 %collective-permute-start.2 = (bf16[128,256]{1,0:T(8,128)(2,1)}, bf16[128,256]{1,0:T(8,128)(2,1)S(1)}, u32[]{:S(2)}, u32[]{:S(2)}) collective-permute-start(bf16[128,256]{1,0:T(8,128)(2,1)} %get-tuple-element.94), channel_id=1, source_target_pairs={{0,6},{2,4},{4,2},{6,0},{8,14},{10,12},{12,10},{14,8},{16,22},{18,... | collective-permute-start | bytes 196616 | tf_op jit(solution)/shard_map/ppermute | solution.py:384
  10.0 2.0 %copy-start.6 = (bf16[128,256]{1,0:T(8,128)(2,1)S(1)}, bf16[128,256]{1,0:T(8,128)(2,1)}, u32[]{:S(2)}) copy-start(bf16[128,256]{1,0:T(8,128)(2,1)} %get-tuple-element.104) | copy-start | bytes 196612
  10.0 2.0 %copy-start.5 = (bf16[128,256]{1,0:T(8,128)(2,1)S(1)}, bf16[128,256]{1,0:T(8,128)(2,1)}, u32[]{:S(2)}) copy-start(bf16[128,256]{1,0:T(8,128)(2,1)} %get-tuple-element.105) | copy-start | bytes 196612
  10.0 3.4 %copy-start.4 = (bf16[128,256]{1,0:T(8,128)(2,1)S(1)}, bf16[128,256]{1,0:T(8,128)(2,1)}, u32[]{:S(2)}) copy-start(bf16[128,256]{1,0:T(8,128)(2,1)} %get-tuple-element.106) | copy-start | bytes 196612
  10.4 15.5 %copy-start.1 = (bf16[128,256]{1,0:T(8,128)(2,1)S(1)}, bf16[128,256]{1,0:T(8,128)(2,1)}, u32[]{:S(2)}) copy-start(bf16[128,256]{1,0:T(8,128)(2,1)} %get-tuple-element.115.refs_0_) | copy-start | bytes 196612
  10.5 10.2 %collective-permute-start.3 = (bf16[512,256]{1,0:T(8,128)(2,1)S(1)}, bf16[512,256]{1,0:T(8,128)(2,1)S(1)}, u32[]{:S(2)}, u32[]{:S(2)}) collective-permute-start(bf16[512,256]{1,0:T(8,128)(2,1)S(1)} %stack_keys_bwd.1.refs_4_), channel_id=1, source_target_pairs={{0,8},{2,10},{4,12},{6,14},{8,16},{10,18},{12,20},{14,22},{16,24},... | collective-permute-start | bytes 786440 | tf_op jit(solution)/shard_map/ppermute | solution.py:390
  12.1 5.7 %collective-permute-start.4 = (bf16[128,256]{1,0:T(8,128)(2,1)S(1)}, bf16[128,256]{1,0:T(8,128)(2,1)S(1)}, u32[]{:S(2)}, u32[]{:S(2)}) collective-permute-start(bf16[128,256]{1,0:T(8,128)(2,1)S(1)} %copy-done.6), channel_id=1, source_target_pairs={{0,2},{2,0},{4,6},{6,4},{8,10},{10,8},{12,14},{14,12},{16,18},{18,... | collective-permute-start | bytes 196616 | tf_op jit(solution)/shard_map/ppermute | solution.py:384
  12.1 5.7 %collective-permute-start.5 = (bf16[128,256]{1,0:T(8,128)(2,1)S(1)}, bf16[128,256]{1,0:T(8,128)(2,1)S(1)}, u32[]{:S(2)}, u32[]{:S(2)}) collective-permute-start(bf16[128,256]{1,0:T(8,128)(2,1)S(1)} %copy-done.5), channel_id=1, source_target_pairs={{0,4},{2,6},{4,0},{6,2},{8,12},{10,14},{12,8},{14,10},{16,20},{18,... | collective-permute-start | bytes 196616 | tf_op jit(solution)/shard_map/ppermute | solution.py:384
  13.4 4.4 %collective-permute-start.6 = (bf16[128,256]{1,0:T(8,128)(2,1)S(1)}, bf16[128,256]{1,0:T(8,128)(2,1)S(1)}, u32[]{:S(2)}, u32[]{:S(2)}) collective-permute-start(bf16[128,256]{1,0:T(8,128)(2,1)S(1)} %copy-done.4), channel_id=1, source_target_pairs={{0,6},{2,4},{4,2},{6,0},{8,14},{10,12},{12,10},{14,8},{16,22},{18,... | collective-permute-start | bytes 196616 | tf_op jit(solution)/shard_map/ppermute | solution.py:384
  17.8 25.4 %copy-start = (bf16[128,1536]{1,0:T(8,128)(2,1)S(1)}, bf16[128,1536]{1,0:T(8,128)(2,1)}, u32[]{:S(2)}) copy-start(bf16[128,1536]{1,0:T(8,128)(2,1)} %get-tuple-element.112.refs_0_) | copy-start | bytes 1179652
  20.7 22.5 %copy-start.3 = (s32[1,32]{1,0:T(1,128)S(1)}, s32[1,32]{1,0:T(1,128)}, u32[]{:S(2)}) copy-start(s32[1,32]{1,0:T(1,128)} %order_ref.3) | copy-start | bytes 388
  20.7 14.3 %collective-permute-start.9 = (bf16[128,1536]{1,0:T(8,128)(2,1)}, bf16[128,1536]{1,0:T(8,128)(2,1)S(1)}, u32[]{:S(2)}, u32[]{:S(2)}) collective-permute-start(bf16[128,1536]{1,0:T(8,128)(2,1)} %get-tuple-element.119), channel_id=1, source_target_pairs={{0,2},{2,0},{4,6},{6,4},{8,10},{10,8},{12,14},{14,12},{16,18},{18,... | collective-permute-start | bytes 1179656 | tf_op jit(solution)/shard_map/ppermute | solution.py:384
  20.7 10.9 %collective-permute-start.7 = (bf16[512,256]{1,0:T(8,128)(2,1)S(1)}, bf16[512,256]{1,0:T(8,128)(2,1)S(1)}, u32[]{:S(2)}, u32[]{:S(2)}) collective-permute-start(bf16[512,256]{1,0:T(8,128)(2,1)S(1)} %collective-permute-done.3.refs_5_), channel_id=1, source_target_pairs={{0,8},{2,10},{4,12},{6,14},{8,16},{10,18},{12,20},{14,22},{16,24},... | collective-permute-start | bytes 786440 | tf_op jit(solution)/shard_map/ppermute | solution.py:390
  20.7 14.3 %collective-permute-start.8 = (bf16[512,256]{1,0:T(8,128)(2,1)S(1)}, bf16[512,256]{1,0:T(8,128)(2,1)S(1)}, u32[]{:S(2)}, u32[]{:S(2)}) collective-permute-start(bf16[512,256]{1,0:T(8,128)(2,1)S(1)} %stack_keys_bwd.1.refs_4_), channel_id=1, source_target_pairs={{0,24},{2,26},{4,28},{6,30},{8,0},{10,2},{12,4},{14,6},{16,8},{18,... | collective-permute-start | bytes 786440 | tf_op jit(solution)/shard_map/ppermute | solution.py:390
  24.5 14.7 %collective-permute-start.10 = (bf16[128,1536]{1,0:T(8,128)(2,1)}, bf16[128,1536]{1,0:T(8,128)(2,1)S(1)}, u32[]{:S(2)}, u32[]{:S(2)}) collective-permute-start(bf16[128,1536]{1,0:T(8,128)(2,1)} %get-tuple-element.122), channel_id=1, source_target_pairs={{0,4},{2,6},{4,0},{6,2},{8,12},{10,14},{12,8},{14,10},{16,20},{18,... | collective-permute-start | bytes 1179656 | tf_op jit(solution)/shard_map/ppermute | solution.py:384
  25.9 17.2 %collective-permute-start.11 = (bf16[128,1536]{1,0:T(8,128)(2,1)}, bf16[128,1536]{1,0:T(8,128)(2,1)S(1)}, u32[]{:S(2)}, u32[]{:S(2)}) collective-permute-start(bf16[128,1536]{1,0:T(8,128)(2,1)} %get-tuple-element.123), channel_id=1, source_target_pairs={{0,6},{2,4},{4,2},{6,0},{8,14},{10,12},{12,10},{14,8},{16,22},{18,... | collective-permute-start | bytes 1179656 | tf_op jit(solution)/shard_map/ppermute | solution.py:384
  35.0 20.9 %collective-permute-start.15 = (bf16[144,2048]{1,0:T(8,128)(2,1)}, bf16[144,2048]{1,0:T(8,128)(2,1)S(1)}, u32[]{:S(2)}, u32[]{:S(2)}) collective-permute-start(bf16[144,2048]{1,0:T(8,128)(2,1)} %get-tuple-element.137), channel_id=1, source_target_pairs={{0,1},{1,0},{2,3},{3,2},{4,5},{5,4},{6,7},{7,6},{8,9},{9,8},{10,11... | collective-permute-start | bytes 1769480 | tf_op jit(solution)/shard_map/ppermute | solution.py:401
  36.6 19.4 %collective-permute-start.12 = (bf16[512,256]{1,0:T(8,128)(2,1)S(1)}, bf16[512,256]{1,0:T(8,128)(2,1)S(1)}, u32[]{:S(2)}, u32[]{:S(2)}) collective-permute-start(bf16[512,256]{1,0:T(8,128)(2,1)S(1)} %stack_keys_fwd.1.refs_4_), channel_id=1, source_target_pairs={{0,8},{2,10},{4,12},{6,14},{8,16},{10,18},{12,20},{14,22},{16,24},... | collective-permute-start | bytes 786440 | tf_op jit(solution)/shard_map/ppermute | solution.py:390
  37.6 19.8 %collective-permute-start.13 = (bf16[512,256]{1,0:T(8,128)(2,1)S(1)}, bf16[512,256]{1,0:T(8,128)(2,1)S(1)}, u32[]{:S(2)}, u32[]{:S(2)}) collective-permute-start(bf16[512,256]{1,0:T(8,128)(2,1)S(1)} %stack_keys_fwd.1.refs_4_), channel_id=1, source_target_pairs={{0,16},{2,18},{4,20},{6,22},{8,24},{10,26},{12,28},{14,30},{16,0},... | collective-permute-start | bytes 786440 | tf_op jit(solution)/shard_map/ppermute | solution.py:390
  39.2 18.2 %collective-permute-start.14 = (bf16[512,256]{1,0:T(8,128)(2,1)S(1)}, bf16[512,256]{1,0:T(8,128)(2,1)S(1)}, u32[]{:S(2)}, u32[]{:S(2)}) collective-permute-start(bf16[512,256]{1,0:T(8,128)(2,1)S(1)} %stack_keys_fwd.1.refs_4_), channel_id=1, source_target_pairs={{0,24},{2,26},{4,28},{6,30},{8,0},{10,2},{12,4},{14,6},{16,8},{18,... | collective-permute-start | bytes 786440 | tf_op jit(solution)/shard_map/ppermute | solution.py:390
  57.4 12.8 %collective-permute-start.16 = (bf16[512,256]{1,0:T(8,128)(2,1)S(1)}, bf16[512,256]{1,0:T(8,128)(2,1)S(1)}, u32[]{:S(2)}, u32[]{:S(2)}) collective-permute-start(bf16[512,256]{1,0:T(8,128)(2,1)S(1)} %get-tuple-element.150), channel_id=1, source_target_pairs={{0,8},{2,10},{4,12},{6,14},{8,16},{10,18},{12,20},{14,22},{16,24},... | collective-permute-start | bytes 786440 | tf_op jit(solution)/shard_map/ppermute | solution.py:390
  63.0 6.9 %collective-permute-start.17 = (bf16[128,512]{1,0:T(8,128)(2,1)S(1)}, bf16[128,512]{1,0:T(8,128)(2,1)S(1)}, u32[]{:S(2)}, u32[]{:S(2)}) collective-permute-start(bf16[128,512]{1,0:T(8,128)(2,1)S(1)} %get-tuple-element.153), channel_id=1, source_target_pairs={{0,4},{2,6},{4,0},{6,2},{8,12},{10,14},{12,8},{14,10},{16,20},{18,... | collective-permute-start | bytes 393224 | tf_op jit(solution)/shard_map/ppermute | solution.py:384
  64.4 5.8 %collective-permute-start.18 = (bf16[128,512]{1,0:T(8,128)(2,1)S(1)}, bf16[128,512]{1,0:T(8,128)(2,1)S(1)}, u32[]{:S(2)}, u32[]{:S(2)}) collective-permute-start(bf16[128,512]{1,0:T(8,128)(2,1)S(1)} %get-tuple-element.154), channel_id=1, source_target_pairs={{0,6},{2,4},{4,2},{6,0},{8,14},{10,12},{12,10},{14,8},{16,22},{18,... | collective-permute-start | bytes 393224 | tf_op jit(solution)/shard_map/ppermute | solution.py:384
  64.4 11.0 %collective-permute-start.22 = (bf16[512,256]{1,0:T(8,128)(2,1)S(1)}, bf16[512,256]{1,0:T(8,128)(2,1)S(1)}, u32[]{:S(2)}, u32[]{:S(2)}) collective-permute-start(bf16[512,256]{1,0:T(8,128)(2,1)S(1)} %get-tuple-element.161), channel_id=1, source_target_pairs={{0,24},{2,26},{4,28},{6,30},{8,0},{10,2},{12,4},{14,6},{16,8},{18,... | collective-permute-start | bytes 786440 | tf_op jit(solution)/shard_map/ppermute | solution.py:390
  70.2 10.8 %collective-permute-start.25 = (bf16[512,256]{1,0:T(8,128)(2,1)S(1)}, bf16[512,256]{1,0:T(8,128)(2,1)S(1)}, u32[]{:S(2)}, u32[]{:S(2)}) collective-permute-start(bf16[512,256]{1,0:T(8,128)(2,1)S(1)} %add_convert_fusion), channel_id=1, source_target_pairs={{0,8},{2,10},{4,12},{6,14},{8,16},{10,18},{12,20},{14,22},{16,24},... | collective-permute-start | bytes 786440 | tf_op jit(solution)/shard_map/ppermute | solution.py:390
  72.3 6.2 %collective-permute-start.19 = (bf16[128,512]{1,0:T(8,128)(2,1)S(1)}, bf16[128,512]{1,0:T(8,128)(2,1)S(1)}, u32[]{:S(2)}, u32[]{:S(2)}) collective-permute-start(bf16[128,512]{1,0:T(8,128)(2,1)S(1)} %get-tuple-element.155), channel_id=1, source_target_pairs={{0,1},{1,0},{2,3},{3,2},{4,5},{5,4},{6,7},{7,6},{8,9},{9,8},{10,11... | collective-permute-start | bytes 393224 | tf_op jit(solution)/shard_map/ppermute | solution.py:401
  75.4 6.7 %collective-permute-start.23 = (bf16[128,512]{1,0:T(8,128)(2,1)S(1)}, bf16[128,512]{1,0:T(8,128)(2,1)S(1)}, u32[]{:S(2)}, u32[]{:S(2)}) collective-permute-start(bf16[128,512]{1,0:T(8,128)(2,1)S(1)} %get-tuple-element.162), channel_id=1, source_target_pairs={{0,7},{1,6},{2,5},{3,4},{4,3},{5,2},{6,1},{7,0},{8,15},{9,14},{10,... | collective-permute-start | bytes 393224 | tf_op jit(solution)/shard_map/ppermute | solution.py:401
  76.0 11.5 %collective-permute-start.20 = (bf16[128,512]{1,0:T(8,128)(2,1)S(1)}, bf16[128,512]{1,0:T(8,128)(2,1)S(1)}, u32[]{:S(2)}, u32[]{:S(2)}) collective-permute-start(bf16[128,512]{1,0:T(8,128)(2,1)S(1)} %get-tuple-element.158), channel_id=1, source_target_pairs={{0,3},{1,2},{2,1},{3,0},{4,7},{5,6},{6,5},{7,4},{8,11},{9,10},{10,... | collective-permute-start | bytes 393224 | tf_op jit(solution)/shard_map/ppermute | solution.py:401
  78.0 9.7 %collective-permute-start.21 = (bf16[128,512]{1,0:T(8,128)(2,1)S(1)}, bf16[128,512]{1,0:T(8,128)(2,1)S(1)}, u32[]{:S(2)}, u32[]{:S(2)}) collective-permute-start(bf16[128,512]{1,0:T(8,128)(2,1)S(1)} %get-tuple-element.159), channel_id=1, source_target_pairs={{0,5},{1,4},{2,7},{3,6},{4,1},{5,0},{6,3},{7,2},{8,13},{9,12},{10,... | collective-permute-start | bytes 393224 | tf_op jit(solution)/shard_map/ppermute | solution.py:401
  78.5 10.3 %collective-permute-start.24 = (bf16[128,512]{1,0:T(8,128)(2,1)S(1)}, bf16[128,512]{1,0:T(8,128)(2,1)S(1)}, u32[]{:S(2)}, u32[]{:S(2)}) collective-permute-start(bf16[128,512]{1,0:T(8,128)(2,1)S(1)} %get-tuple-element.165), channel_id=1, source_target_pairs={{0,2},{2,0},{4,6},{6,4},{8,10},{10,8},{12,14},{14,12},{16,18},{18,... | collective-permute-start | bytes 393224 | tf_op jit(solution)/shard_map/ppermute | solution.py:384
  81.1 8.5 %collective-permute-start.26 = (bf16[128,256]{1,0:T(8,128)(2,1)S(1)}, bf16[128,256]{1,0:T(8,128)(2,1)S(1)}, u32[]{:S(2)}, u32[]{:S(2)}) collective-permute-start(bf16[128,256]{1,0:T(8,128)(2,1)S(1)} %get-tuple-element.173), channel_id=1, source_target_pairs={{0,2},{2,0},{4,6},{6,4},{8,10},{10,8},{12,14},{14,12},{16,18},{18,... | collective-permute-start | bytes 196616 | tf_op jit(solution)/shard_map/ppermute | solution.py:384
  82.1 7.6 %collective-permute-start.27 = (bf16[128,256]{1,0:T(8,128)(2,1)S(1)}, bf16[128,256]{1,0:T(8,128)(2,1)S(1)}, u32[]{:S(2)}, u32[]{:S(2)}) collective-permute-start(bf16[128,256]{1,0:T(8,128)(2,1)S(1)} %get-tuple-element.174), channel_id=1, source_target_pairs={{0,4},{2,6},{4,0},{6,2},{8,12},{10,14},{12,8},{14,10},{16,20},{18,... | collective-permute-start | bytes 196616 | tf_op jit(solution)/shard_map/ppermute | solution.py:384
  87.5 4.1 %collective-permute-start.28 = (bf16[128,256]{1,0:T(8,128)(2,1)S(1)}, bf16[128,256]{1,0:T(8,128)(2,1)S(1)}, u32[]{:S(2)}, u32[]{:S(2)}) collective-permute-start(bf16[128,256]{1,0:T(8,128)(2,1)S(1)} %get-tuple-element.175), channel_id=1, source_target_pairs={{0,6},{2,4},{4,2},{6,0},{8,14},{10,12},{12,10},{14,8},{16,22},{18,... | collective-permute-start | bytes 196616 | tf_op jit(solution)/shard_map/ppermute | solution.py:384

commit v9 on v7

--- a/solution.py
+++ b/solution.py
@@ -12,7 +12,6 @@
 QUAD = 4
 SCALE = HEAD ** (-0.5)
 EXP2_SCALE = -SCALE / math.log(2.0)
-GAIN_ROWS = 16
 norm_eps = 1e-06
 
 VMEM = pl.BlockSpec(memory_space=pltpu.VMEM)
@@ -85,11 +84,10 @@
         copy.wait()
 
 
-def pack_queries(query_ref, grad_ref, forward_ref, gate_ref, gain_ref, *refs):
-    pieces, (gate_out, placed) = refs[:QUAD], refs[QUAD:]
+def pack_queries(query_ref, grad_ref, forward_ref, *refs):
+    pieces, placed = refs[:QUAD], refs[QUAD]
     _, member = place()
     width = query_ref.shape[2] // QUAD
-    rows = gate_ref.shape[1]
     copies = [
         pltpu.make_async_copy(
             source.at[0, :, columns(member ^ d, width)],
@@ -99,19 +97,8 @@
         for d in reversed(range(QUAD))
         for i, source in enumerate([query_ref, grad_ref, forward_ref])
     ]
-    copies.append(
-        pltpu.make_async_copy(gate_ref.at[0], gate_out.at[:rows, :], placed.at[3 * QUAD])
-    )
     for copy in copies:
         copy.start()
-    rest = gain_ref[...]
-    parts = []
-    for _ in range(3):
-        part = rest.astype(jnp.bfloat16).astype(jnp.float32)
-        parts.append(part)
-        rest = rest - part
-    parts.append(jnp.zeros((GAIN_ROWS - 3, rest.shape[1]), jnp.float32))
-    gate_out[rows:, :] = jnp.concatenate(parts, axis=0).astype(jnp.bfloat16)
     for copy in copies:
         copy.wait()
 
@@ -323,17 +310,15 @@
 
 
 def gate_kernel(*refs):
-    pieces, (gate_ref, out) = refs[:QUAD], refs[QUAD:]
+    pieces, (gate_ref, gain_ref, out) = refs[:QUAD], refs[QUAD:]
     _, member = place()
-    rows = out.shape[1]
     attended = [piece[...].astype(jnp.float32) for piece in pieces]
     square = sum(jnp.sum(part * part, axis=1, keepdims=True) for part in attended)
     factor = lax.rsqrt(square / out.shape[2] + norm_eps)
     for d in range(QUAD):
         head = columns(member ^ d, pieces[d].shape[1])
-        gain = sum(gate_ref[rows : rows + GAIN_ROWS, head].astype(jnp.float32)[i : i + 1] for i in range(3))
         out[0, :, head] = (
-            attended[d] * factor * gain * gate_ref[:rows, head].astype(jnp.float32)
+            attended[d] * factor * gain_ref[:, head] * gate_ref[0, :, head].astype(jnp.float32)
         ).astype(jnp.bfloat16)
 
 
@@ -463,35 +448,38 @@
             scratch=[pltpu.SemaphoreType.DMA((QUAD,))],
         )[0]
 
-    back_pieces = swap(pack(key_bwd, value_bwd, types_bwd, "pack_keys_bwd"))
+    back_pieces, gate_before = lax.optimization_barrier(
+        (pack(key_bwd, value_bwd, types_bwd, "pack_keys_bwd"), gate_fwd)
+    )
+    back_pieces, gate_before = swap(back_pieces), hand(gate_before, 0)
     pieces = pack(key_fwd, value_fwd, types_fwd, "pack_keys_fwd")
     back_pieces, pieces = lax.optimization_barrier((back_pieces, pieces))
     pieces = swap(pieces)
     packed = call(
         pack_queries,
         "pack_queries",
-        [bf16(rows, 3 * width)] * QUAD + [bf16(rows + GAIN_ROWS, QUAD * width)],
-        [HBM] * 4 + [VMEM],
+        [bf16(rows, 3 * width)] * QUAD,
+        [HBM] * 3,
         query_bwd,
         grad_out,
         query_fwd,
-        gate_fwd,
-        norm_gain,
-        scratch=[pltpu.SemaphoreType.DMA((3 * QUAD + 1,))],
+        scratch=[pltpu.SemaphoreType.DMA((3 * QUAD,))],
         vmem=60,
     )
     packed = list(packed)
     back_stack = stacked_keys(back_pieces, "stack_keys_bwd")
     up = [back_stack, ring_up(back_stack)]
-    up, pieces, packed = lax.optimization_barrier((up, pieces, packed))
+    up, pieces, packed, gate_before, gain_before = lax.optimization_barrier(
+        (up, pieces, packed, gate_before, norm_gain)
+    )
     back_stacks = gather_ring(up)
     stack = stacked_keys(pieces, "stack_keys_fwd")
-    back_stacks, stack, packed[1], packed[QUAD] = lax.optimization_barrier(
-        (back_stacks, stack, packed[1], packed[QUAD])
-    )
-    queries = swap(packed[:QUAD])
+    gain_before = hand(gain_before, 0)
+    back_stacks, stack, packed[1], gain_before = lax.optimization_barrier(
+        (back_stacks, stack, packed[1], gain_before)
+    )
+    queries = swap(packed)
     stacks = gather(stack)
-    gate_before = hand(packed[QUAD], 0)
 
     sequence = [pltpu.VMEM((total_rows, HEAD), jnp.bfloat16)] * 2
     stacked = pltpu.VMEM((2 * QUAD, block_rows, HEAD), jnp.bfloat16)
@@ -518,9 +506,6 @@
         transcendentals=2 * pairs,
     )
     query_pieces, key_parts = outs[:QUAD], outs[QUAD:]
-    query_pieces, key_parts, gate_before = lax.optimization_barrier(
-        (query_pieces, key_parts, gate_before)
-    )
     query_pieces = list(query_pieces)
     query_pieces[2:] = [swap_one(query_pieces[d], d) for d in range(2, QUAD)]
     stacks, key_parts = lax.optimization_barrier((stacks, key_parts))
@@ -547,9 +532,10 @@
         gate_kernel,
         "gate",
         [bf16(*gate_fwd.shape)],
-        [VMEM] * (QUAD + 1),
+        [VMEM] * (QUAD + 2),
         *attended,
         gate_before,
+        gain_before,
     )
     key_sums = reduce_rest(key_parts, key_up, key_sums[1])
     key_pieces = swap(

time: 89.7 us -> 90.4 us (level)
  starting transfers between devices: 32.4 us -> 35.3 us
  waiting for transfers between devices: 28 us -> 26.9 us
  Pallas kernels: 28.2 us -> 27.1 us
    ppermute x9, waiting for transfers between devices: 13 us -> 10.6 us  [turn(): lax.ppermute(block, 'ctx', [(i, (i + s * QUAD) % devices) for i in range(...]
    ppermute x5 -> x6, starting transfers between devices: 4.45 us -> 6.58 us  [hand(): return lax.ppermute(block, ('ctx', 'pipe'), route)]
    ppermute x9, starting transfers between devices: 16.4 us -> 18.3 us  [turn(): lax.ppermute(block, 'ctx', [(i, (i + s * QUAD) % devices) for i in range(...]
    pallas_call x11, Pallas kernels: 28.2 us -> 27.1 us  [call(): pl.pallas_call(kernel, name=name, out_shape=out_shape, in_specs=specs, ou...]
    ppermute x5 -> x6, waiting for transfers between devices: 7.73 us -> 8.83 us  [hand(): return lax.ppermute(block, ('ctx', 'pipe'), route)]
    ppermute x15, starting transfers between devices: 11.5 us -> 10.5 us  [swap_one(): return lax.ppermute(piece, 'ctx', [(i, i ^ d) for i in range(devices)])]
  transfers between devices with their start and end apart: 29 -> 30, of which waited for: 13 -> 14; matrix products, arithmetic and copies ran while one was open for 0% -> 0% of each run, Pallas kernels for 28% -> 27%
where the time goes in v9:
time: 90.4 us; the launch traced here: 90.3 us
  starting transfers between devices  35.3 us (39%)
  Pallas kernels  27.1 us (30%)
  waiting for transfers between devices  26.9 us (30%)
    pallas_call x11, Pallas kernels, call(): pl.pallas_call(kernel, name=name, out_shape=out_shape, in_specs=specs, ou...  27.1 us
    ppermute x9, starting transfers between devices, turn(): lax.ppermute(block, 'ctx', [(i, (i + s * QUAD) % devices) for i in range(...  18.3 us
    ppermute x9, waiting for transfers between devices, turn(): lax.ppermute(block, 'ctx', [(i, (i + s * QUAD) % devices) for i in range(...  10.6 us
    ppermute x15, starting transfers between devices, swap_one(): return lax.ppermute(piece, 'ctx', [(i, i ^ d) for i in range(devices)])  10.5 us
    ppermute x6, waiting for transfers between devices, hand(): return lax.ppermute(block, ('ctx', 'pipe'), route)  8.83 us
    ppermute x15, waiting for transfers between devices, swap_one(): return lax.ppermute(piece, 'ctx', [(i, i ^ d) for i in range(devices)])  7.42 us
    ppermute x6, starting transfers between devices, hand(): return lax.ppermute(block, ('ctx', 'pipe'), route)  6.58 us
  transfers between devices with their start and end apart: 30, of which 14 were waited for; matrix products, arithmetic and copies ran while one was open for 0% of the time, Pallas kernels for 27%

profile of v9, /device:TPU:0, one launch (start us, length us, event | category | flops | bytes accessed | tf_op | source)
XLA Modules:
  0.0 90.3 jit_solution(5116719036261034036)
XLA Ops:
  0.6 2.0 %pack_keys_bwd.1 = (bf16[128,256]{1,0:T(8,128)(2,1)}, bf16[128,256]{1,0:T(8,128)(2,1)}, bf16[128,256]{1,0:T(8,128)(2,1)}, bf16[128,256]{1,0:T(8,128)(2,1)}) custom-call(bf16[1,128,512]{2,1,0:T(8,128)(2,1)} %key_ref.2, bf16[1,128,512]{2,1,0:T(8,128)(2,1)} %value_ref.2, s32[1,128]{1,0:T(1,128)} %types_ref.2, bf16[1,64,512]{2,1,0:T(8,128)(2,1)} %table_ref.3), custom_call_target="tpu_custom_call" | custom-call | bytes 590336 | tf_op jit(solution)/shard_map/pack_keys_bwd/pallas_call | solution.py:328
  2.6 3.0 %collective-permute-start.7 = (bf16[1,128,2048]{2,1,0:T(8,128)(2,1)}, bf16[1,128,2048]{2,1,0:T(8,128)(2,1)S(1)}, u32[]{:S(2)}, u32[]{:S(2)}) collective-permute-start(bf16[1,128,2048]{2,1,0:T(8,128)(2,1)} %param.16), channel_id=1, source_target_pairs={{0,1},{1,0},{2,3},{3,2},{4,5},{5,4},{6,7},{7,6},{8,9},{9,8},{10,11... | collective-permute-start | bytes 1572872 | tf_op jit(solution)/shard_map/ppermute | solution.py:386
  5.6 0.0 collective-permute-start
  5.7 1.5 %collective-permute-start.1 = (bf16[128,256]{1,0:T(8,128)(2,1)}, bf16[128,256]{1,0:T(8,128)(2,1)S(1)}, u32[]{:S(2)}, u32[]{:S(2)}) collective-permute-start(bf16[128,256]{1,0:T(8,128)(2,1)} %get-tuple-element.91), channel_id=1, source_target_pairs={{0,4},{2,6},{4,0},{6,2},{8,12},{10,14},{12,8},{14,10},{16,20},{18,... | collective-permute-start | bytes 196616 | tf_op jit(solution)/shard_map/ppermute | solution.py:369
  7.1 0.4 collective-permute-start.2
  7.5 2.0 %pack_keys_fwd.1 = (bf16[128,256]{1,0:T(8,128)(2,1)}, bf16[128,256]{1,0:T(8,128)(2,1)}, bf16[128,256]{1,0:T(8,128)(2,1)}, bf16[128,256]{1,0:T(8,128)(2,1)}) custom-call(bf16[1,128,512]{2,1,0:T(8,128)(2,1)} %key_ref.3, bf16[1,128,512]{2,1,0:T(8,128)(2,1)} %value_ref.3, s32[1,128]{1,0:T(1,128)} %types_ref.3, bf16[1,64,512]{2,1,0:T(8,128)(2,1)} %table_ref.3), custom_call_target="tpu_custom_call" | custom-call | bytes 590336 | tf_op jit(solution)/shard_map/pack_keys_fwd/pallas_call | solution.py:328
  9.5 0.0 collective-permute-done.refs_1_
  9.5 0.9 %collective-permute-done.1.refs_2_ = bf16[128,256]{1,0:T(8,128)(2,1)S(1)} collective-permute-done((bf16[128,256]{1,0:T(8,128)(2,1)}, bf16[128,256]{1,0:T(8,128)(2,1)S(1)}, u32[]{:S(2)}, u32[]{:S(2)}) %collective-permute-start.1) | collective-permute-done | bytes 65568 | tf_op jit(solution)/shard_map/ppermute | solution.py:369
  10.4 1.1 %collective-permute-done.2.refs_3_ = bf16[128,256]{1,0:T(8,128)(2,1)S(1)} collective-permute-done((bf16[128,256]{1,0:T(8,128)(2,1)}, bf16[128,256]{1,0:T(8,128)(2,1)S(1)}, u32[]{:S(2)}, u32[]{:S(2)}) %collective-permute-start.2) | collective-permute-done | bytes 65568 | tf_op jit(solution)/shard_map/ppermute | solution.py:369
  11.5 0.4 stack_keys_bwd.1.refs_4_
  11.9 0.0 copy-start.7
  11.9 0.0 copy-start.1
  11.9 1.6 %collective-permute-start.3 = (bf16[512,256]{1,0:T(8,128)(2,1)S(1)}, bf16[512,256]{1,0:T(8,128)(2,1)S(1)}, u32[]{:S(2)}, u32[]{:S(2)}) collective-permute-start(bf16[512,256]{1,0:T(8,128)(2,1)S(1)} %stack_keys_bwd.1.refs_4_), channel_id=1, source_target_pairs={{0,8},{2,10},{4,12},{6,14},{8,16},{10,18},{12,20},{14,22},{16,24},... | collective-permute-start | bytes 786440 | tf_op jit(solution)/shard_map/ppermute | solution.py:375
  13.5 0.1 collective-permute-start.4
  13.7 1.5 %collective-permute-start.5 = (bf16[128,256]{1,0:T(8,128)(2,1)S(1)}, bf16[128,256]{1,0:T(8,128)(2,1)S(1)}, u32[]{:S(2)}, u32[]{:S(2)}) collective-permute-start(bf16[128,256]{1,0:T(8,128)(2,1)S(1)} %copy-done.5), channel_id=1, source_target_pairs={{0,4},{2,6},{4,0},{6,2},{8,12},{10,14},{12,8},{14,10},{16,20},{18,... | collective-permute-start | bytes 196616 | tf_op jit(solution)/shard_map/ppermute | solution.py:369
  15.2 0.2 collective-permute-start.6
  15.4 2.7 %pack_queries.1 = (bf16[128,1536]{1,0:T(8,128)(2,1)}, bf16[128,1536]{1,0:T(8,128)(2,1)}, bf16[128,1536]{1,0:T(8,128)(2,1)}, bf16[128,1536]{1,0:T(8,128)(2,1)}) custom-call(bf16[1,128,2048]{2,1,0:T(8,128)(2,1)} %query_ref.1, bf16[1,128,2048]{2,1,0:T(8,128)(2,1)} %grad_ref.1, bf16[1,128,2048]{2,1,0:T(8,128)(2,1)} %forward_ref.1), custom_call_target="tpu_custom_call" | custom-call | bytes 3145728 | tf_op jit(solution)/shard_map/pack_queries/pallas_call | solution.py:328
  18.1 0.0 copy-start
  18.1 0.0 collective-permute-done.4.refs_1_
  18.1 0.0 collective-permute-done.5.refs_2_
  18.2 1.2 %collective-permute-done.6.refs_3_ = bf16[128,256]{1,0:T(8,128)(2,1)S(1)} collective-permute-done((bf16[128,256]{1,0:T(8,128)(2,1)S(1)}, bf16[128,256]{1,0:T(8,128)(2,1)S(1)}, u32[]{:S(2)}, u32[]{:S(2)}) %collective-permute-start.6) | collective-permute-done | bytes 65568 | tf_op jit(solution)/shard_map/ppermute | solution.py:369
  19.4 3.1 %collective-permute-done.3.refs_5_ = bf16[512,256]{1,0:T(8,128)(2,1)S(1)} collective-permute-done((bf16[512,256]{1,0:T(8,128)(2,1)S(1)}, bf16[512,256]{1,0:T(8,128)(2,1)S(1)}, u32[]{:S(2)}, u32[]{:S(2)}) %collective-permute-start.3) | collective-permute-done | bytes 262176 | tf_op jit(solution)/shard_map/ppermute | solution.py:375
  22.4 0.0 collective-permute-done.7.refs_4_
  22.5 3.8 %collective-permute-start.9 = (bf16[512,256]{1,0:T(8,128)(2,1)S(1)}, bf16[512,256]{1,0:T(8,128)(2,1)S(1)}, u32[]{:S(2)}, u32[]{:S(2)}) collective-permute-start(bf16[512,256]{1,0:T(8,128)(2,1)S(1)} %stack_keys_bwd.1.refs_4_), channel_id=1, source_target_pairs={{0,24},{2,26},{4,28},{6,30},{8,0},{10,2},{12,4},{14,6},{16,8},{18,... | collective-permute-start | bytes 786440 | tf_op jit(solution)/shard_map/ppermute | solution.py:375
  26.3 0.5 collective-permute-start.10
  26.8 1.5 %collective-permute-start.12 = (bf16[128,1536]{1,0:T(8,128)(2,1)}, bf16[128,1536]{1,0:T(8,128)(2,1)S(1)}, u32[]{:S(2)}, u32[]{:S(2)}) collective-permute-start(bf16[128,1536]{1,0:T(8,128)(2,1)} %get-tuple-element.120), channel_id=1, source_target_pairs={{0,4},{2,6},{4,0},{6,2},{8,12},{10,14},{12,8},{14,10},{16,20},{18,... | collective-permute-start | bytes 1179656 | tf_op jit(solution)/shard_map/ppermute | solution.py:369
  28.3 0.0 collective-permute-start.13
  28.3 0.4 stack_keys_fwd.1.refs_4_
  28.7 1.3 %collective-permute-done.10.refs_5_ = f32[1,2048]{1,0:T(1,128)S(1)} collective-permute-done((f32[1,2048]{1,0:T(1,128)S(1)}, f32[1,2048]{1,0:T(1,128)S(1)}, u32[]{:S(2)}, u32[]{:S(2)}) %collective-permute-start.10) | collective-permute-done | bytes 8224 | tf_op jit(solution)/shard_map/ppermute | solution.py:386
  29.9 3.5 %collective-permute-done.8.refs_6_ = bf16[512,256]{1,0:T(8,128)(2,1)S(1)} collective-permute-done((bf16[512,256]{1,0:T(8,128)(2,1)S(1)}, bf16[512,256]{1,0:T(8,128)(2,1)S(1)}, u32[]{:S(2)}, u32[]{:S(2)}) %collective-permute-start.8) | collective-permute-done | bytes 262176 | tf_op jit(solution)/shard_map/ppermute | solution.py:375
  33.5 2.6 %collective-permute-done.9.refs_7_ = bf16[512,256]{1,0:T(8,128)(2,1)S(1)} collective-permute-done((bf16[512,256]{1,0:T(8,128)(2,1)S(1)}, bf16[512,256]{1,0:T(8,128)(2,1)S(1)}, u32[]{:S(2)}, u32[]{:S(2)}) %collective-permute-start.9) | collective-permute-done | bytes 262176 | tf_op jit(solution)/shard_map/ppermute | solution.py:375
  36.0 0.9 %collective-permute-start.14 = (bf16[512,256]{1,0:T(8,128)(2,1)S(1)}, bf16[512,256]{1,0:T(8,128)(2,1)S(1)}, u32[]{:S(2)}, u32[]{:S(2)}) collective-permute-start(bf16[512,256]{1,0:T(8,128)(2,1)S(1)} %stack_keys_fwd.1.refs_4_), channel_id=1, source_target_pairs={{0,8},{2,10},{4,12},{6,14},{8,16},{10,18},{12,20},{14,22},{16,24},... | collective-permute-start | bytes 786440 | tf_op jit(solution)/shard_map/ppermute | solution.py:375
  36.9 1.7 %collective-permute-start.15 = (bf16[512,256]{1,0:T(8,128)(2,1)S(1)}, bf16[512,256]{1,0:T(8,128)(2,1)S(1)}, u32[]{:S(2)}, u32[]{:S(2)}) collective-permute-start(bf16[512,256]{1,0:T(8,128)(2,1)S(1)} %stack_keys_fwd.1.refs_4_), channel_id=1, source_target_pairs={{0,16},{2,18},{4,20},{6,22},{8,24},{10,26},{12,28},{14,30},{16,0},... | collective-permute-start | bytes 786440 | tf_op jit(solution)/shard_map/ppermute | solution.py:375
  38.6 0.4 collective-permute-done.12.refs_2_
  39.0 2.3 %collective-permute-start.16 = (bf16[512,256]{1,0:T(8,128)(2,1)S(1)}, bf16[512,256]{1,0:T(8,128)(2,1)S(1)}, u32[]{:S(2)}, u32[]{:S(2)}) collective-permute-start(bf16[512,256]{1,0:T(8,128)(2,1)S(1)} %stack_keys_fwd.1.refs_4_), channel_id=1, source_target_pairs={{0,24},{2,26},{4,28},{6,30},{8,0},{10,2},{12,4},{14,6},{16,8},{18,... | collective-permute-start | bytes 786440 | tf_op jit(solution)/shard_map/ppermute | solution.py:375
  41.3 3.2 %collective-permute-done.13.refs_3_ = bf16[128,1536]{1,0:T(8,128)(2,1)S(1)} collective-permute-done((bf16[128,1536]{1,0:T(8,128)(2,1)}, bf16[128,1536]{1,0:T(8,128)(2,1)S(1)}, u32[]{:S(2)}, u32[]{:S(2)}) %collective-permute-start.13) | collective-permute-done | bytes 393248 | tf_op jit(solution)/shard_map/ppermute | solution.py:369
  44.5 0.0 collective-permute-done.11.refs_1_
  44.5 12.8 %backward.1 = (bf16[128,512]{1,0:T(8,128)(2,1)S(1)}, bf16[128,512]{1,0:T(8,128)(2,1)S(1)}, bf16[128,512]{1,0:T(8,128)(2,1)S(1)}, bf16[128,512]{1,0:T(8,128)(2,1)...) custom-call(s32[1,32]{1,0:T(1,128)S(1)} %copy-done.3, ...), custom_call_target="tpu_custom_call" | custom-call | flops 3019898880 | bytes 4194432 | tf_op jit(solution)/shard_map/backward/pallas_call | solution.py:328
  57.3 0.6 collective-permute-done.15.refs_6_
  57.9 0.0 collective-permute-done.16.refs_7_
  57.9 5.9 %collective-permute-start.17 = (bf16[512,256]{1,0:T(8,128)(2,1)S(1)}, bf16[512,256]{1,0:T(8,128)(2,1)S(1)}, u32[]{:S(2)}, u32[]{:S(2)}) collective-permute-start(bf16[512,256]{1,0:T(8,128)(2,1)S(1)} %get-tuple-element.139), channel_id=1, source_target_pairs={{0,8},{2,10},{4,12},{6,14},{8,16},{10,18},{12,20},{14,22},{16,24},... | collective-permute-start | bytes 786440 | tf_op jit(solution)/shard_map/ppermute | solution.py:375
  63.7 1.6 %collective-permute-start.18 = (bf16[128,512]{1,0:T(8,128)(2,1)S(1)}, bf16[128,512]{1,0:T(8,128)(2,1)S(1)}, u32[]{:S(2)}, u32[]{:S(2)}) collective-permute-start(bf16[128,512]{1,0:T(8,128)(2,1)S(1)} %get-tuple-element.142), channel_id=1, source_target_pairs={{0,4},{2,6},{4,0},{6,2},{8,12},{10,14},{12,8},{14,10},{16,20},{18,... | collective-permute-start | bytes 393224 | tf_op jit(solution)/shard_map/ppermute | solution.py:369
  65.3 1.1 %collective-permute-start.26 = (bf16[512,256]{1,0:T(8,128)(2,1)S(1)}, bf16[512,256]{1,0:T(8,128)(2,1)S(1)}, u32[]{:S(2)}, u32[]{:S(2)}) collective-permute-start(bf16[512,256]{1,0:T(8,128)(2,1)S(1)} %get-tuple-element.159), channel_id=1, source_target_pairs={{0,24},{2,26},{4,28},{6,30},{8,0},{10,2},{12,4},{14,6},{16,8},{18,... | collective-permute-start | bytes 786440 | tf_op jit(solution)/shard_map/ppermute | solution.py:375
  66.5 4.1 %forward.1 = (bf16[128,512]{1,0:T(8,128)(2,1)S(1)}, bf16[128,512]{1,0:T(8,128)(2,1)S(1)}, bf16[128,512]{1,0:T(8,128)(2,1)S(1)}, bf16[128,512]{1,0:T(8,128)(2,1)S(1)}) custom-call(s32[1,32]{1,0:T(1,128)S(1)} %copy-done.3, bf16[128,1536]{1,0:T(8,128)(2,1)S(1)} %copy-done, bf16[128,1536]{1,0:T(8,128)(2,1)S(1)} %collective-permute-done.11.refs_1_, ...), custom_call_target="tpu_custom_call" | custom-call | bytes 3145856 | tf_op jit(solution)/shard_map/forward/pallas_call | solution.py:328
  70.5 0.0 collective-permute-done.18.refs_2_
  70.5 0.6 collective-permute-done.19.refs_3_
  71.1 0.9 %collective-permute-done.17 = bf16[512,256]{1,0:T(8,128)(2,1)S(1)} collective-permute-done((bf16[512,256]{1,0:T(8,128)(2,1)S(1)}, bf16[512,256]{1,0:T(8,128)(2,1)S(1)}, u32[]{:S(2)}, u32[]{:S(2)}) %collective-permute-start.17) | collective-permute-done | bytes 262176 | tf_op jit(solution)/shard_map/ppermute | solution.py:375
  72.0 0.1 add_convert_fusion
  72.1 1.0 %collective-permute-start.25 = (bf16[512,256]{1,0:T(8,128)(2,1)S(1)}, bf16[512,256]{1,0:T(8,128)(2,1)S(1)}, u32[]{:S(2)}, u32[]{:S(2)}) collective-permute-start(bf16[512,256]{1,0:T(8,128)(2,1)S(1)} %add_convert_fusion), channel_id=1, source_target_pairs={{0,8},{2,10},{4,12},{6,14},{8,16},{10,18},{12,20},{14,22},{16,24},... | collective-permute-start | bytes 786440 | tf_op jit(solution)/shard_map/ppermute | solution.py:375
  73.1 0.5 collective-permute-start.20
  73.6 2.5 %collective-permute-start.22 = (bf16[128,512]{1,0:T(8,128)(2,1)S(1)}, bf16[128,512]{1,0:T(8,128)(2,1)S(1)}, u32[]{:S(2)}, u32[]{:S(2)}) collective-permute-start(bf16[128,512]{1,0:T(8,128)(2,1)S(1)} %get-tuple-element.148), channel_id=1, source_target_pairs={{0,5},{1,4},{2,7},{3,6},{4,1},{5,0},{6,3},{7,2},{8,13},{9,12},{10,... | collective-permute-start | bytes 393224 | tf_op jit(solution)/shard_map/ppermute | solution.py:386
  76.1 6.1 %collective-permute-done.20.refs_0_ = bf16[128,512]{1,0:T(8,128)(2,1)S(1)} collective-permute-done((bf16[128,512]{1,0:T(8,128)(2,1)S(1)}, bf16[128,512]{1,0:T(8,128)(2,1)S(1)}, u32[]{:S(2)}, u32[]{:S(2)}) %collective-permute-start.20) | collective-permute-done | bytes 131104 | tf_op jit(solution)/shard_map/ppermute | solution.py:386
  82.2 0.7 collective-permute-start.24
  82.8 0.0 collective-permute-done.25.refs_1_
  82.9 0.1 sum_key_parts.1
  83.0 0.1 collective-permute-start.27
  83.0 1.4 %collective-permute-start.28 = (bf16[128,256]{1,0:T(8,128)(2,1)S(1)}, bf16[128,256]{1,0:T(8,128)(2,1)S(1)}, u32[]{:S(2)}, u32[]{:S(2)}) collective-permute-start(bf16[128,256]{1,0:T(8,128)(2,1)S(1)} %get-tuple-element.162), channel_id=1, source_target_pairs={{0,4},{2,6},{4,0},{6,2},{8,12},{10,14},{12,8},{14,10},{16,20},{18,... | collective-permute-start | bytes 196616 | tf_op jit(solution)/shard_map/ppermute | solution.py:369
  84.4 1.6 %collective-permute-start.29 = (bf16[128,256]{1,0:T(8,128)(2,1)S(1)}, bf16[128,256]{1,0:T(8,128)(2,1)S(1)}, u32[]{:S(2)}, u32[]{:S(2)}) collective-permute-start(bf16[128,256]{1,0:T(8,128)(2,1)S(1)} %get-tuple-element.163), channel_id=1, source_target_pairs={{0,6},{2,4},{4,2},{6,0},{8,14},{10,12},{12,10},{14,8},{16,22},{18,... | collective-permute-start | bytes 196616 | tf_op jit(solution)/shard_map/ppermute | solution.py:369
  86.0 1.5 %collective-permute-done.23.refs_3_ = bf16[128,512]{1,0:T(8,128)(2,1)S(1)} collective-permute-done((bf16[128,512]{1,0:T(8,128)(2,1)S(1)}, bf16[128,512]{1,0:T(8,128)(2,1)S(1)}, u32[]{:S(2)}, u32[]{:S(2)}) %collective-permute-start.23) | collective-permute-done | bytes 131104 | tf_op jit(solution)/shard_map/ppermute | solution.py:386
  87.5 1.2 %gate.1 = bf16[1,128,2048]{2,1,0:T(8,128)(2,1)} custom-call(bf16[128,512]{1,0:T(8,128)(2,1)S(1)} %collective-permute-done.20.refs_0_, bf16[128,512]{1,0:T(8,128)(2,1)S(1)} %collective-permute-done.21.refs_1_, bf16[128,512]{1,0:T(8,128)(2,1)S(1)} %collective-permute-done.22.refs_2_, bf16[128,512]{1,0:T(8,128)(2,1)S(1)} %collective-permute-done.23.refs_3_, ...), custom_call_target="tpu_custom_call" | custom-call | bytes 1581056 | tf_op jit(solution)/shard_map/gate/pallas_call | solution.py:328
  88.6 0.0 collective-permute-done.24.refs_1_
  88.6 0.8 query_grad.1
  89.5 0.0 collective-permute-done.27.refs_1_
  89.5 0.8 key_grad.1
  (24 shorter events, 0.1 us)
Async XLA Ops:
  2.6 8.9 %copy-start.2 = (bf16[128,256]{1,0:T(8,128)(2,1)S(1)}, bf16[128,256]{1,0:T(8,128)(2,1)}, u32[]{:S(2)}) copy-start(bf16[128,256]{1,0:T(8,128)(2,1)} %get-tuple-element.97.refs_0_) | copy-start | bytes 196612
  2.6 19.8 %collective-permute-start.7 = (bf16[1,128,2048]{2,1,0:T(8,128)(2,1)}, bf16[1,128,2048]{2,1,0:T(8,128)(2,1)S(1)}, u32[]{:S(2)}, u32[]{:S(2)}) collective-permute-start(bf16[1,128,2048]{2,1,0:T(8,128)(2,1)} %param.16), channel_id=1, source_target_pairs={{0,1},{1,0},{2,3},{3,2},{4,5},{5,4},{6,7},{7,6},{8,9},{9,8},{10,11... | collective-permute-start | bytes 1572872 | tf_op jit(solution)/shard_map/ppermute | solution.py:386
  5.6 3.8 %collective-permute-start = (bf16[128,256]{1,0:T(8,128)(2,1)}, bf16[128,256]{1,0:T(8,128)(2,1)S(1)}, u32[]{:S(2)}, u32[]{:S(2)}) collective-permute-start(bf16[128,256]{1,0:T(8,128)(2,1)} %get-tuple-element.90), channel_id=1, source_target_pairs={{0,2},{2,0},{4,6},{6,4},{8,10},{10,8},{12,14},{14,12},{16,18},{18,... | collective-permute-start | bytes 196616 | tf_op jit(solution)/shard_map/ppermute | solution.py:369
  5.7 4.8 %collective-permute-start.1 = (bf16[128,256]{1,0:T(8,128)(2,1)}, bf16[128,256]{1,0:T(8,128)(2,1)S(1)}, u32[]{:S(2)}, u32[]{:S(2)}) collective-permute-start(bf16[128,256]{1,0:T(8,128)(2,1)} %get-tuple-element.91), channel_id=1, source_target_pairs={{0,4},{2,6},{4,0},{6,2},{8,12},{10,14},{12,8},{14,10},{16,20},{18,... | collective-permute-start | bytes 196616 | tf_op jit(solution)/shard_map/ppermute | solution.py:369
  7.1 4.3 %collective-permute-start.2 = (bf16[128,256]{1,0:T(8,128)(2,1)}, bf16[128,256]{1,0:T(8,128)(2,1)S(1)}, u32[]{:S(2)}, u32[]{:S(2)}) collective-permute-start(bf16[128,256]{1,0:T(8,128)(2,1)} %get-tuple-element.92), channel_id=1, source_target_pairs={{0,6},{2,4},{4,2},{6,0},{8,14},{10,12},{12,10},{14,8},{16,22},{18,... | collective-permute-start | bytes 196616 | tf_op jit(solution)/shard_map/ppermute | solution.py:369
  11.5 2.1 %copy-start.6 = (bf16[128,256]{1,0:T(8,128)(2,1)S(1)}, bf16[128,256]{1,0:T(8,128)(2,1)}, u32[]{:S(2)}) copy-start(bf16[128,256]{1,0:T(8,128)(2,1)} %get-tuple-element.102) | copy-start | bytes 196612
  11.5 2.2 %copy-start.5 = (bf16[128,256]{1,0:T(8,128)(2,1)S(1)}, bf16[128,256]{1,0:T(8,128)(2,1)}, u32[]{:S(2)}) copy-start(bf16[128,256]{1,0:T(8,128)(2,1)} %get-tuple-element.103) | copy-start | bytes 196612
  11.5 3.7 %copy-start.4 = (bf16[128,256]{1,0:T(8,128)(2,1)S(1)}, bf16[128,256]{1,0:T(8,128)(2,1)}, u32[]{:S(2)}) copy-start(bf16[128,256]{1,0:T(8,128)(2,1)} %get-tuple-element.104) | copy-start | bytes 196612
  11.9 14.4 %copy-start.7 = (f32[1,2048]{1,0:T(1,128)S(1)}, f32[1,2048]{1,0:T(1,128)}, u32[]{:S(2)}) copy-start(f32[1,2048]{1,0:T(1,128)} %param.24) | copy-start | bytes 24580
  11.9 16.4 %copy-start.1 = (bf16[128,256]{1,0:T(8,128)(2,1)S(1)}, bf16[128,256]{1,0:T(8,128)(2,1)}, u32[]{:S(2)}) copy-start(bf16[128,256]{1,0:T(8,128)(2,1)} %get-tuple-element.113.refs_0_) | copy-start | bytes 196612
  11.9 10.5 %collective-permute-start.3 = (bf16[512,256]{1,0:T(8,128)(2,1)S(1)}, bf16[512,256]{1,0:T(8,128)(2,1)S(1)}, u32[]{:S(2)}, u32[]{:S(2)}) collective-permute-start(bf16[512,256]{1,0:T(8,128)(2,1)S(1)} %stack_keys_bwd.1.refs_4_), channel_id=1, source_target_pairs={{0,8},{2,10},{4,12},{6,14},{8,16},{10,18},{12,20},{14,22},{16,24},... | collective-permute-start | bytes 786440 | tf_op jit(solution)/shard_map/ppermute | solution.py:375
  13.5 4.6 %collective-permute-start.4 = (bf16[128,256]{1,0:T(8,128)(2,1)S(1)}, bf16[128,256]{1,0:T(8,128)(2,1)S(1)}, u32[]{:S(2)}, u32[]{:S(2)}) collective-permute-start(bf16[128,256]{1,0:T(8,128)(2,1)S(1)} %copy-done.6), channel_id=1, source_target_pairs={{0,2},{2,0},{4,6},{6,4},{8,10},{10,8},{12,14},{14,12},{16,18},{18,... | collective-permute-start | bytes 196616 | tf_op jit(solution)/shard_map/ppermute | solution.py:369
  13.7 4.5 %collective-permute-start.5 = (bf16[128,256]{1,0:T(8,128)(2,1)S(1)}, bf16[128,256]{1,0:T(8,128)(2,1)S(1)}, u32[]{:S(2)}, u32[]{:S(2)}) collective-permute-start(bf16[128,256]{1,0:T(8,128)(2,1)S(1)} %copy-done.5), channel_id=1, source_target_pairs={{0,4},{2,6},{4,0},{6,2},{8,12},{10,14},{12,8},{14,10},{16,20},{18,... | collective-permute-start | bytes 196616 | tf_op jit(solution)/shard_map/ppermute | solution.py:369
  15.2 4.2 %collective-permute-start.6 = (bf16[128,256]{1,0:T(8,128)(2,1)S(1)}, bf16[128,256]{1,0:T(8,128)(2,1)S(1)}, u32[]{:S(2)}, u32[]{:S(2)}) collective-permute-start(bf16[128,256]{1,0:T(8,128)(2,1)S(1)} %copy-done.4), channel_id=1, source_target_pairs={{0,6},{2,4},{4,2},{6,0},{8,14},{10,12},{12,10},{14,8},{16,22},{18,... | collective-permute-start | bytes 196616 | tf_op jit(solution)/shard_map/ppermute | solution.py:369
  18.1 26.4 %copy-start = (bf16[128,1536]{1,0:T(8,128)(2,1)S(1)}, bf16[128,1536]{1,0:T(8,128)(2,1)}, u32[]{:S(2)}) copy-start(bf16[128,1536]{1,0:T(8,128)(2,1)} %get-tuple-element.110.refs_0_) | copy-start | bytes 1179652
  22.4 22.1 %copy-start.3 = (s32[1,32]{1,0:T(1,128)S(1)}, s32[1,32]{1,0:T(1,128)}, u32[]{:S(2)}) copy-start(s32[1,32]{1,0:T(1,128)} %order_ref.3) | copy-start | bytes 388
  22.4 11.0 %collective-permute-start.8 = (bf16[512,256]{1,0:T(8,128)(2,1)S(1)}, bf16[512,256]{1,0:T(8,128)(2,1)S(1)}, u32[]{:S(2)}, u32[]{:S(2)}) collective-permute-start(bf16[512,256]{1,0:T(8,128)(2,1)S(1)} %collective-permute-done.3.refs_5_), channel_id=1, source_target_pairs={{0,8},{2,10},{4,12},{6,14},{8,16},{10,18},{12,20},{14,22},{16,24},... | collective-permute-start | bytes 786440 | tf_op jit(solution)/shard_map/ppermute | solution.py:375
  22.5 13.6 %collective-permute-start.9 = (bf16[512,256]{1,0:T(8,128)(2,1)S(1)}, bf16[512,256]{1,0:T(8,128)(2,1)S(1)}, u32[]{:S(2)}, u32[]{:S(2)}) collective-permute-start(bf16[512,256]{1,0:T(8,128)(2,1)S(1)} %stack_keys_bwd.1.refs_4_), channel_id=1, source_target_pairs={{0,24},{2,26},{4,28},{6,30},{8,0},{10,2},{12,4},{14,6},{16,8},{18,... | collective-permute-start | bytes 786440 | tf_op jit(solution)/shard_map/ppermute | solution.py:375
  26.3 3.7 %collective-permute-start.10 = (f32[1,2048]{1,0:T(1,128)S(1)}, f32[1,2048]{1,0:T(1,128)S(1)}, u32[]{:S(2)}, u32[]{:S(2)}) collective-permute-start(f32[1,2048]{1,0:T(1,128)S(1)} %copy-done.7), channel_id=1, source_target_pairs={{0,1},{1,0},{2,3},{3,2},{4,5},{5,4},{6,7},{7,6},{8,9},{9,8},{10,11... | collective-permute-start | bytes 24584 | tf_op jit(solution)/shard_map/ppermute | solution.py:386
  26.8 12.3 %collective-permute-start.12 = (bf16[128,1536]{1,0:T(8,128)(2,1)}, bf16[128,1536]{1,0:T(8,128)(2,1)S(1)}, u32[]{:S(2)}, u32[]{:S(2)}) collective-permute-start(bf16[128,1536]{1,0:T(8,128)(2,1)} %get-tuple-element.120), channel_id=1, source_target_pairs={{0,4},{2,6},{4,0},{6,2},{8,12},{10,14},{12,8},{14,10},{16,20},{18,... | collective-permute-start | bytes 1179656 | tf_op jit(solution)/shard_map/ppermute | solution.py:369
  28.3 16.2 %collective-permute-start.13 = (bf16[128,1536]{1,0:T(8,128)(2,1)}, bf16[128,1536]{1,0:T(8,128)(2,1)S(1)}, u32[]{:S(2)}, u32[]{:S(2)}) collective-permute-start(bf16[128,1536]{1,0:T(8,128)(2,1)} %get-tuple-element.121), channel_id=1, source_target_pairs={{0,6},{2,4},{4,2},{6,0},{8,14},{10,12},{12,10},{14,8},{16,22},{18,... | collective-permute-start | bytes 1179656 | tf_op jit(solution)/shard_map/ppermute | solution.py:369
  36.0 8.5 %collective-permute-start.11 = (bf16[128,1536]{1,0:T(8,128)(2,1)}, bf16[128,1536]{1,0:T(8,128)(2,1)S(1)}, u32[]{:S(2)}, u32[]{:S(2)}) collective-permute-start(bf16[128,1536]{1,0:T(8,128)(2,1)} %get-tuple-element.119), channel_id=1, source_target_pairs={{0,2},{2,0},{4,6},{6,4},{8,10},{10,8},{12,14},{14,12},{16,18},{18,... | collective-permute-start | bytes 1179656 | tf_op jit(solution)/shard_map/ppermute | solution.py:369
  36.0 21.3 %collective-permute-start.14 = (bf16[512,256]{1,0:T(8,128)(2,1)S(1)}, bf16[512,256]{1,0:T(8,128)(2,1)S(1)}, u32[]{:S(2)}, u32[]{:S(2)}) collective-permute-start(bf16[512,256]{1,0:T(8,128)(2,1)S(1)} %stack_keys_fwd.1.refs_4_), channel_id=1, source_target_pairs={{0,8},{2,10},{4,12},{6,14},{8,16},{10,18},{12,20},{14,22},{16,24},... | collective-permute-start | bytes 786440 | tf_op jit(solution)/shard_map/ppermute | solution.py:375
  36.9 20.9 %collective-permute-start.15 = (bf16[512,256]{1,0:T(8,128)(2,1)S(1)}, bf16[512,256]{1,0:T(8,128)(2,1)S(1)}, u32[]{:S(2)}, u32[]{:S(2)}) collective-permute-start(bf16[512,256]{1,0:T(8,128)(2,1)S(1)} %stack_keys_fwd.1.refs_4_), channel_id=1, source_target_pairs={{0,16},{2,18},{4,20},{6,22},{8,24},{10,26},{12,28},{14,30},{16,0},... | collective-permute-start | bytes 786440 | tf_op jit(solution)/shard_map/ppermute | solution.py:375
  39.0 18.8 %collective-permute-start.16 = (bf16[512,256]{1,0:T(8,128)(2,1)S(1)}, bf16[512,256]{1,0:T(8,128)(2,1)S(1)}, u32[]{:S(2)}, u32[]{:S(2)}) collective-permute-start(bf16[512,256]{1,0:T(8,128)(2,1)S(1)} %stack_keys_fwd.1.refs_4_), channel_id=1, source_target_pairs={{0,24},{2,26},{4,28},{6,30},{8,0},{10,2},{12,4},{14,6},{16,8},{18,... | collective-permute-start | bytes 786440 | tf_op jit(solution)/shard_map/ppermute | solution.py:375
  57.9 14.1 %collective-permute-start.17 = (bf16[512,256]{1,0:T(8,128)(2,1)S(1)}, bf16[512,256]{1,0:T(8,128)(2,1)S(1)}, u32[]{:S(2)}, u32[]{:S(2)}) collective-permute-start(bf16[512,256]{1,0:T(8,128)(2,1)S(1)} %get-tuple-element.139), channel_id=1, source_target_pairs={{0,8},{2,10},{4,12},{6,14},{8,16},{10,18},{12,20},{14,22},{16,24},... | collective-permute-start | bytes 786440 | tf_op jit(solution)/shard_map/ppermute | solution.py:375
  63.7 6.8 %collective-permute-start.18 = (bf16[128,512]{1,0:T(8,128)(2,1)S(1)}, bf16[128,512]{1,0:T(8,128)(2,1)S(1)}, u32[]{:S(2)}, u32[]{:S(2)}) collective-permute-start(bf16[128,512]{1,0:T(8,128)(2,1)S(1)} %get-tuple-element.142), channel_id=1, source_target_pairs={{0,4},{2,6},{4,0},{6,2},{8,12},{10,14},{12,8},{14,10},{16,20},{18,... | collective-permute-start | bytes 393224 | tf_op jit(solution)/shard_map/ppermute | solution.py:369
  65.3 5.8 %collective-permute-start.19 = (bf16[128,512]{1,0:T(8,128)(2,1)S(1)}, bf16[128,512]{1,0:T(8,128)(2,1)S(1)}, u32[]{:S(2)}, u32[]{:S(2)}) collective-permute-start(bf16[128,512]{1,0:T(8,128)(2,1)S(1)} %get-tuple-element.143), channel_id=1, source_target_pairs={{0,6},{2,4},{4,2},{6,0},{8,14},{10,12},{12,10},{14,8},{16,22},{18,... | collective-permute-start | bytes 393224 | tf_op jit(solution)/shard_map/ppermute | solution.py:369
  65.3 16.9 %collective-permute-start.26 = (bf16[512,256]{1,0:T(8,128)(2,1)S(1)}, bf16[512,256]{1,0:T(8,128)(2,1)S(1)}, u32[]{:S(2)}, u32[]{:S(2)}) collective-permute-start(bf16[512,256]{1,0:T(8,128)(2,1)S(1)} %get-tuple-element.159), channel_id=1, source_target_pairs={{0,24},{2,26},{4,28},{6,30},{8,0},{10,2},{12,4},{14,6},{16,8},{18,... | collective-permute-start | bytes 786440 | tf_op jit(solution)/shard_map/ppermute | solution.py:375
  72.1 10.8 %collective-permute-start.25 = (bf16[512,256]{1,0:T(8,128)(2,1)S(1)}, bf16[512,256]{1,0:T(8,128)(2,1)S(1)}, u32[]{:S(2)}, u32[]{:S(2)}) collective-permute-start(bf16[512,256]{1,0:T(8,128)(2,1)S(1)} %add_convert_fusion), channel_id=1, source_target_pairs={{0,8},{2,10},{4,12},{6,14},{8,16},{10,18},{12,20},{14,22},{16,24},... | collective-permute-start | bytes 786440 | tf_op jit(solution)/shard_map/ppermute | solution.py:375
  73.1 9.1 %collective-permute-start.20 = (bf16[128,512]{1,0:T(8,128)(2,1)S(1)}, bf16[128,512]{1,0:T(8,128)(2,1)S(1)}, u32[]{:S(2)}, u32[]{:S(2)}) collective-permute-start(bf16[128,512]{1,0:T(8,128)(2,1)S(1)} %get-tuple-element.144), channel_id=1, source_target_pairs={{0,1},{1,0},{2,3},{3,2},{4,5},{5,4},{6,7},{7,6},{8,9},{9,8},{10,11... | collective-permute-start | bytes 393224 | tf_op jit(solution)/shard_map/ppermute | solution.py:386
  73.6 9.5 %collective-permute-start.21 = (bf16[128,512]{1,0:T(8,128)(2,1)S(1)}, bf16[128,512]{1,0:T(8,128)(2,1)S(1)}, u32[]{:S(2)}, u32[]{:S(2)}) collective-permute-start(bf16[128,512]{1,0:T(8,128)(2,1)S(1)} %get-tuple-element.147), channel_id=1, source_target_pairs={{0,3},{1,2},{2,1},{3,0},{4,7},{5,6},{6,5},{7,4},{8,11},{9,10},{10,... | collective-permute-start | bytes 393224 | tf_op jit(solution)/shard_map/ppermute | solution.py:386
  73.6 10.9 %collective-permute-start.22 = (bf16[128,512]{1,0:T(8,128)(2,1)S(1)}, bf16[128,512]{1,0:T(8,128)(2,1)S(1)}, u32[]{:S(2)}, u32[]{:S(2)}) collective-permute-start(bf16[128,512]{1,0:T(8,128)(2,1)S(1)} %get-tuple-element.148), channel_id=1, source_target_pairs={{0,5},{1,4},{2,7},{3,6},{4,1},{5,0},{6,3},{7,2},{8,13},{9,12},{10,... | collective-permute-start | bytes 393224 | tf_op jit(solution)/shard_map/ppermute | solution.py:386
  82.2 5.3 %collective-permute-start.23 = (bf16[128,512]{1,0:T(8,128)(2,1)S(1)}, bf16[128,512]{1,0:T(8,128)(2,1)S(1)}, u32[]{:S(2)}, u32[]{:S(2)}) collective-permute-start(bf16[128,512]{1,0:T(8,128)(2,1)S(1)} %get-tuple-element.149), channel_id=1, source_target_pairs={{0,7},{1,6},{2,5},{3,4},{4,3},{5,2},{6,1},{7,0},{8,15},{9,14},{10,... | collective-permute-start | bytes 393224 | tf_op jit(solution)/shard_map/ppermute | solution.py:386
  82.2 6.4 %collective-permute-start.24 = (bf16[128,512]{1,0:T(8,128)(2,1)S(1)}, bf16[128,512]{1,0:T(8,128)(2,1)S(1)}, u32[]{:S(2)}, u32[]{:S(2)}) collective-permute-start(bf16[128,512]{1,0:T(8,128)(2,1)S(1)} %get-tuple-element.153), channel_id=1, source_target_pairs={{0,2},{2,0},{4,6},{6,4},{8,10},{10,8},{12,14},{14,12},{16,18},{18,... | collective-permute-start | bytes 393224 | tf_op jit(solution)/shard_map/ppermute | solution.py:369
  83.0 6.5 %collective-permute-start.27 = (bf16[128,256]{1,0:T(8,128)(2,1)S(1)}, bf16[128,256]{1,0:T(8,128)(2,1)S(1)}, u32[]{:S(2)}, u32[]{:S(2)}) collective-permute-start(bf16[128,256]{1,0:T(8,128)(2,1)S(1)} %get-tuple-element.161), channel_id=1, source_target_pairs={{0,2},{2,0},{4,6},{6,4},{8,10},{10,8},{12,14},{14,12},{16,18},{18,... | collective-permute-start | bytes 196616 | tf_op jit(solution)/shard_map/ppermute | solution.py:369
  83.0 6.4 %collective-permute-start.28 = (bf16[128,256]{1,0:T(8,128)(2,1)S(1)}, bf16[128,256]{1,0:T(8,128)(2,1)S(1)}, u32[]{:S(2)}, u32[]{:S(2)}) collective-permute-start(bf16[128,256]{1,0:T(8,128)(2,1)S(1)} %get-tuple-element.162), channel_id=1, source_target_pairs={{0,4},{2,6},{4,0},{6,2},{8,12},{10,14},{12,8},{14,10},{16,20},{18,... | collective-permute-start | bytes 196616 | tf_op jit(solution)/shard_map/ppermute | solution.py:369
  84.4 5.0 %collective-permute-start.29 = (bf16[128,256]{1,0:T(8,128)(2,1)S(1)}, bf16[128,256]{1,0:T(8,128)(2,1)S(1)}, u32[]{:S(2)}, u32[]{:S(2)}) collective-permute-start(bf16[128,256]{1,0:T(8,128)(2,1)S(1)} %get-tuple-element.163), channel_id=1, source_target_pairs={{0,6},{2,4},{4,2},{6,0},{8,14},{10,12},{12,10},{14,8},{16,22},{18,... | collective-permute-start | bytes 196616 | tf_op jit(solution)/shard_map/ppermute | solution.py:369

commit v10 on v7

--- a/solution.py
+++ b/solution.py
@@ -216,12 +216,21 @@
                 ).astype(jnp.bfloat16)
 
 
-def backward_kernel(nz, order_ref, *refs):
-    queries, refs = refs[:QUAD], refs[QUAD:]
+def backward_kernel(nz, parts, first, order_ref, *refs):
+    queries, refs = refs[: len(parts)], refs[len(parts) :]
     stacks, refs = refs[:nz], refs[nz:]
-    query_outs, refs = refs[:QUAD], refs[QUAD:]
-    key_outs, refs = refs[:nz], refs[nz:]
-    keys, values, keys_t, stacked, grads, total_t, key_total, value_total, gap = refs
+    if first:
+        query_outs, refs = refs[: len(parts)], refs[len(parts) :]
+        key_total, value_total, keys, values, keys_t, stacked, grads, total_t, gap = refs
+        key_total[...] = jnp.zeros_like(key_total)
+        value_total[...] = jnp.zeros_like(value_total)
+    else:
+        (key_before, value_before), refs = refs[:2], refs[2:]
+        query_outs, refs = refs[: len(parts)], refs[len(parts) :]
+        key_outs, refs = refs[:nz], refs[nz:]
+        key_total, value_total, keys, values, keys_t, stacked, grads, total_t, gap = refs
+        key_total[...] = key_before[...]
+        value_total[...] = value_before[...]
     z, member = place()
     stretch_rows = queries[0].shape[0] // 2
     groups = query_outs[0].shape[1] // HEAD
@@ -233,33 +242,31 @@
         lower = block * block_rows
         keys_t[block] = keys[lower : lower + block_rows, :].T
     offset = groups * HEAD
-    for d in range(QUAD):
+    for i, d in enumerate(parts):
         for e in range(2):
             shrink = shrink_of(stretch_of(order_ref, z, member, d, e), stretch_rows)
             rows = slice(e * stretch_rows, (e + 1) * stretch_rows)
             for g in range(groups):
                 into = slice(g * stretch_rows, (g + 1) * stretch_rows)
-                stacked[2 * d + e, into, :] = queries[d][rows, g * HEAD : (g + 1) * HEAD]
-                grads[2 * d + e, into, :] = (
-                    queries[d][rows, offset + g * HEAD : offset + (g + 1) * HEAD].astype(
+                stacked[2 * i + e, into, :] = queries[i][rows, g * HEAD : (g + 1) * HEAD]
+                grads[2 * i + e, into, :] = (
+                    queries[i][rows, offset + g * HEAD : offset + (g + 1) * HEAD].astype(
                         jnp.float32
                     )
                     * shrink
                 ).astype(jnp.bfloat16)
     total_t[...] = jnp.zeros_like(total_t)
-    key_total[...] = jnp.zeros_like(key_total)
-    value_total[...] = jnp.zeros_like(value_total)
     gap[...] = lax.broadcasted_iota(jnp.int32, gap.shape, 0) - lax.rem(
         lax.broadcasted_iota(jnp.int32, gap.shape, 1), stretch_rows
     )
 
     def advance(step):
-        for d in range(QUAD):
+        for i, d in enumerate(parts):
             row, stretch, block = step_place(
                 stretch_of(order_ref, z, member, d, 0),
                 stretch_of(order_ref, z, member, d, 1),
                 step,
-                d,
+                i,
                 groups,
             )
             rows = rows_at(block, block_rows)
@@ -275,13 +282,15 @@
             value_total[rows, :] += dot(weights, grads[row], NN)
 
     repeat(steps, 3, advance)
-    for d in range(QUAD):
+    for i in range(len(parts)):
         for e in range(2):
-            query_grad = (total_t[2 * d + e].T * SCALE).astype(jnp.bfloat16)
+            query_grad = (total_t[2 * i + e].T * SCALE).astype(jnp.bfloat16)
             for g in range(groups):
-                query_outs[d][
+                query_outs[i][
                     e * stretch_rows : (e + 1) * stretch_rows, g * HEAD : (g + 1) * HEAD
                 ] = query_grad[g * stretch_rows : (g + 1) * stretch_rows, :]
+    if first:
+        return
     for s in range(nz):
         target = lax.rem(z + s, nz)
         for d in range(QUAD):
@@ -490,40 +499,54 @@
         (back_stacks, stack, packed[1], packed[QUAD])
     )
     queries = swap(packed[:QUAD])
-    stacks = gather(stack)
+    up, down = [stack, ring_up(stack)], [ring_down(stack)]
     gate_before = hand(packed[QUAD], 0)
 
     sequence = [pltpu.VMEM((total_rows, HEAD), jnp.bfloat16)] * 2
     stacked = pltpu.VMEM((2 * QUAD, block_rows, HEAD), jnp.bfloat16)
     gap = pltpu.VMEM((block_rows, block_rows), jnp.int32)
-    outs = call(
-        functools.partial(backward_kernel, nz),
-        "backward",
-        [bf16(rows, width)] * QUAD + [bf16(QUAD * rows, 2 * HEAD)] * nz,
-        [SMEM] + [VMEM] * (QUAD + nz),
-        stretch_order,
-        *queries,
-        *back_stacks,
-        scratch=sequence
-        + [
-            pltpu.VMEM((total_rows // block_rows, HEAD, block_rows), jnp.bfloat16),
-            stacked,
-            stacked,
-            pltpu.VMEM((2 * QUAD, HEAD, block_rows), jnp.float32),
-            pltpu.VMEM((total_rows, HEAD), jnp.float32),
-            pltpu.VMEM((total_rows, HEAD), jnp.float32),
-            gap,
-        ],
-        flops=10 * pairs * HEAD,
-        transcendentals=2 * pairs,
-    )
-    query_pieces, key_parts = outs[:QUAD], outs[QUAD:]
-    query_pieces, key_parts, gate_before = lax.optimization_barrier(
-        (query_pieces, key_parts, gate_before)
-    )
-    query_pieces = list(query_pieces)
-    query_pieces[2:] = [swap_one(query_pieces[d], d) for d in range(2, QUAD)]
-    stacks, key_parts = lax.optimization_barrier((stacks, key_parts))
+    sums = jax.ShapeDtypeStruct((total_rows, HEAD), jnp.float32)
+
+    def backward(parts, name, out_shape, scratch, *before):
+        return call(
+            functools.partial(backward_kernel, nz, parts, not before),
+            name,
+            [bf16(rows, width)] * len(parts) + out_shape,
+            [SMEM] + [VMEM] * (len(parts) + nz + len(before)),
+            stretch_order,
+            *[queries[d] for d in parts],
+            *back_stacks,
+            *before,
+            scratch=scratch
+            + sequence
+            + [
+                pltpu.VMEM((total_rows // block_rows, HEAD, block_rows), jnp.bfloat16),
+                pltpu.VMEM((2 * len(parts), block_rows, HEAD), jnp.bfloat16),
+                pltpu.VMEM((2 * len(parts), block_rows, HEAD), jnp.bfloat16),
+                pltpu.VMEM((2 * len(parts), HEAD, block_rows), jnp.float32),
+                gap,
+            ],
+            flops=5 * pairs * HEAD,
+            transcendentals=pairs,
+        )
+
+    far = backward((0, 2), "backward_first", [sums] * 2, [])
+    far, up, down, gate_before = lax.optimization_barrier((far, up, down, gate_before))
+    while len(up) <= ahead:
+        up.append(ring_up(up[-1]))
+    while len(up) + len(down) < nz:
+        down.append(ring_down(down[-1]))
+    stacks = up + down[::-1]
+    far_piece = swap_one(far[1], 2)
+    near = backward(
+        (1, 3),
+        "backward_second",
+        [bf16(QUAD * rows, 2 * HEAD)] * nz,
+        [pltpu.VMEM(sums.shape, jnp.float32)] * 2,
+        *far[2:],
+    )
+    near, stacks, far_piece = lax.optimization_barrier((near, stacks, far_piece))
+    query_pieces, key_parts = [far[0], near[0], far_piece, swap_one(near[1], 3)], near[2:]
     key_sums = reduce_first(key_parts)
     parts = tuple(range(QUAD))
     attended = call(

time: 89.7 us -> 89.2 us (level)
  starting transfers between devices: 32.4 us -> 29.1 us
  Pallas kernels: 28.2 us -> 29.9 us
    ppermute x9, waiting for transfers between devices: 13 us -> 20.2 us  [turn(): lax.ppermute(block, 'ctx', [(i, (i + s * QUAD) % devices) for i in range(...]
    ppermute x9, starting transfers between devices: 16.4 us -> 10.2 us  [turn(): lax.ppermute(block, 'ctx', [(i, (i + s * QUAD) % devices) for i in range(...]
    ppermute x15, waiting for transfers between devices: 7.27 us -> 2.34 us  [swap_one(): return lax.ppermute(piece, 'ctx', [(i, i ^ d) for i in range(devices)])]
    ppermute x15, starting transfers between devices: 11.5 us -> 13.4 us  [swap_one(): return lax.ppermute(piece, 'ctx', [(i, i ^ d) for i in range(devices)])]
    pallas_call x11 -> x12, Pallas kernels: 28.2 us -> 29.9 us  [call(): pl.pallas_call(kernel, name=name, out_shape=out_shape, in_specs=specs, ou...]
    ppermute x5, waiting for transfers between devices: 7.73 us -> 6.25 us  [hand(): return lax.ppermute(block, ('ctx', 'pipe'), route)]
    ppermute x5, starting transfers between devices: 4.45 us -> 5.52 us  [hand(): return lax.ppermute(block, ('ctx', 'pipe'), route)]
  transfers between devices with their start and end apart: 29 -> 29, of which waited for: 13 -> 10; matrix products, arithmetic and copies ran while one was open for 0% -> 0% of each run, Pallas kernels for 28% -> 30%
where the time goes in v10:
time: 89.2 us; the launch traced here: 88.7 us
  Pallas kernels  29.9 us (34%)
  starting transfers between devices  29.1 us (33%)
  waiting for transfers between devices  28.7 us (32%)
    pallas_call x12, Pallas kernels, call(): pl.pallas_call(kernel, name=name, out_shape=out_shape, in_specs=specs, ou...  29.9 us
    ppermute x9, waiting for transfers between devices, turn(): lax.ppermute(block, 'ctx', [(i, (i + s * QUAD) % devices) for i in range(...  20.2 us
    ppermute x15, starting transfers between devices, swap_one(): return lax.ppermute(piece, 'ctx', [(i, i ^ d) for i in range(devices)])  13.4 us
    ppermute x9, starting transfers between devices, turn(): lax.ppermute(block, 'ctx', [(i, (i + s * QUAD) % devices) for i in range(...  10.2 us
    ppermute x5, waiting for transfers between devices, hand(): return lax.ppermute(block, ('ctx', 'pipe'), route)  6.25 us
    ppermute x5, starting transfers between devices, hand(): return lax.ppermute(block, ('ctx', 'pipe'), route)  5.52 us
    ppermute x15, waiting for transfers between devices, swap_one(): return lax.ppermute(piece, 'ctx', [(i, i ^ d) for i in range(devices)])  2.34 us
  transfers between devices with their start and end apart: 29, of which 10 were waited for; matrix products, arithmetic and copies ran while one was open for 0% of the time, Pallas kernels for 30%

profile of v10, /device:TPU:0, one launch (start us, length us, event | category | flops | bytes accessed | tf_op | source)
XLA Modules:
  0.0 88.7 jit_solution(14828487989074974401)
XLA Ops:
  0.6 2.0 %pack_keys_bwd.1 = (bf16[128,256]{1,0:T(8,128)(2,1)}, bf16[128,256]{1,0:T(8,128)(2,1)}, bf16[128,256]{1,0:T(8,128)(2,1)}, bf16[128,256]{1,0:T(8,128)(2,1)}) custom-call(bf16[1,128,512]{2,1,0:T(8,128)(2,1)} %key_ref.2, bf16[1,128,512]{2,1,0:T(8,128)(2,1)} %value_ref.2, s32[1,128]{1,0:T(1,128)} %types_ref.2, bf16[1,64,512]{2,1,0:T(8,128)(2,1)} %table_ref.3), custom_call_target="tpu_custom_call" | custom-call | bytes 590336 | tf_op jit(solution)/shard_map/pack_keys_bwd/pallas_call | solution.py:352
  2.6 0.5 collective-permute-start
  3.1 2.6 %collective-permute-start.1 = (bf16[128,256]{1,0:T(8,128)(2,1)}, bf16[128,256]{1,0:T(8,128)(2,1)S(1)}, u32[]{:S(2)}, u32[]{:S(2)}) collective-permute-start(bf16[128,256]{1,0:T(8,128)(2,1)} %get-tuple-element.95), channel_id=1, source_target_pairs={{0,4},{2,6},{4,0},{6,2},{8,12},{10,14},{12,8},{14,10},{16,20},{18,... | collective-permute-start | bytes 196616 | tf_op jit(solution)/shard_map/ppermute | solution.py:393
  5.7 0.1 collective-permute-start.2
  5.8 2.0 %pack_keys_fwd.1 = (bf16[128,256]{1,0:T(8,128)(2,1)}, bf16[128,256]{1,0:T(8,128)(2,1)}, bf16[128,256]{1,0:T(8,128)(2,1)}, bf16[128,256]{1,0:T(8,128)(2,1)}) custom-call(bf16[1,128,512]{2,1,0:T(8,128)(2,1)} %key_ref.3, bf16[1,128,512]{2,1,0:T(8,128)(2,1)} %value_ref.3, s32[1,128]{1,0:T(1,128)} %types_ref.3, bf16[1,64,512]{2,1,0:T(8,128)(2,1)} %table_ref.3), custom_call_target="tpu_custom_call" | custom-call | bytes 590336 | tf_op jit(solution)/shard_map/pack_keys_fwd/pallas_call | solution.py:352
  7.7 0.9 collective-permute-done.1.refs_2_
  8.6 1.5 %collective-permute-done.2.refs_3_ = bf16[128,256]{1,0:T(8,128)(2,1)S(1)} collective-permute-done((bf16[128,256]{1,0:T(8,128)(2,1)}, bf16[128,256]{1,0:T(8,128)(2,1)S(1)}, u32[]{:S(2)}, u32[]{:S(2)}) %collective-permute-start.2) | collective-permute-done | bytes 65568 | tf_op jit(solution)/shard_map/ppermute | solution.py:393
  10.1 0.4 stack_keys_bwd.1.refs_2_
  10.5 0.0 copy-start.1
  10.5 1.6 %collective-permute-start.3 = (bf16[512,256]{1,0:T(8,128)(2,1)S(1)}, bf16[512,256]{1,0:T(8,128)(2,1)S(1)}, u32[]{:S(2)}, u32[]{:S(2)}) collective-permute-start(bf16[512,256]{1,0:T(8,128)(2,1)S(1)} %stack_keys_bwd.1.refs_2_), channel_id=1, source_target_pairs={{0,8},{2,10},{4,12},{6,14},{8,16},{10,18},{12,20},{14,22},{16,24},... | collective-permute-start | bytes 786440 | tf_op jit(solution)/shard_map/ppermute | solution.py:399
  12.1 0.0 collective-permute-start.4
  12.1 1.3 %collective-permute-start.5 = (bf16[128,256]{1,0:T(8,128)(2,1)S(1)}, bf16[128,256]{1,0:T(8,128)(2,1)S(1)}, u32[]{:S(2)}, u32[]{:S(2)}) collective-permute-start(bf16[128,256]{1,0:T(8,128)(2,1)S(1)} %copy-done.5), channel_id=1, source_target_pairs={{0,4},{2,6},{4,0},{6,2},{8,12},{10,14},{12,8},{14,10},{16,20},{18,... | collective-permute-start | bytes 196616 | tf_op jit(solution)/shard_map/ppermute | solution.py:393
  13.4 0.5 collective-permute-start.6
  14.0 3.8 %pack_queries.1 = (bf16[128,1536]{1,0:T(8,128)(2,1)}, bf16[128,1536]{1,0:T(8,128)(2,1)}, bf16[128,1536]{1,0:T(8,128)(2,1)}, bf16[128,1536]{1,0:T(8,128)(2,1)}, bf16[144,2048]{1,0:T(8,128)(2,1)}) custom-call(bf16[1,128,2048]{2,1,0:T(8,128)(2,1)} %query_ref.1, bf16[1,128,2048]{2,1,0:T(8,128)(2,1)} %grad_ref.1, bf16[1,128,2048]{2,1,0:T(8,128)(2,1)} %forward_ref.1, ...), custom_call_target="tpu_custom_call" | custom-call | bytes 4268032 | tf_op jit(solution)/shard_map/pack_queries/pallas_call | solution.py:352
  17.8 0.0 copy-start
  17.8 0.0 collective-permute-done.4.refs_1_
  17.8 0.0 collective-permute-done.6.refs_3_
  17.8 2.9 %collective-permute-done.3.refs_3_ = bf16[512,256]{1,0:T(8,128)(2,1)S(1)} collective-permute-done((bf16[512,256]{1,0:T(8,128)(2,1)S(1)}, bf16[512,256]{1,0:T(8,128)(2,1)S(1)}, u32[]{:S(2)}, u32[]{:S(2)}) %collective-permute-start.3) | collective-permute-done | bytes 262176 | tf_op jit(solution)/shard_map/ppermute | solution.py:399
  20.7 1.7 %collective-permute-start.8 = (bf16[512,256]{1,0:T(8,128)(2,1)S(1)}, bf16[512,256]{1,0:T(8,128)(2,1)S(1)}, u32[]{:S(2)}, u32[]{:S(2)}) collective-permute-start(bf16[512,256]{1,0:T(8,128)(2,1)S(1)} %stack_keys_bwd.1.refs_2_), channel_id=1, source_target_pairs={{0,24},{2,26},{4,28},{6,30},{8,0},{10,2},{12,4},{14,6},{16,8},{18,... | collective-permute-start | bytes 786440 | tf_op jit(solution)/shard_map/ppermute | solution.py:399
  22.4 0.3 collective-permute-start.7
  22.7 1.4 %collective-permute-start.10 = (bf16[128,1536]{1,0:T(8,128)(2,1)}, bf16[128,1536]{1,0:T(8,128)(2,1)S(1)}, u32[]{:S(2)}, u32[]{:S(2)}) collective-permute-start(bf16[128,1536]{1,0:T(8,128)(2,1)} %get-tuple-element.124), channel_id=1, source_target_pairs={{0,4},{2,6},{4,0},{6,2},{8,12},{10,14},{12,8},{14,10},{16,20},{18,... | collective-permute-start | bytes 1179656 | tf_op jit(solution)/shard_map/ppermute | solution.py:393
  24.2 0.4 stack_keys_fwd.1.refs_4_
  24.5 5.2 %collective-permute-done.8.refs_5_ = bf16[512,256]{1,0:T(8,128)(2,1)S(1)} collective-permute-done((bf16[512,256]{1,0:T(8,128)(2,1)S(1)}, bf16[512,256]{1,0:T(8,128)(2,1)S(1)}, u32[]{:S(2)}, u32[]{:S(2)}) %collective-permute-start.8) | collective-permute-done | bytes 262176 | tf_op jit(solution)/shard_map/ppermute | solution.py:399
  29.7 4.4 %collective-permute-done.7.refs_4_ = bf16[512,256]{1,0:T(8,128)(2,1)S(1)} collective-permute-done((bf16[512,256]{1,0:T(8,128)(2,1)S(1)}, bf16[512,256]{1,0:T(8,128)(2,1)S(1)}, u32[]{:S(2)}, u32[]{:S(2)}) %collective-permute-start.7) | collective-permute-done | bytes 262176 | tf_op jit(solution)/shard_map/ppermute | solution.py:399
  34.1 1.5 %collective-permute-start.14 = (bf16[144,2048]{1,0:T(8,128)(2,1)}, bf16[144,2048]{1,0:T(8,128)(2,1)S(1)}, u32[]{:S(2)}, u32[]{:S(2)}) collective-permute-start(bf16[144,2048]{1,0:T(8,128)(2,1)} %get-tuple-element.135), channel_id=1, source_target_pairs={{0,1},{1,0},{2,3},{3,2},{4,5},{5,4},{6,7},{7,6},{8,9},{9,8},{10,11... | collective-permute-start | bytes 1769480 | tf_op jit(solution)/shard_map/ppermute | solution.py:410
  35.6 0.0 collective-permute-start.11
  35.6 1.6 %collective-permute-start.9 = (bf16[128,1536]{1,0:T(8,128)(2,1)}, bf16[128,1536]{1,0:T(8,128)(2,1)S(1)}, u32[]{:S(2)}, u32[]{:S(2)}) collective-permute-start(bf16[128,1536]{1,0:T(8,128)(2,1)} %get-tuple-element.123), channel_id=1, source_target_pairs={{0,2},{2,0},{4,6},{6,4},{8,10},{10,8},{12,14},{14,12},{16,18},{18,... | collective-permute-start | bytes 1179656 | tf_op jit(solution)/shard_map/ppermute | solution.py:393
  37.2 1.7 %collective-permute-start.13 = (bf16[512,256]{1,0:T(8,128)(2,1)S(1)}, bf16[512,256]{1,0:T(8,128)(2,1)S(1)}, u32[]{:S(2)}, u32[]{:S(2)}) collective-permute-start(bf16[512,256]{1,0:T(8,128)(2,1)S(1)} %stack_keys_fwd.1.refs_4_), channel_id=1, source_target_pairs={{0,24},{2,26},{4,28},{6,30},{8,0},{10,2},{12,4},{14,6},{16,8},{18,... | collective-permute-start | bytes 786440 | tf_op jit(solution)/shard_map/ppermute | solution.py:399
  39.0 0.3 collective-permute-start.12
  39.3 7.2 %backward_first.1 = (bf16[128,512]{1,0:T(8,128)(2,1)S(1)}, bf16[128,512]{1,0:T(8,128)(2,1)S(1)}, f32[2048,128]{1,0:T(8,128)S(1)}, f32[2048,128]{1,0:T(8,128)S(1)}) custom-call(s32[1,32]{1,0:T(1,128)S(1)} %copy-done.3, bf16[128,1536]{1,0:T(8,128)(2,1)S(1)} %copy-done, bf16[128,1536]{1,0:T(8,128)(2,1)S(1)} %collective-permute-done.10.refs_1_.refs_2_, ...), custom_call_target="tpu_custom_call" | custom-call | flops 1509949440 | bytes 4194432 | tf_op jit(solution)/shard_map/backward_first/pallas_call | solution.py:352
  46.5 0.0 collective-permute-done.13.refs_7_
  46.5 5.5 %collective-permute-done.12.refs_5_ = bf16[512,256]{1,0:T(8,128)(2,1)S(1)} collective-permute-done((bf16[512,256]{1,0:T(8,128)(2,1)S(1)}, bf16[512,256]{1,0:T(8,128)(2,1)S(1)}, u32[]{:S(2)}, u32[]{:S(2)}) %collective-permute-start.12) | collective-permute-done | bytes 262176 | tf_op jit(solution)/shard_map/ppermute | solution.py:399
  52.0 0.9 collective-permute-start.15
  52.8 0.5 collective-permute-start.16
  53.4 0.0 collective-permute-done.11.refs_1_.refs_3_
  53.4 0.0 collective-permute-done.9.refs_0_.refs_1_
  53.4 7.3 %backward_second.1 = (bf16[128,512]{1,0:T(8,128)(2,1)S(1)}, bf16[128,512]{1,0:T(8,128)(2,1)S(1)}, bf16[512,256]{1,0:T(8,128)(2,1)S(1)}, bf16[512,256]{1,0:T(8,12...) custom-call(s32[1,32]{1,0:T(1,128)S(1)} %copy-done.3, ...), custom_call_target="tpu_custom_call" | custom-call | flops 1509949440 | bytes 5243008 | tf_op jit(solution)/shard_map/backward_second/pallas_call | solution.py:352
  60.7 0.4 collective-permute-done.15.refs_6_
  61.1 1.1 %collective-permute-start.17 = (bf16[512,256]{1,0:T(8,128)(2,1)S(1)}, bf16[512,256]{1,0:T(8,128)(2,1)S(1)}, u32[]{:S(2)}, u32[]{:S(2)}) collective-permute-start(bf16[512,256]{1,0:T(8,128)(2,1)S(1)} %get-tuple-element.156), channel_id=1, source_target_pairs={{0,8},{2,10},{4,12},{6,14},{8,16},{10,18},{12,20},{14,22},{16,24},... | collective-permute-start | bytes 786440 | tf_op jit(solution)/shard_map/ppermute | solution.py:399
  62.2 0.3 collective-permute-start.18
  62.5 2.5 %collective-permute-start.25 = (bf16[512,256]{1,0:T(8,128)(2,1)S(1)}, bf16[512,256]{1,0:T(8,128)(2,1)S(1)}, u32[]{:S(2)}, u32[]{:S(2)}) collective-permute-start(bf16[512,256]{1,0:T(8,128)(2,1)S(1)} %get-tuple-element.175), channel_id=1, source_target_pairs={{0,24},{2,26},{4,28},{6,30},{8,0},{10,2},{12,4},{14,6},{16,8},{18,... | collective-permute-start | bytes 786440 | tf_op jit(solution)/shard_map/ppermute | solution.py:399
  64.9 4.1 %forward.1 = (bf16[128,512]{1,0:T(8,128)(2,1)S(1)}, bf16[128,512]{1,0:T(8,128)(2,1)S(1)}, bf16[128,512]{1,0:T(8,128)(2,1)S(1)}, bf16[128,512]{1,0:T(8,128)(2,1)S(1)}) custom-call(s32[1,32]{1,0:T(1,128)S(1)} %copy-done.3, bf16[128,1536]{1,0:T(8,128)(2,1)S(1)} %copy-done, bf16[128,1536]{1,0:T(8,128)(2,1)S(1)} %collective-permute-done.9.refs_0_.refs_1_, ...), custom_call_target="tpu_custom_call" | custom-call | bytes 3145856 | tf_op jit(solution)/shard_map/forward/pallas_call | solution.py:352
  69.0 0.0 collective-permute-done.18.refs_3_
  69.0 1.8 %collective-permute-done.17 = bf16[512,256]{1,0:T(8,128)(2,1)S(1)} collective-permute-done((bf16[512,256]{1,0:T(8,128)(2,1)S(1)}, bf16[512,256]{1,0:T(8,128)(2,1)S(1)}, u32[]{:S(2)}, u32[]{:S(2)}) %collective-permute-start.17) | collective-permute-done | bytes 262176 | tf_op jit(solution)/shard_map/ppermute | solution.py:399
  70.8 0.1 add_convert_fusion
  70.9 0.1 collective-permute-start.24
  71.0 0.6 collective-permute-start.19
  71.5 0.0 collective-permute-start.20
  71.6 3.4 %collective-permute-start.21 = (bf16[128,512]{1,0:T(8,128)(2,1)S(1)}, bf16[128,512]{1,0:T(8,128)(2,1)S(1)}, u32[]{:S(2)}, u32[]{:S(2)}) collective-permute-start(bf16[128,512]{1,0:T(8,128)(2,1)S(1)} %get-tuple-element.165), channel_id=1, source_target_pairs={{0,5},{1,4},{2,7},{3,6},{4,1},{5,0},{6,3},{7,2},{8,13},{9,12},{10,... | collective-permute-start | bytes 393224 | tf_op jit(solution)/shard_map/ppermute | solution.py:410
  75.0 5.2 %collective-permute-done.19.refs_0_ = bf16[128,512]{1,0:T(8,128)(2,1)S(1)} collective-permute-done((bf16[128,512]{1,0:T(8,128)(2,1)S(1)}, bf16[128,512]{1,0:T(8,128)(2,1)S(1)}, u32[]{:S(2)}, u32[]{:S(2)}) %collective-permute-start.19) | collective-permute-done | bytes 131104 | tf_op jit(solution)/shard_map/ppermute | solution.py:410
  80.1 0.0 collective-permute-start.22
  80.1 1.6 %collective-permute-start.23 = (bf16[128,512]{1,0:T(8,128)(2,1)S(1)}, bf16[128,512]{1,0:T(8,128)(2,1)S(1)}, u32[]{:S(2)}, u32[]{:S(2)}) collective-permute-start(bf16[128,512]{1,0:T(8,128)(2,1)S(1)} %get-tuple-element.169), channel_id=1, source_target_pairs={{0,2},{2,0},{4,6},{6,4},{8,10},{10,8},{12,14},{14,12},{16,18},{18,... | collective-permute-start | bytes 393224 | tf_op jit(solution)/shard_map/ppermute | solution.py:393
  81.7 0.1 sum_key_parts.1
  81.8 0.1 collective-permute-start.26
  81.9 0.0 collective-permute-done.20.refs_1_
  81.9 1.4 %collective-permute-start.27 = (bf16[128,256]{1,0:T(8,128)(2,1)S(1)}, bf16[128,256]{1,0:T(8,128)(2,1)S(1)}, u32[]{:S(2)}, u32[]{:S(2)}) collective-permute-start(bf16[128,256]{1,0:T(8,128)(2,1)S(1)} %get-tuple-element.178), channel_id=1, source_target_pairs={{0,4},{2,6},{4,0},{6,2},{8,12},{10,14},{12,8},{14,10},{16,20},{18,... | collective-permute-start | bytes 196616 | tf_op jit(solution)/shard_map/ppermute | solution.py:393
  83.3 0.0 collective-permute-done.21.refs_2_
  83.3 1.6 %collective-permute-start.28 = (bf16[128,256]{1,0:T(8,128)(2,1)S(1)}, bf16[128,256]{1,0:T(8,128)(2,1)S(1)}, u32[]{:S(2)}, u32[]{:S(2)}) collective-permute-start(bf16[128,256]{1,0:T(8,128)(2,1)S(1)} %get-tuple-element.179), channel_id=1, source_target_pairs={{0,6},{2,4},{4,2},{6,0},{8,14},{10,12},{12,10},{14,8},{16,22},{18,... | collective-permute-start | bytes 196616 | tf_op jit(solution)/shard_map/ppermute | solution.py:393
  84.9 1.1 %collective-permute-done.22.refs_3_ = bf16[128,512]{1,0:T(8,128)(2,1)S(1)} collective-permute-done((bf16[128,512]{1,0:T(8,128)(2,1)S(1)}, bf16[128,512]{1,0:T(8,128)(2,1)S(1)}, u32[]{:S(2)}, u32[]{:S(2)}) %collective-permute-start.22) | collective-permute-done | bytes 131104 | tf_op jit(solution)/shard_map/ppermute | solution.py:410
  85.9 1.2 %gate.1 = bf16[1,128,2048]{2,1,0:T(8,128)(2,1)} custom-call(bf16[128,512]{1,0:T(8,128)(2,1)S(1)} %collective-permute-done.19.refs_0_, bf16[128,512]{1,0:T(8,128)(2,1)S(1)} %collective-permute-done.20.refs_1_, bf16[128,512]{1,0:T(8,128)(2,1)S(1)} %collective-permute-done.21.refs_2_, bf16[128,512]{1,0:T(8,128)(2,1)S(1)} %collective-permute-done.22.refs_3_, ...), custom_call_target="tpu_custom_call" | custom-call | bytes 1638400 | tf_op jit(solution)/shard_map/gate/pallas_call | solution.py:352
  87.1 0.8 query_grad.1
  87.9 0.0 collective-permute-done.26.refs_1_
  87.9 0.0 collective-permute-done.27.refs_2_
  88.0 0.8 key_grad.1
  (21 shorter events, 0.0 us)
Async XLA Ops:
  2.6 5.1 %collective-permute-start = (bf16[128,256]{1,0:T(8,128)(2,1)}, bf16[128,256]{1,0:T(8,128)(2,1)S(1)}, u32[]{:S(2)}, u32[]{:S(2)}) collective-permute-start(bf16[128,256]{1,0:T(8,128)(2,1)} %get-tuple-element.94), channel_id=1, source_target_pairs={{0,2},{2,0},{4,6},{6,4},{8,10},{10,8},{12,14},{14,12},{16,18},{18,... | collective-permute-start | bytes 196616 | tf_op jit(solution)/shard_map/ppermute | solution.py:393
  3.1 5.5 %collective-permute-start.1 = (bf16[128,256]{1,0:T(8,128)(2,1)}, bf16[128,256]{1,0:T(8,128)(2,1)S(1)}, u32[]{:S(2)}, u32[]{:S(2)}) collective-permute-start(bf16[128,256]{1,0:T(8,128)(2,1)} %get-tuple-element.95), channel_id=1, source_target_pairs={{0,4},{2,6},{4,0},{6,2},{8,12},{10,14},{12,8},{14,10},{16,20},{18,... | collective-permute-start | bytes 196616 | tf_op jit(solution)/shard_map/ppermute | solution.py:393
  5.7 4.4 %copy-start.2 = (bf16[128,256]{1,0:T(8,128)(2,1)S(1)}, bf16[128,256]{1,0:T(8,128)(2,1)}, u32[]{:S(2)}) copy-start(bf16[128,256]{1,0:T(8,128)(2,1)} %get-tuple-element.101.refs_0_) | copy-start | bytes 196612
  5.7 4.3 %collective-permute-start.2 = (bf16[128,256]{1,0:T(8,128)(2,1)}, bf16[128,256]{1,0:T(8,128)(2,1)S(1)}, u32[]{:S(2)}, u32[]{:S(2)}) collective-permute-start(bf16[128,256]{1,0:T(8,128)(2,1)} %get-tuple-element.96), channel_id=1, source_target_pairs={{0,6},{2,4},{4,2},{6,0},{8,14},{10,12},{12,10},{14,8},{16,22},{18,... | collective-permute-start | bytes 196616 | tf_op jit(solution)/shard_map/ppermute | solution.py:393
  10.1 2.0 %copy-start.6 = (bf16[128,256]{1,0:T(8,128)(2,1)S(1)}, bf16[128,256]{1,0:T(8,128)(2,1)}, u32[]{:S(2)}) copy-start(bf16[128,256]{1,0:T(8,128)(2,1)} %get-tuple-element.106) | copy-start | bytes 196612
  10.1 2.0 %copy-start.5 = (bf16[128,256]{1,0:T(8,128)(2,1)S(1)}, bf16[128,256]{1,0:T(8,128)(2,1)}, u32[]{:S(2)}) copy-start(bf16[128,256]{1,0:T(8,128)(2,1)} %get-tuple-element.107) | copy-start | bytes 196612
  10.1 3.4 %copy-start.4 = (bf16[128,256]{1,0:T(8,128)(2,1)S(1)}, bf16[128,256]{1,0:T(8,128)(2,1)}, u32[]{:S(2)}) copy-start(bf16[128,256]{1,0:T(8,128)(2,1)} %get-tuple-element.108) | copy-start | bytes 196612
  10.5 13.7 %copy-start.1 = (bf16[128,256]{1,0:T(8,128)(2,1)S(1)}, bf16[128,256]{1,0:T(8,128)(2,1)}, u32[]{:S(2)}) copy-start(bf16[128,256]{1,0:T(8,128)(2,1)} %get-tuple-element.117.refs_0_) | copy-start | bytes 196612
  10.5 10.2 %collective-permute-start.3 = (bf16[512,256]{1,0:T(8,128)(2,1)S(1)}, bf16[512,256]{1,0:T(8,128)(2,1)S(1)}, u32[]{:S(2)}, u32[]{:S(2)}) collective-permute-start(bf16[512,256]{1,0:T(8,128)(2,1)S(1)} %stack_keys_bwd.1.refs_2_), channel_id=1, source_target_pairs={{0,8},{2,10},{4,12},{6,14},{8,16},{10,18},{12,20},{14,22},{16,24},... | collective-permute-start | bytes 786440 | tf_op jit(solution)/shard_map/ppermute | solution.py:399
  12.1 5.7 %collective-permute-start.4 = (bf16[128,256]{1,0:T(8,128)(2,1)S(1)}, bf16[128,256]{1,0:T(8,128)(2,1)S(1)}, u32[]{:S(2)}, u32[]{:S(2)}) collective-permute-start(bf16[128,256]{1,0:T(8,128)(2,1)S(1)} %copy-done.6), channel_id=1, source_target_pairs={{0,2},{2,0},{4,6},{6,4},{8,10},{10,8},{12,14},{14,12},{16,18},{18,... | collective-permute-start | bytes 196616 | tf_op jit(solution)/shard_map/ppermute | solution.py:393
  12.1 5.7 %collective-permute-start.5 = (bf16[128,256]{1,0:T(8,128)(2,1)S(1)}, bf16[128,256]{1,0:T(8,128)(2,1)S(1)}, u32[]{:S(2)}, u32[]{:S(2)}) collective-permute-start(bf16[128,256]{1,0:T(8,128)(2,1)S(1)} %copy-done.5), channel_id=1, source_target_pairs={{0,4},{2,6},{4,0},{6,2},{8,12},{10,14},{12,8},{14,10},{16,20},{18,... | collective-permute-start | bytes 196616 | tf_op jit(solution)/shard_map/ppermute | solution.py:393
  13.4 4.4 %collective-permute-start.6 = (bf16[128,256]{1,0:T(8,128)(2,1)S(1)}, bf16[128,256]{1,0:T(8,128)(2,1)S(1)}, u32[]{:S(2)}, u32[]{:S(2)}) collective-permute-start(bf16[128,256]{1,0:T(8,128)(2,1)S(1)} %copy-done.4), channel_id=1, source_target_pairs={{0,6},{2,4},{4,2},{6,0},{8,14},{10,12},{12,10},{14,8},{16,22},{18,... | collective-permute-start | bytes 196616 | tf_op jit(solution)/shard_map/ppermute | solution.py:393
  17.8 21.5 %copy-start = (bf16[128,1536]{1,0:T(8,128)(2,1)S(1)}, bf16[128,1536]{1,0:T(8,128)(2,1)}, u32[]{:S(2)}) copy-start(bf16[128,1536]{1,0:T(8,128)(2,1)} %get-tuple-element.114.refs_0_) | copy-start | bytes 1179652
  20.7 18.5 %copy-start.3 = (s32[1,32]{1,0:T(1,128)S(1)}, s32[1,32]{1,0:T(1,128)}, u32[]{:S(2)}) copy-start(s32[1,32]{1,0:T(1,128)} %order_ref.5) | copy-start | bytes 388
  20.7 9.0 %collective-permute-start.8 = (bf16[512,256]{1,0:T(8,128)(2,1)S(1)}, bf16[512,256]{1,0:T(8,128)(2,1)S(1)}, u32[]{:S(2)}, u32[]{:S(2)}) collective-permute-start(bf16[512,256]{1,0:T(8,128)(2,1)S(1)} %stack_keys_bwd.1.refs_2_), channel_id=1, source_target_pairs={{0,24},{2,26},{4,28},{6,30},{8,0},{10,2},{12,4},{14,6},{16,8},{18,... | collective-permute-start | bytes 786440 | tf_op jit(solution)/shard_map/ppermute | solution.py:399
  22.4 11.6 %collective-permute-start.7 = (bf16[512,256]{1,0:T(8,128)(2,1)S(1)}, bf16[512,256]{1,0:T(8,128)(2,1)S(1)}, u32[]{:S(2)}, u32[]{:S(2)}) collective-permute-start(bf16[512,256]{1,0:T(8,128)(2,1)S(1)} %collective-permute-done.3.refs_3_), channel_id=1, source_target_pairs={{0,8},{2,10},{4,12},{6,14},{8,16},{10,18},{12,20},{14,22},{16,24},... | collective-permute-start | bytes 786440 | tf_op jit(solution)/shard_map/ppermute | solution.py:399
  22.7 16.2 %collective-permute-start.10 = (bf16[128,1536]{1,0:T(8,128)(2,1)}, bf16[128,1536]{1,0:T(8,128)(2,1)S(1)}, u32[]{:S(2)}, u32[]{:S(2)}) collective-permute-start(bf16[128,1536]{1,0:T(8,128)(2,1)} %get-tuple-element.124), channel_id=1, source_target_pairs={{0,4},{2,6},{4,0},{6,2},{8,12},{10,14},{12,8},{14,10},{16,20},{18,... | collective-permute-start | bytes 1179656 | tf_op jit(solution)/shard_map/ppermute | solution.py:393
  34.1 17.9 %collective-permute-start.14 = (bf16[144,2048]{1,0:T(8,128)(2,1)}, bf16[144,2048]{1,0:T(8,128)(2,1)S(1)}, u32[]{:S(2)}, u32[]{:S(2)}) collective-permute-start(bf16[144,2048]{1,0:T(8,128)(2,1)} %get-tuple-element.135), channel_id=1, source_target_pairs={{0,1},{1,0},{2,3},{3,2},{4,5},{5,4},{6,7},{7,6},{8,9},{9,8},{10,11... | collective-permute-start | bytes 1769480 | tf_op jit(solution)/shard_map/ppermute | solution.py:410
  35.6 17.8 %collective-permute-start.11 = (bf16[128,1536]{1,0:T(8,128)(2,1)}, bf16[128,1536]{1,0:T(8,128)(2,1)S(1)}, u32[]{:S(2)}, u32[]{:S(2)}) collective-permute-start(bf16[128,1536]{1,0:T(8,128)(2,1)} %get-tuple-element.125), channel_id=1, source_target_pairs={{0,6},{2,4},{4,2},{6,0},{8,14},{10,12},{12,10},{14,8},{16,22},{18,... | collective-permute-start | bytes 1179656 | tf_op jit(solution)/shard_map/ppermute | solution.py:393
  35.6 17.8 %collective-permute-start.9 = (bf16[128,1536]{1,0:T(8,128)(2,1)}, bf16[128,1536]{1,0:T(8,128)(2,1)S(1)}, u32[]{:S(2)}, u32[]{:S(2)}) collective-permute-start(bf16[128,1536]{1,0:T(8,128)(2,1)} %get-tuple-element.123), channel_id=1, source_target_pairs={{0,2},{2,0},{4,6},{6,4},{8,10},{10,8},{12,14},{14,12},{16,18},{18,... | collective-permute-start | bytes 1179656 | tf_op jit(solution)/shard_map/ppermute | solution.py:393
  37.2 9.3 %collective-permute-start.13 = (bf16[512,256]{1,0:T(8,128)(2,1)S(1)}, bf16[512,256]{1,0:T(8,128)(2,1)S(1)}, u32[]{:S(2)}, u32[]{:S(2)}) collective-permute-start(bf16[512,256]{1,0:T(8,128)(2,1)S(1)} %stack_keys_fwd.1.refs_4_), channel_id=1, source_target_pairs={{0,24},{2,26},{4,28},{6,30},{8,0},{10,2},{12,4},{14,6},{16,8},{18,... | collective-permute-start | bytes 786440 | tf_op jit(solution)/shard_map/ppermute | solution.py:399
  39.0 13.0 %collective-permute-start.12 = (bf16[512,256]{1,0:T(8,128)(2,1)S(1)}, bf16[512,256]{1,0:T(8,128)(2,1)S(1)}, u32[]{:S(2)}, u32[]{:S(2)}) collective-permute-start(bf16[512,256]{1,0:T(8,128)(2,1)S(1)} %stack_keys_fwd.1.refs_4_), channel_id=1, source_target_pairs={{0,8},{2,10},{4,12},{6,14},{8,16},{10,18},{12,20},{14,22},{16,24},... | collective-permute-start | bytes 786440 | tf_op jit(solution)/shard_map/ppermute | solution.py:399
  52.0 9.1 %collective-permute-start.15 = (bf16[512,256]{1,0:T(8,128)(2,1)S(1)}, bf16[512,256]{1,0:T(8,128)(2,1)S(1)}, u32[]{:S(2)}, u32[]{:S(2)}) collective-permute-start(bf16[512,256]{1,0:T(8,128)(2,1)S(1)} %collective-permute-done.12.refs_5_), channel_id=1, source_target_pairs={{0,8},{2,10},{4,12},{6,14},{8,16},{10,18},{12,20},{14,22},{16,24},... | collective-permute-start | bytes 786440 | tf_op jit(solution)/shard_map/ppermute | solution.py:399
  52.8 7.8 %collective-permute-start.16 = (bf16[128,512]{1,0:T(8,128)(2,1)S(1)}, bf16[128,512]{1,0:T(8,128)(2,1)S(1)}, u32[]{:S(2)}, u32[]{:S(2)}) collective-permute-start(bf16[128,512]{1,0:T(8,128)(2,1)S(1)} %get-tuple-element.147), channel_id=1, source_target_pairs={{0,4},{2,6},{4,0},{6,2},{8,12},{10,14},{12,8},{14,10},{16,20},{18,... | collective-permute-start | bytes 393224 | tf_op jit(solution)/shard_map/ppermute | solution.py:393
  61.1 9.7 %collective-permute-start.17 = (bf16[512,256]{1,0:T(8,128)(2,1)S(1)}, bf16[512,256]{1,0:T(8,128)(2,1)S(1)}, u32[]{:S(2)}, u32[]{:S(2)}) collective-permute-start(bf16[512,256]{1,0:T(8,128)(2,1)S(1)} %get-tuple-element.156), channel_id=1, source_target_pairs={{0,8},{2,10},{4,12},{6,14},{8,16},{10,18},{12,20},{14,22},{16,24},... | collective-permute-start | bytes 786440 | tf_op jit(solution)/shard_map/ppermute | solution.py:399
  62.2 6.8 %collective-permute-start.18 = (bf16[128,512]{1,0:T(8,128)(2,1)S(1)}, bf16[128,512]{1,0:T(8,128)(2,1)S(1)}, u32[]{:S(2)}, u32[]{:S(2)}) collective-permute-start(bf16[128,512]{1,0:T(8,128)(2,1)S(1)} %get-tuple-element.160), channel_id=1, source_target_pairs={{0,6},{2,4},{4,2},{6,0},{8,14},{10,12},{12,10},{14,8},{16,22},{18,... | collective-permute-start | bytes 393224 | tf_op jit(solution)/shard_map/ppermute | solution.py:393
  62.5 17.7 %collective-permute-start.25 = (bf16[512,256]{1,0:T(8,128)(2,1)S(1)}, bf16[512,256]{1,0:T(8,128)(2,1)S(1)}, u32[]{:S(2)}, u32[]{:S(2)}) collective-permute-start(bf16[512,256]{1,0:T(8,128)(2,1)S(1)} %get-tuple-element.175), channel_id=1, source_target_pairs={{0,24},{2,26},{4,28},{6,30},{8,0},{10,2},{12,4},{14,6},{16,8},{18,... | collective-permute-start | bytes 786440 | tf_op jit(solution)/shard_map/ppermute | solution.py:399
  70.9 10.8 %collective-permute-start.24 = (bf16[512,256]{1,0:T(8,128)(2,1)S(1)}, bf16[512,256]{1,0:T(8,128)(2,1)S(1)}, u32[]{:S(2)}, u32[]{:S(2)}) collective-permute-start(bf16[512,256]{1,0:T(8,128)(2,1)S(1)} %add_convert_fusion), channel_id=1, source_target_pairs={{0,8},{2,10},{4,12},{6,14},{8,16},{10,18},{12,20},{14,22},{16,24},... | collective-permute-start | bytes 786440 | tf_op jit(solution)/shard_map/ppermute | solution.py:399
  71.0 9.2 %collective-permute-start.19 = (bf16[128,512]{1,0:T(8,128)(2,1)S(1)}, bf16[128,512]{1,0:T(8,128)(2,1)S(1)}, u32[]{:S(2)}, u32[]{:S(2)}) collective-permute-start(bf16[128,512]{1,0:T(8,128)(2,1)S(1)} %get-tuple-element.161), channel_id=1, source_target_pairs={{0,1},{1,0},{2,3},{3,2},{4,5},{5,4},{6,7},{7,6},{8,9},{9,8},{10,11... | collective-permute-start | bytes 393224 | tf_op jit(solution)/shard_map/ppermute | solution.py:410
  71.5 10.4 %collective-permute-start.20 = (bf16[128,512]{1,0:T(8,128)(2,1)S(1)}, bf16[128,512]{1,0:T(8,128)(2,1)S(1)}, u32[]{:S(2)}, u32[]{:S(2)}) collective-permute-start(bf16[128,512]{1,0:T(8,128)(2,1)S(1)} %get-tuple-element.164), channel_id=1, source_target_pairs={{0,3},{1,2},{2,1},{3,0},{4,7},{5,6},{6,5},{7,4},{8,11},{9,10},{10,... | collective-permute-start | bytes 393224 | tf_op jit(solution)/shard_map/ppermute | solution.py:410
  71.6 11.7 %collective-permute-start.21 = (bf16[128,512]{1,0:T(8,128)(2,1)S(1)}, bf16[128,512]{1,0:T(8,128)(2,1)S(1)}, u32[]{:S(2)}, u32[]{:S(2)}) collective-permute-start(bf16[128,512]{1,0:T(8,128)(2,1)S(1)} %get-tuple-element.165), channel_id=1, source_target_pairs={{0,5},{1,4},{2,7},{3,6},{4,1},{5,0},{6,3},{7,2},{8,13},{9,12},{10,... | collective-permute-start | bytes 393224 | tf_op jit(solution)/shard_map/ppermute | solution.py:410
  80.1 5.8 %collective-permute-start.22 = (bf16[128,512]{1,0:T(8,128)(2,1)S(1)}, bf16[128,512]{1,0:T(8,128)(2,1)S(1)}, u32[]{:S(2)}, u32[]{:S(2)}) collective-permute-start(bf16[128,512]{1,0:T(8,128)(2,1)S(1)} %get-tuple-element.166), channel_id=1, source_target_pairs={{0,7},{1,6},{2,5},{3,4},{4,3},{5,2},{6,1},{7,0},{8,15},{9,14},{10,... | collective-permute-start | bytes 393224 | tf_op jit(solution)/shard_map/ppermute | solution.py:410
  80.1 7.0 %collective-permute-start.23 = (bf16[128,512]{1,0:T(8,128)(2,1)S(1)}, bf16[128,512]{1,0:T(8,128)(2,1)S(1)}, u32[]{:S(2)}, u32[]{:S(2)}) collective-permute-start(bf16[128,512]{1,0:T(8,128)(2,1)S(1)} %get-tuple-element.169), channel_id=1, source_target_pairs={{0,2},{2,0},{4,6},{6,4},{8,10},{10,8},{12,14},{14,12},{16,18},{18,... | collective-permute-start | bytes 393224 | tf_op jit(solution)/shard_map/ppermute | solution.py:393
  81.8 6.1 %collective-permute-start.26 = (bf16[128,256]{1,0:T(8,128)(2,1)S(1)}, bf16[128,256]{1,0:T(8,128)(2,1)S(1)}, u32[]{:S(2)}, u32[]{:S(2)}) collective-permute-start(bf16[128,256]{1,0:T(8,128)(2,1)S(1)} %get-tuple-element.177), channel_id=1, source_target_pairs={{0,2},{2,0},{4,6},{6,4},{8,10},{10,8},{12,14},{14,12},{16,18},{18,... | collective-permute-start | bytes 196616 | tf_op jit(solution)/shard_map/ppermute | solution.py:393
  81.9 6.0 %collective-permute-start.27 = (bf16[128,256]{1,0:T(8,128)(2,1)S(1)}, bf16[128,256]{1,0:T(8,128)(2,1)S(1)}, u32[]{:S(2)}, u32[]{:S(2)}) collective-permute-start(bf16[128,256]{1,0:T(8,128)(2,1)S(1)} %get-tuple-element.178), channel_id=1, source_target_pairs={{0,4},{2,6},{4,0},{6,2},{8,12},{10,14},{12,8},{14,10},{16,20},{18,... | collective-permute-start | bytes 196616 | tf_op jit(solution)/shard_map/ppermute | solution.py:393
  83.3 4.6 %collective-permute-start.28 = (bf16[128,256]{1,0:T(8,128)(2,1)S(1)}, bf16[128,256]{1,0:T(8,128)(2,1)S(1)}, u32[]{:S(2)}, u32[]{:S(2)}) collective-permute-start(bf16[128,256]{1,0:T(8,128)(2,1)S(1)} %get-tuple-element.179), channel_id=1, source_target_pairs={{0,6},{2,4},{4,2},{6,0},{8,14},{10,12},{12,10},{14,8},{16,22},{18,... | collective-permute-start | bytes 196616 | tf_op jit(solution)/shard_map/ppermute | solution.py:393

commit v11 on v10

--- a/solution.py
+++ b/solution.py
@@ -281,7 +281,7 @@
             key_total[rows, :] += dot(score_grad, stacked[row], NN)
             value_total[rows, :] += dot(weights, grads[row], NN)
 
-    repeat(steps, 3, advance)
+    repeat(steps, 9, advance)
     for i in range(len(parts)):
         for e in range(2):
             query_grad = (total_t[2 * i + e].T * SCALE).astype(jnp.bfloat16)
@@ -546,7 +546,7 @@
         *far[2:],
     )
     near, stacks, far_piece = lax.optimization_barrier((near, stacks, far_piece))
-    query_pieces, key_parts = [far[0], near[0], far_piece, swap_one(near[1], 3)], near[2:]
+    query_pieces, key_parts = [far[0], swap_one(near[0], 1), far_piece, swap_one(near[1], 3)], near[2:]
     key_sums = reduce_first(key_parts)
     parts = tuple(range(QUAD))
     attended = call(
@@ -564,8 +564,14 @@
         (attended, key_sums[0], query_pieces)
     )
     attended = [hand(attended[d], d) for d in range(QUAD)]
-    attended[0], query_pieces[1] = lax.optimization_barrier((attended[0], query_pieces[1]))
-    query_pieces[1] = swap_one(query_pieces[1], 1)
+    (query_grad,) = call(
+        query_grad_kernel,
+        "query_grad",
+        [bf16(*query_bwd.shape)],
+        [VMEM] * QUAD,
+        *query_pieces,
+    )
+    attended, query_grad = lax.optimization_barrier((attended, query_grad))
     (handed,) = call(
         gate_kernel,
         "gate",
@@ -584,13 +590,6 @@
             *key_sums,
         )
     )
-    (query_grad,) = call(
-        query_grad_kernel,
-        "query_grad",
-        [bf16(*query_bwd.shape)],
-        [VMEM] * QUAD,
-        *query_pieces,
-    )
     key_grad, value_grad = call(
         key_grad_kernel,
         "key_grad",

time: 89.2 us -> 90 us (level)
  waiting for transfers between devices: 28.7 us -> 33.8 us
  starting transfers between devices: 29.1 us -> 26.3 us
  Pallas kernels: 29.9 us -> 28.7 us
    ppermute x9, waiting for transfers between devices: 20.2 us -> 27.3 us  [turn(): lax.ppermute(block, 'ctx', [(i, (i + s * QUAD) % devices) for i in range(...]
    ppermute x5, waiting for transfers between devices: 6.25 us -> 2.7 us  [hand(): return lax.ppermute(block, ('ctx', 'pipe'), route)]
    ppermute x15, waiting for transfers between devices: 2.34 us -> 3.81 us  [swap_one(): return lax.ppermute(piece, 'ctx', [(i, i ^ d) for i in range(devices)])]
    pallas_call x12, Pallas kernels: 29.9 us -> 28.7 us  [call(): pl.pallas_call(kernel, name=name, out_shape=out_shape, in_specs=specs, ou...]
    ppermute x5, starting transfers between devices: 5.52 us -> 4.44 us  [hand(): return lax.ppermute(block, ('ctx', 'pipe'), route)]
    ppermute x15, starting transfers between devices: 13.4 us -> 12.4 us  [swap_one(): return lax.ppermute(piece, 'ctx', [(i, i ^ d) for i in range(devices)])]
  transfers between devices with their start and end apart: 29 -> 29, of which waited for: 10 -> 13; matrix products, arithmetic and copies ran while one was open for 0% -> 0% of each run, Pallas kernels for 30% -> 29%
where the time goes in v11:
time: 90 us; the launch traced here: 89.8 us
  waiting for transfers between devices  33.8 us (38%)
  Pallas kernels  28.7 us (32%)
  starting transfers between devices  26.3 us (29%)
    pallas_call x12, Pallas kernels, call(): pl.pallas_call(kernel, name=name, out_shape=out_shape, in_specs=specs, ou...  28.7 us
    ppermute x9, waiting for transfers between devices, turn(): lax.ppermute(block, 'ctx', [(i, (i + s * QUAD) % devices) for i in range(...  27.3 us
    ppermute x15, starting transfers between devices, swap_one(): return lax.ppermute(piece, 'ctx', [(i, i ^ d) for i in range(devices)])  12.4 us
    ppermute x9, starting transfers between devices, turn(): lax.ppermute(block, 'ctx', [(i, (i + s * QUAD) % devices) for i in range(...  9.49 us
    ppermute x5, starting transfers between devices, hand(): return lax.ppermute(block, ('ctx', 'pipe'), route)  4.44 us
    ppermute x15, waiting for transfers between devices, swap_one(): return lax.ppermute(piece, 'ctx', [(i, i ^ d) for i in range(devices)])  3.81 us
    ppermute x5, waiting for transfers between devices, hand(): return lax.ppermute(block, ('ctx', 'pipe'), route)  2.7 us
  transfers between devices with their start and end apart: 29, of which 13 were waited for; matrix products, arithmetic and copies ran while one was open for 0% of the time, Pallas kernels for 29%

profile of v11, /device:TPU:0, one launch (start us, length us, event | category | flops | bytes accessed | tf_op | source)
XLA Modules:
  0.0 89.8 jit_solution(16439323523638847156)
XLA Ops:
  0.6 2.0 %pack_keys_bwd.1 = (bf16[128,256]{1,0:T(8,128)(2,1)}, bf16[128,256]{1,0:T(8,128)(2,1)}, bf16[128,256]{1,0:T(8,128)(2,1)}, bf16[128,256]{1,0:T(8,128)(2,1)}) custom-call(bf16[1,128,512]{2,1,0:T(8,128)(2,1)} %key_ref.2, bf16[1,128,512]{2,1,0:T(8,128)(2,1)} %value_ref.2, s32[1,128]{1,0:T(1,128)} %types_ref.2, bf16[1,64,512]{2,1,0:T(8,128)(2,1)} %table_ref.3), custom_call_target="tpu_custom_call" | custom-call | bytes 590336 | tf_op jit(solution)/shard_map/pack_keys_bwd/pallas_call | solution.py:352
  2.6 0.5 collective-permute-start
  3.1 2.6 %collective-permute-start.1 = (bf16[128,256]{1,0:T(8,128)(2,1)}, bf16[128,256]{1,0:T(8,128)(2,1)S(1)}, u32[]{:S(2)}, u32[]{:S(2)}) collective-permute-start(bf16[128,256]{1,0:T(8,128)(2,1)} %get-tuple-element.98), channel_id=1, source_target_pairs={{0,4},{2,6},{4,0},{6,2},{8,12},{10,14},{12,8},{14,10},{16,20},{18,... | collective-permute-start | bytes 196616 | tf_op jit(solution)/shard_map/ppermute | solution.py:393
  5.7 0.1 collective-permute-start.2
  5.8 2.0 %pack_keys_fwd.1 = (bf16[128,256]{1,0:T(8,128)(2,1)}, bf16[128,256]{1,0:T(8,128)(2,1)}, bf16[128,256]{1,0:T(8,128)(2,1)}, bf16[128,256]{1,0:T(8,128)(2,1)}) custom-call(bf16[1,128,512]{2,1,0:T(8,128)(2,1)} %key_ref.3, bf16[1,128,512]{2,1,0:T(8,128)(2,1)} %value_ref.3, s32[1,128]{1,0:T(1,128)} %types_ref.3, bf16[1,64,512]{2,1,0:T(8,128)(2,1)} %table_ref.3), custom_call_target="tpu_custom_call" | custom-call | bytes 590336 | tf_op jit(solution)/shard_map/pack_keys_fwd/pallas_call | solution.py:352
  7.7 0.0 collective-permute-done.refs_1_
  7.7 0.9 collective-permute-done.1.refs_2_
  8.6 1.5 %collective-permute-done.2.refs_3_ = bf16[128,256]{1,0:T(8,128)(2,1)S(1)} collective-permute-done((bf16[128,256]{1,0:T(8,128)(2,1)}, bf16[128,256]{1,0:T(8,128)(2,1)S(1)}, u32[]{:S(2)}, u32[]{:S(2)}) %collective-permute-start.2) | collective-permute-done | bytes 65568 | tf_op jit(solution)/shard_map/ppermute | solution.py:393
  10.1 0.4 stack_keys_bwd.1.refs_2_
  10.5 0.0 copy-start.1
  10.5 1.6 %collective-permute-start.3 = (bf16[512,256]{1,0:T(8,128)(2,1)S(1)}, bf16[512,256]{1,0:T(8,128)(2,1)S(1)}, u32[]{:S(2)}, u32[]{:S(2)}) collective-permute-start(bf16[512,256]{1,0:T(8,128)(2,1)S(1)} %stack_keys_bwd.1.refs_2_), channel_id=1, source_target_pairs={{0,8},{2,10},{4,12},{6,14},{8,16},{10,18},{12,20},{14,22},{16,24},... | collective-permute-start | bytes 786440 | tf_op jit(solution)/shard_map/ppermute | solution.py:399
  12.1 0.0 collective-permute-start.4
  12.1 1.3 %collective-permute-start.5 = (bf16[128,256]{1,0:T(8,128)(2,1)S(1)}, bf16[128,256]{1,0:T(8,128)(2,1)S(1)}, u32[]{:S(2)}, u32[]{:S(2)}) collective-permute-start(bf16[128,256]{1,0:T(8,128)(2,1)S(1)} %copy-done.5), channel_id=1, source_target_pairs={{0,4},{2,6},{4,0},{6,2},{8,12},{10,14},{12,8},{14,10},{16,20},{18,... | collective-permute-start | bytes 196616 | tf_op jit(solution)/shard_map/ppermute | solution.py:393
  13.4 0.5 collective-permute-start.6
  14.0 3.8 %pack_queries.1 = (bf16[128,1536]{1,0:T(8,128)(2,1)}, bf16[128,1536]{1,0:T(8,128)(2,1)}, bf16[128,1536]{1,0:T(8,128)(2,1)}, bf16[128,1536]{1,0:T(8,128)(2,1)}, bf16[144,2048]{1,0:T(8,128)(2,1)}) custom-call(bf16[1,128,2048]{2,1,0:T(8,128)(2,1)} %query_ref.1, bf16[1,128,2048]{2,1,0:T(8,128)(2,1)} %grad_ref.1, bf16[1,128,2048]{2,1,0:T(8,128)(2,1)} %forward_ref.1, ...), custom_call_target="tpu_custom_call" | custom-call | bytes 4268032 | tf_op jit(solution)/shard_map/pack_queries/pallas_call | solution.py:352
  17.8 0.0 copy-start
  17.8 0.0 collective-permute-done.4.refs_1_
  17.8 0.0 collective-permute-done.5.refs_2_
  17.8 0.0 collective-permute-done.6.refs_3_
  17.8 2.9 %collective-permute-done.3.refs_3_ = bf16[512,256]{1,0:T(8,128)(2,1)S(1)} collective-permute-done((bf16[512,256]{1,0:T(8,128)(2,1)S(1)}, bf16[512,256]{1,0:T(8,128)(2,1)S(1)}, u32[]{:S(2)}, u32[]{:S(2)}) %collective-permute-start.3) | collective-permute-done | bytes 262176 | tf_op jit(solution)/shard_map/ppermute | solution.py:399
  20.7 1.7 %collective-permute-start.8 = (bf16[512,256]{1,0:T(8,128)(2,1)S(1)}, bf16[512,256]{1,0:T(8,128)(2,1)S(1)}, u32[]{:S(2)}, u32[]{:S(2)}) collective-permute-start(bf16[512,256]{1,0:T(8,128)(2,1)S(1)} %stack_keys_bwd.1.refs_2_), channel_id=1, source_target_pairs={{0,24},{2,26},{4,28},{6,30},{8,0},{10,2},{12,4},{14,6},{16,8},{18,... | collective-permute-start | bytes 786440 | tf_op jit(solution)/shard_map/ppermute | solution.py:399
  22.5 0.3 collective-permute-start.7
  22.7 1.4 %collective-permute-start.10 = (bf16[128,1536]{1,0:T(8,128)(2,1)}, bf16[128,1536]{1,0:T(8,128)(2,1)S(1)}, u32[]{:S(2)}, u32[]{:S(2)}) collective-permute-start(bf16[128,1536]{1,0:T(8,128)(2,1)} %get-tuple-element.127), channel_id=1, source_target_pairs={{0,4},{2,6},{4,0},{6,2},{8,12},{10,14},{12,8},{14,10},{16,20},{18,... | collective-permute-start | bytes 1179656 | tf_op jit(solution)/shard_map/ppermute | solution.py:393
  24.2 0.4 stack_keys_fwd.1.refs_4_
  24.5 5.2 %collective-permute-done.8.refs_5_ = bf16[512,256]{1,0:T(8,128)(2,1)S(1)} collective-permute-done((bf16[512,256]{1,0:T(8,128)(2,1)S(1)}, bf16[512,256]{1,0:T(8,128)(2,1)S(1)}, u32[]{:S(2)}, u32[]{:S(2)}) %collective-permute-start.8) | collective-permute-done | bytes 262176 | tf_op jit(solution)/shard_map/ppermute | solution.py:399
  29.7 4.4 %collective-permute-done.7.refs_4_ = bf16[512,256]{1,0:T(8,128)(2,1)S(1)} collective-permute-done((bf16[512,256]{1,0:T(8,128)(2,1)S(1)}, bf16[512,256]{1,0:T(8,128)(2,1)S(1)}, u32[]{:S(2)}, u32[]{:S(2)}) %collective-permute-start.7) | collective-permute-done | bytes 262176 | tf_op jit(solution)/shard_map/ppermute | solution.py:399
  34.1 1.5 %collective-permute-start.14 = (bf16[144,2048]{1,0:T(8,128)(2,1)}, bf16[144,2048]{1,0:T(8,128)(2,1)S(1)}, u32[]{:S(2)}, u32[]{:S(2)}) collective-permute-start(bf16[144,2048]{1,0:T(8,128)(2,1)} %get-tuple-element.138), channel_id=1, source_target_pairs={{0,1},{1,0},{2,3},{3,2},{4,5},{5,4},{6,7},{7,6},{8,9},{9,8},{10,11... | collective-permute-start | bytes 1769480 | tf_op jit(solution)/shard_map/ppermute | solution.py:410
  35.6 1.6 %collective-permute-start.9 = (bf16[128,1536]{1,0:T(8,128)(2,1)}, bf16[128,1536]{1,0:T(8,128)(2,1)S(1)}, u32[]{:S(2)}, u32[]{:S(2)}) collective-permute-start(bf16[128,1536]{1,0:T(8,128)(2,1)} %get-tuple-element.126), channel_id=1, source_target_pairs={{0,2},{2,0},{4,6},{6,4},{8,10},{10,8},{12,14},{14,12},{16,18},{18,... | collective-permute-start | bytes 1179656 | tf_op jit(solution)/shard_map/ppermute | solution.py:393
  37.2 1.7 %collective-permute-start.13 = (bf16[512,256]{1,0:T(8,128)(2,1)S(1)}, bf16[512,256]{1,0:T(8,128)(2,1)S(1)}, u32[]{:S(2)}, u32[]{:S(2)}) collective-permute-start(bf16[512,256]{1,0:T(8,128)(2,1)S(1)} %stack_keys_fwd.1.refs_4_), channel_id=1, source_target_pairs={{0,24},{2,26},{4,28},{6,30},{8,0},{10,2},{12,4},{14,6},{16,8},{18,... | collective-permute-start | bytes 786440 | tf_op jit(solution)/shard_map/ppermute | solution.py:399
  39.0 0.3 collective-permute-start.12
  39.3 6.6 %backward_first.1 = (bf16[128,512]{1,0:T(8,128)(2,1)S(1)}, bf16[128,512]{1,0:T(8,128)(2,1)S(1)}, f32[2048,128]{1,0:T(8,128)S(1)}, f32[2048,128]{1,0:T(8,128)S(1)}) custom-call(s32[1,32]{1,0:T(1,128)S(1)} %copy-done.3, bf16[128,1536]{1,0:T(8,128)(2,1)S(1)} %copy-done, bf16[128,1536]{1,0:T(8,128)(2,1)S(1)} %collective-permute-done.10.refs_1_.refs_2_, ...), custom_call_target="tpu_custom_call" | custom-call | flops 1509949440 | bytes 4194432 | tf_op jit(solution)/shard_map/backward_first/pallas_call | solution.py:352
  45.9 0.0 collective-permute-done.13.refs_7_
  45.9 6.1 %collective-permute-done.12.refs_5_ = bf16[512,256]{1,0:T(8,128)(2,1)S(1)} collective-permute-done((bf16[512,256]{1,0:T(8,128)(2,1)S(1)}, bf16[512,256]{1,0:T(8,128)(2,1)S(1)}, u32[]{:S(2)}, u32[]{:S(2)}) %collective-permute-start.12) | collective-permute-done | bytes 262176 | tf_op jit(solution)/shard_map/ppermute | solution.py:399
  52.0 0.0 collective-permute-done.14.refs_4_
  52.0 0.9 collective-permute-start.15
  52.8 0.5 collective-permute-start.16
  53.4 0.0 collective-permute-done.9.refs_0_.refs_1_
  53.4 6.7 %backward_second.1 = (bf16[128,512]{1,0:T(8,128)(2,1)S(1)}, bf16[128,512]{1,0:T(8,128)(2,1)S(1)}, bf16[512,256]{1,0:T(8,128)(2,1)S(1)}, bf16[512,256]{1,0:T(8,12...) custom-call(s32[1,32]{1,0:T(1,128)S(1)} %copy-done.3, ...), custom_call_target="tpu_custom_call" | custom-call | flops 1509949440 | bytes 5243008 | tf_op jit(solution)/shard_map/backward_second/pallas_call | solution.py:352
  60.1 1.0 %collective-permute-done.15.refs_6_ = bf16[512,256]{1,0:T(8,128)(2,1)S(1)} collective-permute-done((bf16[512,256]{1,0:T(8,128)(2,1)S(1)}, bf16[512,256]{1,0:T(8,128)(2,1)S(1)}, u32[]{:S(2)}, u32[]{:S(2)}) %collective-permute-start.15) | collective-permute-done | bytes 262176 | tf_op jit(solution)/shard_map/ppermute | solution.py:399
  61.1 0.5 collective-permute-start.17
  61.6 1.6 %collective-permute-start.19 = (bf16[128,512]{1,0:T(8,128)(2,1)S(1)}, bf16[128,512]{1,0:T(8,128)(2,1)S(1)}, u32[]{:S(2)}, u32[]{:S(2)}) collective-permute-start(bf16[128,512]{1,0:T(8,128)(2,1)S(1)} %get-tuple-element.163), channel_id=1, source_target_pairs={{0,6},{2,4},{4,2},{6,0},{8,14},{10,12},{12,10},{14,8},{16,22},{18,... | collective-permute-start | bytes 393224 | tf_op jit(solution)/shard_map/ppermute | solution.py:393
  63.2 2.4 %collective-permute-start.25 = (bf16[512,256]{1,0:T(8,128)(2,1)S(1)}, bf16[512,256]{1,0:T(8,128)(2,1)S(1)}, u32[]{:S(2)}, u32[]{:S(2)}) collective-permute-start(bf16[512,256]{1,0:T(8,128)(2,1)S(1)} %get-tuple-element.181), channel_id=1, source_target_pairs={{0,24},{2,26},{4,28},{6,30},{8,0},{10,2},{12,4},{14,6},{16,8},{18,... | collective-permute-start | bytes 786440 | tf_op jit(solution)/shard_map/ppermute | solution.py:399
  65.6 4.1 %forward.1 = (bf16[128,512]{1,0:T(8,128)(2,1)S(1)}, bf16[128,512]{1,0:T(8,128)(2,1)S(1)}, bf16[128,512]{1,0:T(8,128)(2,1)S(1)}, bf16[128,512]{1,0:T(8,128)(2,1)S(1)}) custom-call(s32[1,32]{1,0:T(1,128)S(1)} %copy-done.3, bf16[128,1536]{1,0:T(8,128)(2,1)S(1)} %copy-done, bf16[128,1536]{1,0:T(8,128)(2,1)S(1)} %collective-permute-done.9.refs_0_.refs_1_, ...), custom_call_target="tpu_custom_call" | custom-call | bytes 3145856 | tf_op jit(solution)/shard_map/forward/pallas_call | solution.py:352
  69.6 0.0 collective-permute-done.18.refs_1_
  69.7 0.0 collective-permute-done.19.refs_3_
  69.7 1.6 %collective-permute-done.17 = bf16[512,256]{1,0:T(8,128)(2,1)S(1)} collective-permute-done((bf16[512,256]{1,0:T(8,128)(2,1)S(1)}, bf16[512,256]{1,0:T(8,128)(2,1)S(1)}, u32[]{:S(2)}, u32[]{:S(2)}) %collective-permute-start.17) | collective-permute-done | bytes 262176 | tf_op jit(solution)/shard_map/ppermute | solution.py:399
  71.2 0.1 add_convert_fusion
  71.3 0.1 collective-permute-start.24
  71.4 0.6 collective-permute-start.20
  71.9 2.3 %collective-permute-start.22 = (bf16[128,512]{1,0:T(8,128)(2,1)S(1)}, bf16[128,512]{1,0:T(8,128)(2,1)S(1)}, u32[]{:S(2)}, u32[]{:S(2)}) collective-permute-start(bf16[128,512]{1,0:T(8,128)(2,1)S(1)} %get-tuple-element.166), channel_id=1, source_target_pairs={{0,5},{1,4},{2,7},{3,6},{4,1},{5,0},{6,3},{7,2},{8,13},{9,12},{10,... | collective-permute-start | bytes 393224 | tf_op jit(solution)/shard_map/ppermute | solution.py:410
  74.2 1.5 %collective-permute-done.25.refs_2_ = bf16[512,256]{1,0:T(8,128)(2,1)S(1)} collective-permute-done((bf16[512,256]{1,0:T(8,128)(2,1)S(1)}, bf16[512,256]{1,0:T(8,128)(2,1)S(1)}, u32[]{:S(2)}, u32[]{:S(2)}) %collective-permute-start.25) | collective-permute-done | bytes 262176 | tf_op jit(solution)/shard_map/ppermute | solution.py:399
  75.8 0.1 collective-permute-start.23
  75.8 4.7 %collective-permute-done.24.refs_1_ = bf16[512,256]{1,0:T(8,128)(2,1)S(1)} collective-permute-done((bf16[512,256]{1,0:T(8,128)(2,1)S(1)}, bf16[512,256]{1,0:T(8,128)(2,1)S(1)}, u32[]{:S(2)}, u32[]{:S(2)}) %collective-permute-start.24) | collective-permute-done | bytes 262176 | tf_op jit(solution)/shard_map/ppermute | solution.py:399
  80.5 0.1 sum_key_parts.1
  80.6 0.1 collective-permute-start.26
  80.7 2.7 %collective-permute-done.20.refs_0_ = bf16[128,512]{1,0:T(8,128)(2,1)S(1)} collective-permute-done((bf16[128,512]{1,0:T(8,128)(2,1)S(1)}, bf16[128,512]{1,0:T(8,128)(2,1)S(1)}, u32[]{:S(2)}, u32[]{:S(2)}) %collective-permute-start.20) | collective-permute-done | bytes 131104 | tf_op jit(solution)/shard_map/ppermute | solution.py:410
  83.4 1.3 %collective-permute-start.27 = (bf16[128,256]{1,0:T(8,128)(2,1)S(1)}, bf16[128,256]{1,0:T(8,128)(2,1)S(1)}, u32[]{:S(2)}, u32[]{:S(2)}) collective-permute-start(bf16[128,256]{1,0:T(8,128)(2,1)S(1)} %get-tuple-element.184), channel_id=1, source_target_pairs={{0,4},{2,6},{4,0},{6,2},{8,12},{10,14},{12,8},{14,10},{16,20},{18,... | collective-permute-start | bytes 196616 | tf_op jit(solution)/shard_map/ppermute | solution.py:393
  84.7 0.0 collective-permute-done.21.refs_1_
  84.7 0.8 collective-permute-start.28
  85.5 0.8 query_grad.1
  86.4 1.2 %gate.1 = bf16[1,128,2048]{2,1,0:T(8,128)(2,1)} custom-call(bf16[128,512]{1,0:T(8,128)(2,1)S(1)} %collective-permute-done.20.refs_0_, bf16[128,512]{1,0:T(8,128)(2,1)S(1)} %collective-permute-done.21.refs_1_, bf16[128,512]{1,0:T(8,128)(2,1)S(1)} %collective-permute-done.22.refs_2_, bf16[128,512]{1,0:T(8,128)(2,1)S(1)} %collective-permute-done.23.refs_3_, ...), custom_call_target="tpu_custom_call" | custom-call | bytes 1638400 | tf_op jit(solution)/shard_map/gate/pallas_call | solution.py:352
  87.5 0.1 collective-permute-done.27.refs_2_
  87.6 1.4 %collective-permute-done.28.refs_3_ = bf16[128,256]{1,0:T(8,128)(2,1)S(1)} collective-permute-done((bf16[128,256]{1,0:T(8,128)(2,1)S(1)}, bf16[128,256]{1,0:T(8,128)(2,1)S(1)}, u32[]{:S(2)}, u32[]{:S(2)}) %collective-permute-start.28) | collective-permute-done | bytes 65568 | tf_op jit(solution)/shard_map/ppermute | solution.py:393
  89.0 0.8 key_grad.1
  (21 shorter events, 0.0 us)
Async XLA Ops:
  2.6 5.1 %collective-permute-start = (bf16[128,256]{1,0:T(8,128)(2,1)}, bf16[128,256]{1,0:T(8,128)(2,1)S(1)}, u32[]{:S(2)}, u32[]{:S(2)}) collective-permute-start(bf16[128,256]{1,0:T(8,128)(2,1)} %get-tuple-element.97), channel_id=1, source_target_pairs={{0,2},{2,0},{4,6},{6,4},{8,10},{10,8},{12,14},{14,12},{16,18},{18,... | collective-permute-start | bytes 196616 | tf_op jit(solution)/shard_map/ppermute | solution.py:393
  3.1 5.5 %collective-permute-start.1 = (bf16[128,256]{1,0:T(8,128)(2,1)}, bf16[128,256]{1,0:T(8,128)(2,1)S(1)}, u32[]{:S(2)}, u32[]{:S(2)}) collective-permute-start(bf16[128,256]{1,0:T(8,128)(2,1)} %get-tuple-element.98), channel_id=1, source_target_pairs={{0,4},{2,6},{4,0},{6,2},{8,12},{10,14},{12,8},{14,10},{16,20},{18,... | collective-permute-start | bytes 196616 | tf_op jit(solution)/shard_map/ppermute | solution.py:393
  5.7 4.4 %copy-start.2 = (bf16[128,256]{1,0:T(8,128)(2,1)S(1)}, bf16[128,256]{1,0:T(8,128)(2,1)}, u32[]{:S(2)}) copy-start(bf16[128,256]{1,0:T(8,128)(2,1)} %get-tuple-element.104.refs_0_) | copy-start | bytes 196612
  5.7 4.3 %collective-permute-start.2 = (bf16[128,256]{1,0:T(8,128)(2,1)}, bf16[128,256]{1,0:T(8,128)(2,1)S(1)}, u32[]{:S(2)}, u32[]{:S(2)}) collective-permute-start(bf16[128,256]{1,0:T(8,128)(2,1)} %get-tuple-element.99), channel_id=1, source_target_pairs={{0,6},{2,4},{4,2},{6,0},{8,14},{10,12},{12,10},{14,8},{16,22},{18,... | collective-permute-start | bytes 196616 | tf_op jit(solution)/shard_map/ppermute | solution.py:393
  10.1 2.0 %copy-start.6 = (bf16[128,256]{1,0:T(8,128)(2,1)S(1)}, bf16[128,256]{1,0:T(8,128)(2,1)}, u32[]{:S(2)}) copy-start(bf16[128,256]{1,0:T(8,128)(2,1)} %get-tuple-element.109) | copy-start | bytes 196612
  10.1 2.0 %copy-start.5 = (bf16[128,256]{1,0:T(8,128)(2,1)S(1)}, bf16[128,256]{1,0:T(8,128)(2,1)}, u32[]{:S(2)}) copy-start(bf16[128,256]{1,0:T(8,128)(2,1)} %get-tuple-element.110) | copy-start | bytes 196612
  10.1 3.4 %copy-start.4 = (bf16[128,256]{1,0:T(8,128)(2,1)S(1)}, bf16[128,256]{1,0:T(8,128)(2,1)}, u32[]{:S(2)}) copy-start(bf16[128,256]{1,0:T(8,128)(2,1)} %get-tuple-element.111) | copy-start | bytes 196612
  10.5 13.7 %copy-start.1 = (bf16[128,256]{1,0:T(8,128)(2,1)S(1)}, bf16[128,256]{1,0:T(8,128)(2,1)}, u32[]{:S(2)}) copy-start(bf16[128,256]{1,0:T(8,128)(2,1)} %get-tuple-element.120.refs_0_) | copy-start | bytes 196612
  10.5 10.2 %collective-permute-start.3 = (bf16[512,256]{1,0:T(8,128)(2,1)S(1)}, bf16[512,256]{1,0:T(8,128)(2,1)S(1)}, u32[]{:S(2)}, u32[]{:S(2)}) collective-permute-start(bf16[512,256]{1,0:T(8,128)(2,1)S(1)} %stack_keys_bwd.1.refs_2_), channel_id=1, source_target_pairs={{0,8},{2,10},{4,12},{6,14},{8,16},{10,18},{12,20},{14,22},{16,24},... | collective-permute-start | bytes 786440 | tf_op jit(solution)/shard_map/ppermute | solution.py:399
  12.1 5.7 %collective-permute-start.4 = (bf16[128,256]{1,0:T(8,128)(2,1)S(1)}, bf16[128,256]{1,0:T(8,128)(2,1)S(1)}, u32[]{:S(2)}, u32[]{:S(2)}) collective-permute-start(bf16[128,256]{1,0:T(8,128)(2,1)S(1)} %copy-done.6), channel_id=1, source_target_pairs={{0,2},{2,0},{4,6},{6,4},{8,10},{10,8},{12,14},{14,12},{16,18},{18,... | collective-permute-start | bytes 196616 | tf_op jit(solution)/shard_map/ppermute | solution.py:393
  12.1 5.7 %collective-permute-start.5 = (bf16[128,256]{1,0:T(8,128)(2,1)S(1)}, bf16[128,256]{1,0:T(8,128)(2,1)S(1)}, u32[]{:S(2)}, u32[]{:S(2)}) collective-permute-start(bf16[128,256]{1,0:T(8,128)(2,1)S(1)} %copy-done.5), channel_id=1, source_target_pairs={{0,4},{2,6},{4,0},{6,2},{8,12},{10,14},{12,8},{14,10},{16,20},{18,... | collective-permute-start | bytes 196616 | tf_op jit(solution)/shard_map/ppermute | solution.py:393
  13.4 4.4 %collective-permute-start.6 = (bf16[128,256]{1,0:T(8,128)(2,1)S(1)}, bf16[128,256]{1,0:T(8,128)(2,1)S(1)}, u32[]{:S(2)}, u32[]{:S(2)}) collective-permute-start(bf16[128,256]{1,0:T(8,128)(2,1)S(1)} %copy-done.4), channel_id=1, source_target_pairs={{0,6},{2,4},{4,2},{6,0},{8,14},{10,12},{12,10},{14,8},{16,22},{18,... | collective-permute-start | bytes 196616 | tf_op jit(solution)/shard_map/ppermute | solution.py:393
  17.8 21.5 %copy-start = (bf16[128,1536]{1,0:T(8,128)(2,1)S(1)}, bf16[128,1536]{1,0:T(8,128)(2,1)}, u32[]{:S(2)}) copy-start(bf16[128,1536]{1,0:T(8,128)(2,1)} %get-tuple-element.117.refs_0_) | copy-start | bytes 1179652
  20.7 18.5 %copy-start.3 = (s32[1,32]{1,0:T(1,128)S(1)}, s32[1,32]{1,0:T(1,128)}, u32[]{:S(2)}) copy-start(s32[1,32]{1,0:T(1,128)} %order_ref.5) | copy-start | bytes 388
  20.7 9.0 %collective-permute-start.8 = (bf16[512,256]{1,0:T(8,128)(2,1)S(1)}, bf16[512,256]{1,0:T(8,128)(2,1)S(1)}, u32[]{:S(2)}, u32[]{:S(2)}) collective-permute-start(bf16[512,256]{1,0:T(8,128)(2,1)S(1)} %stack_keys_bwd.1.refs_2_), channel_id=1, source_target_pairs={{0,24},{2,26},{4,28},{6,30},{8,0},{10,2},{12,4},{14,6},{16,8},{18,... | collective-permute-start | bytes 786440 | tf_op jit(solution)/shard_map/ppermute | solution.py:399
  22.5 11.6 %collective-permute-start.7 = (bf16[512,256]{1,0:T(8,128)(2,1)S(1)}, bf16[512,256]{1,0:T(8,128)(2,1)S(1)}, u32[]{:S(2)}, u32[]{:S(2)}) collective-permute-start(bf16[512,256]{1,0:T(8,128)(2,1)S(1)} %collective-permute-done.3.refs_3_), channel_id=1, source_target_pairs={{0,8},{2,10},{4,12},{6,14},{8,16},{10,18},{12,20},{14,22},{16,24},... | collective-permute-start | bytes 786440 | tf_op jit(solution)/shard_map/ppermute | solution.py:399
  22.7 16.2 %collective-permute-start.10 = (bf16[128,1536]{1,0:T(8,128)(2,1)}, bf16[128,1536]{1,0:T(8,128)(2,1)S(1)}, u32[]{:S(2)}, u32[]{:S(2)}) collective-permute-start(bf16[128,1536]{1,0:T(8,128)(2,1)} %get-tuple-element.127), channel_id=1, source_target_pairs={{0,4},{2,6},{4,0},{6,2},{8,12},{10,14},{12,8},{14,10},{16,20},{18,... | collective-permute-start | bytes 1179656 | tf_op jit(solution)/shard_map/ppermute | solution.py:393
  34.1 17.9 %collective-permute-start.14 = (bf16[144,2048]{1,0:T(8,128)(2,1)}, bf16[144,2048]{1,0:T(8,128)(2,1)S(1)}, u32[]{:S(2)}, u32[]{:S(2)}) collective-permute-start(bf16[144,2048]{1,0:T(8,128)(2,1)} %get-tuple-element.138), channel_id=1, source_target_pairs={{0,1},{1,0},{2,3},{3,2},{4,5},{5,4},{6,7},{7,6},{8,9},{9,8},{10,11... | collective-permute-start | bytes 1769480 | tf_op jit(solution)/shard_map/ppermute | solution.py:410
  35.6 17.8 %collective-permute-start.11 = (bf16[128,1536]{1,0:T(8,128)(2,1)}, bf16[128,1536]{1,0:T(8,128)(2,1)S(1)}, u32[]{:S(2)}, u32[]{:S(2)}) collective-permute-start(bf16[128,1536]{1,0:T(8,128)(2,1)} %get-tuple-element.128), channel_id=1, source_target_pairs={{0,6},{2,4},{4,2},{6,0},{8,14},{10,12},{12,10},{14,8},{16,22},{18,... | collective-permute-start | bytes 1179656 | tf_op jit(solution)/shard_map/ppermute | solution.py:393
  35.6 17.8 %collective-permute-start.9 = (bf16[128,1536]{1,0:T(8,128)(2,1)}, bf16[128,1536]{1,0:T(8,128)(2,1)S(1)}, u32[]{:S(2)}, u32[]{:S(2)}) collective-permute-start(bf16[128,1536]{1,0:T(8,128)(2,1)} %get-tuple-element.126), channel_id=1, source_target_pairs={{0,2},{2,0},{4,6},{6,4},{8,10},{10,8},{12,14},{14,12},{16,18},{18,... | collective-permute-start | bytes 1179656 | tf_op jit(solution)/shard_map/ppermute | solution.py:393
  37.2 8.7 %collective-permute-start.13 = (bf16[512,256]{1,0:T(8,128)(2,1)S(1)}, bf16[512,256]{1,0:T(8,128)(2,1)S(1)}, u32[]{:S(2)}, u32[]{:S(2)}) collective-permute-start(bf16[512,256]{1,0:T(8,128)(2,1)S(1)} %stack_keys_fwd.1.refs_4_), channel_id=1, source_target_pairs={{0,24},{2,26},{4,28},{6,30},{8,0},{10,2},{12,4},{14,6},{16,8},{18,... | collective-permute-start | bytes 786440 | tf_op jit(solution)/shard_map/ppermute | solution.py:399
  39.0 13.0 %collective-permute-start.12 = (bf16[512,256]{1,0:T(8,128)(2,1)S(1)}, bf16[512,256]{1,0:T(8,128)(2,1)S(1)}, u32[]{:S(2)}, u32[]{:S(2)}) collective-permute-start(bf16[512,256]{1,0:T(8,128)(2,1)S(1)} %stack_keys_fwd.1.refs_4_), channel_id=1, source_target_pairs={{0,8},{2,10},{4,12},{6,14},{8,16},{10,18},{12,20},{14,22},{16,24},... | collective-permute-start | bytes 786440 | tf_op jit(solution)/shard_map/ppermute | solution.py:399
  52.0 9.1 %collective-permute-start.15 = (bf16[512,256]{1,0:T(8,128)(2,1)S(1)}, bf16[512,256]{1,0:T(8,128)(2,1)S(1)}, u32[]{:S(2)}, u32[]{:S(2)}) collective-permute-start(bf16[512,256]{1,0:T(8,128)(2,1)S(1)} %collective-permute-done.12.refs_5_), channel_id=1, source_target_pairs={{0,8},{2,10},{4,12},{6,14},{8,16},{10,18},{12,20},{14,22},{16,24},... | collective-permute-start | bytes 786440 | tf_op jit(solution)/shard_map/ppermute | solution.py:399
  52.8 7.2 %collective-permute-start.16 = (bf16[128,512]{1,0:T(8,128)(2,1)S(1)}, bf16[128,512]{1,0:T(8,128)(2,1)S(1)}, u32[]{:S(2)}, u32[]{:S(2)}) collective-permute-start(bf16[128,512]{1,0:T(8,128)(2,1)S(1)} %get-tuple-element.150), channel_id=1, source_target_pairs={{0,4},{2,6},{4,0},{6,2},{8,12},{10,14},{12,8},{14,10},{16,20},{18,... | collective-permute-start | bytes 393224 | tf_op jit(solution)/shard_map/ppermute | solution.py:393
  61.1 10.2 %collective-permute-start.17 = (bf16[512,256]{1,0:T(8,128)(2,1)S(1)}, bf16[512,256]{1,0:T(8,128)(2,1)S(1)}, u32[]{:S(2)}, u32[]{:S(2)}) collective-permute-start(bf16[512,256]{1,0:T(8,128)(2,1)S(1)} %get-tuple-element.159), channel_id=1, source_target_pairs={{0,8},{2,10},{4,12},{6,14},{8,16},{10,18},{12,20},{14,22},{16,24},... | collective-permute-start | bytes 786440 | tf_op jit(solution)/shard_map/ppermute | solution.py:399
  61.6 8.1 %collective-permute-start.18 = (bf16[128,512]{1,0:T(8,128)(2,1)S(1)}, bf16[128,512]{1,0:T(8,128)(2,1)S(1)}, u32[]{:S(2)}, u32[]{:S(2)}) collective-permute-start(bf16[128,512]{1,0:T(8,128)(2,1)S(1)} %get-tuple-element.161), channel_id=1, source_target_pairs={{0,2},{2,0},{4,6},{6,4},{8,10},{10,8},{12,14},{14,12},{16,18},{18,... | collective-permute-start | bytes 393224 | tf_op jit(solution)/shard_map/ppermute | solution.py:393
  61.6 8.1 %collective-permute-start.19 = (bf16[128,512]{1,0:T(8,128)(2,1)S(1)}, bf16[128,512]{1,0:T(8,128)(2,1)S(1)}, u32[]{:S(2)}, u32[]{:S(2)}) collective-permute-start(bf16[128,512]{1,0:T(8,128)(2,1)S(1)} %get-tuple-element.163), channel_id=1, source_target_pairs={{0,6},{2,4},{4,2},{6,0},{8,14},{10,12},{12,10},{14,8},{16,22},{18,... | collective-permute-start | bytes 393224 | tf_op jit(solution)/shard_map/ppermute | solution.py:393
  63.2 12.6 %collective-permute-start.25 = (bf16[512,256]{1,0:T(8,128)(2,1)S(1)}, bf16[512,256]{1,0:T(8,128)(2,1)S(1)}, u32[]{:S(2)}, u32[]{:S(2)}) collective-permute-start(bf16[512,256]{1,0:T(8,128)(2,1)S(1)} %get-tuple-element.181), channel_id=1, source_target_pairs={{0,24},{2,26},{4,28},{6,30},{8,0},{10,2},{12,4},{14,6},{16,8},{18,... | collective-permute-start | bytes 786440 | tf_op jit(solution)/shard_map/ppermute | solution.py:399
  71.3 9.2 %collective-permute-start.24 = (bf16[512,256]{1,0:T(8,128)(2,1)S(1)}, bf16[512,256]{1,0:T(8,128)(2,1)S(1)}, u32[]{:S(2)}, u32[]{:S(2)}) collective-permute-start(bf16[512,256]{1,0:T(8,128)(2,1)S(1)} %add_convert_fusion), channel_id=1, source_target_pairs={{0,8},{2,10},{4,12},{6,14},{8,16},{10,18},{12,20},{14,22},{16,24},... | collective-permute-start | bytes 786440 | tf_op jit(solution)/shard_map/ppermute | solution.py:399
  71.4 12.0 %collective-permute-start.20 = (bf16[128,512]{1,0:T(8,128)(2,1)S(1)}, bf16[128,512]{1,0:T(8,128)(2,1)S(1)}, u32[]{:S(2)}, u32[]{:S(2)}) collective-permute-start(bf16[128,512]{1,0:T(8,128)(2,1)S(1)} %get-tuple-element.164), channel_id=1, source_target_pairs={{0,1},{1,0},{2,3},{3,2},{4,5},{5,4},{6,7},{7,6},{8,9},{9,8},{10,11... | collective-permute-start | bytes 393224 | tf_op jit(solution)/shard_map/ppermute | solution.py:410
  71.9 12.8 %collective-permute-start.21 = (bf16[128,512]{1,0:T(8,128)(2,1)S(1)}, bf16[128,512]{1,0:T(8,128)(2,1)S(1)}, u32[]{:S(2)}, u32[]{:S(2)}) collective-permute-start(bf16[128,512]{1,0:T(8,128)(2,1)S(1)} %get-tuple-element.165), channel_id=1, source_target_pairs={{0,3},{1,2},{2,1},{3,0},{4,7},{5,6},{6,5},{7,4},{8,11},{9,10},{10,... | collective-permute-start | bytes 393224 | tf_op jit(solution)/shard_map/ppermute | solution.py:410
  71.9 14.4 %collective-permute-start.22 = (bf16[128,512]{1,0:T(8,128)(2,1)S(1)}, bf16[128,512]{1,0:T(8,128)(2,1)S(1)}, u32[]{:S(2)}, u32[]{:S(2)}) collective-permute-start(bf16[128,512]{1,0:T(8,128)(2,1)S(1)} %get-tuple-element.166), channel_id=1, source_target_pairs={{0,5},{1,4},{2,7},{3,6},{4,1},{5,0},{6,3},{7,2},{8,13},{9,12},{10,... | collective-permute-start | bytes 393224 | tf_op jit(solution)/shard_map/ppermute | solution.py:410
  75.8 10.6 %collective-permute-start.23 = (bf16[128,512]{1,0:T(8,128)(2,1)S(1)}, bf16[128,512]{1,0:T(8,128)(2,1)S(1)}, u32[]{:S(2)}, u32[]{:S(2)}) collective-permute-start(bf16[128,512]{1,0:T(8,128)(2,1)S(1)} %get-tuple-element.167), channel_id=1, source_target_pairs={{0,7},{1,6},{2,5},{3,4},{4,3},{5,2},{6,1},{7,0},{8,15},{9,14},{10,... | collective-permute-start | bytes 393224 | tf_op jit(solution)/shard_map/ppermute | solution.py:410
  80.6 6.9 %collective-permute-start.26 = (bf16[128,256]{1,0:T(8,128)(2,1)S(1)}, bf16[128,256]{1,0:T(8,128)(2,1)S(1)}, u32[]{:S(2)}, u32[]{:S(2)}) collective-permute-start(bf16[128,256]{1,0:T(8,128)(2,1)S(1)} %get-tuple-element.183), channel_id=1, source_target_pairs={{0,2},{2,0},{4,6},{6,4},{8,10},{10,8},{12,14},{14,12},{16,18},{18,... | collective-permute-start | bytes 196616 | tf_op jit(solution)/shard_map/ppermute | solution.py:393
  83.4 4.3 %collective-permute-start.27 = (bf16[128,256]{1,0:T(8,128)(2,1)S(1)}, bf16[128,256]{1,0:T(8,128)(2,1)S(1)}, u32[]{:S(2)}, u32[]{:S(2)}) collective-permute-start(bf16[128,256]{1,0:T(8,128)(2,1)S(1)} %get-tuple-element.184), channel_id=1, source_target_pairs={{0,4},{2,6},{4,0},{6,2},{8,12},{10,14},{12,8},{14,10},{16,20},{18,... | collective-permute-start | bytes 196616 | tf_op jit(solution)/shard_map/ppermute | solution.py:393
  84.7 4.3 %collective-permute-start.28 = (bf16[128,256]{1,0:T(8,128)(2,1)S(1)}, bf16[128,256]{1,0:T(8,128)(2,1)S(1)}, u32[]{:S(2)}, u32[]{:S(2)}) collective-permute-start(bf16[128,256]{1,0:T(8,128)(2,1)S(1)} %get-tuple-element.185), channel_id=1, source_target_pairs={{0,6},{2,4},{4,2},{6,0},{8,14},{10,12},{12,10},{14,8},{16,22},{18,... | collective-permute-start | bytes 196616 | tf_op jit(solution)/shard_map/ppermute | solution.py:393

commit v12 on v11

--- a/solution.py
+++ b/solution.py
@@ -581,7 +581,7 @@
         gate_before,
     )
     key_sums = reduce_rest(key_parts, key_up, key_sums[1])
-    key_pieces = swap(
+    key_pieces = list(
         call(
             sum_kernel,
             "sum_key_parts",
@@ -590,6 +590,9 @@
             *key_sums,
         )
     )
+    key_pieces[1] = swap_one(key_pieces[1], 1)
+    key_pieces = lax.optimization_barrier(key_pieces)
+    key_pieces[2:] = [swap_one(key_pieces[d], d) for d in range(2, QUAD)]
     key_grad, value_grad = call(
         key_grad_kernel,
         "key_grad",

time: 90 us -> 88.6 us (0.984)
  starting transfers between devices: 26.3 us -> 25.2 us
    ppermute x5, waiting for transfers between devices: 2.7 us -> 0.49 us  [hand(): return lax.ppermute(block, ('ctx', 'pipe'), route)]
    ppermute x15, waiting for transfers between devices: 3.81 us -> 5.77 us  [swap_one(): return lax.ppermute(piece, 'ctx', [(i, i ^ d) for i in range(devices)])]
    ppermute x15, starting transfers between devices: 12.4 us -> 11.3 us  [swap_one(): return lax.ppermute(piece, 'ctx', [(i, i ^ d) for i in range(devices)])]
  transfers between devices with their start and end apart: 29 -> 29, of which waited for: 13 -> 14; matrix products, arithmetic and copies ran while one was open for 0% -> 0% of each run, Pallas kernels for 29% -> 29%
where the time goes in v12:
time: 88.6 us; the launch traced here: 88.4 us
  waiting for transfers between devices  33.5 us (38%)
  Pallas kernels  28.7 us (32%)
  starting transfers between devices  25.2 us (28%)
    pallas_call x12, Pallas kernels, call(): pl.pallas_call(kernel, name=name, out_shape=out_shape, in_specs=specs, ou...  28.7 us
    ppermute x9, waiting for transfers between devices, turn(): lax.ppermute(block, 'ctx', [(i, (i + s * QUAD) % devices) for i in range(...  27.3 us
    ppermute x15, starting transfers between devices, swap_one(): return lax.ppermute(piece, 'ctx', [(i, i ^ d) for i in range(devices)])  11.3 us
    ppermute x9, starting transfers between devices, turn(): lax.ppermute(block, 'ctx', [(i, (i + s * QUAD) % devices) for i in range(...  9.49 us
    ppermute x15, waiting for transfers between devices, swap_one(): return lax.ppermute(piece, 'ctx', [(i, i ^ d) for i in range(devices)])  5.77 us
    ppermute x5, starting transfers between devices, hand(): return lax.ppermute(block, ('ctx', 'pipe'), route)  4.44 us
  transfers between devices with their start and end apart: 29, of which 14 were waited for; matrix products, arithmetic and copies ran while one was open for 0% of the time, Pallas kernels for 29%

profile of v12, /device:TPU:0, one launch (start us, length us, event | category | flops | bytes accessed | tf_op | source)
XLA Modules:
  0.0 88.4 jit_solution(15897540117875839904)
XLA Ops:
  0.6 2.0 %pack_keys_bwd.1 = (bf16[128,256]{1,0:T(8,128)(2,1)}, bf16[128,256]{1,0:T(8,128)(2,1)}, bf16[128,256]{1,0:T(8,128)(2,1)}, bf16[128,256]{1,0:T(8,128)(2,1)}) custom-call(bf16[1,128,512]{2,1,0:T(8,128)(2,1)} %key_ref.2, bf16[1,128,512]{2,1,0:T(8,128)(2,1)} %value_ref.2, s32[1,128]{1,0:T(1,128)} %types_ref.2, bf16[1,64,512]{2,1,0:T(8,128)(2,1)} %table_ref.3), custom_call_target="tpu_custom_call" | custom-call | bytes 590336 | tf_op jit(solution)/shard_map/pack_keys_bwd/pallas_call | solution.py:352
  2.6 0.5 collective-permute-start
  3.1 2.6 %collective-permute-start.1 = (bf16[128,256]{1,0:T(8,128)(2,1)}, bf16[128,256]{1,0:T(8,128)(2,1)S(1)}, u32[]{:S(2)}, u32[]{:S(2)}) collective-permute-start(bf16[128,256]{1,0:T(8,128)(2,1)} %get-tuple-element.102), channel_id=1, source_target_pairs={{0,4},{2,6},{4,0},{6,2},{8,12},{10,14},{12,8},{14,10},{16,20},{18,... | collective-permute-start | bytes 196616 | tf_op jit(solution)/shard_map/ppermute | solution.py:393
  5.7 0.1 collective-permute-start.2
  5.8 2.0 %pack_keys_fwd.1 = (bf16[128,256]{1,0:T(8,128)(2,1)}, bf16[128,256]{1,0:T(8,128)(2,1)}, bf16[128,256]{1,0:T(8,128)(2,1)}, bf16[128,256]{1,0:T(8,128)(2,1)}) custom-call(bf16[1,128,512]{2,1,0:T(8,128)(2,1)} %key_ref.3, bf16[1,128,512]{2,1,0:T(8,128)(2,1)} %value_ref.3, s32[1,128]{1,0:T(1,128)} %types_ref.3, bf16[1,64,512]{2,1,0:T(8,128)(2,1)} %table_ref.3), custom_call_target="tpu_custom_call" | custom-call | bytes 590336 | tf_op jit(solution)/shard_map/pack_keys_fwd/pallas_call | solution.py:352
  7.7 0.0 collective-permute-done.refs_1_
  7.7 0.9 collective-permute-done.1.refs_2_
  8.6 1.5 %collective-permute-done.2.refs_3_ = bf16[128,256]{1,0:T(8,128)(2,1)S(1)} collective-permute-done((bf16[128,256]{1,0:T(8,128)(2,1)}, bf16[128,256]{1,0:T(8,128)(2,1)S(1)}, u32[]{:S(2)}, u32[]{:S(2)}) %collective-permute-start.2) | collective-permute-done | bytes 65568 | tf_op jit(solution)/shard_map/ppermute | solution.py:393
  10.1 0.4 stack_keys_bwd.1.refs_2_
  10.5 0.0 copy-start.1
  10.5 1.6 %collective-permute-start.3 = (bf16[512,256]{1,0:T(8,128)(2,1)S(1)}, bf16[512,256]{1,0:T(8,128)(2,1)S(1)}, u32[]{:S(2)}, u32[]{:S(2)}) collective-permute-start(bf16[512,256]{1,0:T(8,128)(2,1)S(1)} %stack_keys_bwd.1.refs_2_), channel_id=1, source_target_pairs={{0,8},{2,10},{4,12},{6,14},{8,16},{10,18},{12,20},{14,22},{16,24},... | collective-permute-start | bytes 786440 | tf_op jit(solution)/shard_map/ppermute | solution.py:399
  12.1 0.0 collective-permute-start.4
  12.1 1.3 %collective-permute-start.5 = (bf16[128,256]{1,0:T(8,128)(2,1)S(1)}, bf16[128,256]{1,0:T(8,128)(2,1)S(1)}, u32[]{:S(2)}, u32[]{:S(2)}) collective-permute-start(bf16[128,256]{1,0:T(8,128)(2,1)S(1)} %copy-done.5), channel_id=1, source_target_pairs={{0,4},{2,6},{4,0},{6,2},{8,12},{10,14},{12,8},{14,10},{16,20},{18,... | collective-permute-start | bytes 196616 | tf_op jit(solution)/shard_map/ppermute | solution.py:393
  13.4 0.5 collective-permute-start.6
  14.0 3.8 %pack_queries.1 = (bf16[128,1536]{1,0:T(8,128)(2,1)}, bf16[128,1536]{1,0:T(8,128)(2,1)}, bf16[128,1536]{1,0:T(8,128)(2,1)}, bf16[128,1536]{1,0:T(8,128)(2,1)}, bf16[144,2048]{1,0:T(8,128)(2,1)}) custom-call(bf16[1,128,2048]{2,1,0:T(8,128)(2,1)} %query_ref.1, bf16[1,128,2048]{2,1,0:T(8,128)(2,1)} %grad_ref.1, bf16[1,128,2048]{2,1,0:T(8,128)(2,1)} %forward_ref.1, ...), custom_call_target="tpu_custom_call" | custom-call | bytes 4268032 | tf_op jit(solution)/shard_map/pack_queries/pallas_call | solution.py:352
  17.8 0.0 copy-start
  17.8 0.0 collective-permute-done.4.refs_1_
  17.8 0.0 collective-permute-done.6.refs_3_
  17.8 2.9 %collective-permute-done.3.refs_3_ = bf16[512,256]{1,0:T(8,128)(2,1)S(1)} collective-permute-done((bf16[512,256]{1,0:T(8,128)(2,1)S(1)}, bf16[512,256]{1,0:T(8,128)(2,1)S(1)}, u32[]{:S(2)}, u32[]{:S(2)}) %collective-permute-start.3) | collective-permute-done | bytes 262176 | tf_op jit(solution)/shard_map/ppermute | solution.py:399
  20.7 1.7 %collective-permute-start.8 = (bf16[512,256]{1,0:T(8,128)(2,1)S(1)}, bf16[512,256]{1,0:T(8,128)(2,1)S(1)}, u32[]{:S(2)}, u32[]{:S(2)}) collective-permute-start(bf16[512,256]{1,0:T(8,128)(2,1)S(1)} %stack_keys_bwd.1.refs_2_), channel_id=1, source_target_pairs={{0,24},{2,26},{4,28},{6,30},{8,0},{10,2},{12,4},{14,6},{16,8},{18,... | collective-permute-start | bytes 786440 | tf_op jit(solution)/shard_map/ppermute | solution.py:399
  22.5 0.3 collective-permute-start.7
  22.7 1.4 %collective-permute-start.10 = (bf16[128,1536]{1,0:T(8,128)(2,1)}, bf16[128,1536]{1,0:T(8,128)(2,1)S(1)}, u32[]{:S(2)}, u32[]{:S(2)}) collective-permute-start(bf16[128,1536]{1,0:T(8,128)(2,1)} %get-tuple-element.131), channel_id=1, source_target_pairs={{0,4},{2,6},{4,0},{6,2},{8,12},{10,14},{12,8},{14,10},{16,20},{18,... | collective-permute-start | bytes 1179656 | tf_op jit(solution)/shard_map/ppermute | solution.py:393
  24.2 0.4 stack_keys_fwd.1.refs_4_
  24.5 5.2 %collective-permute-done.8.refs_5_ = bf16[512,256]{1,0:T(8,128)(2,1)S(1)} collective-permute-done((bf16[512,256]{1,0:T(8,128)(2,1)S(1)}, bf16[512,256]{1,0:T(8,128)(2,1)S(1)}, u32[]{:S(2)}, u32[]{:S(2)}) %collective-permute-start.8) | collective-permute-done | bytes 262176 | tf_op jit(solution)/shard_map/ppermute | solution.py:399
  29.7 4.4 %collective-permute-done.7.refs_4_ = bf16[512,256]{1,0:T(8,128)(2,1)S(1)} collective-permute-done((bf16[512,256]{1,0:T(8,128)(2,1)S(1)}, bf16[512,256]{1,0:T(8,128)(2,1)S(1)}, u32[]{:S(2)}, u32[]{:S(2)}) %collective-permute-start.7) | collective-permute-done | bytes 262176 | tf_op jit(solution)/shard_map/ppermute | solution.py:399
  34.1 1.5 %collective-permute-start.14 = (bf16[144,2048]{1,0:T(8,128)(2,1)}, bf16[144,2048]{1,0:T(8,128)(2,1)S(1)}, u32[]{:S(2)}, u32[]{:S(2)}) collective-permute-start(bf16[144,2048]{1,0:T(8,128)(2,1)} %get-tuple-element.142), channel_id=1, source_target_pairs={{0,1},{1,0},{2,3},{3,2},{4,5},{5,4},{6,7},{7,6},{8,9},{9,8},{10,11... | collective-permute-start | bytes 1769480 | tf_op jit(solution)/shard_map/ppermute | solution.py:410
  35.6 1.6 %collective-permute-start.9 = (bf16[128,1536]{1,0:T(8,128)(2,1)}, bf16[128,1536]{1,0:T(8,128)(2,1)S(1)}, u32[]{:S(2)}, u32[]{:S(2)}) collective-permute-start(bf16[128,1536]{1,0:T(8,128)(2,1)} %get-tuple-element.130), channel_id=1, source_target_pairs={{0,2},{2,0},{4,6},{6,4},{8,10},{10,8},{12,14},{14,12},{16,18},{18,... | collective-permute-start | bytes 1179656 | tf_op jit(solution)/shard_map/ppermute | solution.py:393
  37.2 1.7 %collective-permute-start.13 = (bf16[512,256]{1,0:T(8,128)(2,1)S(1)}, bf16[512,256]{1,0:T(8,128)(2,1)S(1)}, u32[]{:S(2)}, u32[]{:S(2)}) collective-permute-start(bf16[512,256]{1,0:T(8,128)(2,1)S(1)} %stack_keys_fwd.1.refs_4_), channel_id=1, source_target_pairs={{0,24},{2,26},{4,28},{6,30},{8,0},{10,2},{12,4},{14,6},{16,8},{18,... | collective-permute-start | bytes 786440 | tf_op jit(solution)/shard_map/ppermute | solution.py:399
  39.0 0.3 collective-permute-start.12
  39.3 6.6 %backward_first.1 = (bf16[128,512]{1,0:T(8,128)(2,1)S(1)}, bf16[128,512]{1,0:T(8,128)(2,1)S(1)}, f32[2048,128]{1,0:T(8,128)S(1)}, f32[2048,128]{1,0:T(8,128)S(1)}) custom-call(s32[1,32]{1,0:T(1,128)S(1)} %copy-done.3, bf16[128,1536]{1,0:T(8,128)(2,1)S(1)} %copy-done, bf16[128,1536]{1,0:T(8,128)(2,1)S(1)} %collective-permute-done.10.refs_1_.refs_2_, ...), custom_call_target="tpu_custom_call" | custom-call | flops 1509949440 | bytes 4194432 | tf_op jit(solution)/shard_map/backward_first/pallas_call | solution.py:352
  45.9 0.0 collective-permute-done.13.refs_7_
  45.9 6.1 %collective-permute-done.12.refs_5_ = bf16[512,256]{1,0:T(8,128)(2,1)S(1)} collective-permute-done((bf16[512,256]{1,0:T(8,128)(2,1)S(1)}, bf16[512,256]{1,0:T(8,128)(2,1)S(1)}, u32[]{:S(2)}, u32[]{:S(2)}) %collective-permute-start.12) | collective-permute-done | bytes 262176 | tf_op jit(solution)/shard_map/ppermute | solution.py:399
  52.0 0.0 collective-permute-done.14.refs_4_
  52.0 0.9 collective-permute-start.15
  52.8 0.5 collective-permute-start.16
  53.4 0.0 collective-permute-done.9.refs_0_.refs_1_
  53.4 6.7 %backward_second.1 = (bf16[128,512]{1,0:T(8,128)(2,1)S(1)}, bf16[128,512]{1,0:T(8,128)(2,1)S(1)}, bf16[512,256]{1,0:T(8,128)(2,1)S(1)}, bf16[512,256]{1,0:T(8,12...) custom-call(s32[1,32]{1,0:T(1,128)S(1)} %copy-done.3, ...), custom_call_target="tpu_custom_call" | custom-call | flops 1509949440 | bytes 5243008 | tf_op jit(solution)/shard_map/backward_second/pallas_call | solution.py:352
  60.1 1.0 %collective-permute-done.15.refs_6_ = bf16[512,256]{1,0:T(8,128)(2,1)S(1)} collective-permute-done((bf16[512,256]{1,0:T(8,128)(2,1)S(1)}, bf16[512,256]{1,0:T(8,128)(2,1)S(1)}, u32[]{:S(2)}, u32[]{:S(2)}) %collective-permute-start.15) | collective-permute-done | bytes 262176 | tf_op jit(solution)/shard_map/ppermute | solution.py:399
  61.1 0.5 collective-permute-start.17
  61.6 0.0 collective-permute-start.18
  61.6 1.6 %collective-permute-start.19 = (bf16[128,512]{1,0:T(8,128)(2,1)S(1)}, bf16[128,512]{1,0:T(8,128)(2,1)S(1)}, u32[]{:S(2)}, u32[]{:S(2)}) collective-permute-start(bf16[128,512]{1,0:T(8,128)(2,1)S(1)} %get-tuple-element.167), channel_id=1, source_target_pairs={{0,6},{2,4},{4,2},{6,0},{8,14},{10,12},{12,10},{14,8},{16,22},{18,... | collective-permute-start | bytes 393224 | tf_op jit(solution)/shard_map/ppermute | solution.py:393
  63.2 2.4 %collective-permute-start.25 = (bf16[512,256]{1,0:T(8,128)(2,1)S(1)}, bf16[512,256]{1,0:T(8,128)(2,1)S(1)}, u32[]{:S(2)}, u32[]{:S(2)}) collective-permute-start(bf16[512,256]{1,0:T(8,128)(2,1)S(1)} %get-tuple-element.185), channel_id=1, source_target_pairs={{0,24},{2,26},{4,28},{6,30},{8,0},{10,2},{12,4},{14,6},{16,8},{18,... | collective-permute-start | bytes 786440 | tf_op jit(solution)/shard_map/ppermute | solution.py:399
  65.6 4.1 %forward.1 = (bf16[128,512]{1,0:T(8,128)(2,1)S(1)}, bf16[128,512]{1,0:T(8,128)(2,1)S(1)}, bf16[128,512]{1,0:T(8,128)(2,1)S(1)}, bf16[128,512]{1,0:T(8,128)(2,1)S(1)}) custom-call(s32[1,32]{1,0:T(1,128)S(1)} %copy-done.3, bf16[128,1536]{1,0:T(8,128)(2,1)S(1)} %copy-done, bf16[128,1536]{1,0:T(8,128)(2,1)S(1)} %collective-permute-done.9.refs_0_.refs_1_, ...), custom_call_target="tpu_custom_call" | custom-call | bytes 3145856 | tf_op jit(solution)/shard_map/forward/pallas_call | solution.py:352
  69.6 0.0 collective-permute-done.18.refs_1_
  69.7 0.0 collective-permute-done.19.refs_3_
  69.7 1.6 %collective-permute-done.17 = bf16[512,256]{1,0:T(8,128)(2,1)S(1)} collective-permute-done((bf16[512,256]{1,0:T(8,128)(2,1)S(1)}, bf16[512,256]{1,0:T(8,128)(2,1)S(1)}, u32[]{:S(2)}, u32[]{:S(2)}) %collective-permute-start.17) | collective-permute-done | bytes 262176 | tf_op jit(solution)/shard_map/ppermute | solution.py:399
  71.2 0.1 add_convert_fusion
  71.3 0.1 collective-permute-start.24
  71.4 0.6 collective-permute-start.20
  71.9 2.3 %collective-permute-start.22 = (bf16[128,512]{1,0:T(8,128)(2,1)S(1)}, bf16[128,512]{1,0:T(8,128)(2,1)S(1)}, u32[]{:S(2)}, u32[]{:S(2)}) collective-permute-start(bf16[128,512]{1,0:T(8,128)(2,1)S(1)} %get-tuple-element.170), channel_id=1, source_target_pairs={{0,5},{1,4},{2,7},{3,6},{4,1},{5,0},{6,3},{7,2},{8,13},{9,12},{10,... | collective-permute-start | bytes 393224 | tf_op jit(solution)/shard_map/ppermute | solution.py:410
  74.2 1.5 %collective-permute-done.25.refs_2_ = bf16[512,256]{1,0:T(8,128)(2,1)S(1)} collective-permute-done((bf16[512,256]{1,0:T(8,128)(2,1)S(1)}, bf16[512,256]{1,0:T(8,128)(2,1)S(1)}, u32[]{:S(2)}, u32[]{:S(2)}) %collective-permute-start.25) | collective-permute-done | bytes 262176 | tf_op jit(solution)/shard_map/ppermute | solution.py:399
  75.8 0.1 collective-permute-start.23
  75.8 4.7 %collective-permute-done.24.refs_1_ = bf16[512,256]{1,0:T(8,128)(2,1)S(1)} collective-permute-done((bf16[512,256]{1,0:T(8,128)(2,1)S(1)}, bf16[512,256]{1,0:T(8,128)(2,1)S(1)}, u32[]{:S(2)}, u32[]{:S(2)}) %collective-permute-start.24) | collective-permute-done | bytes 262176 | tf_op jit(solution)/shard_map/ppermute | solution.py:399
  80.5 0.1 sum_key_parts.1
  80.6 0.1 collective-permute-start.26
  80.7 1.2 %collective-permute-done.26.refs_1_ = bf16[128,256]{1,0:T(8,128)(2,1)S(1)} collective-permute-done((bf16[128,256]{1,0:T(8,128)(2,1)S(1)}, bf16[128,256]{1,0:T(8,128)(2,1)S(1)}, u32[]{:S(2)}, u32[]{:S(2)}) %collective-permute-start.26) | collective-permute-done | bytes 65568 | tf_op jit(solution)/shard_map/ppermute | solution.py:393
  81.9 1.0 %collective-permute-start.27 = (bf16[128,256]{1,0:T(8,128)(2,1)S(1)}, bf16[128,256]{1,0:T(8,128)(2,1)S(1)}, u32[]{:S(2)}, u32[]{:S(2)}) collective-permute-start(bf16[128,256]{1,0:T(8,128)(2,1)S(1)} %get-tuple-element.192), channel_id=1, source_target_pairs={{0,4},{2,6},{4,0},{6,2},{8,12},{10,14},{12,8},{14,10},{16,20},{18,... | collective-permute-start | bytes 196616 | tf_op jit(solution)/shard_map/ppermute | solution.py:393
  82.9 0.5 collective-permute-done.20.refs_0_
  83.4 0.1 collective-permute-start.28
  83.4 0.8 query_grad.1
  84.3 1.2 %gate.1 = bf16[1,128,2048]{2,1,0:T(8,128)(2,1)} custom-call(bf16[128,512]{1,0:T(8,128)(2,1)S(1)} %collective-permute-done.20.refs_0_, bf16[128,512]{1,0:T(8,128)(2,1)S(1)} %collective-permute-done.21.refs_1_, bf16[128,512]{1,0:T(8,128)(2,1)S(1)} %collective-permute-done.22.refs_2_, bf16[128,512]{1,0:T(8,128)(2,1)S(1)} %collective-permute-done.23.refs_3_, ...), custom_call_target="tpu_custom_call" | custom-call | bytes 1638400 | tf_op jit(solution)/shard_map/gate/pallas_call | solution.py:352
  85.4 0.7 collective-permute-done.27.refs_2_
  86.2 1.5 %collective-permute-done.28.refs_3_ = bf16[128,256]{1,0:T(8,128)(2,1)S(1)} collective-permute-done((bf16[128,256]{1,0:T(8,128)(2,1)S(1)}, bf16[128,256]{1,0:T(8,128)(2,1)S(1)}, u32[]{:S(2)}, u32[]{:S(2)}) %collective-permute-start.28) | collective-permute-done | bytes 65568 | tf_op jit(solution)/shard_map/ppermute | solution.py:393
  87.6 0.8 key_grad.1
  (21 shorter events, 0.0 us)
Async XLA Ops:
  2.6 5.1 %collective-permute-start = (bf16[128,256]{1,0:T(8,128)(2,1)}, bf16[128,256]{1,0:T(8,128)(2,1)S(1)}, u32[]{:S(2)}, u32[]{:S(2)}) collective-permute-start(bf16[128,256]{1,0:T(8,128)(2,1)} %get-tuple-element.101), channel_id=1, source_target_pairs={{0,2},{2,0},{4,6},{6,4},{8,10},{10,8},{12,14},{14,12},{16,18},{18,... | collective-permute-start | bytes 196616 | tf_op jit(solution)/shard_map/ppermute | solution.py:393
  3.1 5.5 %collective-permute-start.1 = (bf16[128,256]{1,0:T(8,128)(2,1)}, bf16[128,256]{1,0:T(8,128)(2,1)S(1)}, u32[]{:S(2)}, u32[]{:S(2)}) collective-permute-start(bf16[128,256]{1,0:T(8,128)(2,1)} %get-tuple-element.102), channel_id=1, source_target_pairs={{0,4},{2,6},{4,0},{6,2},{8,12},{10,14},{12,8},{14,10},{16,20},{18,... | collective-permute-start | bytes 196616 | tf_op jit(solution)/shard_map/ppermute | solution.py:393
  5.7 4.4 %copy-start.2 = (bf16[128,256]{1,0:T(8,128)(2,1)S(1)}, bf16[128,256]{1,0:T(8,128)(2,1)}, u32[]{:S(2)}) copy-start(bf16[128,256]{1,0:T(8,128)(2,1)} %get-tuple-element.108.refs_0_) | copy-start | bytes 196612
  5.7 4.3 %collective-permute-start.2 = (bf16[128,256]{1,0:T(8,128)(2,1)}, bf16[128,256]{1,0:T(8,128)(2,1)S(1)}, u32[]{:S(2)}, u32[]{:S(2)}) collective-permute-start(bf16[128,256]{1,0:T(8,128)(2,1)} %get-tuple-element.103), channel_id=1, source_target_pairs={{0,6},{2,4},{4,2},{6,0},{8,14},{10,12},{12,10},{14,8},{16,22},{18,... | collective-permute-start | bytes 196616 | tf_op jit(solution)/shard_map/ppermute | solution.py:393
  10.1 2.0 %copy-start.6 = (bf16[128,256]{1,0:T(8,128)(2,1)S(1)}, bf16[128,256]{1,0:T(8,128)(2,1)}, u32[]{:S(2)}) copy-start(bf16[128,256]{1,0:T(8,128)(2,1)} %get-tuple-element.113) | copy-start | bytes 196612
  10.1 2.0 %copy-start.5 = (bf16[128,256]{1,0:T(8,128)(2,1)S(1)}, bf16[128,256]{1,0:T(8,128)(2,1)}, u32[]{:S(2)}) copy-start(bf16[128,256]{1,0:T(8,128)(2,1)} %get-tuple-element.114) | copy-start | bytes 196612
  10.1 3.4 %copy-start.4 = (bf16[128,256]{1,0:T(8,128)(2,1)S(1)}, bf16[128,256]{1,0:T(8,128)(2,1)}, u32[]{:S(2)}) copy-start(bf16[128,256]{1,0:T(8,128)(2,1)} %get-tuple-element.115) | copy-start | bytes 196612
  10.5 13.7 %copy-start.1 = (bf16[128,256]{1,0:T(8,128)(2,1)S(1)}, bf16[128,256]{1,0:T(8,128)(2,1)}, u32[]{:S(2)}) copy-start(bf16[128,256]{1,0:T(8,128)(2,1)} %get-tuple-element.124.refs_0_) | copy-start | bytes 196612
  10.5 10.2 %collective-permute-start.3 = (bf16[512,256]{1,0:T(8,128)(2,1)S(1)}, bf16[512,256]{1,0:T(8,128)(2,1)S(1)}, u32[]{:S(2)}, u32[]{:S(2)}) collective-permute-start(bf16[512,256]{1,0:T(8,128)(2,1)S(1)} %stack_keys_bwd.1.refs_2_), channel_id=1, source_target_pairs={{0,8},{2,10},{4,12},{6,14},{8,16},{10,18},{12,20},{14,22},{16,24},... | collective-permute-start | bytes 786440 | tf_op jit(solution)/shard_map/ppermute | solution.py:399
  12.1 5.7 %collective-permute-start.4 = (bf16[128,256]{1,0:T(8,128)(2,1)S(1)}, bf16[128,256]{1,0:T(8,128)(2,1)S(1)}, u32[]{:S(2)}, u32[]{:S(2)}) collective-permute-start(bf16[128,256]{1,0:T(8,128)(2,1)S(1)} %copy-done.6), channel_id=1, source_target_pairs={{0,2},{2,0},{4,6},{6,4},{8,10},{10,8},{12,14},{14,12},{16,18},{18,... | collective-permute-start | bytes 196616 | tf_op jit(solution)/shard_map/ppermute | solution.py:393
  12.1 5.7 %collective-permute-start.5 = (bf16[128,256]{1,0:T(8,128)(2,1)S(1)}, bf16[128,256]{1,0:T(8,128)(2,1)S(1)}, u32[]{:S(2)}, u32[]{:S(2)}) collective-permute-start(bf16[128,256]{1,0:T(8,128)(2,1)S(1)} %copy-done.5), channel_id=1, source_target_pairs={{0,4},{2,6},{4,0},{6,2},{8,12},{10,14},{12,8},{14,10},{16,20},{18,... | collective-permute-start | bytes 196616 | tf_op jit(solution)/shard_map/ppermute | solution.py:393
  13.4 4.4 %collective-permute-start.6 = (bf16[128,256]{1,0:T(8,128)(2,1)S(1)}, bf16[128,256]{1,0:T(8,128)(2,1)S(1)}, u32[]{:S(2)}, u32[]{:S(2)}) collective-permute-start(bf16[128,256]{1,0:T(8,128)(2,1)S(1)} %copy-done.4), channel_id=1, source_target_pairs={{0,6},{2,4},{4,2},{6,0},{8,14},{10,12},{12,10},{14,8},{16,22},{18,... | collective-permute-start | bytes 196616 | tf_op jit(solution)/shard_map/ppermute | solution.py:393
  17.8 21.5 %copy-start = (bf16[128,1536]{1,0:T(8,128)(2,1)S(1)}, bf16[128,1536]{1,0:T(8,128)(2,1)}, u32[]{:S(2)}) copy-start(bf16[128,1536]{1,0:T(8,128)(2,1)} %get-tuple-element.121.refs_0_) | copy-start | bytes 1179652
  20.7 18.5 %copy-start.3 = (s32[1,32]{1,0:T(1,128)S(1)}, s32[1,32]{1,0:T(1,128)}, u32[]{:S(2)}) copy-start(s32[1,32]{1,0:T(1,128)} %order_ref.5) | copy-start | bytes 388
  20.7 9.0 %collective-permute-start.8 = (bf16[512,256]{1,0:T(8,128)(2,1)S(1)}, bf16[512,256]{1,0:T(8,128)(2,1)S(1)}, u32[]{:S(2)}, u32[]{:S(2)}) collective-permute-start(bf16[512,256]{1,0:T(8,128)(2,1)S(1)} %stack_keys_bwd.1.refs_2_), channel_id=1, source_target_pairs={{0,24},{2,26},{4,28},{6,30},{8,0},{10,2},{12,4},{14,6},{16,8},{18,... | collective-permute-start | bytes 786440 | tf_op jit(solution)/shard_map/ppermute | solution.py:399
  22.5 11.6 %collective-permute-start.7 = (bf16[512,256]{1,0:T(8,128)(2,1)S(1)}, bf16[512,256]{1,0:T(8,128)(2,1)S(1)}, u32[]{:S(2)}, u32[]{:S(2)}) collective-permute-start(bf16[512,256]{1,0:T(8,128)(2,1)S(1)} %collective-permute-done.3.refs_3_), channel_id=1, source_target_pairs={{0,8},{2,10},{4,12},{6,14},{8,16},{10,18},{12,20},{14,22},{16,24},... | collective-permute-start | bytes 786440 | tf_op jit(solution)/shard_map/ppermute | solution.py:399
  22.7 16.2 %collective-permute-start.10 = (bf16[128,1536]{1,0:T(8,128)(2,1)}, bf16[128,1536]{1,0:T(8,128)(2,1)S(1)}, u32[]{:S(2)}, u32[]{:S(2)}) collective-permute-start(bf16[128,1536]{1,0:T(8,128)(2,1)} %get-tuple-element.131), channel_id=1, source_target_pairs={{0,4},{2,6},{4,0},{6,2},{8,12},{10,14},{12,8},{14,10},{16,20},{18,... | collective-permute-start | bytes 1179656 | tf_op jit(solution)/shard_map/ppermute | solution.py:393
  34.1 17.9 %collective-permute-start.14 = (bf16[144,2048]{1,0:T(8,128)(2,1)}, bf16[144,2048]{1,0:T(8,128)(2,1)S(1)}, u32[]{:S(2)}, u32[]{:S(2)}) collective-permute-start(bf16[144,2048]{1,0:T(8,128)(2,1)} %get-tuple-element.142), channel_id=1, source_target_pairs={{0,1},{1,0},{2,3},{3,2},{4,5},{5,4},{6,7},{7,6},{8,9},{9,8},{10,11... | collective-permute-start | bytes 1769480 | tf_op jit(solution)/shard_map/ppermute | solution.py:410
  35.6 17.8 %collective-permute-start.11 = (bf16[128,1536]{1,0:T(8,128)(2,1)}, bf16[128,1536]{1,0:T(8,128)(2,1)S(1)}, u32[]{:S(2)}, u32[]{:S(2)}) collective-permute-start(bf16[128,1536]{1,0:T(8,128)(2,1)} %get-tuple-element.132), channel_id=1, source_target_pairs={{0,6},{2,4},{4,2},{6,0},{8,14},{10,12},{12,10},{14,8},{16,22},{18,... | collective-permute-start | bytes 1179656 | tf_op jit(solution)/shard_map/ppermute | solution.py:393
  35.6 17.8 %collective-permute-start.9 = (bf16[128,1536]{1,0:T(8,128)(2,1)}, bf16[128,1536]{1,0:T(8,128)(2,1)S(1)}, u32[]{:S(2)}, u32[]{:S(2)}) collective-permute-start(bf16[128,1536]{1,0:T(8,128)(2,1)} %get-tuple-element.130), channel_id=1, source_target_pairs={{0,2},{2,0},{4,6},{6,4},{8,10},{10,8},{12,14},{14,12},{16,18},{18,... | collective-permute-start | bytes 1179656 | tf_op jit(solution)/shard_map/ppermute | solution.py:393
  37.2 8.7 %collective-permute-start.13 = (bf16[512,256]{1,0:T(8,128)(2,1)S(1)}, bf16[512,256]{1,0:T(8,128)(2,1)S(1)}, u32[]{:S(2)}, u32[]{:S(2)}) collective-permute-start(bf16[512,256]{1,0:T(8,128)(2,1)S(1)} %stack_keys_fwd.1.refs_4_), channel_id=1, source_target_pairs={{0,24},{2,26},{4,28},{6,30},{8,0},{10,2},{12,4},{14,6},{16,8},{18,... | collective-permute-start | bytes 786440 | tf_op jit(solution)/shard_map/ppermute | solution.py:399
  39.0 13.0 %collective-permute-start.12 = (bf16[512,256]{1,0:T(8,128)(2,1)S(1)}, bf16[512,256]{1,0:T(8,128)(2,1)S(1)}, u32[]{:S(2)}, u32[]{:S(2)}) collective-permute-start(bf16[512,256]{1,0:T(8,128)(2,1)S(1)} %stack_keys_fwd.1.refs_4_), channel_id=1, source_target_pairs={{0,8},{2,10},{4,12},{6,14},{8,16},{10,18},{12,20},{14,22},{16,24},... | collective-permute-start | bytes 786440 | tf_op jit(solution)/shard_map/ppermute | solution.py:399
  52.0 9.1 %collective-permute-start.15 = (bf16[512,256]{1,0:T(8,128)(2,1)S(1)}, bf16[512,256]{1,0:T(8,128)(2,1)S(1)}, u32[]{:S(2)}, u32[]{:S(2)}) collective-permute-start(bf16[512,256]{1,0:T(8,128)(2,1)S(1)} %collective-permute-done.12.refs_5_), channel_id=1, source_target_pairs={{0,8},{2,10},{4,12},{6,14},{8,16},{10,18},{12,20},{14,22},{16,24},... | collective-permute-start | bytes 786440 | tf_op jit(solution)/shard_map/ppermute | solution.py:399
  52.8 7.2 %collective-permute-start.16 = (bf16[128,512]{1,0:T(8,128)(2,1)S(1)}, bf16[128,512]{1,0:T(8,128)(2,1)S(1)}, u32[]{:S(2)}, u32[]{:S(2)}) collective-permute-start(bf16[128,512]{1,0:T(8,128)(2,1)S(1)} %get-tuple-element.154), channel_id=1, source_target_pairs={{0,4},{2,6},{4,0},{6,2},{8,12},{10,14},{12,8},{14,10},{16,20},{18,... | collective-permute-start | bytes 393224 | tf_op jit(solution)/shard_map/ppermute | solution.py:393
  61.1 10.2 %collective-permute-start.17 = (bf16[512,256]{1,0:T(8,128)(2,1)S(1)}, bf16[512,256]{1,0:T(8,128)(2,1)S(1)}, u32[]{:S(2)}, u32[]{:S(2)}) collective-permute-start(bf16[512,256]{1,0:T(8,128)(2,1)S(1)} %get-tuple-element.163), channel_id=1, source_target_pairs={{0,8},{2,10},{4,12},{6,14},{8,16},{10,18},{12,20},{14,22},{16,24},... | collective-permute-start | bytes 786440 | tf_op jit(solution)/shard_map/ppermute | solution.py:399
  61.6 8.1 %collective-permute-start.18 = (bf16[128,512]{1,0:T(8,128)(2,1)S(1)}, bf16[128,512]{1,0:T(8,128)(2,1)S(1)}, u32[]{:S(2)}, u32[]{:S(2)}) collective-permute-start(bf16[128,512]{1,0:T(8,128)(2,1)S(1)} %get-tuple-element.165), channel_id=1, source_target_pairs={{0,2},{2,0},{4,6},{6,4},{8,10},{10,8},{12,14},{14,12},{16,18},{18,... | collective-permute-start | bytes 393224 | tf_op jit(solution)/shard_map/ppermute | solution.py:393
  61.6 8.1 %collective-permute-start.19 = (bf16[128,512]{1,0:T(8,128)(2,1)S(1)}, bf16[128,512]{1,0:T(8,128)(2,1)S(1)}, u32[]{:S(2)}, u32[]{:S(2)}) collective-permute-start(bf16[128,512]{1,0:T(8,128)(2,1)S(1)} %get-tuple-element.167), channel_id=1, source_target_pairs={{0,6},{2,4},{4,2},{6,0},{8,14},{10,12},{12,10},{14,8},{16,22},{18,... | collective-permute-start | bytes 393224 | tf_op jit(solution)/shard_map/ppermute | solution.py:393
  63.2 12.6 %collective-permute-start.25 = (bf16[512,256]{1,0:T(8,128)(2,1)S(1)}, bf16[512,256]{1,0:T(8,128)(2,1)S(1)}, u32[]{:S(2)}, u32[]{:S(2)}) collective-permute-start(bf16[512,256]{1,0:T(8,128)(2,1)S(1)} %get-tuple-element.185), channel_id=1, source_target_pairs={{0,24},{2,26},{4,28},{6,30},{8,0},{10,2},{12,4},{14,6},{16,8},{18,... | collective-permute-start | bytes 786440 | tf_op jit(solution)/shard_map/ppermute | solution.py:399
  71.3 9.2 %collective-permute-start.24 = (bf16[512,256]{1,0:T(8,128)(2,1)S(1)}, bf16[512,256]{1,0:T(8,128)(2,1)S(1)}, u32[]{:S(2)}, u32[]{:S(2)}) collective-permute-start(bf16[512,256]{1,0:T(8,128)(2,1)S(1)} %add_convert_fusion), channel_id=1, source_target_pairs={{0,8},{2,10},{4,12},{6,14},{8,16},{10,18},{12,20},{14,22},{16,24},... | collective-permute-start | bytes 786440 | tf_op jit(solution)/shard_map/ppermute | solution.py:399
  71.4 12.0 %collective-permute-start.20 = (bf16[128,512]{1,0:T(8,128)(2,1)S(1)}, bf16[128,512]{1,0:T(8,128)(2,1)S(1)}, u32[]{:S(2)}, u32[]{:S(2)}) collective-permute-start(bf16[128,512]{1,0:T(8,128)(2,1)S(1)} %get-tuple-element.168), channel_id=1, source_target_pairs={{0,1},{1,0},{2,3},{3,2},{4,5},{5,4},{6,7},{7,6},{8,9},{9,8},{10,11... | collective-permute-start | bytes 393224 | tf_op jit(solution)/shard_map/ppermute | solution.py:410
  71.9 12.3 %collective-permute-start.21 = (bf16[128,512]{1,0:T(8,128)(2,1)S(1)}, bf16[128,512]{1,0:T(8,128)(2,1)S(1)}, u32[]{:S(2)}, u32[]{:S(2)}) collective-permute-start(bf16[128,512]{1,0:T(8,128)(2,1)S(1)} %get-tuple-element.169), channel_id=1, source_target_pairs={{0,3},{1,2},{2,1},{3,0},{4,7},{5,6},{6,5},{7,4},{8,11},{9,10},{10,... | collective-permute-start | bytes 393224 | tf_op jit(solution)/shard_map/ppermute | solution.py:410
  71.9 12.3 %collective-permute-start.22 = (bf16[128,512]{1,0:T(8,128)(2,1)S(1)}, bf16[128,512]{1,0:T(8,128)(2,1)S(1)}, u32[]{:S(2)}, u32[]{:S(2)}) collective-permute-start(bf16[128,512]{1,0:T(8,128)(2,1)S(1)} %get-tuple-element.170), channel_id=1, source_target_pairs={{0,5},{1,4},{2,7},{3,6},{4,1},{5,0},{6,3},{7,2},{8,13},{9,12},{10,... | collective-permute-start | bytes 393224 | tf_op jit(solution)/shard_map/ppermute | solution.py:410
  75.8 8.5 %collective-permute-start.23 = (bf16[128,512]{1,0:T(8,128)(2,1)S(1)}, bf16[128,512]{1,0:T(8,128)(2,1)S(1)}, u32[]{:S(2)}, u32[]{:S(2)}) collective-permute-start(bf16[128,512]{1,0:T(8,128)(2,1)S(1)} %get-tuple-element.171), channel_id=1, source_target_pairs={{0,7},{1,6},{2,5},{3,4},{4,3},{5,2},{6,1},{7,0},{8,15},{9,14},{10,... | collective-permute-start | bytes 393224 | tf_op jit(solution)/shard_map/ppermute | solution.py:410
  80.6 1.3 %collective-permute-start.26 = (bf16[128,256]{1,0:T(8,128)(2,1)S(1)}, bf16[128,256]{1,0:T(8,128)(2,1)S(1)}, u32[]{:S(2)}, u32[]{:S(2)}) collective-permute-start(bf16[128,256]{1,0:T(8,128)(2,1)S(1)} %get-tuple-element.187), channel_id=1, source_target_pairs={{0,2},{2,0},{4,6},{6,4},{8,10},{10,8},{12,14},{14,12},{16,18},{18,... | collective-permute-start | bytes 196616 | tf_op jit(solution)/shard_map/ppermute | solution.py:393
  81.9 4.3 %collective-permute-start.27 = (bf16[128,256]{1,0:T(8,128)(2,1)S(1)}, bf16[128,256]{1,0:T(8,128)(2,1)S(1)}, u32[]{:S(2)}, u32[]{:S(2)}) collective-permute-start(bf16[128,256]{1,0:T(8,128)(2,1)S(1)} %get-tuple-element.192), channel_id=1, source_target_pairs={{0,4},{2,6},{4,0},{6,2},{8,12},{10,14},{12,8},{14,10},{16,20},{18,... | collective-permute-start | bytes 196616 | tf_op jit(solution)/shard_map/ppermute | solution.py:393
  83.4 4.3 %collective-permute-start.28 = (bf16[128,256]{1,0:T(8,128)(2,1)S(1)}, bf16[128,256]{1,0:T(8,128)(2,1)S(1)}, u32[]{:S(2)}, u32[]{:S(2)}) collective-permute-start(bf16[128,256]{1,0:T(8,128)(2,1)S(1)} %get-tuple-element.193), channel_id=1, source_target_pairs={{0,6},{2,4},{4,2},{6,0},{8,14},{10,12},{12,10},{14,8},{16,22},{18,... | collective-permute-start | bytes 196616 | tf_op jit(solution)/shard_map/ppermute | solution.py:393
